TPU v7x, 256 devices: a whole 4x4x8 slice. The times are simulated.
256 devices in a mesh: patch: 2 (over core), lat: 8 (over z), lon: 16 (over y, x).
Axes of the slice: x: 4, y: 4, z: 8, core: 2. Of those that a mesh axis runs over, the one named last changes fastest.
Arguments:
- flow_vector: float32 [3, 2, 2, 1024, 2048], P(None, 'patch', None, 'lat', 'lon'), may hold values from -6 to 6
- normal_stress: float32 [2, 2, 1024, 2048], P('patch', None, 'lat', 'lon'), may hold values from -6 to 6
- thermal_field: float32 [2, 2, 1024, 2048], P('patch', None, 'lat', 'lon'), may hold values from 0 to 1
- shear_resistance: float32 [2, 2, 1024, 2048], P('patch', None, 'lat', 'lon'), may hold values from 0.1 to 10
- departing_bands: int32 [2, 8, 16, 1], P('patch', 'lat', 'lon'), may hold values from 0 to 127, as said below
- receiving_processor: int32 [2, 8, 16, 1], P('patch', 'lat', 'lon'), may hold values from -1 to 127, as said below
- shift_filled_by_lane: int32 [2, 8, 16, 128], P('patch', 'lat', 'lon'), may hold values from 0 to 8, as said below
- blending_factors: float32 [2, 8, 16, 8, 128, 128], P('patch', 'lat', 'lon'), may hold values from -2 to 2, as said below
Outputs:
- velocity_out: float32 [3, 2, 2, 1024, 2048], P(None, 'patch', None, 'lat', 'lon')
- pressure_out: float32 [2, 2, 1024, 2048], P('patch', None, 'lat', 'lon')
- temperature_out: float32 [2, 2, 1024, 2048], P('patch', None, 'lat', 'lon')
Inputs may be any that keep to these rules, and one draw needn't show every extreme that they name: `departing_bands`: A row of the sending device's own 128 rows. `receiving_processor`: the flat number a * 16 + b of the device of the other patch that receives the slot, or -1 for an unused slot. A device uses at most 1 slots; some device uses all of them. Consistent with shift_filled_by_lane. `shift_filled_by_lane`: entry q + s of device d names the offset side * 2 + t that slot s of device q of the other patch fills at d, or 8 if that slot fills nothing at d. Sides 0, 1, 2, 3 are the ghost row before the first row, after the last row, the ghost column before the first column and after the last column. A side is filled exactly where it lies on the patch's edge, and then each of its 2 offsets is named by exactly one entry. `blending_factors`: dense interpolation weights, a matrix of 128 by 128 for each offset.
All inputs are finite; a program needn't handle non-finite values.
Results may differ from a plain program's by a relative error of at most 0.0001.
Values sent between devices are 32-bit elements; how exact they have to be, the bound alone decides.
No kernel may reach another device: no remote copies, remote signals or barrier semaphores. Data moves between devices by JAX's collectives and lax.ppermute only.
A program may use at most 64 MiB of HBM per device.

v0:
```python
import jax
import jax.numpy as jnp
from jax import lax
from jax.sharding import PartitionSpec as P

SWEEPS = 4


PRECISE = lax.Precision.HIGHEST


def from_partner(value, axis, bit):
    mask = 2**bit
    pairs = [(source, source ^ mask) for source in range(lax.axis_size(axis))]
    return lax.ppermute(value, axis, pairs)


def padded(cells, sides, width):
    for axis, dim in sides:
        count = lax.axis_size(axis)
        ends = count - 1
        head = lax.slice_in_dim(cells, 0, width, axis=dim)
        tail = lax.slice_in_dim(cells, cells.shape[dim] - width, cells.shape[dim], axis=dim)
        cells = jnp.concatenate(
            [
                lax.ppermute(tail, axis, [(i, (i + 1) % count) for i in range(ends)]),
                cells,
                lax.ppermute(head, axis, [((i + 1) % count, i) for i in range(ends)]),
            ],
            axis=dim,
        )
    return cells


def neighbours(bordered_mesh):
    return (
        bordered_mesh[..., 2:, 1:-1, 1:-1],
        bordered_mesh[..., :-2, 1:-1, 1:-1],
        bordered_mesh[..., 1:-1, 2:, 1:-1],
        bordered_mesh[..., 1:-1, :-2, 1:-1],
        bordered_mesh[..., 1:-1, 1:-1, 2:],
        bordered_mesh[..., 1:-1, 1:-1, :-2],
    )


def widen_sector(
    stack, departing_bands, receiving_processor, shift_filled_by_lane, blending_factors
):
    field_count = stack.shape[0]
    layer_count = stack.shape[1]
    cell_count = stack.shape[3]
    most_slots = departing_bands.shape[-1]
    total_slots = shift_filled_by_lane.shape[-1]
    offset_count = blending_factors.shape[3]
    row_ids = departing_bands.reshape(most_slots)
    blocks = jnp.take(stack, row_ids, axis=2)
    slot_ids = shift_filled_by_lane.reshape(total_slots)
    peer_ids = receiving_processor.reshape(most_slots)
    my_flat = lax.axis_index("lat") * lax.axis_size("lon") + lax.axis_index("lon")
    offset_range = jnp.arange(offset_count, dtype=jnp.int32)[None, :]
    peer_marks = peer_ids.astype(jnp.float32).reshape(1, 1, most_slots, 1)
    crossed = from_partner((blocks, peer_marks), "patch", 0)
    arrived_blocks = lax.all_gather(crossed[0], ("lat", "lon"), axis=2, tiled=True)
    arrived_peers = lax.all_gather(crossed[1], ("lat", "lon"), axis=2, tiled=True)
    reach = arrived_peers.reshape(arrived_blocks.shape[2]) == my_flat.astype(jnp.float32)
    one_hot = ((slot_ids[:, None] == offset_range) & reach[:, None]).astype(jnp.float32)
    chosen = jnp.einsum("fkjc,jo->fkoc", arrived_blocks, one_hot, precision=PRECISE)
    weights = blending_factors.reshape(offset_count, cell_count, cell_count)
    cycle_vals = jnp.einsum("ojc,fkoc->fkoj", weights, chosen, precision=PRECISE)
    cycle_vals = cycle_vals.reshape(field_count, layer_count, 4, offset_count // 4, cell_count).sum(
        axis=3
    )
    bordered_mesh = padded(stack, (("lat", 2), ("lon", 3)), 1)
    bordered_mesh = jnp.pad(bordered_mesh, ((0, 0), (1, 1), (0, 0), (0, 0)))
    bordered_mesh = bordered_mesh.at[:, 1:-1, 0, 1:-1].add(cycle_vals[:, :, 0])
    bordered_mesh = bordered_mesh.at[:, 1:-1, -1, 1:-1].add(cycle_vals[:, :, 1])
    bordered_mesh = bordered_mesh.at[:, 1:-1, 1:-1, 0].add(cycle_vals[:, :, 2])
    bordered_mesh = bordered_mesh.at[:, 1:-1, 1:-1, -1].add(cycle_vals[:, :, 3])
    return bordered_mesh


def creeping_flow_relaxation(
    bordered_mesh,
    earth_interior_fields,
    thermal_mesh,
    resistive_friction,
    boundary_entries,
    main_coefficient,
):
    adjacent_neighbour_entry = neighbours(bordered_mesh)
    second_derivative_sum = sum(
        (
            face * (other - earth_interior_fields)
            for face, other in zip(boundary_entries, adjacent_neighbour_entry)
        )
    )
    middle_entry = [
        (adjacent_neighbour_entry[2 * axis_extent] - adjacent_neighbour_entry[2 * axis_extent + 1])
        * 0.5
        for axis_extent in range(3)
    ]
    divergence = middle_entry[0][0] + middle_entry[1][1] + middle_entry[2][2]
    depthwise = (
        earth_interior_fields[0]
        + 0.8
        * (1.0 * thermal_mesh + second_derivative_sum[0] - middle_entry[0][3])
        / main_coefficient
    )
    colat = (
        earth_interior_fields[1]
        + 0.8 * (second_derivative_sum[1] - middle_entry[1][3]) / main_coefficient
    )
    longit = (
        earth_interior_fields[2]
        + 0.8 * (second_derivative_sum[2] - middle_entry[2][3]) / main_coefficient
    )
    pressure_new = earth_interior_fields[3] - 0.25 * resistive_friction * divergence
    return jnp.stack([depthwise, colat, longit, pressure_new])


def heat_update(bordered_mesh, thermal_mesh, carried_along):
    adjacent_neighbour_entry = neighbours(bordered_mesh)
    transport_flow = jnp.zeros_like(thermal_mesh)
    for axis_extent in range(3):
        flow_magnitude = carried_along[axis_extent]
        transport_flow = transport_flow + jnp.maximum(flow_magnitude, 0.0) * (
            thermal_mesh - adjacent_neighbour_entry[2 * axis_extent + 1]
        )
        transport_flow = transport_flow + jnp.minimum(flow_magnitude, 0.0) * (
            adjacent_neighbour_entry[2 * axis_extent] - thermal_mesh
        )
    second_derivative_sum = sum(adjacent_neighbour_entry) - 6.0 * thermal_mesh
    return thermal_mesh + 0.1 * (1.0 * second_derivative_sum - transport_flow)


def shards(
    flow_vector,
    normal_stress,
    thermal_field,
    shear_resistance,
    departing_bands,
    receiving_processor,
    shift_filled_by_lane,
    blending_factors,
):
    resistive_friction = shear_resistance[0]
    thermal_mesh = thermal_field[0]
    rim = padded(resistive_friction, (("lat", 1), ("lon", 2)), 1)
    lat_pos = lax.axis_index("lat")
    lon_pos = lax.axis_index("lon")
    rim = rim.at[:, 0, 1:-1].set(
        jnp.where(lat_pos == 0, resistive_friction[:, 0, :], rim[:, 0, 1:-1])
    )
    rim = rim.at[:, -1, 1:-1].set(
        jnp.where(
            lat_pos == lax.axis_size("lat") - 1, resistive_friction[:, -1, :], rim[:, -1, 1:-1]
        )
    )
    rim = rim.at[:, 1:-1, 0].set(
        jnp.where(lon_pos == 0, resistive_friction[:, :, 0], rim[:, 1:-1, 0])
    )
    rim = rim.at[:, 1:-1, -1].set(
        jnp.where(
            lon_pos == lax.axis_size("lon") - 1, resistive_friction[:, :, -1], rim[:, 1:-1, -1]
        )
    )
    rim = jnp.concatenate([rim[:1], rim, rim[-1:]], axis=0)
    boundary_entries = tuple((0.5 * (resistive_friction + other) for other in neighbours(rim)))
    main_coefficient = sum(boundary_entries)
    earth_interior_fields = jnp.concatenate([flow_vector[:, 0], normal_stress], axis=0)
    for sweep in range(SWEEPS):
        bordered_mesh = widen_sector(
            earth_interior_fields,
            departing_bands,
            receiving_processor,
            shift_filled_by_lane,
            blending_factors,
        )
        earth_interior_fields = creeping_flow_relaxation(
            bordered_mesh,
            earth_interior_fields,
            thermal_mesh,
            resistive_friction,
            boundary_entries,
            main_coefficient,
        )
    bordered_heat = widen_sector(
        thermal_mesh[None],
        departing_bands,
        receiving_processor,
        shift_filled_by_lane,
        blending_factors,
    )[0]
    bordered_heat = bordered_heat.at[..., 0, :, :].set(1.0)
    thermal_following = heat_update(bordered_heat, thermal_mesh, earth_interior_fields[:3])
    return (earth_interior_fields[:3][:, None], earth_interior_fields[3:4], thermal_following[None])


def solution(mesh):
    placed = (
        P(None, "patch", None, "lat", "lon"),
        P("patch", None, "lat", "lon"),
        P("patch", None, "lat", "lon"),
        P("patch", None, "lat", "lon"),
        P("patch", "lat", "lon", None),
        P("patch", "lat", "lon", None),
        P("patch", "lat", "lon", None),
        P("patch", "lat", "lon", None, None, None),
    )
    return jax.shard_map(
        shards,
        mesh=mesh,
        in_specs=placed,
        out_specs=(
            P(None, "patch", None, "lat", "lon"),
            P("patch", None, "lat", "lon"),
            P("patch", None, "lat", "lon"),
        ),
        check_vma=False,
    )
```

profile of v0, /device:TPU:2, one launch (start us, length us, event | category | flops | bytes accessed | tf_op | source)
XLA Modules:
  0.0 2248.9 jit_solution(15598011311853440232)
XLA Ops:
  1.4 3.8 collective-permute-start
  6.8 3.8 collective-permute-start.4
  10.6 1.3 collective-permute-start.5
  12.6 1.4 collective-permute-start.8
  16.7 4.6 collective-permute-start.25
  21.2 1.3 bitcast_dynamic-update-slice_fusion
  22.6 342.6 %all-reduce.5 = f32[128]{0:T(128)S(1)} all-reduce(f32[128]{0:T(128)S(1)} %bitcast_dynamic-update-slice_fusion), channel_id=1, replica_groups=mesh['patch'=2,'lat'=8,'lon'=16] {'lat','lon'}, use_global_device_ids=true, to_apply=%add.5 | all-reduce | flops 128 | bytes 1024
  365.2 1.3 collective-permute-start.26
  367.2 3.5 collective-permute-done.26
  373.0 2.6 collective-permute-start.27
  375.5 342.8 %all_gather.27 = f32[1,2,128,128]{3,1,0,2:T(2,128)S(1)} all-gather(f32[1,2,1,128]{3,1,0,2:T(2,128)S(1)} %collective-permute-done.29), channel_id=1, replica_groups=mesh['patch'=2,'lat'=8,'lon'=16] {'lat','lon'}, dimensions={2}, use_global_device_ids=true | all-gather | bytes 132096 | tf_op jit(solution)/shard_map/all_gather | solution.py:63
  720.1 1.9 collective-permute-start.28
  722.2 3.9 collective-permute-start.2
  727.1 1.9 collective-permute-start.3
  730.1 1.6 scatter-add.94
  731.7 1.3 fusion.153
  733.8 1.6 scatter-add.95
  735.6 1.7 scatter.16
  741.3 3.9 collective-permute-start.6
  745.5 1.9 collective-permute-start.7
  747.5 340.1 %all_gather.23 = f32[4,2,128,128]{3,0,1,2:T(4,128)S(1)} all-gather(f32[4,2,1,128]{3,0,1,2:T(4,128)S(1)} %copy.372), channel_id=1, replica_groups=mesh['patch'=2,'lat'=8,'lon'=16] {'lat','lon'}, dimensions={2}, use_global_device_ids=true | all-gather | bytes 528384 | tf_op jit(solution)/shard_map/all_gather | solution.py:63
  1093.1 1.8 select_maximum_fusion
  1094.9 1.4 scatter-add.66
  1096.4 1.4 scatter-add.69
  1097.7 1.9 slice_add_fusion.7
  1099.6 2.8 scatter-add.70
  1102.5 2.0 slice_add_fusion.6
  1104.5 4.0 scatter-add.71
  1108.8 2.1 subtract_multiply_fusion.10
  1112.9 1.6 scatter-add.96
  1116.6 1.3 collective-permute-start.11
  1117.9 343.1 %all_gather.24 = f32[4,2,128,128]{3,0,1,2:T(4,128)S(1)} all-gather(f32[4,2,1,128]{3,0,1,2:T(4,128)S(1)} %copy.385), channel_id=1, replica_groups=mesh['patch'=2,'lat'=8,'lon'=16] {'lat','lon'}, dimensions={2}, use_global_device_ids=true | all-gather | bytes 528384 | tf_op jit(solution)/shard_map/all_gather | solution.py:63
  1462.9 1.9 collective-permute-start.12
  1465.2 4.8 collective-permute-start.13
  1473.3 1.4 scatter-add.74
  1474.8 1.4 scatter-add.75
  1476.2 1.9 slice_add_fusion.5
  1478.1 2.9 scatter-add.76
  1481.1 2.0 slice_add_fusion.4
  1483.1 4.0 scatter-add.79
  1487.2 1.9 multiply_add_fusion.2
  1492.2 2.0 scatter-add.99
  1495.5 1.3 collective-permute-start.16
  1496.8 341.2 %all_gather.25 = f32[4,2,128,128]{3,0,1,2:T(4,128)S(1)} all-gather(f32[4,2,1,128]{3,0,1,2:T(4,128)S(1)} %copy.398), channel_id=1, replica_groups=mesh['patch'=2,'lat'=8,'lon'=16] {'lat','lon'}, dimensions={2}, use_global_device_ids=true | all-gather | bytes 528384 | tf_op jit(solution)/shard_map/all_gather | solution.py:63
  1839.9 1.9 collective-permute-start.17
  1842.2 6.3 collective-permute-start.18
  1851.9 1.4 scatter-add.80
  1853.4 1.4 scatter-add.81
  1854.8 1.9 slice_add_fusion.3
  1856.7 2.8 scatter-add.84
  1859.5 2.0 slice_add_fusion.2
  1861.6 4.0 scatter-add.85
  1865.6 2.1 multiply_add_fusion.1
  1872.3 1.3 collective-permute-start.21
  1873.6 341.6 %all_gather.26 = f32[4,2,128,128]{3,0,1,2:T(4,128)S(1)} all-gather(f32[4,2,1,128]{3,0,1,2:T(4,128)S(1)} %copy.411), channel_id=1, replica_groups=mesh['patch'=2,'lat'=8,'lon'=16] {'lat','lon'}, dimensions={2}, use_global_device_ids=true | all-gather | bytes 528384 | tf_op jit(solution)/shard_map/all_gather | solution.py:63
  2217.1 1.9 collective-permute-start.22
  2219.3 6.1 collective-permute-start.23
  2228.8 1.4 scatter-add.86
  2230.3 1.4 scatter-add.89
  2231.6 1.9 slice_add_fusion.1
  2233.5 2.8 scatter-add.90
  2236.4 2.0 slice_add_fusion
  2238.4 4.0 scatter-add.91
  2245.3 2.6 fusion.101
  (261 shorter events, 55.0 us)
Async XLA Ops:
  0.6 718.5 %copy-start = (f32[1,1,1,8,128,128]{5,4,3,2,1,0:T(8,128)S(1)}, f32[1,1,1,8,128,128]{5,4,3,2,1,0:T(8,128)}, u32[]{:S(2)}) copy-start(f32[1,1,1,8,128,128]{5,4,3,2,1,0:T(8,128)} %param.67) | copy-start | bytes 1572868
  0.6 721.4 %copy-start.1 = (f32[1,2,128,128]{3,2,1,0:T(8,128)S(1)}, f32[1,2,128,128]{3,2,1,0:T(8,128)}, u32[]{:S(2)}) copy-start(f32[1,2,128,128]{3,2,1,0:T(8,128)} %param.63) | copy-start | bytes 393220
  0.7 728.4 %copy-start.3 = (f32[1,2,128,128]{3,2,1,0:T(8,128)S(1)}, f32[1,2,128,128]{3,2,1,0:T(8,128)}, u32[]{:S(2)}) copy-start(f32[1,2,128,128]{3,2,1,0:T(8,128)} %param.62) | copy-start | bytes 393220
  1.4 363.7 %collective-permute-start = (f32[2,1,128]{2,1,0:T(1,128)S(1)}, f32[2,1,128]{2,1,0:T(1,128)S(1)}, u32[]{:S(2)}, u32[]{:S(2)}) collective-permute-start(f32[2,1,128]{2,1,0:T(1,128)S(1)} %slice.1368), channel_id=1, source_target_pairs={{0,16},{16,32},{32,48},{48,64},{64,80},{80,96},{96,112},{1,17},{17... | collective-permute-start | bytes 3080 | tf_op jit(solution)/shard_map/ppermute | solution.py:26
  6.8 733.9 %collective-permute-start.4 = (f32[4,2,1,128]{3,2,1,0:T(1,128)S(1)}, f32[4,2,1,128]{3,2,1,0:T(1,128)S(1)}, u32[]{:S(2)}, u32[]{:S(2)}) collective-permute-start(f32[4,2,1,128]{3,2,1,0:T(1,128)S(1)} %get-tuple-element.390), channel_id=1, source_target_pairs={{0,16},{16,32},{32,48},{48,64},{64,80},{80,96},{96,112},{1,17},{17... | collective-permute-start | bytes 12296 | tf_op jit(solution)/shard_map/ppermute | solution.py:26
  10.6 730.0 %collective-permute-start.5 = (f32[4,2,1,128]{3,2,1,0:T(1,128)S(1)}, f32[4,2,1,128]{3,2,1,0:T(1,128)S(1)}, u32[]{:S(2)}, u32[]{:S(2)}) collective-permute-start(f32[4,2,1,128]{3,2,1,0:T(1,128)S(1)} %get-tuple-element.391), channel_id=1, source_target_pairs={{16,0},{32,16},{48,32},{64,48},{80,64},{96,80},{112,96},{17,1},{33... | collective-permute-start | bytes 12296 | tf_op jit(solution)/shard_map/ppermute | solution.py:28
  11.9 735.6 %collective-permute-start.9 = (f32[4,2,1,128]{3,2,1,0:T(1,128)S(1)}, f32[4,2,1,128]{3,2,1,0:T(1,128)S(1)}, u32[]{:S(2)}, u32[]{:S(2)}) collective-permute-start(f32[4,2,1,128]{3,2,1,0:T(1,128)S(1)} %get-tuple-element.389), channel_id=1, source_target_pairs={{0,128},{128,0},{1,129},{129,1},{2,130},{130,2},{3,131},{131,3},{4... | collective-permute-start | bytes 12296 | tf_op jit(solution)/shard_map/ppermute | solution.py:15
  12.6 4.0 collective-permute-start.8
  16.7 350.5 %collective-permute-start.25 = (f32[1,2,1,128]{3,2,1,0:T(1,128)S(1)}, f32[1,2,1,128]{3,2,1,0:T(1,128)S(1)}, u32[]{:S(2)}, u32[]{:S(2)}) collective-permute-start(f32[1,2,1,128]{3,2,1,0:T(1,128)S(1)} %get-tuple-element.408), channel_id=1, source_target_pairs={{0,16},{16,32},{32,48},{48,64},{64,80},{80,96},{96,112},{1,17},{17... | collective-permute-start | bytes 3080 | tf_op jit(solution)/shard_map/ppermute | solution.py:26
  365.2 722.4 %copy-start.51 = (pred[128]{0:T(512)(128)(4,1)}, pred[128]{0:T(512)(128)(4,1)S(1)}, u32[]{:S(2)}) copy-start(pred[128]{0:T(512)(128)(4,1)S(1)} %broadcast_compare_fusion) | copy-start | bytes 388
  365.2 5.5 collective-permute-start.26
  367.2 5.8 collective-permute-start.29
  370.6 349.5 %collective-permute-start.1 = (f32[2,1,128]{2,1,0:T(1,128)S(1)}, f32[2,1,128]{2,1,0:T(1,128)S(1)}, u32[]{:S(2)}, u32[]{:S(2)}) collective-permute-start(f32[2,1,128]{2,1,0:T(1,128)S(1)} %get-tuple-element.405), channel_id=1, source_target_pairs={{16,0},{32,16},{48,32},{64,48},{80,64},{96,80},{112,96},{17,1},{33... | collective-permute-start | bytes 3080 | tf_op jit(solution)/shard_map/ppermute | solution.py:28
  373.0 349.2 %collective-permute-start.27 = (f32[1,2,130,1]{3,2,1,0:T(8,128)S(1)}, f32[1,2,130,1]{3,2,1,0:T(8,128)S(1)}, u32[]{:S(2)}, u32[]{:S(2)}) collective-permute-start(f32[1,2,130,1]{3,2,1,0:T(8,128)S(1)} %get-tuple-element.402), channel_id=1, source_target_pairs={{0,1},{1,2},{2,3},{3,4},{4,5},{5,6},{6,7},{7,8},{8,9},{9,10},{10,1... | collective-permute-start | bytes 3128 | tf_op jit(solution)/shard_map/ppermute | solution.py:26
  720.1 7.0 collective-permute-start.28
  722.2 13.2 collective-permute-start.2
  727.1 8.3 collective-permute-start.3
  735.4 5.2 copy-start.2
  735.4 5.3 copy-start.39
  740.6 370.3 %copy-start.5 = (f32[2,128,128]{2,1,0:T(8,128)}, f32[2,128,128]{2,1,0:T(8,128)S(1)}, u32[]{:S(2)}) copy-start(f32[2,128,128]{2,1,0:T(8,128)S(1)} %get-tuple-element.392) | copy-start | bytes 393220
  740.6 347.0 %copy-start.49 = (s32[1,1,1,128]{3,2,1,0:T(1,128)S(1)}, s32[1,1,1,128]{3,2,1,0:T(1,128)}, u32[]{:S(2)}) copy-start(s32[1,1,1,128]{3,2,1,0:T(1,128)} %param.66) | copy-start | bytes 1540
  741.3 349.7 %collective-permute-start.6 = (f32[4,2,130,1]{2,0,3,1:T(4,128)S(1)}, f32[4,2,130,1]{2,0,3,1:T(4,128)S(1)}, u32[]{:S(2)}, u32[]{:S(2)}) collective-permute-start(f32[4,2,130,1]{2,0,3,1:T(4,128)S(1)} %copy.368), channel_id=1, source_target_pairs={{0,1},{1,2},{2,3},{3,4},{4,5},{5,6},{6,7},{7,8},{8,9},{9,10},{10,1... | collective-permute-start | bytes 12488 | tf_op jit(solution)/shard_map/ppermute | solution.py:26
  745.5 346.5 %collective-permute-start.7 = (f32[4,2,130,1]{2,0,3,1:T(4,128)S(1)}, f32[4,2,130,1]{2,0,3,1:T(4,128)S(1)}, u32[]{:S(2)}, u32[]{:S(2)}) collective-permute-start(f32[4,2,130,1]{2,0,3,1:T(4,128)S(1)} %copy.369), channel_id=1, source_target_pairs={{1,0},{2,1},{3,2},{4,3},{5,4},{6,5},{7,6},{8,7},{9,8},{10,9},{11,1... | collective-permute-start | bytes 12488 | tf_op jit(solution)/shard_map/ppermute | solution.py:28
  1108.8 2.2 copy-start.7
  1108.8 2.2 copy-start.10
  1108.8 2.1 copy-start.13
  1108.8 2.1 copy-start.15
  1108.8 2.1 copy-start.17
  1108.8 2.3 copy-start.40
  1111.1 361.5 %copy-start.19 = (f32[2,128,128]{2,1,0:T(8,128)}, f32[2,128,128]{2,1,0:T(8,128)S(1)}, u32[]{:S(2)}) copy-start(f32[2,128,128]{2,1,0:T(8,128)S(1)} %get-tuple-element.348) | copy-start | bytes 393220
  1111.1 3.4 copy-start.53
  1111.1 349.9 %copy-start.50 = (s32[1,1,1,128]{3,2,1,0:T(1,128)S(1)}, s32[1,1,1,128]{3,2,1,0:T(1,128)}, u32[]{:S(2)}) copy-start(s32[1,1,1,128]{3,2,1,0:T(1,128)} %param.66) | copy-start | bytes 1540
  1111.1 349.9 %copy-start.52 = (pred[128]{0:T(512)(128)(4,1)S(1)}, pred[128]{0:T(512)(128)(4,1)}, u32[]{:S(2)}) copy-start(pred[128]{0:T(512)(128)(4,1)} %copy-done.51) | copy-start | bytes 388
  1111.2 361.4 %copy-start.27 = (f32[1,2,128,128]{3,2,1,0:T(8,128)}, f32[1,2,128,128]{3,2,1,0:T(8,128)S(1)}, u32[]{:S(2)}) copy-start(f32[1,2,128,128]{3,2,1,0:T(8,128)S(1)} %fusion.63) | copy-start | bytes 393220
  1111.8 6.1 collective-permute-start.14
  1115.3 347.0 %collective-permute-start.10 = (f32[4,2,1,128]{3,2,1,0:T(1,128)S(1)}, f32[4,2,1,128]{3,2,1,0:T(1,128)S(1)}, u32[]{:S(2)}, u32[]{:S(2)}) collective-permute-start(f32[4,2,1,128]{3,2,1,0:T(1,128)S(1)} %get-tuple-element.388), channel_id=1, source_target_pairs={{0,16},{16,32},{32,48},{48,64},{64,80},{80,96},{96,112},{1,17},{17... | collective-permute-start | bytes 12296 | tf_op jit(solution)/shard_map/ppermute | solution.py:26
  1116.6 345.7 %collective-permute-start.11 = (f32[4,2,1,128]{3,2,1,0:T(1,128)S(1)}, f32[4,2,1,128]{3,2,1,0:T(1,128)S(1)}, u32[]{:S(2)}, u32[]{:S(2)}) collective-permute-start(f32[4,2,1,128]{3,2,1,0:T(1,128)S(1)} %get-tuple-element.387), channel_id=1, source_target_pairs={{16,0},{32,16},{48,32},{64,48},{80,64},{96,80},{112,96},{17,1},{33... | collective-permute-start | bytes 12296 | tf_op jit(solution)/shard_map/ppermute | solution.py:28
  1462.9 9.2 collective-permute-start.12
  1465.2 7.1 collective-permute-start.13
  1478.1 9.0 copy-start.6
  1478.1 9.0 copy-start.8
  1478.1 9.1 copy-start.11
  1489.1 1.8 copy-start.41
  1489.1 1.8 copy-start.46
  1489.2 1.6 copy-start.32
  1490.3 360.9 %copy-start.29 = (f32[1,2,128,128]{3,2,1,0:T(8,128)}, f32[1,2,128,128]{3,2,1,0:T(8,128)S(1)}, u32[]{:S(2)}) copy-start(f32[1,2,128,128]{3,2,1,0:T(8,128)S(1)} %fusion.48) | copy-start | bytes 393220
  1490.9 360.2 %copy-start.35 = (f32[1,2,128,128]{3,2,1,0:T(8,128)}, f32[1,2,128,128]{3,2,1,0:T(8,128)S(1)}, u32[]{:S(2)}) copy-start(f32[1,2,128,128]{3,2,1,0:T(8,128)S(1)} %get-tuple-element.370) | copy-start | bytes 393220
  1490.9 360.2 %copy-start.36 = (f32[1,2,128,128]{3,2,1,0:T(8,128)}, f32[1,2,128,128]{3,2,1,0:T(8,128)S(1)}, u32[]{:S(2)}) copy-start(f32[1,2,128,128]{3,2,1,0:T(8,128)S(1)} %get-tuple-element.371) | copy-start | bytes 393220
  1491.0 5.8 collective-permute-start.19
  1494.2 345.1 %collective-permute-start.15 = (f32[4,2,1,128]{3,2,1,0:T(1,128)S(1)}, f32[4,2,1,128]{3,2,1,0:T(1,128)S(1)}, u32[]{:S(2)}, u32[]{:S(2)}) collective-permute-start(f32[4,2,1,128]{3,2,1,0:T(1,128)S(1)} %get-tuple-element.385), channel_id=1, source_target_pairs={{0,16},{16,32},{32,48},{48,64},{64,80},{80,96},{96,112},{1,17},{17... | collective-permute-start | bytes 12296 | tf_op jit(solution)/shard_map/ppermute | solution.py:26
  1495.5 343.9 %collective-permute-start.16 = (f32[4,2,1,128]{3,2,1,0:T(1,128)S(1)}, f32[4,2,1,128]{3,2,1,0:T(1,128)S(1)}, u32[]{:S(2)}, u32[]{:S(2)}) collective-permute-start(f32[4,2,1,128]{3,2,1,0:T(1,128)S(1)} %get-tuple-element.384), channel_id=1, source_target_pairs={{16,0},{32,16},{48,32},{64,48},{80,64},{96,80},{112,96},{17,1},{33... | collective-permute-start | bytes 12296 | tf_op jit(solution)/shard_map/ppermute | solution.py:28
  1839.9 10.7 collective-permute-start.17
  1842.2 8.7 collective-permute-start.18
  1867.7 2.5 copy-start.43
  1868.2 347.0 %copy-start.45 = (f32[4,2,128,128]{3,2,1,0:T(8,128)}, f32[4,2,128,128]{3,2,1,0:T(8,128)S(1)}, u32[]{:S(2)}) copy-start(f32[4,2,128,128]{3,2,1,0:T(8,128)S(1)} %get-tuple-element.355) | copy-start | bytes 1572868
  1868.8 359.2 %copy-start.25 = (f32[1,2,128,128]{3,2,1,0:T(8,128)}, f32[1,2,128,128]{3,2,1,0:T(8,128)S(1)}, u32[]{:S(2)}) copy-start(f32[1,2,128,128]{3,2,1,0:T(8,128)S(1)} %fusion.33) | copy-start | bytes 393220
  1870.2 357.9 %copy-start.21 = (f32[2,128,128]{2,1,0:T(8,128)}, f32[2,128,128]{2,1,0:T(8,128)S(1)}, u32[]{:S(2)}) copy-start(f32[2,128,128]{2,1,0:T(8,128)S(1)} %get-tuple-element.364) | copy-start | bytes 393220
  1870.2 357.9 %copy-start.23 = (f32[2,128,128]{2,1,0:T(8,128)}, f32[2,128,128]{2,1,0:T(8,128)S(1)}, u32[]{:S(2)}) copy-start(f32[2,128,128]{2,1,0:T(8,128)S(1)} %get-tuple-element.365) | copy-start | bytes 393220
  1870.2 357.9 %copy-start.37 = (f32[1,2,128,128]{3,2,1,0:T(8,128)}, f32[1,2,128,128]{3,2,1,0:T(8,128)S(1)}, u32[]{:S(2)}) copy-start(f32[1,2,128,128]{3,2,1,0:T(8,128)S(1)} %get-tuple-element.368) | copy-start | bytes 393220
  1870.3 3.4 collective-permute-start.24
  1871.0 345.4 %collective-permute-start.20 = (f32[4,2,1,128]{3,2,1,0:T(1,128)S(1)}, f32[4,2,1,128]{3,2,1,0:T(1,128)S(1)}, u32[]{:S(2)}, u32[]{:S(2)}) collective-permute-start(f32[4,2,1,128]{3,2,1,0:T(1,128)S(1)} %get-tuple-element.382), channel_id=1, source_target_pairs={{0,16},{16,32},{32,48},{48,64},{64,80},{80,96},{96,112},{1,17},{17... | collective-permute-start | bytes 12296 | tf_op jit(solution)/shard_map/ppermute | solution.py:26
  1872.3 344.2 %collective-permute-start.21 = (f32[4,2,1,128]{3,2,1,0:T(1,128)S(1)}, f32[4,2,1,128]{3,2,1,0:T(1,128)S(1)}, u32[]{:S(2)}, u32[]{:S(2)}) collective-permute-start(f32[4,2,1,128]{3,2,1,0:T(1,128)S(1)} %get-tuple-element.381), channel_id=1, source_target_pairs={{16,0},{32,16},{48,32},{64,48},{80,64},{96,80},{112,96},{17,1},{33... | collective-permute-start | bytes 12296 | tf_op jit(solution)/shard_map/ppermute | solution.py:28
  2217.1 10.4 collective-permute-start.22
  2219.3 8.4 collective-permute-start.23
  (20 other events, 23.0 us)
where the time goes:
time: 2270 us; the launch traced here: 2250 us
  blocking collectives  2050 us (90%)
  local copies, waits for them, and re-layouts  75.4 us (3%)
  starting transfers between devices  64.7 us (3%)
  other arithmetic  42.4 us (2%)
    all_gather x5, blocking collectives, widen_sector(): lax.all_gather(crossed[0], ('lat', 'lon'), axis=2, tiled=True)  1710 us
    unnamed x1, blocking collectives  343 us
  transfers between devices with their start and end apart: 30, of which 2 were waited for; matrix products, arithmetic and copies ran while one was open for 2% of the time, Pallas kernels for 0%

commit v1 on v0

v1 whole, which is shorter than its diff:
```python
import functools

import jax
import jax.numpy as jnp
from jax import lax
from jax.experimental import pallas as pl
from jax.experimental.pallas import tpu as pltpu
from jax.sharding import PartitionSpec as P

SWEEPS = 4
CELLS = 128
BLOCKS = 16
F32 = jnp.float32
VMEM = pl.BlockSpec(memory_space=pltpu.VMEM)
SMEM = pl.BlockSpec(memory_space=pltpu.SMEM)
PARAMS = pltpu.CompilerParams(vmem_limit_bytes=32 * 1024 * 1024)


def west_lane(f):
    return 2 * f


def east_lane(f):
    return (2 * f - 1) % CELLS


def lanes():
    return lax.broadcasted_iota(jnp.int32, (8, CELLS), 1)


def sublanes():
    return lax.broadcasted_iota(jnp.int32, (8, CELLS), 0)


def roll_lanes(x, shift):
    shift = shift % CELLS
    return x if shift == 0 else pltpu.roll(x, shift, 1)


def ghost_columns(west, east, count, rows_ref, cols_ref):
    for f in range(count):
        rows_ref[west_lane(f), :] = west[f, :]
        rows_ref[east_lane(f), :] = east[f, :]
    cols_ref[...] = rows_ref[...].T


def collect_edges(planes, count, rows_ref, cols_ref, north, south, west, east):
    lane = lanes()
    for b in range(BLOCKS):
        gathered = jnp.zeros((8, CELLS), F32)
        for f in range(count):
            here = planes(f)[8 * b : 8 * b + 8, :]
            mine = (lane == west_lane(f)) | (lane == east_lane(f))
            gathered = jnp.where(mine, roll_lanes(here, 2 * f), gathered)
        cols_ref[8 * b : 8 * b + 8, :] = gathered
    rows_ref[...] = cols_ref[...].T
    for f in range(count):
        west[f, :] = rows_ref[west_lane(f), :]
        east[f, :] = rows_ref[east_lane(f), :]
        north[f, :] = planes(f)[0, :]
        south[f, :] = planes(f)[CELLS - 1, :]


def around(ref, b, north, south, column, f):
    lo = 8 * b
    here = ref[lo : lo + 8, :]
    sub, lane = sublanes(), lanes()
    if b == 0:
        up = jnp.where(sub == 0, north, pltpu.roll(here, 1, 0))
    else:
        up = ref[lo - 1 : lo + 7, :]
    if b == BLOCKS - 1:
        down = jnp.where(sub == 7, south, pltpu.roll(here, 7, 0))
    else:
        down = ref[lo + 1 : lo + 9, :]
    turned = roll_lanes(column, -2 * f)
    left = jnp.where(lane == 0, turned, pltpu.roll(here, 1, 1))
    right = jnp.where(lane == CELLS - 1, turned, pltpu.roll(here, CELLS - 1, 1))
    return here, up, down, left, right


def start_kernel(meta, flow, pressure, heat, friction, row, north, south, west, east, rows_s, cols_s):
    def planes(f):
        if f < 6:
            return flow.at[f]
        if f < 8:
            return pressure.at[f - 6]
        if f < 10:
            return heat.at[f - 8]
        return friction.at[f - 10]

    at = meta[0]
    for f in range(10):
        row[f, :] = planes(f)[pl.ds(at, 1), :][0]
    collect_edges(planes, 12, rows_s, cols_s, north, south, west, east)


def coefficient_kernel(meta, friction, heat, north, south, west, east, out, rows_s, cols_s):
    lane = lanes()
    sub = sublanes()
    for k in range(2):
        rows_s[west_lane(k), :] = west[10 + k, :]
        rows_s[east_lane(k), :] = east[10 + k, :]
    cols_s[...] = rows_s[...].T
    at_north, at_south = meta[9] > 0, meta[10] > 0
    at_west, at_east = meta[11] > 0, meta[12] > 0
    for b in range(BLOCKS):
        lo = 8 * b
        centre = [friction[k, lo : lo + 8, :] for k in range(2)]
        for k in range(2):
            here, up, down, left, right = around(
                friction.at[k],
                b,
                north[10 + k : 11 + k, :],
                south[10 + k : 11 + k, :],
                cols_s[lo : lo + 8, :],
                k,
            )
            if b == 0:
                up = jnp.where((sub == 0) & at_north, here, up)
            if b == BLOCKS - 1:
                down = jnp.where((sub == 7) & at_south, here, down)
            left = jnp.where((lane == 0) & at_west, here, left)
            right = jnp.where((lane == CELLS - 1) & at_east, here, right)
            faces = [0.5 * (here + other) for other in (up, down, left, right)]
            between = 0.5 * (centre[0] + centre[1])
            diagonal = (faces[0] + faces[1]) + (faces[2] + faces[3]) + (between + here)
            inverse = 0.8 / diagonal
            for n, face in enumerate(faces):
                out[n, k, lo : lo + 8, :] = inverse * face
            out[4, k, lo : lo + 8, :] = inverse * between
            out[5, k, lo : lo + 8, :] = 0.5 * inverse
            out[6, k, lo : lo + 8, :] = inverse * heat[k, lo : lo + 8, :]
            out[7, k, lo : lo + 8, :] = 0.125 * here


def split(x):
    high = x.astype(jnp.bfloat16)
    return high, (x - high.astype(F32)).astype(jnp.bfloat16)


def blended(block, weights):
    dims = (((1,), (1,)), ((), ()))
    b_high, b_low = split(block)
    w_high, w_low = split(weights)
    out = lax.dot_general(b_high, w_low, dims, preferred_element_type=F32)
    out = out + lax.dot_general(b_low, w_high, dims, preferred_element_type=F32)
    return out + lax.dot_general(b_high, w_high, dims, preferred_element_type=F32)


def fill_ghosts(meta, halos, arrived, weights, ghosts, count):
    for side in range(4):
        ghosts[side, :count, :] = halos[side][:count, :]

        @pl.when(meta[9 + side] > 0)
        def _():
            total = ghosts[side, :count, :]
            for term in range(2):
                offset = 2 * side + term
                total = total + blended(arrived[meta[1 + offset]], weights[offset])
            ghosts[side, :count, :] = total


def relaxed_block(coef, flow, pressure, ghosts, column, b):
    lo = 8 * b
    half = [coef[5, k, lo : lo + 8, :] for k in range(2)]
    turn = {}
    for f in range(8):
        ref = flow.at[f] if f < 6 else pressure.at[f - 6]
        turn[f] = around(ref, b, ghosts[0, f : f + 1, :], ghosts[1, f : f + 1, :], column, f)
    new = []
    for component in range(3):
        for k in range(2):
            here, up, down, left, right = turn[2 * component + k]
            vertical = turn[2 * component + 1 - k][0]
            value = 0.2 * here
            value = value + coef[0, k, lo : lo + 8, :] * up
            value = value + coef[1, k, lo : lo + 8, :] * down
            value = value + coef[2, k, lo : lo + 8, :] * left
            value = value + coef[3, k, lo : lo + 8, :] * right
            value = value + coef[4, k, lo : lo + 8, :] * vertical
            if component == 0:
                value = value + coef[6, k, lo : lo + 8, :]
                other = turn[6 + 1 - k][0]
                value = value - half[k] * other if k == 0 else value + half[k] * other
            elif component == 1:
                value = value - half[k] * (turn[6 + k][2] - turn[6 + k][1])
            else:
                value = value - half[k] * (turn[6 + k][4] - turn[6 + k][3])
            new.append(value)
    for k in range(2):
        other = turn[1 - k][0]
        divergence = (turn[2 + k][2] - turn[2 + k][1]) + (turn[4 + k][4] - turn[4 + k][3])
        divergence = divergence + other if k == 0 else divergence - other
        new.append(turn[6 + k][0] - coef[7, k, lo : lo + 8, :] * divergence)
    return new


def sweep_kernel(
    count, meta, flow, pressure, coef, north, south, west, east, arrived, weights, *rest
):
    if count > 8:
        (flow_out, pressure_out, row, n_out, s_out, w_out, e_out, heat_out) = rest[:8]
    else:
        (flow_out, pressure_out, row, n_out, s_out, w_out, e_out) = rest[:7]
    ghosts, rows_s, cols_s, edge_s = rest[-4:]
    fill_ghosts(meta, (north, south, west, east), arrived, weights, ghosts, count)
    ghost_columns(ghosts.at[2], ghosts.at[3], 8, rows_s, cols_s)
    lane = lanes()
    for b in range(BLOCKS):
        lo = 8 * b
        new = relaxed_block(coef, flow, pressure, ghosts, cols_s[lo : lo + 8, :], b)
        gathered = jnp.zeros((8, CELLS), F32)
        for f in range(8):
            if f < 6:
                flow_out[f, lo : lo + 8, :] = new[f]
            else:
                pressure_out[f - 6, lo : lo + 8, :] = new[f]
            mine = (lane == west_lane(f)) | (lane == east_lane(f))
            gathered = jnp.where(mine, roll_lanes(new[f], 2 * f), gathered)
            if b == 0:
                n_out[f : f + 1, :] = new[f][0:1, :]
            if b == BLOCKS - 1:
                s_out[f : f + 1, :] = new[f][7:8, :]
        edge_s[lo : lo + 8, :] = gathered
    at = meta[0]
    for f in range(8):
        ref = flow_out.at[f] if f < 6 else pressure_out.at[f - 6]
        row[f, :] = ref[pl.ds(at, 1), :][0]
    rows_s[...] = edge_s[...].T
    for f in range(8):
        w_out[f, :] = rows_s[west_lane(f), :]
        e_out[f, :] = rows_s[east_lane(f), :]
    if count > 8:
        for side in range(4):
            heat_out[side, :, :] = ghosts[side, 8:10, :]


def final_kernel(
    meta, flow, pressure, coef, north, south, west, east, arrived, weights, heat, heat_ghosts,
    flow_out, pressure_out, heat_out, ghosts, rows_s, cols_s, heat_cols_s,
):
    ghost_columns(heat_ghosts.at[2], heat_ghosts.at[3], 2, rows_s, heat_cols_s)
    fill_ghosts(meta, (north, south, west, east), arrived, weights, ghosts, 8)
    ghost_columns(ghosts.at[2], ghosts.at[3], 8, rows_s, cols_s)
    for b in range(BLOCKS):
        lo = 8 * b
        new = relaxed_block(coef, flow, pressure, ghosts, cols_s[lo : lo + 8, :], b)
        for f in range(8):
            if f < 6:
                flow_out[f, lo : lo + 8, :] = new[f]
            else:
                pressure_out[f - 6, lo : lo + 8, :] = new[f]
        layers = [
            around(
                heat.at[k],
                b,
                heat_ghosts[0, k : k + 1, :],
                heat_ghosts[1, k : k + 1, :],
                heat_cols_s[lo : lo + 8, :],
                k,
            )
            for k in range(2)
        ]
        for k in range(2):
            here, up, down, left, right = layers[k]
            below = jnp.ones((8, CELLS), F32) if k == 0 else layers[0][0]
            above = layers[1][0] if k == 0 else jnp.zeros((8, CELLS), F32)
            advect = jnp.zeros((8, CELLS), F32)
            for component, minus, plus in ((0, below, above), (1, up, down), (2, left, right)):
                speed = new[2 * component + k]
                advect = advect + jnp.maximum(speed, 0.0) * (here - minus)
                advect = advect + jnp.minimum(speed, 0.0) * (plus - here)
            spread = (up + down) + (left + right) + (below + above) - 6.0 * here
            heat_out[k, lo : lo + 8, :] = here + 0.1 * (spread - advect)


def shape(*dims):
    return jax.ShapeDtypeStruct(dims, F32)


def square(*lead):
    return pltpu.VMEM((*lead, CELLS, CELLS), F32)


def call(kernel, outs, ins, scratch):
    return pl.pallas_call(
        kernel,
        out_shape=outs,
        in_specs=[SMEM] + [VMEM] * (len(ins) - 1),
        out_specs=[VMEM] * len(outs),
        scratch_shapes=scratch,
        compiler_params=PARAMS,
    )(*ins)


def shards(
    flow_vector,
    normal_stress,
    thermal_field,
    shear_resistance,
    departing_bands,
    receiving_processor,
    shift_filled_by_lane,
    blending_factors,
):
    flow = flow_vector.reshape(6, CELLS, CELLS)
    pressure = normal_stress[0]
    heat = thermal_field[0]
    friction = shear_resistance[0]
    weights = blending_factors.reshape(8, CELLS, CELLS)
    slots = shift_filled_by_lane.reshape(CELLS)
    lat, lon = lax.axis_index("lat"), lax.axis_index("lon")
    n_lat, n_lon = lax.axis_size("lat"), lax.axis_size("lon")

    named = slots[None, :] == jnp.arange(8, dtype=jnp.int32)[:, None]
    position = jnp.sum(jnp.where(named, jnp.arange(CELLS, dtype=jnp.int32)[None, :], 0), axis=1)
    on_edge = jnp.stack([lat == 0, lat == n_lat - 1, lon == 0, lon == n_lon - 1]).astype(jnp.int32)
    own_row = departing_bands.reshape(1)
    meta = jnp.concatenate([own_row, position, on_edge])

    def swap(x):
        return lax.ppermute(x, "patch", [(0, 1), (1, 0)])

    target = swap(receiving_processor.reshape(1).astype(F32))
    chosen = jnp.arange(n_lat * n_lon, dtype=jnp.int32).astype(F32) == target

    def deliver(row):
        crossed = swap(row)
        sent = jnp.where(chosen[:, None, None], crossed[None], 0.0)
        return lax.all_to_all(sent, ("lat", "lon"), 0, 0, tiled=True)

    def exchange(north, south, west, east):
        up = [(i + 1, i) for i in range(n_lat - 1)]
        down = [(i, i + 1) for i in range(n_lat - 1)]
        left = [(i + 1, i) for i in range(n_lon - 1)]
        right = [(i, i + 1) for i in range(n_lon - 1)]
        return (
            lax.ppermute(south, "lat", down),
            lax.ppermute(north, "lat", up),
            lax.ppermute(east, "lon", right),
            lax.ppermute(west, "lon", left),
        )

    edges = [shape(12, CELLS)] * 4
    row, *sides = call(
        start_kernel,
        [shape(10, CELLS)] + edges,
        (meta[:1], flow, pressure, heat, friction),
        [square(), square()],
    )
    arrived = deliver(row)
    halos = exchange(*sides)
    (coef,) = call(
        coefficient_kernel,
        [shape(8, 2, CELLS, CELLS)],
        (meta, friction, heat, *halos),
        [square(), square()],
    )
    state = [shape(6, CELLS, CELLS), shape(2, CELLS, CELLS)]
    heat_ghosts = None
    for sweep in range(SWEEPS - 1):
        count = 10 if sweep == 0 else 8
        outs = state + [shape(8, CELLS)] * 5 + ([shape(4, 2, CELLS)] if sweep == 0 else [])
        got = call(
            functools.partial(sweep_kernel, count),
            outs,
            (meta, flow, pressure, coef, *halos, arrived, weights),
            [pltpu.VMEM((4, count, CELLS), F32), square(), square(), square()],
        )
        flow, pressure, row = got[:3]
        if sweep == 0:
            heat_ghosts = got[7]
        arrived = deliver(row)
        halos = exchange(*got[3:7])
    flow, pressure, heat = call(
        final_kernel,
        state + [shape(2, CELLS, CELLS)],
        (meta, flow, pressure, coef, *halos, arrived, weights, heat, heat_ghosts),
        [pltpu.VMEM((4, 8, CELLS), F32), square(), square(), square()],
    )
    return flow.reshape(3, 1, 2, CELLS, CELLS), pressure[None], heat[None]


def solution(mesh):
    placed = (
        P(None, "patch", None, "lat", "lon"),
        P("patch", None, "lat", "lon"),
        P("patch", None, "lat", "lon"),
        P("patch", None, "lat", "lon"),
        P("patch", "lat", "lon", None),
        P("patch", "lat", "lon", None),
        P("patch", "lat", "lon", None),
        P("patch", "lat", "lon", None, None, None),
    )
    return jax.shard_map(
        shards,
        mesh=mesh,
        in_specs=placed,
        out_specs=(
            P(None, "patch", None, "lat", "lon"),
            P("patch", None, "lat", "lon"),
            P("patch", None, "lat", "lon"),
        ),
        check_vma=False,
    )
```

time: 2270 us -> 166 us (0.07)
  blocking collectives: 2050 us -> 0 us
  local copies, waits for them, and re-layouts: 75.4 us -> 8.78 us
  waiting for transfers between devices: 4.52 us -> 52.1 us
  other arithmetic: 42.4 us -> 5.07 us
    all_gather x5 -> x0, blocking collectives: 1710 us -> none  [widen_sector(): lax.all_gather(crossed[0], ('lat', 'lon'), axis=2, tiled=True)]
    unnamed x1 -> x0, blocking collectives: 343 us -> none
    scatter-add x20 -> x0, local copies, waits for them, and re-layouts: 45.6 us -> none  [the longest x5 18.2 us: widen_sector(): bordered_mesh = bordered_mesh.at[:, 1:-1, 1:-1, -1].add(cycle_vals[:, :, 3])]
    all_to_all x0 -> x4, starting transfers between devices: none -> 43.5 us  [deliver(): return lax.all_to_all(sent, ('lat', 'lon'), 0, 0, tiled=True)]
    all_to_all x0 -> x4, waiting for transfers between devices: none -> 27 us  [deliver(): return lax.all_to_all(sent, ('lat', 'lon'), 0, 0, tiled=True)]
    add x25 -> x0, other arithmetic: 23.2 us -> none  [the longest x5 8.54 us: widen_sector(): bordered_mesh = bordered_mesh.at[:, 1:-1, 1:-1, 0].add(cycle_vals[:, :, 2])]
    ppermute x30 -> x21, starting transfers between devices: 64.7 us -> 43.8 us  [the longest x4 13.6 us: exchange(): lax.ppermute(south, 'lat', down)]
  transfers between devices with their start and end apart: 30 -> 25, of which waited for: 2 -> 16; matrix products, arithmetic and copies ran while one was open for 2% -> 1% of each run, Pallas kernels for 0% -> 1%
where the time goes in v1:
time: 166 us; the launch traced here: 165 us
  starting transfers between devices  87.3 us (53%)
  waiting for transfers between devices  52.1 us (31%)
  Pallas kernels  9.82 us (6%)
  local copies, waits for them, and re-layouts  8.78 us (5%)
  other arithmetic  5.07 us (3%)
  between operations  2.29 us (1%)
    all_to_all x4, starting transfers between devices, deliver(): return lax.all_to_all(sent, ('lat', 'lon'), 0, 0, tiled=True)  43.5 us
    all_to_all x4, waiting for transfers between devices, deliver(): return lax.all_to_all(sent, ('lat', 'lon'), 0, 0, tiled=True)  27 us
    ppermute x4, starting transfers between devices, exchange(): lax.ppermute(south, 'lat', down)  13.6 us
    ppermute x4, starting transfers between devices, exchange(): lax.ppermute(east, 'lon', right)  13.5 us
    ppermute x4, waiting for transfers between devices, exchange(): lax.ppermute(north, 'lat', up)  10.3 us
    ppermute x4, starting transfers between devices, exchange(): lax.ppermute(west, 'lon', left)  9.86 us
    pallas_call x6, Pallas kernels, call(): pl.pallas_call(kernel, out_shape=outs, in_specs=[SMEM] + [VMEM] * (len(in...  9.82 us
    unnamed x48, local copies, waits for them, and re-layouts  8.78 us
  transfers between devices with their start and end apart: 25, of which 16 were waited for; matrix products, arithmetic and copies ran while one was open for 1% of the time, Pallas kernels for 1%

profile of v1, /device:TPU:2, one launch (start us, length us, event | category | flops | bytes accessed | tf_op | source)
XLA Modules:
  0.0 165.3 jit_solution(950690014901832259)
XLA Ops:
  1.3 0.9 collective-permute-start.4
  2.9 1.0 copy-done.1
  3.8 0.9 copy-done.3
  4.7 0.9 copy-done.5
  5.7 0.9 copy-done.7
  6.6 0.3 shard_map.103
  6.9 0.6 collective-permute-start.5
  7.5 0.6 convert_compare_fusion
  8.1 0.2 collective-permute-done.5
  8.3 0.3 copy-done.20
  8.6 1.2 broadcast_select_fusion
  9.8 15.6 %all-to-all-start = ((f32[128,10,128]{2,1,0:T(8,128)}), f32[128,10,128]{2,1,0:T(8,128)S(1)}, u32[]{:S(2)}, u32[]{:S(2)}) async-start(f32[128,10,128]{2,1,0:T(8,128)} %broadcast_select_fusion), calls=%async_computation | async-start | bytes 2097152 | tf_op jit(solution)/shard_map/all_to_all | solution.py:331
  25.4 3.4 %collective-permute-start = (f32[12,128]{1,0:T(8,128)S(1)}, f32[12,128]{1,0:T(8,128)S(1)}, u32[]{:S(2)}, u32[]{:S(2)}) collective-permute-start(f32[12,128]{1,0:T(8,128)S(1)} %get-tuple-element.33), channel_id=1, source_target_pairs={{0,16},{16,32},{32,48},{48,64},{64,80},{80,96},{96,112},{1,17},{17... | collective-permute-start | bytes 18440 | tf_op jit(solution)/shard_map/ppermute | solution.py:339
  28.8 1.3 collective-permute-start.1
  30.1 3.4 %collective-permute-start.2 = (f32[12,128]{1,0:T(8,128)S(1)}, f32[12,128]{1,0:T(8,128)S(1)}, u32[]{:S(2)}, u32[]{:S(2)}) collective-permute-start(f32[12,128]{1,0:T(8,128)S(1)} %get-tuple-element.35), channel_id=1, source_target_pairs={{0,1},{1,2},{2,3},{3,4},{4,5},{5,6},{6,7},{7,8},{8,9},{9,10},{10,1... | collective-permute-start | bytes 18440 | tf_op jit(solution)/shard_map/ppermute | solution.py:341
  33.5 2.5 %collective-permute-start.3 = (f32[12,128]{1,0:T(8,128)S(1)}, f32[12,128]{1,0:T(8,128)S(1)}, u32[]{:S(2)}, u32[]{:S(2)}) collective-permute-start(f32[12,128]{1,0:T(8,128)S(1)} %get-tuple-element.36), channel_id=1, source_target_pairs={{1,0},{2,1},{3,2},{4,3},{5,4},{6,5},{7,6},{8,7},{9,8},{10,9},{11,1... | collective-permute-start | bytes 18440 | tf_op jit(solution)/shard_map/ppermute | solution.py:342
  36.0 0.7 copy-done.23
  36.7 0.1 select_reduce_fusion
  36.9 8.4 %collective-permute-done.north = f32[12,128]{1,0:T(8,128)S(1)} collective-permute-done((f32[12,128]{1,0:T(8,128)S(1)}, f32[12,128]{1,0:T(8,128)S(1)}, u32[]{:S(2)}, u32[]{:S(2)}) %collective-permute-start) | collective-permute-done | bytes 6176 | tf_op jit(solution)/shard_map/ppermute | solution.py:339
  45.3 3.9 %collective-permute-done.1.south = f32[12,128]{1,0:T(8,128)S(1)} collective-permute-done((f32[12,128]{1,0:T(8,128)S(1)}, f32[12,128]{1,0:T(8,128)S(1)}, u32[]{:S(2)}, u32[]{:S(2)}) %collective-permute-start.1) | collective-permute-done | bytes 6176 | tf_op jit(solution)/shard_map/ppermute | solution.py:340
  49.2 0.8 shard_map.104.coef
  50.0 6.2 %all-to-all-done.arrived = f32[128,10,128]{2,1,0:T(8,128)S(1)} async-done(((f32[128,10,128]{2,1,0:T(8,128)}), f32[128,10,128]{2,1,0:T(8,128)S(1)}, u32[]{:S(2)}, u32[]{:S(2)}) %all-to-all-start) | async-done | bytes 655392 | tf_op jit(solution)/shard_map/all_to_all | solution.py:331
  56.2 0.7 copy-done.16
  56.9 0.7 copy-done.12
  57.6 0.7 copy-done.14
  58.3 2.1 %shard_map.105 = (f32[6,128,128]{2,1,0:T(8,128)S(1)}, f32[2,128,128]{2,1,0:T(8,128)S(1)}, f32[8,128]{1,0:T(8,128)S(1)}, f32[8,128]{1,0:T(8,128)S(1)}, f32[8,128]...) custom-call(s32[13]{0:T(128)S(1)} %copy-done.16, ...), custom_call_target="tpu_custom_call" | custom-call | tf_op jit(solution)/shard_map/pallas_call | solution.py:287
  60.4 0.7 copy-done.9
  61.2 0.6 copy-done.18
  61.8 1.2 collective-permute-done.10
  62.9 1.0 broadcast_select_fusion.3
  63.9 7.0 %all-to-all-start.1 = ((f32[128,8,128]{2,1,0:T(8,128)}), f32[128,8,128]{2,1,0:T(8,128)S(1)}, u32[]{:S(2)}, u32[]{:S(2)}) async-start(f32[128,8,128]{2,1,0:T(8,128)} %broadcast_select_fusion.3), calls=%async_computation.1 | async-start | bytes 1048576 | tf_op jit(solution)/shard_map/all_to_all | solution.py:331
  70.9 3.5 %collective-permute-start.6 = (f32[8,128]{1,0:T(8,128)S(1)}, f32[8,128]{1,0:T(8,128)S(1)}, u32[]{:S(2)}, u32[]{:S(2)}) collective-permute-start(f32[8,128]{1,0:T(8,128)S(1)} %get-tuple-element.40), channel_id=1, source_target_pairs={{0,16},{16,32},{32,48},{48,64},{64,80},{80,96},{96,112},{1,17},{17... | collective-permute-start | bytes 12296 | tf_op jit(solution)/shard_map/ppermute | solution.py:339
  74.4 1.3 collective-permute-start.7
  75.7 3.4 %collective-permute-start.8 = (f32[8,128]{1,0:T(8,128)S(1)}, f32[8,128]{1,0:T(8,128)S(1)}, u32[]{:S(2)}, u32[]{:S(2)}) collective-permute-start(f32[8,128]{1,0:T(8,128)S(1)} %get-tuple-element.42), channel_id=1, source_target_pairs={{0,1},{1,2},{2,3},{3,4},{4,5},{5,6},{6,7},{7,8},{8,9},{9,10},{10,1... | collective-permute-start | bytes 12296 | tf_op jit(solution)/shard_map/ppermute | solution.py:341
  79.1 2.5 %collective-permute-start.9 = (f32[8,128]{1,0:T(8,128)S(1)}, f32[8,128]{1,0:T(8,128)S(1)}, u32[]{:S(2)}, u32[]{:S(2)}) collective-permute-start(f32[8,128]{1,0:T(8,128)S(1)} %get-tuple-element.43), channel_id=1, source_target_pairs={{1,0},{2,1},{3,2},{4,3},{5,4},{6,5},{7,6},{8,7},{9,8},{10,9},{11,1... | collective-permute-start | bytes 12296 | tf_op jit(solution)/shard_map/ppermute | solution.py:342
  81.6 2.3 %collective-permute-done.7.south = f32[8,128]{1,0:T(8,128)S(1)} collective-permute-done((f32[8,128]{1,0:T(8,128)S(1)}, f32[8,128]{1,0:T(8,128)S(1)}, u32[]{:S(2)}, u32[]{:S(2)}) %collective-permute-start.7) | collective-permute-done | bytes 4128 | tf_op jit(solution)/shard_map/ppermute | solution.py:340
  83.9 0.8 collective-permute-done.9.east
  84.6 7.0 %all-to-all-done.1.arrived = f32[128,8,128]{2,1,0:T(8,128)S(1)} async-done(((f32[128,8,128]{2,1,0:T(8,128)}), f32[128,8,128]{2,1,0:T(8,128)S(1)}, u32[]{:S(2)}, u32[]{:S(2)}) %all-to-all-start.1) | async-done | bytes 524320 | tf_op jit(solution)/shard_map/all_to_all | solution.py:331
  91.6 0.7 copy-done.17
  92.3 2.1 %shard_map.106 = (f32[6,128,128]{2,1,0:T(8,128)S(1)}, f32[2,128,128]{2,1,0:T(8,128)S(1)}, f32[8,128]{1,0:T(8,128)S(1)}, f32[8,128]{1,0:T(8,128)S(1)}, f32[8,128]...) custom-call(s32[13]{0:T(128)S(1)} %copy-done.17, f32[6,128,128]{2,1,0:T(8,128)S(1)} %copy-done.10, ...), custom_call_target="tpu_custom_call" | custom-call | tf_op jit(solution)/shard_map/pallas_call | solution.py:287
  94.5 0.1 collective-permute-start.15
  94.5 1.2 collective-permute-done.15
  95.7 1.0 broadcast_select_fusion.2
  96.7 10.4 %all-to-all-start.2 = ((f32[128,8,128]{2,1,0:T(8,128)}), f32[128,8,128]{2,1,0:T(8,128)S(1)}, u32[]{:S(2)}, u32[]{:S(2)}) async-start(f32[128,8,128]{2,1,0:T(8,128)} %broadcast_select_fusion.2), calls=%async_computation.2 | async-start | bytes 1048576 | tf_op jit(solution)/shard_map/all_to_all | solution.py:331
  107.1 3.4 %collective-permute-start.11 = (f32[8,128]{1,0:T(8,128)S(1)}, f32[8,128]{1,0:T(8,128)S(1)}, u32[]{:S(2)}, u32[]{:S(2)}) collective-permute-start(f32[8,128]{1,0:T(8,128)S(1)} %get-tuple-element.47), channel_id=1, source_target_pairs={{0,16},{16,32},{32,48},{48,64},{64,80},{80,96},{96,112},{1,17},{17... | collective-permute-start | bytes 12296 | tf_op jit(solution)/shard_map/ppermute | solution.py:339
  110.5 1.3 collective-permute-start.12
  111.8 3.4 %collective-permute-start.13 = (f32[8,128]{1,0:T(8,128)S(1)}, f32[8,128]{1,0:T(8,128)S(1)}, u32[]{:S(2)}, u32[]{:S(2)}) collective-permute-start(f32[8,128]{1,0:T(8,128)S(1)} %get-tuple-element.49), channel_id=1, source_target_pairs={{0,1},{1,2},{2,3},{3,4},{4,5},{5,6},{6,7},{7,8},{8,9},{9,10},{10,1... | collective-permute-start | bytes 12296 | tf_op jit(solution)/shard_map/ppermute | solution.py:341
  115.2 2.5 %collective-permute-start.14 = (f32[8,128]{1,0:T(8,128)S(1)}, f32[8,128]{1,0:T(8,128)S(1)}, u32[]{:S(2)}, u32[]{:S(2)}) collective-permute-start(f32[8,128]{1,0:T(8,128)S(1)} %get-tuple-element.50), channel_id=1, source_target_pairs={{1,0},{2,1},{3,2},{4,3},{5,4},{6,5},{7,6},{8,7},{9,8},{10,9},{11,1... | collective-permute-start | bytes 12296 | tf_op jit(solution)/shard_map/ppermute | solution.py:342
  117.7 2.0 %collective-permute-done.12.south = f32[8,128]{1,0:T(8,128)S(1)} collective-permute-done((f32[8,128]{1,0:T(8,128)S(1)}, f32[8,128]{1,0:T(8,128)S(1)}, u32[]{:S(2)}, u32[]{:S(2)}) %collective-permute-start.12) | collective-permute-done | bytes 4128 | tf_op jit(solution)/shard_map/ppermute | solution.py:340
  119.7 1.0 collective-permute-done.14.east
  120.7 6.9 %all-to-all-done.2.arrived = f32[128,8,128]{2,1,0:T(8,128)S(1)} async-done(((f32[128,8,128]{2,1,0:T(8,128)}), f32[128,8,128]{2,1,0:T(8,128)S(1)}, u32[]{:S(2)}, u32[]{:S(2)}) %all-to-all-start.2) | async-done | bytes 524320 | tf_op jit(solution)/shard_map/all_to_all | solution.py:331
  127.6 2.1 %shard_map.107 = (f32[6,128,128]{2,1,0:T(8,128)S(1)}, f32[2,128,128]{2,1,0:T(8,128)S(1)}, f32[8,128]{1,0:T(8,128)S(1)}, f32[8,128]{1,0:T(8,128)S(1)}, f32[8,128]...) custom-call(s32[13]{0:T(128)S(1)} %copy-done.17, f32[6,128,128]{2,1,0:T(8,128)S(1)} %get-tuple-element.45.flow, ...), custom_call_target="tpu_custom_call" | custom-call | tf_op jit(solution)/shard_map/pallas_call | solution.py:287
  129.7 0.1 collective-permute-start.20
  129.8 1.2 collective-permute-done.20
  131.0 1.0 broadcast_select_fusion.1
  132.0 10.6 %all-to-all-start.3 = ((f32[128,8,128]{2,1,0:T(8,128)}), f32[128,8,128]{2,1,0:T(8,128)S(1)}, u32[]{:S(2)}, u32[]{:S(2)}) async-start(f32[128,8,128]{2,1,0:T(8,128)} %broadcast_select_fusion.1), calls=%async_computation.3 | async-start | bytes 1048576 | tf_op jit(solution)/shard_map/all_to_all | solution.py:331
  142.6 3.4 %collective-permute-start.16 = (f32[8,128]{1,0:T(8,128)S(1)}, f32[8,128]{1,0:T(8,128)S(1)}, u32[]{:S(2)}, u32[]{:S(2)}) collective-permute-start(f32[8,128]{1,0:T(8,128)S(1)} %get-tuple-element.54), channel_id=1, source_target_pairs={{0,16},{16,32},{32,48},{48,64},{64,80},{80,96},{96,112},{1,17},{17... | collective-permute-start | bytes 12296 | tf_op jit(solution)/shard_map/ppermute | solution.py:339
  145.9 1.3 collective-permute-start.17
  147.3 3.4 %collective-permute-start.18 = (f32[8,128]{1,0:T(8,128)S(1)}, f32[8,128]{1,0:T(8,128)S(1)}, u32[]{:S(2)}, u32[]{:S(2)}) collective-permute-start(f32[8,128]{1,0:T(8,128)S(1)} %get-tuple-element.56), channel_id=1, source_target_pairs={{0,1},{1,2},{2,3},{3,4},{4,5},{5,6},{6,7},{7,8},{8,9},{9,10},{10,1... | collective-permute-start | bytes 12296 | tf_op jit(solution)/shard_map/ppermute | solution.py:341
  150.6 2.5 %collective-permute-start.19 = (f32[8,128]{1,0:T(8,128)S(1)}, f32[8,128]{1,0:T(8,128)S(1)}, u32[]{:S(2)}, u32[]{:S(2)}) collective-permute-start(f32[8,128]{1,0:T(8,128)S(1)} %get-tuple-element.57), channel_id=1, source_target_pairs={{1,0},{2,1},{3,2},{4,3},{5,4},{6,5},{7,6},{8,7},{9,8},{10,9},{11,1... | collective-permute-start | bytes 12296 | tf_op jit(solution)/shard_map/ppermute | solution.py:342
  153.1 2.0 %collective-permute-done.17.south = f32[8,128]{1,0:T(8,128)S(1)} collective-permute-done((f32[8,128]{1,0:T(8,128)S(1)}, f32[8,128]{1,0:T(8,128)S(1)}, u32[]{:S(2)}, u32[]{:S(2)}) %collective-permute-start.17) | collective-permute-done | bytes 4128 | tf_op jit(solution)/shard_map/ppermute | solution.py:340
  155.1 1.0 collective-permute-done.19.east
  156.1 6.9 %all-to-all-done.3.arrived = f32[128,8,128]{2,1,0:T(8,128)S(1)} async-done(((f32[128,8,128]{2,1,0:T(8,128)}), f32[128,8,128]{2,1,0:T(8,128)S(1)}, u32[]{:S(2)}, u32[]{:S(2)}) %all-to-all-start.3) | async-done | bytes 524320 | tf_op jit(solution)/shard_map/all_to_all | solution.py:331
  163.0 2.3 %shard_map.108 = (f32[6,128,128]{2,1,0:T(8,128)}, f32[2,128,128]{2,1,0:T(8,128)}, f32[2,128,128]{2,1,0:T(8,128)}) custom-call(s32[13]{0:T(128)S(1)} %copy-done.17, f32[6,128,128]{2,1,0:T(8,128)S(1)} %get-tuple-element.52.flow, f32[2,128,128]{2,1,0:T(8,128)S(1)} %get-tuple-element.53.pressure, f32[8,2,128,128]{3,2,1,0:T(8,128)S(1)} %shard_map.104.coef, ...), custom_call_target="tpu_custom_call" | custom-call | tf_op jit(solution)/shard_map/pallas_call | solution.py:287
  (48 shorter events, 0.3 us)
Async XLA Ops:
  1.3 6.2 %collective-permute-start.4 = (f32[1]{0:T(128)}, f32[1]{0:T(128)}, u32[]{:S(2)}, u32[]{:S(2)}) collective-permute-start(f32[1]{0:T(128)} %bitcast.10), channel_id=1, source_target_pairs={{0,128},{128,0},{1,129},{129,1},{2,130},{130,2},{3,131},{131,3},{4... | collective-permute-start | bytes 20 | tf_op jit(solution)/shard_map/ppermute | solution.py:323
  2.8 1.0 copy-start.1
  3.8 0.9 copy-start.3
  4.7 0.9 copy-start.5
  5.7 0.9 copy-start.7
  6.9 1.4 collective-permute-start.5
  8.1 0.5 copy-start.20
  9.8 39.4 %copy-start.4 = (f32[1,2,128,128]{3,2,1,0:T(8,128)S(1)}, f32[1,2,128,128]{3,2,1,0:T(8,128)}, u32[]{:S(2)}) copy-start(f32[1,2,128,128]{3,2,1,0:T(8,128)} %param.10) | copy-start | bytes 393220
  9.8 39.4 %copy-start.6 = (f32[1,2,128,128]{3,2,1,0:T(8,128)S(1)}, f32[1,2,128,128]{3,2,1,0:T(8,128)}, u32[]{:S(2)}) copy-start(f32[1,2,128,128]{3,2,1,0:T(8,128)} %param.11) | copy-start | bytes 393220
  9.8 46.4 %all-to-all-start = ((f32[128,10,128]{2,1,0:T(8,128)}), f32[128,10,128]{2,1,0:T(8,128)S(1)}, u32[]{:S(2)}, u32[]{:S(2)}) async-start(f32[128,10,128]{2,1,0:T(8,128)} %broadcast_select_fusion), calls=%async_computation | async-start | bytes 2097152 | tf_op jit(solution)/shard_map/all_to_all | solution.py:331
  25.4 19.9 %collective-permute-start = (f32[12,128]{1,0:T(8,128)S(1)}, f32[12,128]{1,0:T(8,128)S(1)}, u32[]{:S(2)}, u32[]{:S(2)}) collective-permute-start(f32[12,128]{1,0:T(8,128)S(1)} %get-tuple-element.33), channel_id=1, source_target_pairs={{0,16},{16,32},{32,48},{48,64},{64,80},{80,96},{96,112},{1,17},{17... | collective-permute-start | bytes 18440 | tf_op jit(solution)/shard_map/ppermute | solution.py:339
  28.8 20.4 %collective-permute-start.1 = (f32[12,128]{1,0:T(8,128)S(1)}, f32[12,128]{1,0:T(8,128)S(1)}, u32[]{:S(2)}, u32[]{:S(2)}) collective-permute-start(f32[12,128]{1,0:T(8,128)S(1)} %get-tuple-element.34), channel_id=1, source_target_pairs={{16,0},{32,16},{48,32},{64,48},{80,64},{96,80},{112,96},{17,1},{33... | collective-permute-start | bytes 18440 | tf_op jit(solution)/shard_map/ppermute | solution.py:340
  30.1 19.1 %collective-permute-start.2 = (f32[12,128]{1,0:T(8,128)S(1)}, f32[12,128]{1,0:T(8,128)S(1)}, u32[]{:S(2)}, u32[]{:S(2)}) collective-permute-start(f32[12,128]{1,0:T(8,128)S(1)} %get-tuple-element.35), channel_id=1, source_target_pairs={{0,1},{1,2},{2,3},{3,4},{4,5},{5,6},{6,7},{7,8},{8,9},{9,10},{10,1... | collective-permute-start | bytes 18440 | tf_op jit(solution)/shard_map/ppermute | solution.py:341
  33.5 15.7 %collective-permute-start.3 = (f32[12,128]{1,0:T(8,128)S(1)}, f32[12,128]{1,0:T(8,128)S(1)}, u32[]{:S(2)}, u32[]{:S(2)}) collective-permute-start(f32[12,128]{1,0:T(8,128)S(1)} %get-tuple-element.36), channel_id=1, source_target_pairs={{1,0},{2,1},{3,2},{4,3},{5,4},{6,5},{7,6},{8,7},{9,8},{10,9},{11,1... | collective-permute-start | bytes 18440 | tf_op jit(solution)/shard_map/ppermute | solution.py:342
  36.0 0.7 copy-start.23
  36.9 13.1 %copy-start.15 = (s32[13]{0:T(128)}, s32[13]{0:T(128)S(1)}, u32[]{:S(2)}) copy-start(s32[13]{0:T(128)S(1)} %pad_add_fusion.meta) | copy-start | bytes 160
  36.9 19.3 %copy-start = (f32[1,1,1,8,128,128]{5,4,3,2,1,0:T(8,128)S(1)}, f32[1,1,1,8,128,128]{5,4,3,2,1,0:T(8,128)}, u32[]{:S(2)}) copy-start(f32[1,1,1,8,128,128]{5,4,3,2,1,0:T(8,128)} %param.15) | copy-start | bytes 1572868
  36.9 19.3 %copy-start.2 = (f32[3,1,2,128,128]{4,3,2,1,0:T(8,128)S(1)}, f32[3,1,2,128,128]{4,3,2,1,0:T(8,128)}, u32[]{:S(2)}) copy-start(f32[3,1,2,128,128]{4,3,2,1,0:T(8,128)} %param.8) | copy-start | bytes 1179652
  36.9 19.3 %copy-start.8 = (f32[1,2,128,128]{3,2,1,0:T(8,128)S(1)}, f32[1,2,128,128]{3,2,1,0:T(8,128)}, u32[]{:S(2)}) copy-start(f32[1,2,128,128]{3,2,1,0:T(8,128)} %param.9) | copy-start | bytes 393220
  49.2 0.8 copy-start.11
  49.2 0.8 copy-start.13
  56.2 0.7 copy-start.16
  56.9 0.7 copy-start.12
  57.6 0.7 copy-start.14
  60.4 0.8 copy-start.9
  61.2 0.6 copy-start.18
  61.8 1.2 copy-start.21
  61.8 1.2 collective-permute-start.10
  63.9 27.7 %copy-start.10 = (f32[6,128,128]{2,1,0:T(8,128)S(1)}, f32[6,128,128]{2,1,0:T(8,128)}, u32[]{:S(2)}) copy-start(f32[6,128,128]{2,1,0:T(8,128)} %copy-done.9) | copy-start | bytes 1179652
  63.9 27.7 %all-to-all-start.1 = ((f32[128,8,128]{2,1,0:T(8,128)}), f32[128,8,128]{2,1,0:T(8,128)S(1)}, u32[]{:S(2)}, u32[]{:S(2)}) async-start(f32[128,8,128]{2,1,0:T(8,128)} %broadcast_select_fusion.3), calls=%async_computation.1 | async-start | bytes 1048576 | tf_op jit(solution)/shard_map/all_to_all | solution.py:331
  70.9 10.6 %collective-permute-start.6 = (f32[8,128]{1,0:T(8,128)S(1)}, f32[8,128]{1,0:T(8,128)S(1)}, u32[]{:S(2)}, u32[]{:S(2)}) collective-permute-start(f32[8,128]{1,0:T(8,128)S(1)} %get-tuple-element.40), channel_id=1, source_target_pairs={{0,16},{16,32},{32,48},{48,64},{64,80},{80,96},{96,112},{1,17},{17... | collective-permute-start | bytes 12296 | tf_op jit(solution)/shard_map/ppermute | solution.py:339
  74.4 9.5 %collective-permute-start.7 = (f32[8,128]{1,0:T(8,128)S(1)}, f32[8,128]{1,0:T(8,128)S(1)}, u32[]{:S(2)}, u32[]{:S(2)}) collective-permute-start(f32[8,128]{1,0:T(8,128)S(1)} %get-tuple-element.41), channel_id=1, source_target_pairs={{16,0},{32,16},{48,32},{64,48},{80,64},{96,80},{112,96},{17,1},{33... | collective-permute-start | bytes 12296 | tf_op jit(solution)/shard_map/ppermute | solution.py:340
  75.7 8.2 %collective-permute-start.8 = (f32[8,128]{1,0:T(8,128)S(1)}, f32[8,128]{1,0:T(8,128)S(1)}, u32[]{:S(2)}, u32[]{:S(2)}) collective-permute-start(f32[8,128]{1,0:T(8,128)S(1)} %get-tuple-element.42), channel_id=1, source_target_pairs={{0,1},{1,2},{2,3},{3,4},{4,5},{5,6},{6,7},{7,8},{8,9},{9,10},{10,1... | collective-permute-start | bytes 12296 | tf_op jit(solution)/shard_map/ppermute | solution.py:341
  79.1 5.6 %collective-permute-start.9 = (f32[8,128]{1,0:T(8,128)S(1)}, f32[8,128]{1,0:T(8,128)S(1)}, u32[]{:S(2)}, u32[]{:S(2)}) collective-permute-start(f32[8,128]{1,0:T(8,128)S(1)} %get-tuple-element.43), channel_id=1, source_target_pairs={{1,0},{2,1},{3,2},{4,3},{5,4},{6,5},{7,6},{8,7},{9,8},{10,9},{11,1... | collective-permute-start | bytes 12296 | tf_op jit(solution)/shard_map/ppermute | solution.py:342
  91.6 0.7 copy-start.17
  94.5 1.3 collective-permute-start.15
  96.7 30.9 %all-to-all-start.2 = ((f32[128,8,128]{2,1,0:T(8,128)}), f32[128,8,128]{2,1,0:T(8,128)S(1)}, u32[]{:S(2)}, u32[]{:S(2)}) async-start(f32[128,8,128]{2,1,0:T(8,128)} %broadcast_select_fusion.2), calls=%async_computation.2 | async-start | bytes 1048576 | tf_op jit(solution)/shard_map/all_to_all | solution.py:331
  107.1 10.5 %collective-permute-start.11 = (f32[8,128]{1,0:T(8,128)S(1)}, f32[8,128]{1,0:T(8,128)S(1)}, u32[]{:S(2)}, u32[]{:S(2)}) collective-permute-start(f32[8,128]{1,0:T(8,128)S(1)} %get-tuple-element.47), channel_id=1, source_target_pairs={{0,16},{16,32},{32,48},{48,64},{64,80},{80,96},{96,112},{1,17},{17... | collective-permute-start | bytes 12296 | tf_op jit(solution)/shard_map/ppermute | solution.py:339
  110.5 9.2 %collective-permute-start.12 = (f32[8,128]{1,0:T(8,128)S(1)}, f32[8,128]{1,0:T(8,128)S(1)}, u32[]{:S(2)}, u32[]{:S(2)}) collective-permute-start(f32[8,128]{1,0:T(8,128)S(1)} %get-tuple-element.48), channel_id=1, source_target_pairs={{16,0},{32,16},{48,32},{64,48},{80,64},{96,80},{112,96},{17,1},{33... | collective-permute-start | bytes 12296 | tf_op jit(solution)/shard_map/ppermute | solution.py:340
  111.8 7.9 %collective-permute-start.13 = (f32[8,128]{1,0:T(8,128)S(1)}, f32[8,128]{1,0:T(8,128)S(1)}, u32[]{:S(2)}, u32[]{:S(2)}) collective-permute-start(f32[8,128]{1,0:T(8,128)S(1)} %get-tuple-element.49), channel_id=1, source_target_pairs={{0,1},{1,2},{2,3},{3,4},{4,5},{5,6},{6,7},{7,8},{8,9},{9,10},{10,1... | collective-permute-start | bytes 12296 | tf_op jit(solution)/shard_map/ppermute | solution.py:341
  115.2 5.5 %collective-permute-start.14 = (f32[8,128]{1,0:T(8,128)S(1)}, f32[8,128]{1,0:T(8,128)S(1)}, u32[]{:S(2)}, u32[]{:S(2)}) collective-permute-start(f32[8,128]{1,0:T(8,128)S(1)} %get-tuple-element.50), channel_id=1, source_target_pairs={{1,0},{2,1},{3,2},{4,3},{5,4},{6,5},{7,6},{8,7},{9,8},{10,9},{11,1... | collective-permute-start | bytes 12296 | tf_op jit(solution)/shard_map/ppermute | solution.py:342
  129.7 1.3 copy-start.22
  129.7 1.3 collective-permute-start.20
  132.0 31.0 %all-to-all-start.3 = ((f32[128,8,128]{2,1,0:T(8,128)}), f32[128,8,128]{2,1,0:T(8,128)S(1)}, u32[]{:S(2)}, u32[]{:S(2)}) async-start(f32[128,8,128]{2,1,0:T(8,128)} %broadcast_select_fusion.1), calls=%async_computation.3 | async-start | bytes 1048576 | tf_op jit(solution)/shard_map/all_to_all | solution.py:331
  142.6 10.6 %collective-permute-start.16 = (f32[8,128]{1,0:T(8,128)S(1)}, f32[8,128]{1,0:T(8,128)S(1)}, u32[]{:S(2)}, u32[]{:S(2)}) collective-permute-start(f32[8,128]{1,0:T(8,128)S(1)} %get-tuple-element.54), channel_id=1, source_target_pairs={{0,16},{16,32},{32,48},{48,64},{64,80},{80,96},{96,112},{1,17},{17... | collective-permute-start | bytes 12296 | tf_op jit(solution)/shard_map/ppermute | solution.py:339
  145.9 9.2 %collective-permute-start.17 = (f32[8,128]{1,0:T(8,128)S(1)}, f32[8,128]{1,0:T(8,128)S(1)}, u32[]{:S(2)}, u32[]{:S(2)}) collective-permute-start(f32[8,128]{1,0:T(8,128)S(1)} %get-tuple-element.55), channel_id=1, source_target_pairs={{16,0},{32,16},{48,32},{64,48},{80,64},{96,80},{112,96},{17,1},{33... | collective-permute-start | bytes 12296 | tf_op jit(solution)/shard_map/ppermute | solution.py:340
  147.2 15.8 %copy-start.19 = (f32[4,2,128]{2,1,0:T(2,128)S(1)}, f32[4,2,128]{2,1,0:T(2,128)}, u32[]{:S(2)}) copy-start(f32[4,2,128]{2,1,0:T(2,128)} %copy-done.18) | copy-start | bytes 12292
  147.3 7.9 %collective-permute-start.18 = (f32[8,128]{1,0:T(8,128)S(1)}, f32[8,128]{1,0:T(8,128)S(1)}, u32[]{:S(2)}, u32[]{:S(2)}) collective-permute-start(f32[8,128]{1,0:T(8,128)S(1)} %get-tuple-element.56), channel_id=1, source_target_pairs={{0,1},{1,2},{2,3},{3,4},{4,5},{5,6},{6,7},{7,8},{8,9},{9,10},{10,1... | collective-permute-start | bytes 12296 | tf_op jit(solution)/shard_map/ppermute | solution.py:341
  150.6 5.5 %collective-permute-start.19 = (f32[8,128]{1,0:T(8,128)S(1)}, f32[8,128]{1,0:T(8,128)S(1)}, u32[]{:S(2)}, u32[]{:S(2)}) collective-permute-start(f32[8,128]{1,0:T(8,128)S(1)} %get-tuple-element.57), channel_id=1, source_target_pairs={{1,0},{2,1},{3,2},{4,3},{5,4},{6,5},{7,6},{8,7},{9,8},{10,9},{11,1... | collective-permute-start | bytes 12296 | tf_op jit(solution)/shard_map/ppermute | solution.py:342

commit v2 on v0

v2 whole, which is shorter than its diff:
```python
import jax
import jax.numpy as jnp
from jax import lax
from jax.experimental import pallas as pl
from jax.experimental.pallas import tpu as pltpu
from jax.sharding import PartitionSpec as P

SWEEPS = 4
CELLS = 128
TILES = 16
ROWS = CELLS + 16
LANES = 2 * CELLS
HALO = 4
PLANES = 12
F32 = jnp.float32
VMEM = pl.BlockSpec(memory_space=pltpu.VMEM)
SMEM = pl.BlockSpec(memory_space=pltpu.SMEM)
ANY = pl.BlockSpec(memory_space=pl.ANY)
NORTH, SOUTH, WEST, EAST = 1, 2, 3, 4
PLACES = 5
LAT_BASE, LON_BASE = 17, 18


def lanes():
    return lax.broadcasted_iota(jnp.int32, (8, CELLS), 1)


def sublanes():
    return lax.broadcasted_iota(jnp.int32, (8, CELLS), 0)


def turn(x, shift):
    shift = shift % CELLS
    return x if shift == 0 else pltpu.roll(x, shift, 1)


def tile(b):
    return pl.ds(8 * b, 8)


def plane_of(flow, pressure, heat, friction, f):
    if f < 6:
        return flow.at[f]
    if f < 8:
        return pressure.at[f - 6]
    if f < 10:
        return heat.at[f - 8]
    return friction.at[f - 10]


def start_kernel(at, slots, flow, pressure, heat, friction, weights, row, top, bottom, near, sems):
    start = pl.multiple_of((at[0] // 8) * 8, 8)
    copies = []

    def fetch(source, target):
        copy = pltpu.make_async_copy(source, target, sems.at[len(copies)])
        copy.start()
        copies.append(copy)

    fetch(flow.at[:, pl.ds(start, 8), :], near.at[0:6])
    fetch(pressure.at[:, pl.ds(start, 8), :], near.at[6:8])
    fetch(heat.at[:, pl.ds(start, 8), :], near.at[8:10])
    for out, lo in ((top, 0), (bottom, CELLS - 8)):
        fetch(flow.at[:, lo : lo + 8, :], out.at[0:6])
        fetch(pressure.at[:, lo : lo + 8, :], out.at[6:8])
        fetch(heat.at[:, lo : lo + 8, :], out.at[8:10])
        fetch(friction.at[:, lo : lo + 8, :], out.at[10:12])
        fetch(weights.at[4:8, lo : lo + 8, :], out.at[12:16])
    named = jnp.broadcast_to(slots[...], (8, CELLS)) == sublanes()
    place = jnp.sum(jnp.where(named, lanes(), 0).astype(F32), axis=1, keepdims=True)
    top[16] = jnp.broadcast_to(place, (8, CELLS))
    bottom[16] = jnp.broadcast_to(place, (8, CELLS))
    row[...] = jnp.zeros((16, CELLS), F32)
    for copy in copies:
        copy.wait()
    inside = at[0] - start
    for f in range(10):
        row[f : f + 1, :] = near[f, pl.ds(inside, 1), :]


def fill_kernel(chunks, row, out):
    out[...] = jnp.zeros((CELLS, 8, CELLS), F32)
    for n in range(5):
        out[chunks[n]] = row[0:8, :]
    out[chunks[5]] = row[8:16, :]


def refill_kernel(chunks, row, old, out):
    del old
    for n in range(5):
        out[chunks[n]] = row[...]


def columns_kernel(flow, pressure, heat, friction, weights, north, south, to_west, to_east, cols_s, rows_s):
    lane = lanes()

    def pack(block):
        gathered = jnp.zeros((8, CELLS), F32)
        for f in range(PLANES):
            gathered = jnp.where(lane // 8 == f, turn(block(f), 8 * f + HALO), gathered)
        return gathered

    def unload(first):
        rows_s[...] = cols_s[...].T
        for f in range(PLANES):
            lo = first + HALO * f
            to_east[lo : lo + HALO, :] = rows_s[8 * f : 8 * f + HALO, :]
            to_west[lo : lo + HALO, :] = rows_s[8 * f + HALO : 8 * f + 8, :]

    for b in range(TILES):
        cols_s[tile(b), :] = pack(lambda f: plane_of(flow, pressure, heat, friction, f)[tile(b), :])
    unload(0)
    cols_s[tile(TILES - 1), :] = pack(lambda f: north[f])
    cols_s[tile(0), :] = pack(lambda f: south[f])
    unload(HALO * PLANES)
    for n in range(4):
        lo = 2 * HALO * PLANES + 8 * n
        to_west[lo : lo + 8, :] = weights[n, 0:8, :]
        to_east[lo : lo + 8, :] = weights[n, CELLS - 8 : CELLS, :]


def sideways(first, second):
    lane = lanes()
    f_up, s_up = pltpu.roll(first, 1, 1), pltpu.roll(second, 1, 1)
    f_down, s_down = pltpu.roll(first, CELLS - 1, 1), pltpu.roll(second, CELLS - 1, 1)
    lefts = (jnp.where(lane == 0, s_up, f_up), jnp.where(lane == 0, f_up, s_up))
    rights = (
        jnp.where(lane == CELLS - 1, s_down, f_down),
        jnp.where(lane == CELLS - 1, f_down, s_down),
    )
    return lefts, rights


def around(ref, b, halves):
    both = [ref[half, tile(b), :] for half in range(2)]
    lefts, rights = sideways(*both)
    found = []
    for half in range(halves):
        up = pltpu.roll(both[half], 1, 0) if b == 0 else ref[half, 8 * b - 1 : 8 * b + 7, :]
        down = pltpu.roll(both[half], 7, 0) if b == TILES + 1 else ref[half, 8 * b + 1 : 8 * b + 9, :]
        found.append((both[half], up, down, lefts[half], rights[half]))
    return found


def build_kernel(
    ints, flow, pressure, heat, friction, north, south, west, east,
    fields, coef, warm, mixed, thick, cols_s, rows_s,
):
    lane = lanes()

    def target(f):
        if f < 8:
            return fields.at[f]
        return warm.at[f - 8] if f < 10 else thick.at[f - 10]

    outer = (lane < HALO) | (lane >= CELLS - HALO)

    def load(first):
        for f in range(PLANES):
            lo = first + HALO * f
            rows_s[8 * f : 8 * f + HALO, :] = west[lo : lo + HALO, :]
            rows_s[8 * f + HALO : 8 * f + 8, :] = east[lo : lo + HALO, :]
        cols_s[...] = rows_s[...].T

    def place(f, b, block):
        target(f)[1, tile(b), :] = jnp.where(outer, turn(block, -8 * f - HALO), 0.0)

    rows_s[8 * PLANES : CELLS, :] = jnp.zeros((CELLS - 8 * PLANES, CELLS), F32)
    load(0)
    for f in range(PLANES):
        source = plane_of(flow, pressure, heat, friction, f)
        target(f)[0, tile(0), :] = north[f]
        target(f)[0, tile(TILES + 1), :] = south[f]
        for b in range(TILES):
            target(f)[0, tile(b + 1), :] = source[tile(b), :]
            place(f, b + 1, cols_s[tile(b), :])
    load(HALO * PLANES)
    for f in range(PLANES):
        place(f, 0, cols_s[tile(TILES - 1), :])
        place(f, TILES + 1, cols_s[tile(0), :])

    at_north, at_south = ints[NORTH] > 0, ints[SOUTH] > 0
    at_west, at_east = ints[WEST] > 0, ints[EAST] > 0
    for k in range(2):
        for half in range(2):
            first = jnp.broadcast_to(thick[k, half, 8:9, :], (8, CELLS))
            last = jnp.broadcast_to(thick[k, half, ROWS - 9 : ROWS - 8, :], (8, CELLS))
            for b, at_end, line in ((0, at_north, first), (TILES + 1, at_south, last)):
                thick[k, half, tile(b), :] = jnp.where(at_end, line, thick[k, half, tile(b), :])
        for b in range(TILES + 2):
            own, other = thick[k, 0, tile(b), :], thick[k, 1, tile(b), :]
            other = jnp.where((lane == CELLS - 1) & at_west, turn(own, -1), other)
            other = jnp.where((lane == 0) & at_east, turn(own, 1), other)
            thick[k, 1, tile(b), :] = jnp.where(other > 0.0, other, 1.0)

    for b in range(TILES + 2):
        found = [around(thick.at[k], b, 2) for k in range(2)]
        for half in range(2):
            between = 0.5 * (found[0][half][0] + found[1][half][0])
            for k in range(2):
                here, *others = found[k][half]
                faces = [0.5 * (here + other) for other in others]
                diagonal = (faces[0] + faces[1]) + (faces[2] + faces[3]) + (between + here)
                inverse = 0.8 / diagonal
                for n, face in enumerate(faces):
                    coef[n, k, half, tile(b), :] = inverse * face
                coef[4, k, half, tile(b), :] = inverse * between
                coef[5, k, half, tile(b), :] = 0.5 * inverse
                coef[6, k, half, tile(b), :] = inverse * warm[k, half, tile(b), :]
                coef[7, k, half, tile(b), :] = 0.125 * here

    mixed[...] = jnp.zeros((4, CELLS, CELLS), F32)
    for term in range(2):
        lo = pl.multiple_of(2 * HALO * PLANES + 8 * (ints[LAT_BASE] + term), 8)
        mixed[term, tile(TILES - 1), :] = west[pl.ds(lo, 8), :]
        mixed[term, tile(0), :] = east[pl.ds(lo, 8), :]
        mixed[2 + term, tile(TILES - 1), :] = north[8 + ints[LON_BASE] + term]
        mixed[2 + term, tile(0), :] = south[8 + ints[LON_BASE] + term]


def split(x):
    high = x.astype(jnp.bfloat16)
    return high, (x - high.astype(F32)).astype(jnp.bfloat16)


def blended(block, weights):
    dims = (((1,), (1,)), ((), ()))
    b_high, b_low = split(block)
    w_high, w_low = split(weights)
    out = lax.dot_general(b_high, w_low, dims, preferred_element_type=F32)
    out = out + lax.dot_general(b_low, w_high, dims, preferred_element_type=F32)
    return out + lax.dot_general(b_high, w_high, dims, preferred_element_type=F32)


def blend_sides(ints, arrived, weights, mixed, lat_ghost, lon_ghost):
    sides = (
        (lat_ghost, (ints[NORTH] + ints[SOUTH]) > 0, PLACES, ints[LAT_BASE], 0),
        (lon_ghost, (ints[WEST] + ints[EAST]) > 0, PLACES + 6, ints[LON_BASE], 2),
    )
    for ghost, active, places, base, near in sides:
        ghost[...] = jnp.zeros((8, LANES), F32)

        @pl.when(active)
        def _():
            own = jnp.zeros((8, CELLS), F32)
            ends = jnp.zeros((16, CELLS), F32)
            for term in range(2):
                own = own + blended(arrived[ints[places + term]], weights[base + term])
                low, high = arrived[ints[places + 2 + term]], arrived[ints[places + 4 + term]]
                ends = ends + blended(jnp.concatenate([low, high], axis=0), mixed[near + term])
            ghost[:, 0:CELLS] = own
            ghost[:, CELLS:LANES] = jnp.where(lanes() < CELLS // 2, ends[8:16], ends[0:8])


def blend_kernel(ints, fields, coef, arrived, weights, mixed, lat_ghost, lon_ghost, row, packed):
    blend_sides(ints, arrived, weights, mixed, lat_ghost, lon_ghost)
    at = ints[0] + 8
    lane, sub = lanes(), sublanes()
    for f in range(8):
        packed[0, f : f + 1, :] = fields[f, 0, pl.ds(at, 1), :]
        packed[1, f : f + 1, :] = fields[f, 1, pl.ds(at, 1), :]
        packed[2, f : f + 1, :] = fields[f, 0, pl.ds(at - 1, 1), :]
        packed[3, f : f + 1, :] = fields[f, 0, pl.ds(at + 1, 1), :]
    here, outside, up, down = packed[0], packed[1], packed[2], packed[3]
    up = jnp.where((ints[NORTH] > 0) & (at == 8), lat_ghost[:, 0:CELLS], up)
    down = jnp.where((ints[SOUTH] > 0) & (at == CELLS + 7), lat_ghost[:, 0:CELLS], down)
    beside = jnp.sum(jnp.where(lane == ints[0], lon_ghost[:, 0:CELLS], 0.0), axis=1, keepdims=True)
    on_side = ((lane == CELLS - 1) & (ints[WEST] > 0)) | ((lane == 0) & (ints[EAST] > 0))
    outside = jnp.where(on_side, beside, outside)
    lefts, rights = sideways(here, outside)
    left, right = lefts[0], rights[0]
    even = sub % 2 == 0

    def factor(n):
        return jnp.where(even, coef[n, 0, 0, pl.ds(at, 1), :], coef[n, 1, 0, pl.ds(at, 1), :])

    partner = jnp.where(even, pltpu.roll(here, 7, 0), pltpu.roll(here, 1, 0))
    value = 0.2 * here + factor(0) * up + factor(1) * down
    value = value + factor(2) * left + factor(3) * right + factor(4) * partner
    value = value + jnp.where(sub < 2, factor(6), 0.0)
    steps = (jnp.where(even, partner, -partner), down - up, right - left)
    slope = jnp.where(
        sub < 2,
        pltpu.roll(steps[0], 2, 0),
        jnp.where(sub < 4, pltpu.roll(steps[1], 4, 0), pltpu.roll(steps[2], 6, 0)),
    )
    value = value - factor(5) * slope
    divergence = (
        pltpu.roll(steps[0], 6, 0) + pltpu.roll(steps[1], 4, 0) + pltpu.roll(steps[2], 2, 0)
    )
    row[...] = jnp.where(sub < 6, value, here - factor(7) * divergence)


def with_ghosts(ints, count, fields, lat_ghost, lon_ghost, full, cols_s, ends_s, rows_s):
    lane, sub = lanes(), sublanes()
    rows_s[...] = jnp.zeros((CELLS, CELLS), F32)
    for cut, out in ((slice(0, CELLS), cols_s), (slice(CELLS, LANES), ends_s)):
        for f in range(count):
            rows_s[2 * f : 2 * f + 1, :] = lon_ghost[f : f + 1, cut]
            last = (2 * f - 1) % CELLS
            rows_s[last : last + 1, :] = lon_ghost[f : f + 1, cut]
        out[...] = rows_s[...].T
    at_north, at_south = ints[NORTH] > 0, ints[SOUTH] > 0
    on_side = ((lane == CELLS - 1) & (ints[WEST] > 0)) | ((lane == 0) & (ints[EAST] > 0))
    for b in range(TILES + 2):
        if b == 0:
            column = ends_s[tile(TILES - 1), :]
        elif b == TILES + 1:
            column = ends_s[tile(0), :]
        else:
            column = cols_s[tile(b - 1), :]
        for f in range(count):
            own, other = fields[f, 0, tile(b), :], fields[f, 1, tile(b), :]
            if b == 0 or b == TILES + 1:
                edge = (sub == 7) & at_north if b == 0 else (sub == 0) & at_south
                own = jnp.where(edge, lat_ghost[f : f + 1, 0:CELLS], own)
                other = jnp.where(edge, lat_ghost[f : f + 1, CELLS:LANES], other)
            full[f, 0, tile(b), :] = own
            full[f, 1, tile(b), :] = jnp.where(on_side, turn(column, -2 * f), other)


def relaxed(full, coef, b, halves):
    found = [around(full.at[f], b, halves) for f in range(8)]
    answers = []
    for half in range(halves):
        at = [found[f][half] for f in range(8)]

        def factor(n, k):
            return coef[n, k, half, tile(b), :]

        new = []
        for component in range(3):
            for k in range(2):
                here, up, down, left, right = at[2 * component + k]
                value = 0.2 * here + factor(0, k) * up + factor(1, k) * down
                value = value + factor(2, k) * left + factor(3, k) * right
                value = value + factor(4, k) * at[2 * component + 1 - k][0]
                if component == 0:
                    value = value + factor(6, k)
                    slope = at[7][0] if k == 0 else -at[6][0]
                elif component == 1:
                    slope = at[6 + k][2] - at[6 + k][1]
                else:
                    slope = at[6 + k][4] - at[6 + k][3]
                new.append(value - factor(5, k) * slope)
        for k in range(2):
            divergence = (at[2 + k][2] - at[2 + k][1]) + (at[4 + k][4] - at[4 + k][3])
            divergence = divergence + at[1][0] if k == 0 else divergence - at[0][0]
            new.append(at[6 + k][0] - factor(7, k) * divergence)
        answers.append(new)
    return answers


def sweep_kernel(ints, fields, coef, lat_ghost, lon_ghost, out, full, cols_s, ends_s, rows_s):
    with_ghosts(ints, 8, fields, lat_ghost, lon_ghost, full, cols_s, ends_s, rows_s)
    for b in range(TILES + 2):
        for half, new in enumerate(relaxed(full, coef, b, 2)):
            for f in range(8):
                out[f, half, tile(b), :] = new[f]


def relay_kernel(places, arrived, out):
    for n in range(8):
        out[2 * n : 2 * n + 2, :] = arrived[places[n], 0:2, :]


def heat_kernel(ints, warm, blocks, weights, out, lat_ghost, lon_ghost, cols_s, ends_s, rows_s):
    sides = (
        (lat_ghost, (ints[NORTH] + ints[SOUTH]) > 0, ints[LAT_BASE]),
        (lon_ghost, (ints[WEST] + ints[EAST]) > 0, ints[LON_BASE]),
    )
    for ghost, active, base in sides:
        ghost[...] = jnp.zeros((8, LANES), F32)

        @pl.when(active)
        def _():
            total = jnp.zeros((16, CELLS), F32)
            for term in range(2):
                total = total + blended(blocks[base + term], weights[base + term])
            ghost[:, 0:CELLS] = total[0:8]

    with_ghosts(ints, 2, warm, lat_ghost, lon_ghost, out, cols_s, ends_s, rows_s)


def final_kernel(
    ints, fields, coef, arrived, weights, mixed, warm,
    flow_out, pressure_out, heat_out, lat_ghost, lon_ghost, full, cols_s, ends_s, rows_s,
):
    blend_sides(ints, arrived, weights, mixed, lat_ghost, lon_ghost)
    with_ghosts(ints, 8, fields, lat_ghost, lon_ghost, full, cols_s, ends_s, rows_s)
    for b in range(TILES):
        (new,) = relaxed(full, coef, b + 1, 1)
        for f in range(6):
            flow_out[f, tile(b), :] = new[f]
        for k in range(2):
            pressure_out[k, tile(b), :] = new[6 + k]
        layers = [around(warm.at[k], b + 1, 1)[0] for k in range(2)]
        for k in range(2):
            here, up, down, left, right = layers[k]
            below = jnp.ones((8, CELLS), F32) if k == 0 else layers[0][0]
            above = layers[1][0] if k == 0 else jnp.zeros((8, CELLS), F32)
            advect = jnp.zeros((8, CELLS), F32)
            for component, minus, plus in ((0, below, above), (1, up, down), (2, left, right)):
                speed = new[2 * component + k]
                advect = advect + jnp.maximum(speed, 0.0) * (here - minus)
                advect = advect + jnp.minimum(speed, 0.0) * (plus - here)
            spread = (up + down) + (left + right) + (below + above) - 6.0 * here
            heat_out[k, tile(b), :] = here + 0.1 * (spread - advect)


def shape(*dims):
    return jax.ShapeDtypeStruct(dims, F32)


def scratch(*dims):
    return pltpu.VMEM(dims, F32)


def call(kernel, outs, ins, scratches, specs=None, aliases=None, name=None):
    return pl.pallas_call(
        kernel,
        out_shape=outs,
        in_specs=specs or [SMEM] + [VMEM] * (len(ins) - 1),
        out_specs=[VMEM] * len(outs),
        scratch_shapes=scratches,
        input_output_aliases=aliases or {},
        compiler_params=pltpu.CompilerParams(vmem_limit_bytes=32 * 1024 * 1024),
        name=name,
    )(*ins)


def shards(
    flow_vector,
    normal_stress,
    thermal_field,
    shear_resistance,
    departing_bands,
    receiving_processor,
    shift_filled_by_lane,
    blending_factors,
):
    flow = flow_vector.reshape(6, CELLS, CELLS)
    pressure = normal_stress[0]
    heat = thermal_field[0]
    friction = shear_resistance[0]
    weights = blending_factors.reshape(8, CELLS, CELLS)
    lat, lon = lax.axis_index("lat"), lax.axis_index("lon")
    n_lat, n_lon = lax.axis_size("lat"), lax.axis_size("lon")
    devices = n_lat * n_lon
    own_row = departing_bands.reshape(1)

    def swap(x):
        return lax.ppermute(x, "patch", [(0, 1), (1, 0)])

    def ring(x, axis, step):
        count = lax.axis_size(axis)
        pairs = [(i, i + step) for i in range(count) if 0 <= i + step < count]
        return lax.ppermute(x, axis, pairs)

    def to_relay(x):
        return lax.ppermute(x, "lon", [(i, i ^ 2) for i in range(n_lon)])

    def deliver(buffer):
        return lax.all_to_all(buffer, ("lat", "lon"), 0, 0, tiled=True)

    receiver = swap(receiving_processor.reshape(1).astype(F32)).astype(jnp.int32)
    receiver = jnp.maximum(receiver, 0)
    near = receiver + jnp.array([0, 1, -1, n_lon, -n_lon], jnp.int32)
    near = jnp.where((near >= 0) & (near < devices), near, receiver)
    chunks = jnp.concatenate([near, receiver ^ 2])

    row, top, bottom = call(
        start_kernel,
        [shape(16, CELLS), shape(17, 8, CELLS), shape(17, 8, CELLS)],
        (own_row, shift_filled_by_lane.reshape(1, CELLS), flow, pressure, heat, friction, weights),
        [scratch(10, 8, CELLS), pltpu.SemaphoreType.DMA((13,))],
        specs=[SMEM, VMEM] + [ANY] * 5,
        name="start",
    )
    (buffer,) = call(
        fill_kernel, [shape(devices, 8, CELLS)], (chunks, swap(row)), [], name="fill"
    )
    arrived = deliver(buffer)
    north, south = ring(bottom, "lat", 1), ring(top, "lat", -1)
    wide = shape(2 * HALO * PLANES + 32, CELLS)
    to_west, to_east = call(
        columns_kernel,
        [wide, wide],
        (flow, pressure, heat, friction, weights, north, south),
        [scratch(CELLS, CELLS)] * 2,
        specs=[VMEM] * 7,
        name="columns",
    )
    places = top[16]
    to_west = jnp.concatenate([to_west, places])
    to_east = jnp.concatenate([to_east, places])
    west, east = ring(to_east, "lon", 1), ring(to_west, "lon", -1)

    def numbers(block):
        return block[:, 0].astype(jnp.int32)

    on_edge = jnp.stack([lat == 0, lat == n_lat - 1, lon == 0, lon == n_lon - 1]).astype(jnp.int32)
    own = numbers(places)

    def side(block, base, last):
        return jnp.where(last, block[base + 2 : base + 4], block[base : base + 2])

    pick = [side(numbers(x), 0, lat > 0) for x in (places, west[-8:], east[-8:])]
    pick += [side(numbers(x), 4, lon > 0) for x in (places, north[16], south[16])]
    bases = jnp.stack([jnp.where(lat > 0, 2, 0), jnp.where(lon > 0, 6, 4)]).astype(jnp.int32)
    ints = jnp.concatenate([own_row, on_edge] + pick + [bases])

    fields, coef, warm, mixed = call(
        build_kernel,
        [
            shape(8, 2, ROWS, CELLS),
            shape(8, 2, 2, ROWS, CELLS),
            shape(2, 2, ROWS, CELLS),
            shape(4, CELLS, CELLS),
        ],
        (ints, flow, pressure, heat, friction, north, south, west, east),
        [scratch(2, 2, ROWS, CELLS)] + [scratch(CELLS, CELLS)] * 2,
        name="build",
    )
    relayed = numbers(to_relay(places))
    squares = [scratch(CELLS, CELLS)] * 3
    ghost = shape(8, LANES)
    first_arrived = arrived
    for sweep in range(SWEEPS - 1):
        lat_ghost, lon_ghost, row = call(
            blend_kernel,
            [ghost, ghost, shape(8, CELLS)],
            (ints, fields, coef, arrived, weights, mixed),
            [scratch(4, 8, CELLS)],
            name="blend",
        )
        (buffer,) = call(
            refill_kernel,
            [shape(devices, 8, CELLS)],
            (chunks, swap(row), buffer),
            [],
            aliases={2: 0},
            name="refill",
        )
        arrived = deliver(buffer)
        (fields,) = call(
            sweep_kernel,
            [shape(8, 2, ROWS, CELLS)],
            (ints, fields, coef, lat_ghost, lon_ghost),
            [scratch(8, 2, ROWS, CELLS)] + squares,
            name="sweep",
        )
        if sweep == 0:
            (blocks,) = call(
                relay_kernel, [shape(16, CELLS)], (relayed, first_arrived), [], name="relay"
            )
            blocks = to_relay(blocks).reshape(8, 2, CELLS)
            blocks = jnp.pad(blocks, ((0, 0), (0, 14), (0, 0)))
            (warm,) = call(
                heat_kernel,
                [shape(2, 2, ROWS, CELLS)],
                (ints, warm, blocks, weights),
                [scratch(8, LANES)] * 2 + squares,
                name="heat",
            )
    flow, pressure, heat = call(
        final_kernel,
        [shape(6, CELLS, CELLS), shape(2, CELLS, CELLS), shape(2, CELLS, CELLS)],
        (ints, fields, coef, arrived, weights, mixed, warm),
        [scratch(8, LANES)] * 2 + [scratch(8, 2, ROWS, CELLS)] + squares,
        name="final",
    )
    return flow.reshape(3, 1, 2, CELLS, CELLS), pressure[None], heat[None]


def solution(mesh):
    placed = (
        P(None, "patch", None, "lat", "lon"),
        P("patch", None, "lat", "lon"),
        P("patch", None, "lat", "lon"),
        P("patch", None, "lat", "lon"),
        P("patch", "lat", "lon", None),
        P("patch", "lat", "lon", None),
        P("patch", "lat", "lon", None),
        P("patch", "lat", "lon", None, None, None),
    )
    return jax.shard_map(
        shards,
        mesh=mesh,
        in_specs=placed,
        out_specs=(
            P(None, "patch", None, "lat", "lon"),
            P("patch", None, "lat", "lon"),
            P("patch", None, "lat", "lon"),
        ),
        check_vma=False,
    )
```

time: 2270 us -> 174 us (0.08)
  blocking collectives: 2050 us -> 0 us
  waiting for transfers between devices: 4.52 us -> 50.1 us
  local copies, waits for them, and re-layouts: 75.4 us -> 30.1 us
  other arithmetic: 42.4 us -> 0.92 us
    all_gather x5 -> x0, blocking collectives: 1710 us -> none  [widen_sector(): lax.all_gather(crossed[0], ('lat', 'lon'), axis=2, tiled=True)]
    unnamed x1 -> x0, blocking collectives: 343 us -> none
    all_to_all x0 -> x4, starting transfers between devices: none -> 48.4 us  [deliver(): return lax.all_to_all(buffer, ('lat', 'lon'), 0, 0, tiled=True)]
    ppermute x30 -> x11, starting transfers between devices: 64.7 us -> 17 us  [the longest x4 10.9 us: ring(): return lax.ppermute(x, axis, pairs)]
    scatter-add x20 -> x0, local copies, waits for them, and re-layouts: 45.6 us -> none  [the longest x5 18.2 us: widen_sector(): bordered_mesh = bordered_mesh.at[:, 1:-1, 1:-1, -1].add(cycle_vals[:, :, 3])]
    all_to_all x0 -> x4, waiting for transfers between devices: none -> 37.5 us  [deliver(): return lax.all_to_all(buffer, ('lat', 'lon'), 0, 0, tiled=True)]
    unnamed x111 -> x82, local copies, waits for them, and re-layouts: 5.56 us -> 30 us
    add x25 -> x0, other arithmetic: 23.2 us -> none  [the longest x5 8.54 us: widen_sector(): bordered_mesh = bordered_mesh.at[:, 1:-1, 1:-1, 0].add(cycle_vals[:, :, 2])]
  transfers between devices with their start and end apart: 30 -> 15, of which waited for: 2 -> 10; matrix products, arithmetic and copies ran while one was open for 2% -> 1% of each run, Pallas kernels for 0% -> 5%
where the time goes in v2:
time: 174 us; the launch traced here: 172 us
  starting transfers between devices  65.4 us (38%)
  waiting for transfers between devices  50.1 us (29%)
  local copies, waits for them, and re-layouts  30.1 us (17%)
  Pallas kernels  22.1 us (13%)
  between operations  3.06 us (2%)
    all_to_all x4, starting transfers between devices, deliver(): return lax.all_to_all(buffer, ('lat', 'lon'), 0, 0, tiled=True)  48.4 us
    all_to_all x4, waiting for transfers between devices, deliver(): return lax.all_to_all(buffer, ('lat', 'lon'), 0, 0, tiled=True)  37.5 us
    unnamed x82, local copies, waits for them, and re-layouts  30 us
    pallas_call x16, Pallas kernels, call(): pl.pallas_call(kernel, out_shape=outs, in_specs=specs or [SMEM] + [VMEM]...  22.1 us
    ppermute x4, starting transfers between devices, ring(): return lax.ppermute(x, axis, pairs)  10.9 us
    ppermute x2, waiting for transfers between devices, to_relay(): return lax.ppermute(x, 'lon', [(i, i ^ 2) for i in range(n_lon)])  6.35 us
    ppermute x2, starting transfers between devices, to_relay(): return lax.ppermute(x, 'lon', [(i, i ^ 2) for i in range(n_lon)])  4.3 us
  transfers between devices with their start and end apart: 15, of which 10 were waited for; matrix products, arithmetic and copies ran while one was open for 1% of the time, Pallas kernels for 5%

profile of v2, /device:TPU:2, one launch (start us, length us, event | category | flops | bytes accessed | tf_op | source)
XLA Modules:
  0.0 171.8 jit_solution(14005654830711952954)
XLA Ops:
  1.3 1.0 collective-permute-start.4
  3.0 1.0 copy-done
  4.0 1.0 copy-done.18
  5.0 0.9 copy-done.21
  5.9 0.9 copy-done.23
  6.9 0.9 copy-done.26
  7.8 0.7 copy-done.39
  9.3 3.8 %collective-permute-start = (f32[17,8,128]{2,1,0:T(8,128)S(1)}, f32[17,8,128]{2,1,0:T(8,128)S(1)}, u32[]{:S(2)}, u32[]{:S(2)}) collective-permute-start(f32[17,8,128]{2,1,0:T(8,128)S(1)} %get-tuple-element.25), channel_id=1, source_target_pairs={{0,16},{16,32},{32,48},{48,64},{64,80},{80,96},{96,112},{1,17},{17... | collective-permute-start | bytes 208904 | tf_op jit(solution)/shard_map/ppermute | solution.py:458
  13.2 1.3 collective-permute-start.1
  15.5 1.4 fill.1.old
  16.9 17.4 %all-to-all-start = ((f32[128,8,128]{2,1,0:T(8,128)}), f32[128,8,128]{2,1,0:T(8,128)S(1)}, u32[]{:S(2)}, u32[]{:S(2)}) async-start(f32[128,8,128]{2,1,0:T(8,128)} %fill.1.old), calls=%async_computation | async-start | bytes 1048576 | tf_op jit(solution)/shard_map/all_to_all | solution.py:464
  34.9 2.8 %collective-permute-start.3 = (f32[136,128]{1,0:T(8,128)S(1)}, f32[136,128]{1,0:T(8,128)S(1)}, u32[]{:S(2)}, u32[]{:S(2)}) collective-permute-start(f32[136,128]{1,0:T(8,128)S(1)} %get-tuple-element.53), channel_id=1, source_target_pairs={{1,0},{2,1},{3,2},{4,3},{5,4},{6,5},{7,6},{8,7},{9,8},{10,9},{11,1... | collective-permute-start | bytes 208904 | tf_op jit(solution)/shard_map/ppermute | solution.py:458
  37.7 3.0 %collective-permute-start.2 = (f32[136,128]{1,0:T(8,128)S(1)}, f32[136,128]{1,0:T(8,128)S(1)}, u32[]{:S(2)}, u32[]{:S(2)}) collective-permute-start(f32[136,128]{1,0:T(8,128)S(1)} %get-tuple-element.54), channel_id=1, source_target_pairs={{0,1},{1,2},{2,3},{3,4},{4,5},{5,6},{6,7},{7,8},{8,9},{9,10},{10,1... | collective-permute-start | bytes 208904 | tf_op jit(solution)/shard_map/ppermute | solution.py:458
  40.9 1.2 collective-permute-done.3.east
  42.8 1.7 collective-permute-done.2.west
  44.5 0.6 copy-done.37
  45.3 1.0 copy-done.20
  46.3 0.9 copy-done.25
  47.2 0.9 copy-done.28
  48.1 0.9 copy-done.30
  49.0 0.9 copy-done.32
  49.9 0.9 copy-done.36
  50.8 0.9 copy-done.38
  51.7 1.4 build.1
  53.1 1.0 copy-done.8
  54.1 0.7 copy-done.13
  54.8 0.7 copy-done.33
  55.6 1.3 copy-done.9
  56.8 0.9 copy-done.14
  57.8 1.0 blend.3
  58.8 1.2 collective-permute-done.6.row
  60.0 1.9 %refill.3.old = f32[128,8,128]{2,1,0:T(8,128)} custom-call(s32[6]{0:T(128)S(1)} %pad_add_fusion.chunks, f32[8,128]{1,0:T(8,128)S(1)} %collective-permute-done.6.row, f32[128,8,128]{2,1,0:T(8,128)} %fill.1.old), custom_call_target="tpu_custom_call", output_to_operand_aliasing={{}: (2, {})} | custom-call | tf_op jit(solution)/shard_map/refill/pallas_call | solution.py:420
  61.9 14.9 %all-to-all-start.1 = ((f32[128,8,128]{2,1,0:T(8,128)}), f32[128,8,128]{2,1,0:T(8,128)}, u32[]{:S(2)}, u32[]{:S(2)}) async-start(f32[128,8,128]{2,1,0:T(8,128)} %refill.3.old), calls=%async_computation.1 | async-start | bytes 1048576 | tf_op jit(solution)/shard_map/all_to_all | solution.py:464
  76.8 1.3 copy-done.10
  78.0 1.4 sweep.3.fields
  79.5 1.0 copy-done.5
  80.5 16.3 %all-to-all-done.1.arrived = f32[128,8,128]{2,1,0:T(8,128)} async-done(((f32[128,8,128]{2,1,0:T(8,128)}), f32[128,8,128]{2,1,0:T(8,128)}, u32[]{:S(2)}, u32[]{:S(2)}) %all-to-all-start.1) | async-done | bytes 524320 | tf_op jit(solution)/shard_map/all_to_all | solution.py:464
  96.8 1.3 copy-done.6
  98.1 0.9 copy-done.15
  99.0 1.5 blend.4
  100.6 1.2 collective-permute-done.7.row
  101.8 1.9 %refill.4.old = f32[128,8,128]{2,1,0:T(8,128)} custom-call(s32[6]{0:T(128)S(1)} %pad_add_fusion.chunks, f32[8,128]{1,0:T(8,128)S(1)} %collective-permute-done.7.row, f32[128,8,128]{2,1,0:T(8,128)} %refill.3.old), custom_call_target="tpu_custom_call", output_to_operand_aliasing={{}: (2, {})} | custom-call | tf_op jit(solution)/shard_map/refill/pallas_call | solution.py:420
  103.6 8.0 %all-to-all-start.2 = ((f32[128,8,128]{2,1,0:T(8,128)}), f32[128,8,128]{2,1,0:T(8,128)}, u32[]{:S(2)}, u32[]{:S(2)}) async-start(f32[128,8,128]{2,1,0:T(8,128)} %refill.4.old), calls=%async_computation.2 | async-start | bytes 1048576 | tf_op jit(solution)/shard_map/all_to_all | solution.py:464
  111.7 1.3 copy-done.7
  112.9 1.4 sweep.4.fields
  114.4 1.0 copy-done.2
  115.4 16.6 %all-to-all-done.2.arrived = f32[128,8,128]{2,1,0:T(8,128)} async-done(((f32[128,8,128]{2,1,0:T(8,128)}), f32[128,8,128]{2,1,0:T(8,128)}, u32[]{:S(2)}, u32[]{:S(2)}) %all-to-all-start.2) | async-done | bytes 524320 | tf_op jit(solution)/shard_map/all_to_all | solution.py:464
  132.0 1.3 copy-done.3
  133.3 0.9 copy-done.16
  134.2 1.5 blend.5
  135.8 1.2 collective-permute-done.8.row
  136.9 1.9 %refill.5 = f32[128,8,128]{2,1,0:T(8,128)} custom-call(s32[6]{0:T(128)S(1)} %pad_add_fusion.chunks, f32[8,128]{1,0:T(8,128)S(1)} %collective-permute-done.8.row, f32[128,8,128]{2,1,0:T(8,128)} %refill.4.old), custom_call_target="tpu_custom_call", output_to_operand_aliasing={{}: (2, {})} | custom-call | tf_op jit(solution)/shard_map/refill/pallas_call | solution.py:420
  138.8 8.1 %all-to-all-start.3 = ((f32[128,8,128]{2,1,0:T(8,128)}), f32[128,8,128]{2,1,0:T(8,128)}, u32[]{:S(2)}, u32[]{:S(2)}) async-start(f32[128,8,128]{2,1,0:T(8,128)} %refill.5), calls=%async_computation.3 | async-start | bytes 1048576 | tf_op jit(solution)/shard_map/all_to_all | solution.py:464
  147.0 2.2 %collective-permute-start.9 = (f32[8,128]{1,0:T(8,128)S(1)}, f32[8,128]{1,0:T(8,128)S(1)}, u32[]{:S(2)}, u32[]{:S(2)}) collective-permute-start(f32[8,128]{1,0:T(8,128)S(1)} %slice_bitcast_fusion.2), channel_id=1, source_target_pairs={{0,2},{1,3},{2,0},{3,1},{4,6},{5,7},{6,4},{7,5},{8,10},{9,11},{10,... | collective-permute-start | bytes 12296 | tf_op jit(solution)/shard_map/ppermute | solution.py:461
  149.1 3.1 %collective-permute-done.9 = f32[8,128]{1,0:T(8,128)S(1)} collective-permute-done((f32[8,128]{1,0:T(8,128)S(1)}, f32[8,128]{1,0:T(8,128)S(1)}, u32[]{:S(2)}, u32[]{:S(2)}) %collective-permute-start.9) | collective-permute-done | bytes 4128 | tf_op jit(solution)/shard_map/ppermute | solution.py:461
  152.9 2.1 %collective-permute-start.10 = (f32[16,128]{1,0:T(8,128)S(1)}, f32[16,128]{1,0:T(8,128)S(1)}, u32[]{:S(2)}, u32[]{:S(2)}) collective-permute-start(f32[16,128]{1,0:T(8,128)S(1)} %relay.1), channel_id=1, source_target_pairs={{0,2},{1,3},{2,0},{3,1},{4,6},{5,7},{6,4},{7,5},{8,10},{9,11},{10,... | collective-permute-start | bytes 24584 | tf_op jit(solution)/shard_map/ppermute | solution.py:461
  155.0 3.3 %collective-permute-done.10 = f32[16,128]{1,0:T(8,128)S(1)} collective-permute-done((f32[16,128]{1,0:T(8,128)S(1)}, f32[16,128]{1,0:T(8,128)S(1)}, u32[]{:S(2)}, u32[]{:S(2)}) %collective-permute-start.10) | collective-permute-done | bytes 8224 | tf_op jit(solution)/shard_map/ppermute | solution.py:461
  158.3 1.0 copy-done.34
  159.3 1.0 heat.1.warm
  160.2 1.4 sweep.5.fields
  161.7 1.0 copy-done.11
  162.7 4.6 %all-to-all-done.3.arrived = f32[128,8,128]{2,1,0:T(8,128)} async-done(((f32[128,8,128]{2,1,0:T(8,128)}), f32[128,8,128]{2,1,0:T(8,128)}, u32[]{:S(2)}, u32[]{:S(2)}) %all-to-all-start.3) | async-done | bytes 524320 | tf_op jit(solution)/shard_map/all_to_all | solution.py:464
  167.3 1.3 copy-done.12
  168.6 3.2 %final.1 = (f32[6,128,128]{2,1,0:T(8,128)}, f32[2,128,128]{2,1,0:T(8,128)}, f32[2,128,128]{2,1,0:T(8,128)}) custom-call(s32[19]{0:T(128)S(1)} %concatenate.14.ints, f32[8,2,144,128]{3,2,1,0:T(8,128)S(1)} %copy-done.12, f32[8,2,2,144,128]{4,3,2,1,0:T(8,128)S(1)} %get-tuple-element.29.coef, f32[128,8,128]{2,1,0:T(8,128)} %all-to-all-done.3.arrived, ...), custom_call_target="tpu_custom_call" | custom-call | tf_op jit(solution)/shard_map/final/pallas_call | solution.py:420
  (84 shorter events, 3.7 us)
Async XLA Ops:
  0.6 14.8 %copy-start.40 = (s32[5]{0:T(128)S(1)}, s32[5]{0:T(128)}, u32[]{:S(2)}) copy-start(s32[5]{0:T(128)} %constant.32.clone) | copy-start | bytes 64
  1.3 13.4 %collective-permute-start.4 = (f32[1]{0:T(128)}, f32[1]{0:T(128)}, u32[]{:S(2)}, u32[]{:S(2)}) collective-permute-start(f32[1]{0:T(128)} %bitcast.16), channel_id=1, source_target_pairs={{0,128},{128,0},{1,129},{129,1},{2,130},{130,2},{3,131},{131,3},{4... | collective-permute-start | bytes 20 | tf_op jit(solution)/shard_map/ppermute | solution.py:453
  3.0 1.0 copy-start
  4.0 1.0 copy-start.18
  5.0 0.9 copy-start.21
  5.9 0.9 copy-start.23
  6.8 0.9 copy-start.26
  7.8 0.7 copy-start.39
  8.4 26.0 %copy-start.1 = (f32[1,1,1,8,128,128]{5,4,3,2,1,0:T(8,128)S(1)}, f32[1,1,1,8,128,128]{5,4,3,2,1,0:T(8,128)}, u32[]{:S(2)}) copy-start(f32[1,1,1,8,128,128]{5,4,3,2,1,0:T(8,128)} %param.16) | copy-start | bytes 1572868
  8.4 26.0 %copy-start.19 = (f32[3,1,2,128,128]{4,3,2,1,0:T(8,128)S(1)}, f32[3,1,2,128,128]{4,3,2,1,0:T(8,128)}, u32[]{:S(2)}) copy-start(f32[3,1,2,128,128]{4,3,2,1,0:T(8,128)} %param.9) | copy-start | bytes 1179652
  8.4 26.0 %copy-start.22 = (f32[1,2,128,128]{3,2,1,0:T(8,128)S(1)}, f32[1,2,128,128]{3,2,1,0:T(8,128)}, u32[]{:S(2)}) copy-start(f32[1,2,128,128]{3,2,1,0:T(8,128)} %param.10) | copy-start | bytes 393220
  8.4 26.0 %copy-start.24 = (f32[1,2,128,128]{3,2,1,0:T(8,128)S(1)}, f32[1,2,128,128]{3,2,1,0:T(8,128)}, u32[]{:S(2)}) copy-start(f32[1,2,128,128]{3,2,1,0:T(8,128)} %param.11) | copy-start | bytes 393220
  8.4 26.0 %copy-start.27 = (f32[1,2,128,128]{3,2,1,0:T(8,128)S(1)}, f32[1,2,128,128]{3,2,1,0:T(8,128)}, u32[]{:S(2)}) copy-start(f32[1,2,128,128]{3,2,1,0:T(8,128)} %param.12) | copy-start | bytes 393220
  8.7 6.8 %collective-permute-start.5 = (f32[16,128]{1,0:T(8,128)S(1)}, f32[16,128]{1,0:T(8,128)S(1)}, u32[]{:S(2)}, u32[]{:S(2)}) collective-permute-start(f32[16,128]{1,0:T(8,128)S(1)} %get-tuple-element.30), channel_id=1, source_target_pairs={{0,128},{128,0},{1,129},{129,1},{2,130},{130,2},{3,131},{131,3},{4... | collective-permute-start | bytes 24584 | tf_op jit(solution)/shard_map/ppermute | solution.py:453
  9.3 24.9 %collective-permute-start = (f32[17,8,128]{2,1,0:T(8,128)S(1)}, f32[17,8,128]{2,1,0:T(8,128)S(1)}, u32[]{:S(2)}, u32[]{:S(2)}) collective-permute-start(f32[17,8,128]{2,1,0:T(8,128)S(1)} %get-tuple-element.25), channel_id=1, source_target_pairs={{0,16},{16,32},{32,48},{48,64},{64,80},{80,96},{96,112},{1,17},{17... | collective-permute-start | bytes 208904 | tf_op jit(solution)/shard_map/ppermute | solution.py:458
  13.2 21.3 %collective-permute-start.1 = (f32[17,8,128]{2,1,0:T(8,128)S(1)}, f32[17,8,128]{2,1,0:T(8,128)S(1)}, u32[]{:S(2)}, u32[]{:S(2)}) collective-permute-start(f32[17,8,128]{2,1,0:T(8,128)S(1)} %get-tuple-element.24), channel_id=1, source_target_pairs={{16,0},{32,16},{48,32},{64,48},{80,64},{96,80},{112,96},{17,1},{33... | collective-permute-start | bytes 208904 | tf_op jit(solution)/shard_map/ppermute | solution.py:458
  16.9 38.7 %all-to-all-start = ((f32[128,8,128]{2,1,0:T(8,128)}), f32[128,8,128]{2,1,0:T(8,128)S(1)}, u32[]{:S(2)}, u32[]{:S(2)}) async-start(f32[128,8,128]{2,1,0:T(8,128)} %fill.1.old), calls=%async_computation | async-start | bytes 1048576 | tf_op jit(solution)/shard_map/all_to_all | solution.py:464
  34.3 11.0 %copy-start.29 = (f32[17,8,128]{2,1,0:T(8,128)}, f32[17,8,128]{2,1,0:T(8,128)S(1)}, u32[]{:S(2)}) copy-start(f32[17,8,128]{2,1,0:T(8,128)S(1)} %collective-permute-done.north) | copy-start | bytes 208900
  34.5 10.8 %copy-start.31 = (f32[17,8,128]{2,1,0:T(8,128)}, f32[17,8,128]{2,1,0:T(8,128)S(1)}, u32[]{:S(2)}) copy-start(f32[17,8,128]{2,1,0:T(8,128)S(1)} %collective-permute-done.1.south) | copy-start | bytes 208900
  34.9 7.2 %collective-permute-start.3 = (f32[136,128]{1,0:T(8,128)S(1)}, f32[136,128]{1,0:T(8,128)S(1)}, u32[]{:S(2)}, u32[]{:S(2)}) collective-permute-start(f32[136,128]{1,0:T(8,128)S(1)} %get-tuple-element.53), channel_id=1, source_target_pairs={{1,0},{2,1},{3,2},{4,3},{5,4},{6,5},{7,6},{8,7},{9,8},{10,9},{11,1... | collective-permute-start | bytes 208904 | tf_op jit(solution)/shard_map/ppermute | solution.py:458
  37.7 6.8 %collective-permute-start.2 = (f32[136,128]{1,0:T(8,128)S(1)}, f32[136,128]{1,0:T(8,128)S(1)}, u32[]{:S(2)}, u32[]{:S(2)}) collective-permute-start(f32[136,128]{1,0:T(8,128)S(1)} %get-tuple-element.54), channel_id=1, source_target_pairs={{0,1},{1,2},{2,3},{3,4},{4,5},{5,6},{6,7},{7,8},{8,9},{9,10},{10,1... | collective-permute-start | bytes 208904 | tf_op jit(solution)/shard_map/ppermute | solution.py:458
  42.1 0.6 copy-start.35
  44.5 0.6 copy-start.37
  45.3 1.0 copy-start.20
  46.3 0.9 copy-start.25
  47.2 0.9 copy-start.28
  48.1 0.9 copy-start.30
  49.0 0.9 copy-start.32
  49.9 0.9 copy-start.36
  50.8 0.9 copy-start.38
  53.1 1.0 copy-start.8
  54.1 0.7 copy-start.13
  54.8 0.7 copy-start.33
  55.6 1.3 copy-start.9
  56.8 0.9 copy-start.14
  58.8 1.2 collective-permute-start.6
  61.9 35.0 %all-to-all-start.1 = ((f32[128,8,128]{2,1,0:T(8,128)}), f32[128,8,128]{2,1,0:T(8,128)}, u32[]{:S(2)}, u32[]{:S(2)}) async-start(f32[128,8,128]{2,1,0:T(8,128)} %refill.3.old), calls=%async_computation.1 | async-start | bytes 1048576 | tf_op jit(solution)/shard_map/all_to_all | solution.py:464
  76.7 1.3 copy-start.10
  79.5 1.0 copy-start.5
  96.8 1.3 copy-start.6
  98.1 0.9 copy-start.15
  100.6 1.2 collective-permute-start.7
  103.6 28.3 %all-to-all-start.2 = ((f32[128,8,128]{2,1,0:T(8,128)}), f32[128,8,128]{2,1,0:T(8,128)}, u32[]{:S(2)}, u32[]{:S(2)}) async-start(f32[128,8,128]{2,1,0:T(8,128)} %refill.4.old), calls=%async_computation.2 | async-start | bytes 1048576 | tf_op jit(solution)/shard_map/all_to_all | solution.py:464
  111.7 1.3 copy-start.7
  114.4 1.0 copy-start.2
  132.0 1.3 copy-start.3
  133.3 0.9 copy-start.16
  135.7 1.2 collective-permute-start.8
  138.8 28.5 %all-to-all-start.3 = ((f32[128,8,128]{2,1,0:T(8,128)}), f32[128,8,128]{2,1,0:T(8,128)}, u32[]{:S(2)}, u32[]{:S(2)}) async-start(f32[128,8,128]{2,1,0:T(8,128)} %refill.5), calls=%async_computation.3 | async-start | bytes 1048576 | tf_op jit(solution)/shard_map/all_to_all | solution.py:464
  147.0 13.3 %copy-start.4 = (f32[8,2,144,128]{3,2,1,0:T(8,128)S(1)}, f32[8,2,144,128]{3,2,1,0:T(8,128)}, u32[]{:S(2)}) copy-start(f32[8,2,144,128]{3,2,1,0:T(8,128)} %copy-done.2) | copy-start | bytes 3538948
  147.0 5.2 %collective-permute-start.9 = (f32[8,128]{1,0:T(8,128)S(1)}, f32[8,128]{1,0:T(8,128)S(1)}, u32[]{:S(2)}, u32[]{:S(2)}) collective-permute-start(f32[8,128]{1,0:T(8,128)S(1)} %slice_bitcast_fusion.2), channel_id=1, source_target_pairs={{0,2},{1,3},{2,0},{3,1},{4,6},{5,7},{6,4},{7,5},{8,10},{9,11},{10,... | collective-permute-start | bytes 12296 | tf_op jit(solution)/shard_map/ppermute | solution.py:461
  152.9 5.4 %collective-permute-start.10 = (f32[16,128]{1,0:T(8,128)S(1)}, f32[16,128]{1,0:T(8,128)S(1)}, u32[]{:S(2)}, u32[]{:S(2)}) collective-permute-start(f32[16,128]{1,0:T(8,128)S(1)} %relay.1), channel_id=1, source_target_pairs={{0,2},{1,3},{2,0},{3,1},{4,6},{5,7},{6,4},{7,5},{8,10},{9,11},{10,... | collective-permute-start | bytes 24584 | tf_op jit(solution)/shard_map/ppermute | solution.py:461
  158.3 1.0 copy-start.34
  160.2 7.1 %copy-start.17 = (f32[4,128,128]{2,1,0:T(8,128)S(1)}, f32[4,128,128]{2,1,0:T(8,128)}, u32[]{:S(2)}) copy-start(f32[4,128,128]{2,1,0:T(8,128)} %copy-done.13) | copy-start | bytes 786436
  161.7 1.0 copy-start.11
  167.3 1.3 copy-start.12

commit v3 on v2

v3 whole, which is shorter than its diff:
```python
import jax
import jax.numpy as jnp
from jax import lax
from jax.experimental import pallas as pl
from jax.experimental.pallas import tpu as pltpu
from jax.sharding import PartitionSpec as P

SWEEPS = 4
CELLS = 128
TILES = 16
ROWS = CELLS + 16
LANES = 2 * CELLS
HALO = 4
PLANES = 12
F32 = jnp.float32
VMEM = pl.BlockSpec(memory_space=pltpu.VMEM)
SMEM = pl.BlockSpec(memory_space=pltpu.SMEM)
HBM = pl.BlockSpec(memory_space=pltpu.HBM)
NORTH, SOUTH, WEST, EAST = 1, 2, 3, 4
PLACES = 5
LAT_BASE, LON_BASE = 17, 18


def lanes():
    return lax.broadcasted_iota(jnp.int32, (8, CELLS), 1)


def sublanes():
    return lax.broadcasted_iota(jnp.int32, (8, CELLS), 0)


def turn(x, shift):
    shift = shift % CELLS
    return x if shift == 0 else pltpu.roll(x, shift, 1)


def tile(b):
    return pl.ds(8 * b, 8)


class Copies:
    def __init__(self, sems):
        self.sems, self.going = sems, []

    def start(self, source, target):
        copy = pltpu.make_async_copy(source, target, self.sems.at[len(self.going)])
        copy.start()
        self.going.append(copy)

    def wait(self, first=0, last=None):
        for copy in self.going[first:last]:
            copy.wait()


def start_kernel(
    at, slots, flow, pressure, heat, friction, weights, row, top, bottom, places, near, named, sems
):
    start = pl.multiple_of((at[0] // 8) * 8, 8)
    copies = Copies(sems)
    copies.start(slots, named)
    copies.start(flow.at[:, pl.ds(start, 8), :], near.at[0:6])
    copies.start(pressure.at[:, pl.ds(start, 8), :], near.at[6:8])
    copies.start(heat.at[:, pl.ds(start, 8), :], near.at[8:10])
    for out, lo in ((top, 0), (bottom, CELLS - 8)):
        copies.start(flow.at[:, lo : lo + 8, :], out.at[0:6])
        copies.start(pressure.at[:, lo : lo + 8, :], out.at[6:8])
        copies.start(heat.at[:, lo : lo + 8, :], out.at[8:10])
        copies.start(friction.at[:, lo : lo + 8, :], out.at[10:12])
        copies.start(weights.at[4:8, lo : lo + 8, :], out.at[12:16])
    row[...] = jnp.zeros((16, CELLS), F32)
    copies.wait()
    own = jnp.broadcast_to(named[...], (8, CELLS)) == sublanes()
    place = jnp.sum(jnp.where(own, lanes(), 0).astype(F32), axis=1, keepdims=True)
    place = jnp.broadcast_to(place, (8, CELLS))
    for out in (top.at[16], bottom.at[16], places):
        out[...] = place
    inside = at[0] - start
    for f in range(10):
        row[f : f + 1, :] = near[f, pl.ds(inside, 1), :]


def fill_kernel(chunks, row, out):
    out[...] = jnp.zeros((CELLS, 8, CELLS), F32)
    for n in range(5):
        out[chunks[n]] = row[0:8, :]
    out[chunks[5]] = row[8:16, :]


def refill_kernel(chunks, row, old, out):
    del old
    for n in range(5):
        out[chunks[n]] = row[...]


def columns_kernel(
    flow, pressure, heat, friction, weights, north, south, places,
    to_west, to_east, own, cols_s, rows_s, sems,
):
    lane = lanes()
    copies = Copies(sems)
    copies.start(flow, own.at[0:6])
    copies.start(pressure, own.at[6:8])
    copies.start(heat, own.at[8:10])
    copies.start(friction, own.at[10:12])
    for n in range(4):
        lo = 2 * HALO * PLANES + 8 * n
        copies.start(weights.at[n, 0:8, :], to_west.at[lo : lo + 8, :])
        copies.start(weights.at[n, CELLS - 8 : CELLS, :], to_east.at[lo : lo + 8, :])
    for out in (to_west, to_east):
        out[2 * HALO * PLANES + 32 :, :] = places[...]

    def pack(block):
        gathered = jnp.zeros((8, CELLS), F32)
        for f in range(PLANES):
            gathered = jnp.where(lane // 8 == f, turn(block(f), 8 * f + HALO), gathered)
        return gathered

    def unload(first):
        rows_s[...] = cols_s[...].T
        for f in range(PLANES):
            lo = first + HALO * f
            to_east[lo : lo + HALO, :] = rows_s[8 * f : 8 * f + HALO, :]
            to_west[lo : lo + HALO, :] = rows_s[8 * f + HALO : 8 * f + 8, :]

    cols_s[...] = jnp.zeros((CELLS, CELLS), F32)
    cols_s[tile(TILES - 1), :] = pack(lambda f: north[f])
    cols_s[tile(0), :] = pack(lambda f: south[f])
    unload(HALO * PLANES)
    copies.wait()
    for b in range(TILES):
        cols_s[tile(b), :] = pack(lambda f: own[f, tile(b), :])
    unload(0)


def sideways(first, second):
    lane = lanes()
    f_up, s_up = pltpu.roll(first, 1, 1), pltpu.roll(second, 1, 1)
    f_down, s_down = pltpu.roll(first, CELLS - 1, 1), pltpu.roll(second, CELLS - 1, 1)
    lefts = (jnp.where(lane == 0, s_up, f_up), jnp.where(lane == 0, f_up, s_up))
    rights = (
        jnp.where(lane == CELLS - 1, s_down, f_down),
        jnp.where(lane == CELLS - 1, f_down, s_down),
    )
    return lefts, rights


def around(ref, b, halves):
    both = [ref[half, tile(b), :] for half in range(2)]
    lefts, rights = sideways(*both)
    found = []
    for half in range(halves):
        up = pltpu.roll(both[half], 1, 0) if b == 0 else ref[half, 8 * b - 1 : 8 * b + 7, :]
        down = pltpu.roll(both[half], 7, 0) if b == TILES + 1 else ref[half, 8 * b + 1 : 8 * b + 9, :]
        found.append((both[half], up, down, lefts[half], rights[half]))
    return found


def build_kernel(
    ints, flow, pressure, heat, friction, weights, north, south, west, east,
    fields_out, coef_out, warm_out, strip, factors, high, low,
    fields, coef, warm, thick, chosen, cols_s, rows_s, sems,
):
    lane = lanes()
    copies = Copies(sems)
    inner = pl.ds(8, CELLS)
    copies.start(friction, thick.at[:, 0, inner, :])
    copies.start(heat, warm.at[:, 0, inner, :])
    copies.start(flow, fields.at[0:6, 0, inner, :])
    copies.start(pressure, fields.at[6:8, 0, inner, :])
    copies.start(weights.at[pl.ds(ints[LAT_BASE], 2)], chosen.at[0:2])
    copies.start(weights.at[pl.ds(ints[LON_BASE], 2)], chosen.at[2:4])

    def target(f):
        if f < 8:
            return fields.at[f]
        return warm.at[f - 8] if f < 10 else thick.at[f - 10]

    outer = (lane < HALO) | (lane >= CELLS - HALO)

    def load(first):
        for f in range(PLANES):
            lo = first + HALO * f
            rows_s[8 * f : 8 * f + HALO, :] = west[lo : lo + HALO, :]
            rows_s[8 * f + HALO : 8 * f + 8, :] = east[lo : lo + HALO, :]
        cols_s[...] = rows_s[...].T

    def place(f, b, block):
        target(f)[1, tile(b), :] = jnp.where(outer, turn(block, -8 * f - HALO), 0.0)

    rows_s[8 * PLANES : CELLS, :] = jnp.zeros((CELLS - 8 * PLANES, CELLS), F32)
    load(0)
    for f in range(PLANES):
        target(f)[0, tile(0), :] = north[f]
        target(f)[0, tile(TILES + 1), :] = south[f]
        for b in range(TILES):
            place(f, b + 1, cols_s[tile(b), :])
    load(HALO * PLANES)
    for f in range(PLANES):
        place(f, 0, cols_s[tile(TILES - 1), :])
        place(f, TILES + 1, cols_s[tile(0), :])
    copies.wait()
    copies.start(fields, fields_out)
    copies.start(warm, warm_out)
    strip_of(ints, fields, strip)

    at_north, at_south = ints[NORTH] > 0, ints[SOUTH] > 0
    at_west, at_east = ints[WEST] > 0, ints[EAST] > 0
    for k in range(2):
        for half in range(2):
            first = jnp.broadcast_to(thick[k, half, 8:9, :], (8, CELLS))
            last = jnp.broadcast_to(thick[k, half, ROWS - 9 : ROWS - 8, :], (8, CELLS))
            for b, at_end, line in ((0, at_north, first), (TILES + 1, at_south, last)):
                thick[k, half, tile(b), :] = jnp.where(at_end, line, thick[k, half, tile(b), :])
        for b in range(TILES + 2):
            own, other = thick[k, 0, tile(b), :], thick[k, 1, tile(b), :]
            other = jnp.where((lane == CELLS - 1) & at_west, turn(own, -1), other)
            other = jnp.where((lane == 0) & at_east, turn(own, 1), other)
            thick[k, 1, tile(b), :] = jnp.where(other > 0.0, other, 1.0)

    for b in range(TILES + 2):
        found = [around(thick.at[k], b, 2) for k in range(2)]
        for half in range(2):
            between = 0.5 * (found[0][half][0] + found[1][half][0])
            for k in range(2):
                here, *others = found[k][half]
                faces = [0.5 * (here + other) for other in others]
                diagonal = (faces[0] + faces[1]) + (faces[2] + faces[3]) + (between + here)
                inverse = 0.8 / diagonal
                for n, face in enumerate(faces):
                    coef[n, k, half, tile(b), :] = inverse * face
                coef[4, k, half, tile(b), :] = inverse * between
                coef[5, k, half, tile(b), :] = 0.5 * inverse
                coef[6, k, half, tile(b), :] = inverse * warm[k, half, tile(b), :]
                coef[7, k, half, tile(b), :] = 0.125 * here
    copies.start(coef, coef_out)
    at = ints[0] + 8
    for n in range(8):
        for f in range(8):
            factors[n, f : f + 1, :] = coef[n, f % 2, 0, pl.ds(at, 1), :]

    blank = jnp.zeros((8, CELLS), F32)
    for side in range(2):
        for term in range(2):
            cut = slice(term * CELLS, (term + 1) * CELLS)
            if side == 0:
                lo = pl.multiple_of(2 * HALO * PLANES + 8 * (ints[LAT_BASE] + term), 8)
                before, after = west[pl.ds(lo, 8), :], east[pl.ds(lo, 8), :]
            else:
                before = north[8 + ints[LON_BASE] + term]
                after = south[8 + ints[LON_BASE] + term]
            ends = [jnp.concatenate([after, blank], axis=0)]
            ends += [jnp.zeros((16, CELLS), F32)] * 6
            ends += [jnp.concatenate([blank, before], axis=0)]
            for n in range(16):
                if n < 8:
                    block = chosen[2 * side + term, 16 * n : 16 * n + 16, :]
                else:
                    block = ends[n - 8]
                for out, part in zip((high, low), split(block)):
                    out[side, 16 * n : 16 * n + 16, cut] = part
    copies.wait(6)


def strip_of(ints, fields, strip):
    at = ints[0] + 8
    for f in range(8):
        strip[0, f : f + 1, :] = fields[f, 0, pl.ds(at, 1), :]
        strip[1, f : f + 1, :] = fields[f, 1, pl.ds(at, 1), :]
        strip[2, f : f + 1, :] = fields[f, 0, pl.ds(at - 1, 1), :]
        strip[3, f : f + 1, :] = fields[f, 0, pl.ds(at + 1, 1), :]


def split(x):
    high = x.astype(jnp.bfloat16)
    return high, (x - high.astype(F32)).astype(jnp.bfloat16)


def times(left, right):
    return lax.dot_general(left, right, (((1,), (1,)), ((), ())), preferred_element_type=F32)


def blend_sides(ints, arrived, high, low, lat_ghost, lon_ghost):
    sides = (
        (lat_ghost, (ints[NORTH] + ints[SOUTH]) > 0, PLACES),
        (lon_ghost, (ints[WEST] + ints[EAST]) > 0, PLACES + 6),
    )
    for n, (ghost, active, places) in enumerate(sides):
        ghost[...] = jnp.zeros((8, LANES), F32)

        @pl.when(active)
        def _():
            blocks = [
                jnp.concatenate([arrived[ints[places + 2 * who + t]] for t in range(2)], axis=1)
                for who in range(3)
            ]
            b_high, b_low = split(jnp.concatenate(blocks, axis=0))
            both = times(jnp.concatenate([b_high, b_low], axis=0), high[n])
            total = both[0:24] + both[24:48] + times(b_high, low[n])
            ghost[:, 0:CELLS] = total[0:8, 0:CELLS]
            ghost[:, CELLS:LANES] = jnp.where(
                lanes() < CELLS // 2, total[16:24, CELLS:LANES], total[8:16, CELLS:LANES]
            )


def blend_kernel(ints, strip, factors, arrived, high, low, lat_ghost, lon_ghost, row):
    blend_sides(ints, arrived, high, low, lat_ghost, lon_ghost)
    at = ints[0]
    lane, sub = lanes(), sublanes()
    here, outside, up, down = strip[0], strip[1], strip[2], strip[3]
    up = jnp.where((ints[NORTH] > 0) & (at == 0), lat_ghost[:, 0:CELLS], up)
    down = jnp.where((ints[SOUTH] > 0) & (at == CELLS - 1), lat_ghost[:, 0:CELLS], down)
    beside = jnp.sum(jnp.where(lane == at, lon_ghost[:, 0:CELLS], 0.0), axis=1, keepdims=True)
    on_side = ((lane == CELLS - 1) & (ints[WEST] > 0)) | ((lane == 0) & (ints[EAST] > 0))
    outside = jnp.where(on_side, beside, outside)
    lefts, rights = sideways(here, outside)
    left, right = lefts[0], rights[0]
    even = sub % 2 == 0
    partner = jnp.where(even, pltpu.roll(here, 7, 0), pltpu.roll(here, 1, 0))
    value = 0.2 * here + factors[0] * up + factors[1] * down
    value = value + factors[2] * left + factors[3] * right + factors[4] * partner
    value = value + jnp.where(sub < 2, factors[6], 0.0)
    steps = (jnp.where(even, partner, -partner), down - up, right - left)
    slope = jnp.where(
        sub < 2,
        pltpu.roll(steps[0], 2, 0),
        jnp.where(sub < 4, pltpu.roll(steps[1], 4, 0), pltpu.roll(steps[2], 6, 0)),
    )
    value = value - factors[5] * slope
    divergence = (
        pltpu.roll(steps[0], 6, 0) + pltpu.roll(steps[1], 4, 0) + pltpu.roll(steps[2], 2, 0)
    )
    row[...] = jnp.where(sub < 6, value, here - factors[7] * divergence)


def ghost_columns(count, lon_ghost, cut, rows_s, out):
    for f in range(count):
        for lane in (2 * f, (2 * f - 1) % CELLS):
            rows_s[lane : lane + 1, :] = lon_ghost[f : f + 1, cut]
    out[...] = rows_s[...].T


def put_ghosts(ints, count, lat_ghost, lon_ghost, full, cols_s, ends_s, rows_s):
    lane, sub = lanes(), sublanes()
    rows_s[...] = jnp.zeros((CELLS, CELLS), F32)
    ghost_columns(count, lon_ghost, slice(0, CELLS), rows_s, cols_s)
    ghost_columns(count, lon_ghost, slice(CELLS, LANES), rows_s, ends_s)
    on_side = ((lane == CELLS - 1) & (ints[WEST] > 0)) | ((lane == 0) & (ints[EAST] > 0))
    ends = ((0, (sub == 7) & (ints[NORTH] > 0)), (TILES + 1, (sub == 0) & (ints[SOUTH] > 0)))
    for b, edge in ends:
        for f in range(count):
            for half in range(2):
                line = lat_ghost[f : f + 1, half * CELLS : (half + 1) * CELLS]
                full[f, half, tile(b), :] = jnp.where(edge, line, full[f, half, tile(b), :])
    for b in range(TILES + 2):
        if b == 0:
            column = ends_s[tile(TILES - 1), :]
        elif b == TILES + 1:
            column = ends_s[tile(0), :]
        else:
            column = cols_s[tile(b - 1), :]
        for f in range(count):
            other = full[f, 1, tile(b), :]
            full[f, 1, tile(b), :] = jnp.where(on_side, turn(column, -2 * f), other)


def relaxed(full, coef, b, halves):
    found = [around(full.at[f], b, halves) for f in range(8)]
    answers = []
    for half in range(halves):
        at = [found[f][half] for f in range(8)]

        def factor(n, k):
            return coef[n, k, half, tile(b), :]

        new = []
        for component in range(3):
            for k in range(2):
                here, up, down, left, right = at[2 * component + k]
                value = 0.2 * here + factor(0, k) * up + factor(1, k) * down
                value = value + factor(2, k) * left + factor(3, k) * right
                value = value + factor(4, k) * at[2 * component + 1 - k][0]
                if component == 0:
                    value = value + factor(6, k)
                    slope = at[7][0] if k == 0 else -at[6][0]
                elif component == 1:
                    slope = at[6 + k][2] - at[6 + k][1]
                else:
                    slope = at[6 + k][4] - at[6 + k][3]
                new.append(value - factor(5, k) * slope)
        for k in range(2):
            divergence = (at[2 + k][2] - at[2 + k][1]) + (at[4 + k][4] - at[4 + k][3])
            divergence = divergence + at[1][0] if k == 0 else divergence - at[0][0]
            new.append(at[6 + k][0] - factor(7, k) * divergence)
        answers.append(new)
    return answers


def sweep_kernel(
    ints, fields, coef, lat_ghost, lon_ghost, out, strip,
    full, factor, new_full, cols_s, ends_s, rows_s, sems,
):
    copies = Copies(sems)
    copies.start(fields, full)
    copies.start(coef, factor)
    copies.wait(0, 1)
    put_ghosts(ints, 8, lat_ghost, lon_ghost, full, cols_s, ends_s, rows_s)
    copies.wait(1, 2)
    for b in range(TILES + 2):
        for half, new in enumerate(relaxed(full, factor, b, 2)):
            for f in range(8):
                new_full[f, half, tile(b), :] = new[f]
    copies.start(new_full, out)
    strip_of(ints, new_full, strip)
    copies.wait(2)


def relay_kernel(places, arrived, out):
    for n in range(8):
        out[2 * n : 2 * n + 2, :] = arrived[places[n], 0:2, :]


def heat_kernel(
    ints, warm, blocks, weights, out, chosen, lat_ghost, lon_ghost, cols_s, ends_s, rows_s, sems
):
    copies = Copies(sems)
    copies.start(warm, out)
    copies.start(weights.at[pl.ds(ints[LAT_BASE], 2)], chosen.at[0:2])
    copies.start(weights.at[pl.ds(ints[LON_BASE], 2)], chosen.at[2:4])
    copies.wait()
    sides = (
        (lat_ghost, (ints[NORTH] + ints[SOUTH]) > 0, LAT_BASE),
        (lon_ghost, (ints[WEST] + ints[EAST]) > 0, LON_BASE),
    )
    for n, (ghost, active, base) in enumerate(sides):
        ghost[...] = jnp.zeros((8, LANES), F32)

        @pl.when(active)
        def _():
            total = jnp.zeros((16, CELLS), F32)
            for term in range(2):
                b_high, b_low = split(blocks[ints[base] + term])
                w_high, w_low = split(chosen[2 * n + term])
                total = total + times(b_high, w_low) + times(b_low, w_high) + times(b_high, w_high)
            ghost[:, 0:CELLS] = total[0:8]

    put_ghosts(ints, 2, lat_ghost, lon_ghost, out, cols_s, ends_s, rows_s)


def ahead_kernel(ints, fields, coef, new, beside, above, full, factor, cols_s, ends_s, rows_s, blank, sems):
    copies = Copies(sems)
    copies.start(fields, full)
    copies.start(coef, factor)
    blank[...] = jnp.zeros((8, LANES), F32)
    copies.wait(0, 1)
    put_ghosts(ints, 8, blank, blank, full, cols_s, ends_s, rows_s)
    copies.wait(1, 2)
    lane, sub = lanes(), sublanes()
    first, last = (lane == 0) & (ints[WEST] > 0), (lane == CELLS - 1) & (ints[EAST] > 0)
    ends = ((1, 0, (sub == 0) & (ints[NORTH] > 0), 1.0), (TILES, 1, (sub == 7) & (ints[SOUTH] > 0), -1.0))
    for b in range(1, TILES + 1):
        (answer,) = relaxed(full, factor, b, 1)
        for f in range(8):
            new[f, tile(b - 1), :] = answer[f]
        for k in range(2):
            at = [factor[n, k, 0, tile(b), :] for n in (2, 3, 5, 7)]
            beside[0, k, tile(b - 1), :] = jnp.where(first, at[0], jnp.where(last, at[1], 0.0))
            for n in (1, 2):
                beside[n, k, tile(b - 1), :] = jnp.where(
                    first, at[n + 1], jnp.where(last, -at[n + 1], 0.0)
                )
    for end, (b, n, edge, sign) in enumerate(ends):
        for k in range(2):
            above[end, 0, k] = jnp.where(edge, factor[n, k, 0, tile(b), :], 0.0)
            above[end, 1, k] = jnp.where(edge, sign * factor[5, k, 0, tile(b), :], 0.0)
            above[end, 2, k] = jnp.where(edge, sign * factor[7, k, 0, tile(b), :], 0.0)


def corrected(new, ghost, parts, component):
    out = []
    for f in range(6):
        k = f % 2
        value = new[f] + parts[0][k] * ghost[f]
        if f // 2 == component:
            value = value + parts[1][k] * ghost[6 + k]
        out.append(value)
    for k in range(2):
        out.append(new[6 + k] + parts[2][k] * ghost[2 * component + k])
    return out


def final_kernel(
    ints, arrived, high, low, ready, beside, above, warm,
    flow_out, pressure_out, heat_out, lat_ghost, lon_ghost, cols_s, rows_s,
):
    blend_sides(ints, arrived, high, low, lat_ghost, lon_ghost)
    rows_s[...] = jnp.zeros((CELLS, CELLS), F32)
    ghost_columns(8, lon_ghost, slice(0, CELLS), rows_s, cols_s)
    for b in range(TILES):
        new = [ready[f, tile(b), :] for f in range(8)]
        if b == 0 or b == TILES - 1:
            end = 0 if b == 0 else 1
            ghost = [lat_ghost[f : f + 1, 0:CELLS] for f in range(8)]
            new = corrected(new, ghost, [[above[end, n, k] for k in range(2)] for n in range(3)], 1)
        column = cols_s[tile(b), :]
        ghost = [turn(column, -2 * f) for f in range(8)]
        parts = [[beside[n, k, tile(b), :] for k in range(2)] for n in range(3)]
        new = corrected(new, ghost, parts, 2)
        for f in range(6):
            flow_out[f, tile(b), :] = new[f]
        for k in range(2):
            pressure_out[k, tile(b), :] = new[6 + k]
        layers = [around(warm.at[k], b + 1, 1)[0] for k in range(2)]
        for k in range(2):
            here, up, down, left, right = layers[k]
            under = jnp.ones((8, CELLS), F32) if k == 0 else layers[0][0]
            over = layers[1][0] if k == 0 else jnp.zeros((8, CELLS), F32)
            advect = jnp.zeros((8, CELLS), F32)
            for component, minus, plus in ((0, under, over), (1, up, down), (2, left, right)):
                speed = new[2 * component + k]
                advect = advect + jnp.maximum(speed, 0.0) * (here - minus)
                advect = advect + jnp.minimum(speed, 0.0) * (plus - here)
            spread = (up + down) + (left + right) + (under + over) - 6.0 * here
            heat_out[k, tile(b), :] = here + 0.1 * (spread - advect)


def shape(*dims):
    return jax.ShapeDtypeStruct(dims, F32)


def scratch(*dims):
    return pltpu.VMEM(dims, F32)


def call(kernel, outs, ins, scratches, specs=None, out_specs=None, aliases=None, name=None, limit=16):
    return pl.pallas_call(
        kernel,
        out_shape=outs,
        in_specs=specs or [SMEM] + [VMEM] * (len(ins) - 1),
        out_specs=out_specs or [VMEM] * len(outs),
        scratch_shapes=scratches,
        input_output_aliases=aliases or {},
        compiler_params=pltpu.CompilerParams(vmem_limit_bytes=limit * 1024 * 1024),
        name=name,
    )(*ins)


def semaphores(count):
    return pltpu.SemaphoreType.DMA((count,))


def shards(
    flow_vector,
    normal_stress,
    thermal_field,
    shear_resistance,
    departing_bands,
    receiving_processor,
    shift_filled_by_lane,
    blending_factors,
):
    flow = flow_vector.reshape(6, CELLS, CELLS)
    pressure = normal_stress[0]
    heat = thermal_field[0]
    friction = shear_resistance[0]
    weights = blending_factors.reshape(8, CELLS, CELLS)
    lat, lon = lax.axis_index("lat"), lax.axis_index("lon")
    n_lat, n_lon = lax.axis_size("lat"), lax.axis_size("lon")
    devices = n_lat * n_lon
    own_row = departing_bands.reshape(1)

    def swap(x):
        return lax.ppermute(x, "patch", [(0, 1), (1, 0)])

    def ring(x, axis, step):
        count = lax.axis_size(axis)
        pairs = [(i, i + step) for i in range(count) if 0 <= i + step < count]
        return lax.ppermute(x, axis, pairs)

    def to_relay(x):
        return lax.ppermute(x, "lon", [(i, i ^ 2) for i in range(n_lon)])

    def deliver(buffer):
        return lax.all_to_all(buffer, ("lat", "lon"), 0, 0, tiled=True)

    receiver = swap(receiving_processor.reshape(1).astype(F32)).astype(jnp.int32)
    receiver = jnp.maximum(receiver, 0)
    near = receiver + jnp.array([0, 1, -1, n_lon, -n_lon], jnp.int32)
    near = jnp.where((near >= 0) & (near < devices), near, receiver)
    chunks = jnp.concatenate([near, receiver ^ 2])

    planes = (flow, pressure, heat, friction, weights)
    row, top, bottom, places = call(
        start_kernel,
        [shape(16, CELLS), shape(17, 8, CELLS), shape(17, 8, CELLS), shape(8, CELLS)],
        (own_row, shift_filled_by_lane.reshape(1, CELLS), *planes),
        [scratch(10, 8, CELLS), pltpu.VMEM((1, CELLS), jnp.int32), semaphores(14)],
        specs=[SMEM] + [HBM] * 6,
        name="start",
    )
    (buffer,) = call(
        fill_kernel, [shape(devices, 8, CELLS)], (chunks, swap(row)), [], name="fill", limit=4
    )
    arrived = deliver(buffer)
    north, south = ring(bottom, "lat", 1), ring(top, "lat", -1)
    wide = shape(2 * HALO * PLANES + 40, CELLS)
    square = scratch(CELLS, CELLS)
    to_west, to_east = call(
        columns_kernel,
        [wide, wide],
        (*planes, north, south, places),
        [scratch(PLANES, CELLS, CELLS), square, square, semaphores(12)],
        specs=[HBM] * 5 + [VMEM] * 3,
        name="columns",
    )
    west, east = ring(to_east, "lon", 1), ring(to_west, "lon", -1)

    def numbers(block):
        return block[:, 0].astype(jnp.int32)

    on_edge = jnp.stack([lat == 0, lat == n_lat - 1, lon == 0, lon == n_lon - 1]).astype(jnp.int32)
    own = numbers(places)

    def side(block, base, last):
        return jnp.where(last, block[base + 2 : base + 4], block[base : base + 2])

    pick = [side(x, 0, lat > 0) for x in (own, numbers(west[-8:]), numbers(east[-8:]))]
    pick += [side(x, 4, lon > 0) for x in (own, numbers(north[16]), numbers(south[16]))]
    bases = jnp.stack([jnp.where(lat > 0, 2, 0), jnp.where(lon > 0, 6, 4)]).astype(jnp.int32)
    ints = jnp.concatenate([own_row, on_edge] + pick + [bases])

    state = shape(8, 2, ROWS, CELLS)
    state_s = scratch(8, 2, ROWS, CELLS)
    coef_s = scratch(8, 2, 2, ROWS, CELLS)
    warm_s = scratch(2, 2, ROWS, CELLS)
    strips = shape(4, 8, CELLS)
    joined = jax.ShapeDtypeStruct((2, LANES, LANES), jnp.bfloat16)
    fields, coef, warm, strip, factors, high, low = call(
        build_kernel,
        [
            state,
            shape(8, 2, 2, ROWS, CELLS),
            shape(2, 2, ROWS, CELLS),
            strips,
            shape(8, 8, CELLS),
            joined,
            joined,
        ],
        (ints, *planes, north, south, west, east),
        [state_s, coef_s, warm_s, warm_s, scratch(4, CELLS, CELLS), square, square, semaphores(9)],
        specs=[SMEM] + [HBM] * 5 + [VMEM] * 4,
        out_specs=[HBM] * 3 + [VMEM] * 4,
        name="build",
    )
    relayed = numbers(to_relay(places))
    ghost = shape(8, LANES)
    ghost_s = scratch(8, LANES)
    first_arrived = arrived
    for sweep in range(SWEEPS - 1):
        lat_ghost, lon_ghost, row = call(
            blend_kernel,
            [ghost, ghost, shape(8, CELLS)],
            (ints, strip, factors, arrived, high, low),
            [],
            name="blend",
            limit=4,
        )
        (buffer,) = call(
            refill_kernel,
            [shape(devices, 8, CELLS)],
            (chunks, swap(row), buffer),
            [],
            aliases={2: 0},
            name="refill",
            limit=4,
        )
        arrived = deliver(buffer)
        fields, strip = call(
            sweep_kernel,
            [state, strips],
            (ints, fields, coef, lat_ghost, lon_ghost),
            [state_s, coef_s, state_s, square, square, square, semaphores(3)],
            specs=[SMEM, HBM, HBM, VMEM, VMEM],
            out_specs=[HBM, VMEM],
            name="sweep",
        )
        if sweep == 0:
            (blocks,) = call(
                relay_kernel,
                [shape(16, CELLS)],
                (relayed, first_arrived),
                [],
                name="relay",
                limit=4,
            )
            blocks = to_relay(blocks).reshape(8, 2, CELLS)
            blocks = jnp.pad(blocks, ((0, 0), (0, 14), (0, 0)))
            (warm,) = call(
                heat_kernel,
                [shape(2, 2, ROWS, CELLS)],
                (ints, warm, blocks, weights),
                [scratch(4, CELLS, CELLS), ghost_s, ghost_s, square, square, square, semaphores(3)],
                specs=[SMEM, HBM, VMEM, HBM],
                name="heat",
                limit=4,
            )
    ready, beside, above = call(
        ahead_kernel,
        [shape(8, CELLS, CELLS), shape(3, 2, CELLS, CELLS), shape(2, 3, 2, 8, CELLS)],
        (ints, fields, coef),
        [state_s, coef_s, square, square, square, ghost_s, semaphores(2)],
        specs=[SMEM, HBM, HBM],
        name="ahead",
    )
    flow, pressure, heat = call(
        final_kernel,
        [shape(6, CELLS, CELLS), shape(2, CELLS, CELLS), shape(2, CELLS, CELLS)],
        (ints, arrived, high, low, ready, beside, above, warm),
        [ghost_s, ghost_s, square, square],
        name="final",
        limit=8,
    )
    return flow.reshape(3, 1, 2, CELLS, CELLS), pressure[None], heat[None]


def solution(mesh):
    placed = (
        P(None, "patch", None, "lat", "lon"),
        P("patch", None, "lat", "lon"),
        P("patch", None, "lat", "lon"),
        P("patch", None, "lat", "lon"),
        P("patch", "lat", "lon", None),
        P("patch", "lat", "lon", None),
        P("patch", "lat", "lon", None),
        P("patch", "lat", "lon", None, None, None),
    )
    return jax.shard_map(
        shards,
        mesh=mesh,
        in_specs=placed,
        out_specs=(
            P(None, "patch", None, "lat", "lon"),
            P("patch", None, "lat", "lon"),
            P("patch", None, "lat", "lon"),
        ),
        check_vma=False,
    )
```

time: 174 us -> 178 us (1.023)
  Pallas kernels: 22.1 us -> 28.3 us
  waiting for transfers between devices: 50.1 us -> 45.1 us
  local copies, waits for them, and re-layouts: 30.1 us -> 33.9 us
    pallas_call x16 -> x17, Pallas kernels: 22.1 us -> 28.3 us  [call(): pl.pallas_call(kernel, out_shape=outs, in_specs=specs or [SMEM] + [VMEM]...]
    all_to_all x4, waiting for transfers between devices: 37.5 us -> 31.7 us  [deliver(): return lax.all_to_all(buffer, ('lat', 'lon'), 0, 0, tiled=True)]
    unnamed x82 -> x100, local copies, waits for them, and re-layouts: 30 us -> 33.8 us
  transfers between devices with their start and end apart: 15 -> 15, of which waited for: 10 -> 10; matrix products, arithmetic and copies ran while one was open for 1% -> 1% of each run, Pallas kernels for 5% -> 9%
where the time goes in v3:
time: 178 us; the launch traced here: 176 us
  starting transfers between devices  65.2 us (37%)
  waiting for transfers between devices  45.1 us (25%)
  local copies, waits for them, and re-layouts  33.9 us (19%)
  Pallas kernels  28.3 us (16%)
  between operations  3 us (2%)
    all_to_all x4, starting transfers between devices, deliver(): return lax.all_to_all(buffer, ('lat', 'lon'), 0, 0, tiled=True)  48.1 us
    unnamed x100, local copies, waits for them, and re-layouts  33.8 us
    all_to_all x4, waiting for transfers between devices, deliver(): return lax.all_to_all(buffer, ('lat', 'lon'), 0, 0, tiled=True)  31.7 us
    pallas_call x17, Pallas kernels, call(): pl.pallas_call(kernel, out_shape=outs, in_specs=specs or [SMEM] + [VMEM]...  28.3 us
    ppermute x4, starting transfers between devices, ring(): return lax.ppermute(x, axis, pairs)  10.9 us
    ppermute x2, waiting for transfers between devices, to_relay(): return lax.ppermute(x, 'lon', [(i, i ^ 2) for i in range(n_lon)])  6.35 us
    ppermute x2, starting transfers between devices, to_relay(): return lax.ppermute(x, 'lon', [(i, i ^ 2) for i in range(n_lon)])  4.3 us
    ppermute x4, waiting for transfers between devices, ring(): return lax.ppermute(x, axis, pairs)  3.57 us
  transfers between devices with their start and end apart: 15, of which 10 were waited for; matrix products, arithmetic and copies ran while one was open for 1% of the time, Pallas kernels for 9%

profile of v3, /device:TPU:2, one launch (start us, length us, event | category | flops | bytes accessed | tf_op | source)
XLA Modules:
  0.0 176.4 jit_solution(8325277367182266689)
XLA Ops:
  1.3 1.0 collective-permute-start.4
  3.0 1.0 copy-done
  4.0 1.0 copy-done.12
  5.0 0.9 copy-done.15
  5.9 0.9 copy-done.17
  6.9 0.9 copy-done.20
  9.3 3.8 %collective-permute-start = (f32[17,8,128]{2,1,0:T(8,128)S(1)}, f32[17,8,128]{2,1,0:T(8,128)S(1)}, u32[]{:S(2)}, u32[]{:S(2)}) collective-permute-start(f32[17,8,128]{2,1,0:T(8,128)S(1)} %get-tuple-element.37), channel_id=1, source_target_pairs={{0,16},{16,32},{32,48},{48,64},{64,80},{80,96},{96,112},{1,17},{17... | collective-permute-start | bytes 208904 | tf_op jit(solution)/shard_map/ppermute | solution.py:577
  13.2 1.3 collective-permute-start.1
  15.4 1.4 fill.1.old
  16.8 17.4 %all-to-all-start = ((f32[128,8,128]{2,1,0:T(8,128)}), f32[128,8,128]{2,1,0:T(8,128)S(1)}, u32[]{:S(2)}, u32[]{:S(2)}) async-start(f32[128,8,128]{2,1,0:T(8,128)} %fill.1.old), calls=%async_computation | async-start | bytes 1048576 | tf_op jit(solution)/shard_map/all_to_all | solution.py:583
  34.4 1.4 columns.1
  35.8 3.4 %collective-permute-start.2 = (f32[136,128]{1,0:T(8,128)S(1)}, f32[136,128]{1,0:T(8,128)S(1)}, u32[]{:S(2)}, u32[]{:S(2)}) collective-permute-start(f32[136,128]{1,0:T(8,128)S(1)} %get-tuple-element.39), channel_id=1, source_target_pairs={{0,1},{1,2},{2,3},{3,4},{4,5},{5,6},{6,7},{7,8},{8,9},{9,10},{10,1... | collective-permute-start | bytes 208904 | tf_op jit(solution)/shard_map/ppermute | solution.py:577
  39.2 2.5 %collective-permute-start.3 = (f32[136,128]{1,0:T(8,128)S(1)}, f32[136,128]{1,0:T(8,128)S(1)}, u32[]{:S(2)}, u32[]{:S(2)}) collective-permute-start(f32[136,128]{1,0:T(8,128)S(1)} %get-tuple-element.40), channel_id=1, source_target_pairs={{1,0},{2,1},{3,2},{4,3},{5,4},{6,5},{7,6},{8,7},{9,8},{10,9},{11,1... | collective-permute-start | bytes 208904 | tf_op jit(solution)/shard_map/ppermute | solution.py:577
  43.2 2.9 %collective-permute-done.3.east = f32[136,128]{1,0:T(8,128)S(1)} collective-permute-done((f32[136,128]{1,0:T(8,128)S(1)}, f32[136,128]{1,0:T(8,128)S(1)}, u32[]{:S(2)}, u32[]{:S(2)}) %collective-permute-start.3) | collective-permute-done | bytes 69664 | tf_op jit(solution)/shard_map/ppermute | solution.py:577
  47.0 1.0 copy-done.14
  48.0 0.9 copy-done.19
  48.9 0.9 copy-done.22
  49.8 0.9 copy-done.34
  50.6 0.9 copy-done.36
  51.5 0.9 copy-done.43
  52.4 0.9 copy-done.45
  53.3 2.7 %build.1 = (f32[8,2,144,128]{3,2,1,0:T(8,128)S(1)}, f32[8,2,2,144,128]{4,3,2,1,0:T(8,128)S(1)}, f32[2,2,144,128]{3,2,1,0:T(8,128)S(1)}, f32[4,8,128]{2,1,0:T(8,1...) custom-call(s32[19]{0:T(128)S(1)} %concatenate.6.ints, ...), custom_call_target="tpu_custom_call" | custom-call | tf_op jit(solution)/shard_map/build/pallas_call | solution.py:535
  57.4 1.0 copy-done.25
  60.4 0.9 copy-done.3
  61.3 0.9 copy-done.8
  62.3 0.8 copy-done.38
  63.0 0.7 copy-done.47
  63.7 0.8 blend.3
  64.7 1.2 collective-permute-done.6.row
  65.8 1.8 %refill.3.old = f32[128,8,128]{2,1,0:T(8,128)} custom-call(s32[6]{0:T(128)S(1)} %pad_add_fusion.chunks, f32[8,128]{1,0:T(8,128)S(1)} %collective-permute-done.6.row, f32[128,8,128]{2,1,0:T(8,128)} %fill.1.old), custom_call_target="tpu_custom_call", output_to_operand_aliasing={{}: (2, {})} | custom-call | tf_op jit(solution)/shard_map/refill/pallas_call | solution.py:535
  67.7 14.8 %all-to-all-start.1 = ((f32[128,8,128]{2,1,0:T(8,128)}), f32[128,8,128]{2,1,0:T(8,128)}, u32[]{:S(2)}, u32[]{:S(2)}) async-start(f32[128,8,128]{2,1,0:T(8,128)} %refill.3.old), calls=%async_computation.1 | async-start | bytes 1048576 | tf_op jit(solution)/shard_map/all_to_all | solution.py:583
  82.5 1.3 copy-done.26
  83.8 2.2 %sweep.3 = (f32[8,2,144,128]{3,2,1,0:T(8,128)S(1)}, f32[4,8,128]{2,1,0:T(8,128)S(1)}) custom-call(s32[19]{0:T(128)S(1)} %concatenate.6.ints, f32[8,2,144,128]{3,2,1,0:T(8,128)S(1)} %copy-done.26, f32[8,2,2,144,128]{4,3,2,1,0:T(8,128)S(1)} %get-tuple-element.42.coef, f32[8,256]{1,0:T(8,128)S(1)} %get-tuple-element.48.lat_ghost, ...), custom_call_target="tpu_custom_call" | custom-call | tf_op jit(solution)/shard_map/sweep/pallas_call | solution.py:535
  86.0 1.0 copy-done.27
  87.0 15.6 %all-to-all-done.1.arrived = f32[128,8,128]{2,1,0:T(8,128)} async-done(((f32[128,8,128]{2,1,0:T(8,128)}), f32[128,8,128]{2,1,0:T(8,128)}, u32[]{:S(2)}, u32[]{:S(2)}) %all-to-all-start.1) | async-done | bytes 524320 | tf_op jit(solution)/shard_map/all_to_all | solution.py:583
  102.6 0.9 copy-done.4
  103.5 0.9 copy-done.9
  104.5 1.4 blend.4
  105.9 1.2 collective-permute-done.7.row
  107.1 1.8 %refill.4.old = f32[128,8,128]{2,1,0:T(8,128)} custom-call(s32[6]{0:T(128)S(1)} %pad_add_fusion.chunks, f32[8,128]{1,0:T(8,128)S(1)} %collective-permute-done.7.row, f32[128,8,128]{2,1,0:T(8,128)} %refill.3.old), custom_call_target="tpu_custom_call", output_to_operand_aliasing={{}: (2, {})} | custom-call | tf_op jit(solution)/shard_map/refill/pallas_call | solution.py:535
  108.9 7.9 %all-to-all-start.2 = ((f32[128,8,128]{2,1,0:T(8,128)}), f32[128,8,128]{2,1,0:T(8,128)}, u32[]{:S(2)}, u32[]{:S(2)}) async-start(f32[128,8,128]{2,1,0:T(8,128)} %refill.4.old), calls=%async_computation.2 | async-start | bytes 1048576 | tf_op jit(solution)/shard_map/all_to_all | solution.py:583
  116.8 1.3 copy-done.28
  118.1 2.2 %sweep.4 = (f32[8,2,144,128]{3,2,1,0:T(8,128)S(1)}, f32[4,8,128]{2,1,0:T(8,128)S(1)}) custom-call(s32[19]{0:T(128)S(1)} %concatenate.6.ints, f32[8,2,144,128]{3,2,1,0:T(8,128)S(1)} %copy-done.28, f32[8,2,2,144,128]{4,3,2,1,0:T(8,128)S(1)} %get-tuple-element.42.coef, f32[8,256]{1,0:T(8,128)S(1)} %get-tuple-element.53.lat_ghost, ...), custom_call_target="tpu_custom_call" | custom-call | tf_op jit(solution)/shard_map/sweep/pallas_call | solution.py:535
  120.3 1.0 copy-done.23
  121.3 15.8 %all-to-all-done.2.arrived = f32[128,8,128]{2,1,0:T(8,128)} async-done(((f32[128,8,128]{2,1,0:T(8,128)}), f32[128,8,128]{2,1,0:T(8,128)}, u32[]{:S(2)}, u32[]{:S(2)}) %all-to-all-start.2) | async-done | bytes 524320 | tf_op jit(solution)/shard_map/all_to_all | solution.py:583
  137.2 0.9 copy-done.5
  138.1 0.9 copy-done.10
  139.1 1.4 blend.5
  140.5 1.2 collective-permute-done.8.row
  141.7 1.8 %refill.5 = f32[128,8,128]{2,1,0:T(8,128)} custom-call(s32[6]{0:T(128)S(1)} %pad_add_fusion.chunks, f32[8,128]{1,0:T(8,128)S(1)} %collective-permute-done.8.row, f32[128,8,128]{2,1,0:T(8,128)} %refill.4.old), custom_call_target="tpu_custom_call", output_to_operand_aliasing={{}: (2, {})} | custom-call | tf_op jit(solution)/shard_map/refill/pallas_call | solution.py:535
  143.5 8.0 %all-to-all-start.3 = ((f32[128,8,128]{2,1,0:T(8,128)}), f32[128,8,128]{2,1,0:T(8,128)}, u32[]{:S(2)}, u32[]{:S(2)}) async-start(f32[128,8,128]{2,1,0:T(8,128)} %refill.5), calls=%async_computation.3 | async-start | bytes 1048576 | tf_op jit(solution)/shard_map/all_to_all | solution.py:583
  151.6 2.2 %collective-permute-start.9 = (f32[8,128]{1,0:T(8,128)S(1)}, f32[8,128]{1,0:T(8,128)S(1)}, u32[]{:S(2)}, u32[]{:S(2)}) collective-permute-start(f32[8,128]{1,0:T(8,128)S(1)} %get-tuple-element.36.places), channel_id=1, source_target_pairs={{0,2},{1,3},{2,0},{3,1},{4,6},{5,7},{6,4},{7,5},{8,10},{9,11},{10,... | collective-permute-start | bytes 12296 | tf_op jit(solution)/shard_map/ppermute | solution.py:580
  153.7 3.1 %collective-permute-done.9 = f32[8,128]{1,0:T(8,128)S(1)} collective-permute-done((f32[8,128]{1,0:T(8,128)S(1)}, f32[8,128]{1,0:T(8,128)S(1)}, u32[]{:S(2)}, u32[]{:S(2)}) %collective-permute-start.9) | collective-permute-done | bytes 4128 | tf_op jit(solution)/shard_map/ppermute | solution.py:580
  157.5 2.1 %collective-permute-start.10 = (f32[16,128]{1,0:T(8,128)S(1)}, f32[16,128]{1,0:T(8,128)S(1)}, u32[]{:S(2)}, u32[]{:S(2)}) collective-permute-start(f32[16,128]{1,0:T(8,128)S(1)} %relay.1), channel_id=1, source_target_pairs={{0,2},{1,3},{2,0},{3,1},{4,6},{5,7},{6,4},{7,5},{8,10},{9,11},{10,... | collective-permute-start | bytes 24584 | tf_op jit(solution)/shard_map/ppermute | solution.py:580
  159.6 3.3 %collective-permute-done.10 = f32[16,128]{1,0:T(8,128)S(1)} collective-permute-done((f32[16,128]{1,0:T(8,128)S(1)}, f32[16,128]{1,0:T(8,128)S(1)}, u32[]{:S(2)}, u32[]{:S(2)}) %collective-permute-start.10) | collective-permute-done | bytes 8224 | tf_op jit(solution)/shard_map/ppermute | solution.py:580
  162.9 1.0 copy-done.41
  163.9 1.4 heat.1.warm
  165.3 2.8 %sweep.5 = (f32[8,2,144,128]{3,2,1,0:T(8,128)S(1)}, f32[4,8,128]{2,1,0:T(8,128)}) custom-call(s32[19]{0:T(128)S(1)} %concatenate.6.ints, f32[8,2,144,128]{3,2,1,0:T(8,128)S(1)} %copy-done.24, f32[8,2,2,144,128]{4,3,2,1,0:T(8,128)S(1)} %get-tuple-element.42.coef, f32[8,256]{1,0:T(8,128)S(1)} %get-tuple-element.59.lat_ghost, ...), custom_call_target="tpu_custom_call" | custom-call | tf_op jit(solution)/shard_map/sweep/pallas_call | solution.py:535
  168.1 1.9 %ahead.1 = (f32[8,128,128]{2,1,0:T(8,128)S(1)}, f32[3,2,128,128]{3,2,1,0:T(8,128)S(1)}, f32[2,3,2,8,128]{4,3,2,1,0:T(8,128)S(1)}) custom-call(s32[19]{0:T(128)S(1)} %concatenate.6.ints, f32[8,2,144,128]{3,2,1,0:T(8,128)S(1)} %get-tuple-element.61.fields, f32[8,2,2,144,128]{4,3,2,1,0:T(8,128)S(1)} %get-tuple-element.42.coef), custom_call_target="tpu_custom_call" | custom-call | tf_op jit(solution)/shard_map/ahead/pallas_call | solution.py:535
  170.0 0.8 copy-done.29
  170.8 0.7 copy-done.31
  171.9 1.0 copy-done.30
  172.9 1.0 copy-done.32
  173.9 2.5 %final.1 = (f32[6,128,128]{2,1,0:T(8,128)}, f32[2,128,128]{2,1,0:T(8,128)}, f32[2,128,128]{2,1,0:T(8,128)}) custom-call(s32[19]{0:T(128)S(1)} %concatenate.6.ints, f32[128,8,128]{2,1,0:T(8,128)} %all-to-all-done.3.arrived, bf16[2,256,256]{2,1,0:T(8,128)(2,1)S(1)} %copy-done.6, bf16[2,256,256]{2,1,0:T(8,128)(2,1)S(1)} %copy-done.11, ...), custom_call_target="tpu_custom_call" | custom-call | tf_op jit(solution)/shard_map/final/pallas_call | solution.py:535
  (101 shorter events, 9.1 us)
Async XLA Ops:
  0.6 14.7 %copy-start.49 = (s32[5]{0:T(128)S(1)}, s32[5]{0:T(128)}, u32[]{:S(2)}) copy-start(s32[5]{0:T(128)} %constant.32.clone) | copy-start | bytes 64
  1.3 13.4 %collective-permute-start.4 = (f32[1]{0:T(128)}, f32[1]{0:T(128)}, u32[]{:S(2)}, u32[]{:S(2)}) collective-permute-start(f32[1]{0:T(128)} %bitcast.15), channel_id=1, source_target_pairs={{0,128},{128,0},{1,129},{129,1},{2,130},{130,2},{3,131},{131,3},{4... | collective-permute-start | bytes 20 | tf_op jit(solution)/shard_map/ppermute | solution.py:572
  3.0 1.0 copy-start
  4.0 1.0 copy-start.12
  5.0 0.9 copy-start.15
  5.9 0.9 copy-start.17
  6.8 0.9 copy-start.20
  7.8 0.7 copy-start.48
  8.4 25.9 %copy-start.1 = (f32[1,1,1,8,128,128]{5,4,3,2,1,0:T(8,128)S(1)}, f32[1,1,1,8,128,128]{5,4,3,2,1,0:T(8,128)}, u32[]{:S(2)}) copy-start(f32[1,1,1,8,128,128]{5,4,3,2,1,0:T(8,128)} %param.16) | copy-start | bytes 1572868
  8.4 25.9 %copy-start.13 = (f32[3,1,2,128,128]{4,3,2,1,0:T(8,128)S(1)}, f32[3,1,2,128,128]{4,3,2,1,0:T(8,128)}, u32[]{:S(2)}) copy-start(f32[3,1,2,128,128]{4,3,2,1,0:T(8,128)} %param.9) | copy-start | bytes 1179652
  8.4 25.9 %copy-start.16 = (f32[1,2,128,128]{3,2,1,0:T(8,128)S(1)}, f32[1,2,128,128]{3,2,1,0:T(8,128)}, u32[]{:S(2)}) copy-start(f32[1,2,128,128]{3,2,1,0:T(8,128)} %param.10) | copy-start | bytes 393220
  8.4 25.9 %copy-start.18 = (f32[1,2,128,128]{3,2,1,0:T(8,128)S(1)}, f32[1,2,128,128]{3,2,1,0:T(8,128)}, u32[]{:S(2)}) copy-start(f32[1,2,128,128]{3,2,1,0:T(8,128)} %param.11) | copy-start | bytes 393220
  8.4 25.9 %copy-start.21 = (f32[1,2,128,128]{3,2,1,0:T(8,128)S(1)}, f32[1,2,128,128]{3,2,1,0:T(8,128)}, u32[]{:S(2)}) copy-start(f32[1,2,128,128]{3,2,1,0:T(8,128)} %param.12) | copy-start | bytes 393220
  8.8 6.7 %collective-permute-start.5 = (f32[16,128]{1,0:T(8,128)S(1)}, f32[16,128]{1,0:T(8,128)S(1)}, u32[]{:S(2)}, u32[]{:S(2)}) collective-permute-start(f32[16,128]{1,0:T(8,128)S(1)} %get-tuple-element.45), channel_id=1, source_target_pairs={{0,128},{128,0},{1,129},{129,1},{2,130},{130,2},{3,131},{131,3},{4... | collective-permute-start | bytes 24584 | tf_op jit(solution)/shard_map/ppermute | solution.py:572
  9.3 24.8 %collective-permute-start = (f32[17,8,128]{2,1,0:T(8,128)S(1)}, f32[17,8,128]{2,1,0:T(8,128)S(1)}, u32[]{:S(2)}, u32[]{:S(2)}) collective-permute-start(f32[17,8,128]{2,1,0:T(8,128)S(1)} %get-tuple-element.37), channel_id=1, source_target_pairs={{0,16},{16,32},{32,48},{48,64},{64,80},{80,96},{96,112},{1,17},{17... | collective-permute-start | bytes 208904 | tf_op jit(solution)/shard_map/ppermute | solution.py:577
  13.2 21.2 %collective-permute-start.1 = (f32[17,8,128]{2,1,0:T(8,128)S(1)}, f32[17,8,128]{2,1,0:T(8,128)S(1)}, u32[]{:S(2)}, u32[]{:S(2)}) collective-permute-start(f32[17,8,128]{2,1,0:T(8,128)S(1)} %get-tuple-element.38), channel_id=1, source_target_pairs={{16,0},{32,16},{48,32},{64,48},{80,64},{96,80},{112,96},{17,1},{33... | collective-permute-start | bytes 208904 | tf_op jit(solution)/shard_map/ppermute | solution.py:577
  16.8 43.6 %all-to-all-start = ((f32[128,8,128]{2,1,0:T(8,128)}), f32[128,8,128]{2,1,0:T(8,128)S(1)}, u32[]{:S(2)}, u32[]{:S(2)}) async-start(f32[128,8,128]{2,1,0:T(8,128)} %fill.1.old), calls=%async_computation | async-start | bytes 1048576 | tf_op jit(solution)/shard_map/all_to_all | solution.py:583
  34.2 12.7 %copy-start.33 = (f32[17,8,128]{2,1,0:T(8,128)}, f32[17,8,128]{2,1,0:T(8,128)S(1)}, u32[]{:S(2)}) copy-start(f32[17,8,128]{2,1,0:T(8,128)S(1)} %collective-permute-done.north) | copy-start | bytes 208900
  34.4 12.5 %copy-start.35 = (f32[17,8,128]{2,1,0:T(8,128)}, f32[17,8,128]{2,1,0:T(8,128)S(1)}, u32[]{:S(2)}) copy-start(f32[17,8,128]{2,1,0:T(8,128)S(1)} %collective-permute-done.1.south) | copy-start | bytes 208900
  35.8 6.6 %collective-permute-start.2 = (f32[136,128]{1,0:T(8,128)S(1)}, f32[136,128]{1,0:T(8,128)S(1)}, u32[]{:S(2)}, u32[]{:S(2)}) collective-permute-start(f32[136,128]{1,0:T(8,128)S(1)} %get-tuple-element.39), channel_id=1, source_target_pairs={{0,1},{1,2},{2,3},{3,4},{4,5},{5,6},{6,7},{7,8},{8,9},{9,10},{10,1... | collective-permute-start | bytes 208904 | tf_op jit(solution)/shard_map/ppermute | solution.py:577
  39.2 6.9 %collective-permute-start.3 = (f32[136,128]{1,0:T(8,128)S(1)}, f32[136,128]{1,0:T(8,128)S(1)}, u32[]{:S(2)}, u32[]{:S(2)}) collective-permute-start(f32[136,128]{1,0:T(8,128)S(1)} %get-tuple-element.40), channel_id=1, source_target_pairs={{1,0},{2,1},{3,2},{4,3},{5,4},{6,5},{7,6},{8,7},{9,8},{10,9},{11,1... | collective-permute-start | bytes 208904 | tf_op jit(solution)/shard_map/ppermute | solution.py:577
  42.4 0.6 copy-start.42
  46.1 0.6 copy-start.44
  47.0 1.0 copy-start.14
  48.0 0.9 copy-start.19
  48.9 0.9 copy-start.22
  49.8 0.9 copy-start.34
  50.6 0.9 copy-start.36
  51.5 0.9 copy-start.43
  52.4 0.9 copy-start.45
  56.0 0.7 copy-start.2
  56.7 0.7 copy-start.7
  57.4 1.0 copy-start.25
  58.4 0.6 copy-start.37
  59.0 0.7 copy-start.40
  60.4 1.0 copy-start.3
  61.3 0.9 copy-start.8
  62.3 0.8 copy-start.38
  63.0 0.7 copy-start.47
  64.6 1.2 collective-permute-start.6
  67.7 34.9 %all-to-all-start.1 = ((f32[128,8,128]{2,1,0:T(8,128)}), f32[128,8,128]{2,1,0:T(8,128)}, u32[]{:S(2)}, u32[]{:S(2)}) async-start(f32[128,8,128]{2,1,0:T(8,128)} %refill.3.old), calls=%async_computation.1 | async-start | bytes 1048576 | tf_op jit(solution)/shard_map/all_to_all | solution.py:583
  82.5 1.3 copy-start.26
  83.8 18.8 %copy-start.39 = (f32[8,8,128]{2,1,0:T(8,128)S(1)}, f32[8,8,128]{2,1,0:T(8,128)}, u32[]{:S(2)}) copy-start(f32[8,8,128]{2,1,0:T(8,128)} %copy-done.37) | copy-start | bytes 98308
  86.0 1.0 copy-start.27
  102.6 1.0 copy-start.4
  103.5 0.9 copy-start.9
  105.8 1.3 collective-permute-start.7
  108.9 28.2 %all-to-all-start.2 = ((f32[128,8,128]{2,1,0:T(8,128)}), f32[128,8,128]{2,1,0:T(8,128)}, u32[]{:S(2)}, u32[]{:S(2)}) async-start(f32[128,8,128]{2,1,0:T(8,128)} %refill.4.old), calls=%async_computation.2 | async-start | bytes 1048576 | tf_op jit(solution)/shard_map/all_to_all | solution.py:583
  116.8 1.3 copy-start.28
  120.3 1.0 copy-start.23
  137.2 1.0 copy-start.5
  138.1 0.9 copy-start.10
  140.4 1.3 collective-permute-start.8
  143.5 28.4 %all-to-all-start.3 = ((f32[128,8,128]{2,1,0:T(8,128)}), f32[128,8,128]{2,1,0:T(8,128)}, u32[]{:S(2)}, u32[]{:S(2)}) async-start(f32[128,8,128]{2,1,0:T(8,128)} %refill.5), calls=%async_computation.3 | async-start | bytes 1048576 | tf_op jit(solution)/shard_map/all_to_all | solution.py:583
  151.5 13.7 %copy-start.24 = (f32[8,2,144,128]{3,2,1,0:T(8,128)S(1)}, f32[8,2,144,128]{3,2,1,0:T(8,128)}, u32[]{:S(2)}) copy-start(f32[8,2,144,128]{3,2,1,0:T(8,128)} %copy-done.23) | copy-start | bytes 3538948
  151.6 5.2 %collective-permute-start.9 = (f32[8,128]{1,0:T(8,128)S(1)}, f32[8,128]{1,0:T(8,128)S(1)}, u32[]{:S(2)}, u32[]{:S(2)}) collective-permute-start(f32[8,128]{1,0:T(8,128)S(1)} %get-tuple-element.36.places), channel_id=1, source_target_pairs={{0,2},{1,3},{2,0},{3,1},{4,6},{5,7},{6,4},{7,5},{8,10},{9,11},{10,... | collective-permute-start | bytes 12296 | tf_op jit(solution)/shard_map/ppermute | solution.py:580
  157.5 5.4 %collective-permute-start.10 = (f32[16,128]{1,0:T(8,128)S(1)}, f32[16,128]{1,0:T(8,128)S(1)}, u32[]{:S(2)}, u32[]{:S(2)}) collective-permute-start(f32[16,128]{1,0:T(8,128)S(1)} %relay.1), channel_id=1, source_target_pairs={{0,2},{1,3},{2,0},{3,1},{4,6},{5,7},{6,4},{7,5},{8,10},{9,11},{10,... | collective-permute-start | bytes 24584 | tf_op jit(solution)/shard_map/ppermute | solution.py:580
  162.9 1.0 copy-start.41
  168.1 3.8 %copy-start.6 = (bf16[2,256,256]{2,1,0:T(8,128)(2,1)S(1)}, bf16[2,256,256]{2,1,0:T(8,128)(2,1)}, u32[]{:S(2)}) copy-start(bf16[2,256,256]{2,1,0:T(8,128)(2,1)} %copy-done.2) | copy-start | bytes 786436
  168.1 3.8 %copy-start.11 = (bf16[2,256,256]{2,1,0:T(8,128)(2,1)S(1)}, bf16[2,256,256]{2,1,0:T(8,128)(2,1)}, u32[]{:S(2)}) copy-start(bf16[2,256,256]{2,1,0:T(8,128)(2,1)} %copy-done.7) | copy-start | bytes 786436
  170.0 0.8 copy-start.29
  170.8 0.7 copy-start.31
  171.9 1.0 copy-start.30
  172.9 1.0 copy-start.32
  (1 other events, 0.6 us)

commit v4 on v3

--- a/solution.py
+++ b/solution.py
@@ -531,17 +531,27 @@
     return pltpu.VMEM(dims, F32)
 
 
-def call(kernel, outs, ins, scratches, specs=None, out_specs=None, aliases=None, name=None, limit=16):
+def call(
+    kernel, outs, ins, scratches, specs=None, out_specs=None, aliases=None, name=None, limit=16, keep=()
+):
+    specs = specs or [SMEM] + [VMEM] * (len(ins) - 1)
+    out_specs = out_specs or [VMEM] * len(outs)
+    placed = []
+    for n, (x, spec) in enumerate(zip(ins, specs)):
+        if spec is HBM or n in keep:
+            x = pltpu.with_memory_space_constraint(x, spec.memory_space)
+        placed.append(x)
+    outs = [pltpu.HBM(x.shape, x.dtype) if spec is HBM else x for x, spec in zip(outs, out_specs)]
     return pl.pallas_call(
         kernel,
         out_shape=outs,
-        in_specs=specs or [SMEM] + [VMEM] * (len(ins) - 1),
-        out_specs=out_specs or [VMEM] * len(outs),
+        in_specs=specs,
+        out_specs=out_specs,
         scratch_shapes=scratches,
         input_output_aliases=aliases or {},
         compiler_params=pltpu.CompilerParams(vmem_limit_bytes=limit * 1024 * 1024),
         name=name,
-    )(*ins)
+    )(*placed)
 
 
 def semaphores(count):
@@ -663,6 +673,7 @@
             [],
             name="blend",
             limit=4,
+            keep=(1, 2, 3, 4, 5),
         )
         (buffer,) = call(
             refill_kernel,
@@ -672,6 +683,7 @@
             aliases={2: 0},
             name="refill",
             limit=4,
+            keep=(2,),
         )
         arrived = deliver(buffer)
         fields, strip = call(
@@ -718,6 +730,7 @@
         [ghost_s, ghost_s, square, square],
         name="final",
         limit=8,
+        keep=(1, 2, 3),
     )
     return flow.reshape(3, 1, 2, CELLS, CELLS), pressure[None], heat[None]
 

time: 178 us -> 152 us (0.85)
  local copies, waits for them, and re-layouts: 33.9 us -> 0.1 us
  Pallas kernels: 28.3 us -> 37.6 us
  starting transfers between devices: 65.2 us -> 59.4 us
  waiting for transfers between devices: 45.1 us -> 49.7 us
    unnamed x100 -> x2, local copies, waits for them, and re-layouts: 33.8 us -> 0.01 us
    pallas_call x17, Pallas kernels: 28.3 us -> 37.6 us  [call(): pl.pallas_call(kernel, out_shape=outs, in_specs=specs, out_specs=out_spec...]
    all_to_all x4, starting transfers between devices: 48.1 us -> 42.3 us  [deliver(): return lax.all_to_all(buffer, ('lat', 'lon'), 0, 0, tiled=True)]
    all_to_all x4, waiting for transfers between devices: 31.7 us -> 35.8 us  [deliver(): return lax.all_to_all(buffer, ('lat', 'lon'), 0, 0, tiled=True)]
  transfers between devices with their start and end apart: 15 -> 15, of which waited for: 10 -> 10; matrix products, arithmetic and copies ran while one was open for 1% -> 1% of each run, Pallas kernels for 9% -> 18%
where the time goes in v4:
time: 152 us; the launch traced here: 151 us
  starting transfers between devices  59.4 us (39%)
  waiting for transfers between devices  49.7 us (33%)
  Pallas kernels  37.6 us (25%)
  between operations  2.87 us (2%)
    all_to_all x4, starting transfers between devices, deliver(): return lax.all_to_all(buffer, ('lat', 'lon'), 0, 0, tiled=True)  42.3 us
    pallas_call x17, Pallas kernels, call(): pl.pallas_call(kernel, out_shape=outs, in_specs=specs, out_specs=out_spec...  37.6 us
    all_to_all x4, waiting for transfers between devices, deliver(): return lax.all_to_all(buffer, ('lat', 'lon'), 0, 0, tiled=True)  35.8 us
    ppermute x4, starting transfers between devices, ring(): return lax.ppermute(x, axis, pairs)  10.9 us
    ppermute x2, waiting for transfers between devices, to_relay(): return lax.ppermute(x, 'lon', [(i, i ^ 2) for i in range(n_lon)])  6.27 us
    ppermute x2, starting transfers between devices, to_relay(): return lax.ppermute(x, 'lon', [(i, i ^ 2) for i in range(n_lon)])  4.3 us
    ppermute x4, waiting for transfers between devices, ring(): return lax.ppermute(x, axis, pairs)  4.15 us
    ppermute x5, waiting for transfers between devices, swap(): return lax.ppermute(x, 'patch', [(0, 1), (1, 0)])  3.46 us
  transfers between devices with their start and end apart: 15, of which 10 were waited for; matrix products, arithmetic and copies ran while one was open for 1% of the time, Pallas kernels for 18%

profile of v4, /device:TPU:2, one launch (start us, length us, event | category | flops | bytes accessed | tf_op | source)
XLA Modules:
  0.0 150.6 jit_solution(4171833141379736192)
XLA Ops:
  0.6 0.0 copy-start
  1.3 1.0 collective-permute-start.4
  3.0 1.1 start.1
  4.1 0.6 collective-permute-start.5
  4.7 3.8 %collective-permute-start = (f32[17,8,128]{2,1,0:T(8,128)S(1)}, f32[17,8,128]{2,1,0:T(8,128)S(1)}, u32[]{:S(2)}, u32[]{:S(2)}) collective-permute-start(f32[17,8,128]{2,1,0:T(8,128)S(1)} %get-tuple-element.37), channel_id=1, source_target_pairs={{0,16},{16,32},{32,48},{48,64},{64,80},{80,96},{96,112},{1,17},{17... | collective-permute-start | bytes 208904 | tf_op jit(solution)/shard_map/ppermute | solution.py:587
  8.5 1.3 collective-permute-start.1
  9.8 0.1 select_reduce_fusion.2
  10.0 0.1 add_convert_fusion
  10.1 0.0 collective-permute-done.4
  10.7 0.0 copy-done
  10.7 0.1 pad_add_fusion.chunks
  10.8 0.0 collective-permute-done.5.row
  10.8 1.4 fill.1.old
  12.2 17.4 %all-to-all-start = ((f32[128,8,128]{2,1,0:T(8,128)}), f32[128,8,128]{2,1,0:T(8,128)S(1)}, u32[]{:S(2)}, u32[]{:S(2)}) async-start(f32[128,8,128]{2,1,0:T(8,128)} %fill.1.old), calls=%async_computation | async-start | bytes 1048576 | tf_op jit(solution)/shard_map/all_to_all | solution.py:593
  29.6 0.0 collective-permute-done.north
  29.6 0.1 select_reduce_fusion.1
  29.7 0.0 collective-permute-done.1.south
  29.7 1.6 %columns.1 = (f32[136,128]{1,0:T(8,128)S(1)}, f32[136,128]{1,0:T(8,128)S(1)}) custom-call(f32[6,128,128]{2,1,0:T(8,128)} %bitcast.32, f32[2,128,128]{2,1,0:T(8,128)} %bitcast.35, f32[2,128,128]{2,1,0:T(8,128)} %bitcast.38, f32[2,128,128]{2,1,0:T(8,128)} %bitcast.41, f32[8,128,128]{2,1,0:T(8,128)} %bitcast.28, f32[17,8,128]{2,1,0:T(8,128)S(1)} %collective-permute-done.north, ...), custom_call_target="tpu_custom_call" | custom-call | tf_op jit(solution)/shard_map/columns/pallas_call | solution.py:545
  31.3 3.4 %collective-permute-start.2 = (f32[136,128]{1,0:T(8,128)S(1)}, f32[136,128]{1,0:T(8,128)S(1)}, u32[]{:S(2)}, u32[]{:S(2)}) collective-permute-start(f32[136,128]{1,0:T(8,128)S(1)} %get-tuple-element.39), channel_id=1, source_target_pairs={{0,1},{1,2},{2,3},{3,4},{4,5},{5,6},{6,7},{7,8},{8,9},{9,10},{10,1... | collective-permute-start | bytes 208904 | tf_op jit(solution)/shard_map/ppermute | solution.py:587
  34.7 2.5 %collective-permute-start.3 = (f32[136,128]{1,0:T(8,128)S(1)}, f32[136,128]{1,0:T(8,128)S(1)}, u32[]{:S(2)}, u32[]{:S(2)}) collective-permute-start(f32[136,128]{1,0:T(8,128)S(1)} %get-tuple-element.40), channel_id=1, source_target_pairs={{1,0},{2,1},{3,2},{4,3},{5,4},{6,5},{7,6},{8,7},{9,8},{10,9},{11,1... | collective-permute-start | bytes 208904 | tf_op jit(solution)/shard_map/ppermute | solution.py:587
  37.2 0.1 select_reduce_fusion
  37.3 0.8 collective-permute-done.2.west
  38.2 0.1 select_reduce_fusion.4
  38.3 3.3 %collective-permute-done.3.east = f32[136,128]{1,0:T(8,128)S(1)} collective-permute-done((f32[136,128]{1,0:T(8,128)S(1)}, f32[136,128]{1,0:T(8,128)S(1)}, u32[]{:S(2)}, u32[]{:S(2)}) %collective-permute-start.3) | collective-permute-done | bytes 69664 | tf_op jit(solution)/shard_map/ppermute | solution.py:587
  41.6 0.1 select_reduce_fusion.3
  41.7 0.1 concatenate.6.ints
  41.8 4.2 %build.1 = (f32[8,2,144,128]{3,2,1,0:T(8,128)}, f32[8,2,2,144,128]{4,3,2,1,0:T(8,128)}, f32[2,2,144,128]{3,2,1,0:T(8,128)}, f32[4,8,128]{2,1,0:T(8,128)S(1)}, f3...) custom-call(s32[19]{0:T(128)S(1)} %concatenate.6.ints, ...), custom_call_target="tpu_custom_call" | custom-call | tf_op jit(solution)/shard_map/build/pallas_call | solution.py:545
  46.0 3.3 %all-to-all-done.arrived = f32[128,8,128]{2,1,0:T(8,128)S(1)} async-done(((f32[128,8,128]{2,1,0:T(8,128)}), f32[128,8,128]{2,1,0:T(8,128)S(1)}, u32[]{:S(2)}, u32[]{:S(2)}) %all-to-all-start) | async-done | bytes 524320 | tf_op jit(solution)/shard_map/all_to_all | solution.py:593
  49.3 0.8 blend.3
  50.2 0.1 collective-permute-start.6
  50.2 1.2 collective-permute-done.6.row
  51.4 1.9 %refill.3.old = f32[128,8,128]{2,1,0:T(8,128)} custom-call(s32[6]{0:T(128)S(1)} %pad_add_fusion.chunks, f32[8,128]{1,0:T(8,128)S(1)} %collective-permute-done.6.row, f32[128,8,128]{2,1,0:T(8,128)} %fill.1.old), custom_call_target="tpu_custom_call", output_to_operand_aliasing={{}: (2, {})} | custom-call | tf_op jit(solution)/shard_map/refill/pallas_call | solution.py:545
  53.3 11.1 %all-to-all-start.1 = ((f32[128,8,128]{2,1,0:T(8,128)}), f32[128,8,128]{2,1,0:T(8,128)S(1)}, u32[]{:S(2)}, u32[]{:S(2)}) async-start(f32[128,8,128]{2,1,0:T(8,128)} %refill.3.old), calls=%async_computation.1 | async-start | bytes 1048576 | tf_op jit(solution)/shard_map/all_to_all | solution.py:593
  64.4 4.3 %sweep.3 = (f32[8,2,144,128]{3,2,1,0:T(8,128)}, f32[4,8,128]{2,1,0:T(8,128)S(1)}) custom-call(s32[19]{0:T(128)S(1)} %concatenate.6.ints, f32[8,2,144,128]{3,2,1,0:T(8,128)} %get-tuple-element.41.fields, f32[8,2,2,144,128]{4,3,2,1,0:T(8,128)} %get-tuple-element.42.coef, f32[8,256]{1,0:T(8,128)S(1)} %get-tuple-element.48.lat_ghost, ...), custom_call_target="tpu_custom_call" | custom-call | tf_op jit(solution)/shard_map/sweep/pallas_call | solution.py:545
  68.7 16.1 %all-to-all-done.1.arrived = f32[128,8,128]{2,1,0:T(8,128)S(1)} async-done(((f32[128,8,128]{2,1,0:T(8,128)}), f32[128,8,128]{2,1,0:T(8,128)S(1)}, u32[]{:S(2)}, u32[]{:S(2)}) %all-to-all-start.1) | async-done | bytes 524320 | tf_op jit(solution)/shard_map/all_to_all | solution.py:593
  84.8 0.8 blend.4
  85.7 0.1 collective-permute-start.7
  85.8 1.2 collective-permute-done.7.row
  86.9 1.9 %refill.4.old = f32[128,8,128]{2,1,0:T(8,128)} custom-call(s32[6]{0:T(128)S(1)} %pad_add_fusion.chunks, f32[8,128]{1,0:T(8,128)S(1)} %collective-permute-done.7.row, f32[128,8,128]{2,1,0:T(8,128)} %refill.3.old), custom_call_target="tpu_custom_call", output_to_operand_aliasing={{}: (2, {})} | custom-call | tf_op jit(solution)/shard_map/refill/pallas_call | solution.py:545
  88.8 6.8 %all-to-all-start.2 = ((f32[128,8,128]{2,1,0:T(8,128)}), f32[128,8,128]{2,1,0:T(8,128)S(1)}, u32[]{:S(2)}, u32[]{:S(2)}) async-start(f32[128,8,128]{2,1,0:T(8,128)} %refill.4.old), calls=%async_computation.2 | async-start | bytes 1048576 | tf_op jit(solution)/shard_map/all_to_all | solution.py:593
  95.6 4.3 %sweep.4 = (f32[8,2,144,128]{3,2,1,0:T(8,128)}, f32[4,8,128]{2,1,0:T(8,128)S(1)}) custom-call(s32[19]{0:T(128)S(1)} %concatenate.6.ints, f32[8,2,144,128]{3,2,1,0:T(8,128)} %get-tuple-element.50.fields, f32[8,2,2,144,128]{4,3,2,1,0:T(8,128)} %get-tuple-element.42.coef, f32[8,256]{1,0:T(8,128)S(1)} %get-tuple-element.53.lat_ghost, ...), custom_call_target="tpu_custom_call" | custom-call | tf_op jit(solution)/shard_map/sweep/pallas_call | solution.py:545
  99.9 16.4 %all-to-all-done.2.arrived = f32[128,8,128]{2,1,0:T(8,128)S(1)} async-done(((f32[128,8,128]{2,1,0:T(8,128)}), f32[128,8,128]{2,1,0:T(8,128)S(1)}, u32[]{:S(2)}, u32[]{:S(2)}) %all-to-all-start.2) | async-done | bytes 524320 | tf_op jit(solution)/shard_map/all_to_all | solution.py:593
  116.3 0.8 blend.5
  117.1 0.1 collective-permute-start.8
  117.2 1.2 collective-permute-done.8.row
  118.4 1.9 %refill.5 = f32[128,8,128]{2,1,0:T(8,128)} custom-call(s32[6]{0:T(128)S(1)} %pad_add_fusion.chunks, f32[8,128]{1,0:T(8,128)S(1)} %collective-permute-done.8.row, f32[128,8,128]{2,1,0:T(8,128)} %refill.4.old), custom_call_target="tpu_custom_call", output_to_operand_aliasing={{}: (2, {})} | custom-call | tf_op jit(solution)/shard_map/refill/pallas_call | solution.py:545
  120.2 7.0 %all-to-all-start.3 = ((f32[128,8,128]{2,1,0:T(8,128)}), f32[128,8,128]{2,1,0:T(8,128)S(1)}, u32[]{:S(2)}, u32[]{:S(2)}) async-start(f32[128,8,128]{2,1,0:T(8,128)} %refill.5), calls=%async_computation.3 | async-start | bytes 1048576 | tf_op jit(solution)/shard_map/all_to_all | solution.py:593
  127.2 2.2 %collective-permute-start.9 = (f32[8,128]{1,0:T(8,128)S(1)}, f32[8,128]{1,0:T(8,128)S(1)}, u32[]{:S(2)}, u32[]{:S(2)}) collective-permute-start(f32[8,128]{1,0:T(8,128)S(1)} %get-tuple-element.36.places), channel_id=1, source_target_pairs={{0,2},{1,3},{2,0},{3,1},{4,6},{5,7},{6,4},{7,5},{8,10},{9,11},{10,... | collective-permute-start | bytes 12296 | tf_op jit(solution)/shard_map/ppermute | solution.py:590
  129.4 3.1 %collective-permute-done.9 = f32[8,128]{1,0:T(8,128)S(1)} collective-permute-done((f32[8,128]{1,0:T(8,128)S(1)}, f32[8,128]{1,0:T(8,128)S(1)}, u32[]{:S(2)}, u32[]{:S(2)}) %collective-permute-start.9) | collective-permute-done | bytes 4128 | tf_op jit(solution)/shard_map/ppermute | solution.py:590
  132.5 0.1 convert_reduce_fusion.places
  132.6 0.6 relay.1
  133.1 2.1 %collective-permute-start.10 = (f32[16,128]{1,0:T(8,128)S(1)}, f32[16,128]{1,0:T(8,128)S(1)}, u32[]{:S(2)}, u32[]{:S(2)}) collective-permute-start(f32[16,128]{1,0:T(8,128)S(1)} %relay.1), channel_id=1, source_target_pairs={{0,2},{1,3},{2,0},{3,1},{4,6},{5,7},{6,4},{7,5},{8,10},{9,11},{10,... | collective-permute-start | bytes 24584 | tf_op jit(solution)/shard_map/ppermute | solution.py:590
  135.3 3.2 %collective-permute-done.10 = f32[16,128]{1,0:T(8,128)S(1)} collective-permute-done((f32[16,128]{1,0:T(8,128)S(1)}, f32[16,128]{1,0:T(8,128)S(1)}, u32[]{:S(2)}, u32[]{:S(2)}) %collective-permute-start.10) | collective-permute-done | bytes 8224 | tf_op jit(solution)/shard_map/ppermute | solution.py:590
  138.4 2.0 %heat.1.warm = f32[2,2,144,128]{3,2,1,0:T(8,128)S(1)} custom-call(s32[19]{0:T(128)S(1)} %concatenate.6.ints, f32[2,2,144,128]{3,2,1,0:T(8,128)} %get-tuple-element.65.warm, f32[8,16,128]{2,1,0:T(8,128)S(1)} %pad.4.blocks, f32[8,128,128]{2,1,0:T(8,128)} %bitcast.30), custom_call_target="tpu_custom_call" | custom-call | tf_op jit(solution)/shard_map/heat/pallas_call | solution.py:545
  140.5 4.9 %sweep.5 = (f32[8,2,144,128]{3,2,1,0:T(8,128)}, f32[4,8,128]{2,1,0:T(8,128)}) custom-call(s32[19]{0:T(128)S(1)} %concatenate.6.ints, f32[8,2,144,128]{3,2,1,0:T(8,128)} %get-tuple-element.58.fields, f32[8,2,2,144,128]{4,3,2,1,0:T(8,128)} %get-tuple-element.42.coef, f32[8,256]{1,0:T(8,128)S(1)} %get-tuple-element.59.lat_ghost, ...), custom_call_target="tpu_custom_call" | custom-call | tf_op jit(solution)/shard_map/sweep/pallas_call | solution.py:545
  145.4 3.2 %ahead.1 = (f32[8,128,128]{2,1,0:T(8,128)S(1)}, f32[3,2,128,128]{3,2,1,0:T(8,128)S(1)}, f32[2,3,2,8,128]{4,3,2,1,0:T(8,128)S(1)}) custom-call(s32[19]{0:T(128)S(1)} %concatenate.6.ints, f32[8,2,144,128]{3,2,1,0:T(8,128)} %get-tuple-element.61.fields, f32[8,2,2,144,128]{4,3,2,1,0:T(8,128)} %get-tuple-element.42.coef), custom_call_target="tpu_custom_call" | custom-call | tf_op jit(solution)/shard_map/ahead/pallas_call | solution.py:545
  148.6 0.0 all-to-all-done.3.arrived
  148.6 1.9 %final.1 = (f32[6,128,128]{2,1,0:T(8,128)}, f32[2,128,128]{2,1,0:T(8,128)}, f32[2,128,128]{2,1,0:T(8,128)}) custom-call(s32[19]{0:T(128)S(1)} %concatenate.6.ints, f32[128,8,128]{2,1,0:T(8,128)S(1)} %all-to-all-done.3.arrived, bf16[2,256,256]{2,1,0:T(8,128)(2,1)S(1)} %get-tuple-element.46.high, bf16[2,256,256]{2,1,0:T(8,128)(2,1)S(1)} %get-tuple-element.47.low, ...), custom_call_target="tpu_custom_call" | custom-call | tf_op jit(solution)/shard_map/final/pallas_call | solution.py:545
  (9 shorter events, 0.0 us)
Async XLA Ops:
  0.6 10.1 %copy-start = (s32[5]{0:T(128)S(1)}, s32[5]{0:T(128)}, u32[]{:S(2)}) copy-start(s32[5]{0:T(128)} %constant.32.clone) | copy-start | bytes 64
  1.3 8.8 %collective-permute-start.4 = (f32[1]{0:T(128)}, f32[1]{0:T(128)}, u32[]{:S(2)}, u32[]{:S(2)}) collective-permute-start(f32[1]{0:T(128)} %bitcast.15), channel_id=1, source_target_pairs={{0,128},{128,0},{1,129},{129,1},{2,130},{130,2},{3,131},{131,3},{4... | collective-permute-start | bytes 20 | tf_op jit(solution)/shard_map/ppermute | solution.py:582
  4.1 6.7 %collective-permute-start.5 = (f32[16,128]{1,0:T(8,128)S(1)}, f32[16,128]{1,0:T(8,128)S(1)}, u32[]{:S(2)}, u32[]{:S(2)}) collective-permute-start(f32[16,128]{1,0:T(8,128)S(1)} %get-tuple-element.45), channel_id=1, source_target_pairs={{0,128},{128,0},{1,129},{129,1},{2,130},{130,2},{3,131},{131,3},{4... | collective-permute-start | bytes 24584 | tf_op jit(solution)/shard_map/ppermute | solution.py:582
  4.7 24.9 %collective-permute-start = (f32[17,8,128]{2,1,0:T(8,128)S(1)}, f32[17,8,128]{2,1,0:T(8,128)S(1)}, u32[]{:S(2)}, u32[]{:S(2)}) collective-permute-start(f32[17,8,128]{2,1,0:T(8,128)S(1)} %get-tuple-element.37), channel_id=1, source_target_pairs={{0,16},{16,32},{32,48},{48,64},{64,80},{80,96},{96,112},{1,17},{17... | collective-permute-start | bytes 208904 | tf_op jit(solution)/shard_map/ppermute | solution.py:587
  8.5 21.2 %collective-permute-start.1 = (f32[17,8,128]{2,1,0:T(8,128)S(1)}, f32[17,8,128]{2,1,0:T(8,128)S(1)}, u32[]{:S(2)}, u32[]{:S(2)}) collective-permute-start(f32[17,8,128]{2,1,0:T(8,128)S(1)} %get-tuple-element.38), channel_id=1, source_target_pairs={{16,0},{32,16},{48,32},{64,48},{80,64},{96,80},{112,96},{17,1},{33... | collective-permute-start | bytes 208904 | tf_op jit(solution)/shard_map/ppermute | solution.py:587
  12.2 37.1 %all-to-all-start = ((f32[128,8,128]{2,1,0:T(8,128)}), f32[128,8,128]{2,1,0:T(8,128)S(1)}, u32[]{:S(2)}, u32[]{:S(2)}) async-start(f32[128,8,128]{2,1,0:T(8,128)} %fill.1.old), calls=%async_computation | async-start | bytes 1048576 | tf_op jit(solution)/shard_map/all_to_all | solution.py:593
  31.3 6.8 %collective-permute-start.2 = (f32[136,128]{1,0:T(8,128)S(1)}, f32[136,128]{1,0:T(8,128)S(1)}, u32[]{:S(2)}, u32[]{:S(2)}) collective-permute-start(f32[136,128]{1,0:T(8,128)S(1)} %get-tuple-element.39), channel_id=1, source_target_pairs={{0,1},{1,2},{2,3},{3,4},{4,5},{5,6},{6,7},{7,8},{8,9},{9,10},{10,1... | collective-permute-start | bytes 208904 | tf_op jit(solution)/shard_map/ppermute | solution.py:587
  34.7 6.9 %collective-permute-start.3 = (f32[136,128]{1,0:T(8,128)S(1)}, f32[136,128]{1,0:T(8,128)S(1)}, u32[]{:S(2)}, u32[]{:S(2)}) collective-permute-start(f32[136,128]{1,0:T(8,128)S(1)} %get-tuple-element.40), channel_id=1, source_target_pairs={{1,0},{2,1},{3,2},{4,3},{5,4},{6,5},{7,6},{8,7},{9,8},{10,9},{11,1... | collective-permute-start | bytes 208904 | tf_op jit(solution)/shard_map/ppermute | solution.py:587
  50.2 1.2 collective-permute-start.6
  53.3 31.6 %all-to-all-start.1 = ((f32[128,8,128]{2,1,0:T(8,128)}), f32[128,8,128]{2,1,0:T(8,128)S(1)}, u32[]{:S(2)}, u32[]{:S(2)}) async-start(f32[128,8,128]{2,1,0:T(8,128)} %refill.3.old), calls=%async_computation.1 | async-start | bytes 1048576 | tf_op jit(solution)/shard_map/all_to_all | solution.py:593
  85.7 1.2 collective-permute-start.7
  88.8 27.5 %all-to-all-start.2 = ((f32[128,8,128]{2,1,0:T(8,128)}), f32[128,8,128]{2,1,0:T(8,128)S(1)}, u32[]{:S(2)}, u32[]{:S(2)}) async-start(f32[128,8,128]{2,1,0:T(8,128)} %refill.4.old), calls=%async_computation.2 | async-start | bytes 1048576 | tf_op jit(solution)/shard_map/all_to_all | solution.py:593
  117.1 1.2 collective-permute-start.8
  120.2 28.4 %all-to-all-start.3 = ((f32[128,8,128]{2,1,0:T(8,128)}), f32[128,8,128]{2,1,0:T(8,128)S(1)}, u32[]{:S(2)}, u32[]{:S(2)}) async-start(f32[128,8,128]{2,1,0:T(8,128)} %refill.5), calls=%async_computation.3 | async-start | bytes 1048576 | tf_op jit(solution)/shard_map/all_to_all | solution.py:593
  127.2 5.3 %collective-permute-start.9 = (f32[8,128]{1,0:T(8,128)S(1)}, f32[8,128]{1,0:T(8,128)S(1)}, u32[]{:S(2)}, u32[]{:S(2)}) collective-permute-start(f32[8,128]{1,0:T(8,128)S(1)} %get-tuple-element.36.places), channel_id=1, source_target_pairs={{0,2},{1,3},{2,0},{3,1},{4,6},{5,7},{6,4},{7,5},{8,10},{9,11},{10,... | collective-permute-start | bytes 12296 | tf_op jit(solution)/shard_map/ppermute | solution.py:590
  133.1 5.3 %collective-permute-start.10 = (f32[16,128]{1,0:T(8,128)S(1)}, f32[16,128]{1,0:T(8,128)S(1)}, u32[]{:S(2)}, u32[]{:S(2)}) collective-permute-start(f32[16,128]{1,0:T(8,128)S(1)} %relay.1), channel_id=1, source_target_pairs={{0,2},{1,3},{2,0},{3,1},{4,6},{5,7},{6,4},{7,5},{8,10},{9,11},{10,... | collective-permute-start | bytes 24584 | tf_op jit(solution)/shard_map/ppermute | solution.py:590

commit v5 on v4

--- a/solution.py
+++ b/solution.py
@@ -17,8 +17,11 @@
 SMEM = pl.BlockSpec(memory_space=pltpu.SMEM)
 HBM = pl.BlockSpec(memory_space=pltpu.HBM)
 NORTH, SOUTH, WEST, EAST = 1, 2, 3, 4
-PLACES = 5
-LAT_BASE, LON_BASE = 17, 18
+LAT_BASE, LON_BASE = 5, 6
+CHUNKS = 7
+PLACES = 10
+WARM = 22
+SLOTS = 8
 
 
 def lanes():
@@ -53,7 +56,7 @@
 
 
 def start_kernel(
-    at, slots, flow, pressure, heat, friction, weights, row, top, bottom, places, near, named, sems
+    at, slots, flow, pressure, heat, friction, weights, chunks, top, bottom, places, near, named, row, sems
 ):
     start = pl.multiple_of((at[0] // 8) * 8, 8)
     copies = Copies(sems)
@@ -67,29 +70,31 @@
         copies.start(heat.at[:, lo : lo + 8, :], out.at[8:10])
         copies.start(friction.at[:, lo : lo + 8, :], out.at[10:12])
         copies.start(weights.at[4:8, lo : lo + 8, :], out.at[12:16])
-    row[...] = jnp.zeros((16, CELLS), F32)
+    row[8:16, :] = jnp.broadcast_to((at[4] + 1).astype(F32), (8, CELLS))
+    chunks[...] = jnp.zeros(chunks.shape, F32)
     copies.wait()
     own = jnp.broadcast_to(named[...], (8, CELLS)) == sublanes()
-    place = jnp.sum(jnp.where(own, lanes(), 0).astype(F32), axis=1, keepdims=True)
+    place = jnp.sum(jnp.where(own, lanes() + 1, 0).astype(F32), axis=1, keepdims=True)
     place = jnp.broadcast_to(place, (8, CELLS))
     for out in (top.at[16], bottom.at[16], places):
         out[...] = place
     inside = at[0] - start
     for f in range(10):
-        row[f : f + 1, :] = near[f, pl.ds(inside, 1), :]
-
-
-def fill_kernel(chunks, row, out):
-    out[...] = jnp.zeros((CELLS, 8, CELLS), F32)
-    for n in range(5):
-        out[chunks[n]] = row[0:8, :]
-    out[chunks[5]] = row[8:16, :]
-
-
-def refill_kernel(chunks, row, old, out):
-    del old
-    for n in range(5):
-        out[chunks[n]] = row[...]
+        to = f if f < 8 else f + 1
+        row[to : to + 1, :] = near[f, pl.ds(inside, 1), :]
+    for n in range(3):
+        chunks[at[1 + n]] = row[...]
+
+
+def pack_kernel(table, arrived, out):
+    count = out.shape[1]
+    for lat in range(out.shape[0]):
+        for n in range(SLOTS):
+            out[lat, n] = arrived[table[SLOTS * lat + n], 0:8, :]
+        if count > SLOTS:
+            for n in range(4):
+                block = table[SLOTS * out.shape[0] + 4 * lat + n]
+                out[lat, SLOTS, 2 * n : 2 * n + 2, :] = arrived[block, 9:11, :]
 
 
 def columns_kernel(
@@ -302,7 +307,7 @@
             )
 
 
-def blend_kernel(ints, strip, factors, arrived, high, low, lat_ghost, lon_ghost, row):
+def blend_kernel(ints, strip, factors, arrived, high, low, lat_ghost, lon_ghost, chunks):
     blend_sides(ints, arrived, high, low, lat_ghost, lon_ghost)
     at = ints[0]
     lane, sub = lanes(), sublanes()
@@ -329,7 +334,10 @@
     divergence = (
         pltpu.roll(steps[0], 6, 0) + pltpu.roll(steps[1], 4, 0) + pltpu.roll(steps[2], 2, 0)
     )
-    row[...] = jnp.where(sub < 6, value, here - factors[7] * divergence)
+    row = jnp.where(sub < 6, value, here - factors[7] * divergence)
+    chunks[...] = jnp.zeros(chunks.shape, F32)
+    for n in range(3):
+        chunks[ints[CHUNKS + n]] = row
 
 
 def ghost_columns(count, lon_ghost, cut, rows_s, out):
@@ -414,13 +422,8 @@
     copies.wait(2)
 
 
-def relay_kernel(places, arrived, out):
-    for n in range(8):
-        out[2 * n : 2 * n + 2, :] = arrived[places[n], 0:2, :]
-
-
 def heat_kernel(
-    ints, warm, blocks, weights, out, chosen, lat_ghost, lon_ghost, cols_s, ends_s, rows_s, sems
+    ints, warm, arrived, weights, out, chosen, block, lat_ghost, lon_ghost, cols_s, ends_s, rows_s, sems
 ):
     copies = Copies(sems)
     copies.start(warm, out)
@@ -428,17 +431,21 @@
     copies.start(weights.at[pl.ds(ints[LON_BASE], 2)], chosen.at[2:4])
     copies.wait()
     sides = (
-        (lat_ghost, (ints[NORTH] + ints[SOUTH]) > 0, LAT_BASE),
-        (lon_ghost, (ints[WEST] + ints[EAST]) > 0, LON_BASE),
-    )
-    for n, (ghost, active, base) in enumerate(sides):
+        (lat_ghost, (ints[NORTH] + ints[SOUTH]) > 0),
+        (lon_ghost, (ints[WEST] + ints[EAST]) > 0),
+    )
+    block[...] = jnp.zeros((16, CELLS), F32)
+    for n, (ghost, active) in enumerate(sides):
         ghost[...] = jnp.zeros((8, LANES), F32)
 
         @pl.when(active)
         def _():
             total = jnp.zeros((16, CELLS), F32)
             for term in range(2):
-                b_high, b_low = split(blocks[ints[base] + term])
+                at = WARM + 2 * n + term
+                for k in range(2):
+                    block[k : k + 1, :] = arrived[ints[at], pl.ds(2 * ints[at + 4] + k, 1), :]
+                b_high, b_low = split(block[...])
                 w_high, w_low = split(chosen[2 * n + term])
                 total = total + times(b_high, w_low) + times(b_low, w_high) + times(b_high, w_high)
             ghost[:, 0:CELLS] = total[0:8]
@@ -578,39 +585,64 @@
     devices = n_lat * n_lon
     own_row = departing_bands.reshape(1)
 
-    def swap(x):
-        return lax.ppermute(x, "patch", [(0, 1), (1, 0)])
-
     def ring(x, axis, step):
         count = lax.axis_size(axis)
         pairs = [(i, i + step) for i in range(count) if 0 <= i + step < count]
         return lax.ppermute(x, axis, pairs)
 
-    def to_relay(x):
-        return lax.ppermute(x, "lon", [(i, i ^ 2) for i in range(n_lon)])
-
-    def deliver(buffer):
-        return lax.all_to_all(buffer, ("lat", "lon"), 0, 0, tiled=True)
-
-    receiver = swap(receiving_processor.reshape(1).astype(F32)).astype(jnp.int32)
-    receiver = jnp.maximum(receiver, 0)
-    near = receiver + jnp.array([0, 1, -1, n_lon, -n_lon], jnp.int32)
-    near = jnp.where((near >= 0) & (near < devices), near, receiver)
-    chunks = jnp.concatenate([near, receiver ^ 2])
+    receiver = receiving_processor.reshape(1)
+    other = (1 - lax.axis_index("patch")) * n_lon
+    column = jnp.maximum(receiver, 0) % n_lon + jnp.array([0, -1, 1], jnp.int32)
+    chunk = other + jnp.clip(column, 0, n_lon - 1)
+    first = jnp.concatenate([own_row, chunk, receiver])
 
     planes = (flow, pressure, heat, friction, weights)
-    row, top, bottom, places = call(
+    chunks, top, bottom, places = call(
         start_kernel,
-        [shape(16, CELLS), shape(17, 8, CELLS), shape(17, 8, CELLS), shape(8, CELLS)],
-        (own_row, shift_filled_by_lane.reshape(1, CELLS), *planes),
-        [scratch(10, 8, CELLS), pltpu.VMEM((1, CELLS), jnp.int32), semaphores(14)],
+        [shape(2 * n_lon, 16, CELLS), shape(17, 8, CELLS), shape(17, 8, CELLS), shape(8, CELLS)],
+        (first, shift_filled_by_lane.reshape(1, CELLS), *planes),
+        [scratch(10, 8, CELLS), pltpu.VMEM((1, CELLS), jnp.int32), scratch(16, CELLS), semaphores(14)],
         specs=[SMEM] + [HBM] * 6,
         name="start",
     )
-    (buffer,) = call(
-        fill_kernel, [shape(devices, 8, CELLS)], (chunks, swap(row)), [], name="fill", limit=4
-    )
-    arrived = deliver(buffer)
+
+    def across(chunks):
+        return lax.all_to_all(chunks, ("patch", "lon"), 0, 0, tiled=True)
+
+    def along(table, blocks, slots):
+        (packed,) = call(
+            pack_kernel,
+            [shape(n_lat, slots, 8, CELLS)],
+            (table, blocks),
+            [],
+            name="pack",
+            limit=4,
+            keep=(1,),
+        )
+        return lax.all_to_all(packed, "lat", 0, 0, tiled=True).reshape(n_lat * slots, 8, CELLS)
+
+    arrived = across(chunks)
+    sent_to = lax.dynamic_slice(arrived, (other, 8, 0), (n_lon, 1, 1)).reshape(n_lon)
+    sent_to = sent_to.astype(jnp.int32) - 1
+    every_lat = jnp.arange(n_lat, dtype=jnp.int32)[:, None]
+    to_lat, to_lon = (sent_to // n_lon)[None], (sent_to % n_lon)[None]
+    exact = (sent_to >= 0)[None] & (to_lat == every_lat)
+    close = (sent_to >= 0)[None] & (jnp.abs(to_lat - every_lat) == 1) & (to_lon == lon)
+
+    def sorted_blocks(wanted, count):
+        rank = jnp.sum(
+            (wanted[:, None, :] & (jnp.arange(n_lon)[None, None, :] < jnp.arange(n_lon)[None, :, None]))
+            .astype(jnp.int32),
+            axis=2,
+        )
+        mine = wanted[:, None, :] & (rank[:, None, :] == jnp.arange(count)[None, :, None])
+        found = jnp.sum(jnp.where(mine, jnp.arange(n_lon, dtype=jnp.int32)[None, None, :], 0), axis=2)
+        return other + found.reshape(-1)
+
+    table = jnp.concatenate(
+        [sorted_blocks(exact | close, SLOTS), sorted_blocks(exact & (to_lon == lon), 4)]
+    ).astype(jnp.int32)
+    arrived = along(table, arrived, SLOTS + 1)
     north, south = ring(bottom, "lat", 1), ring(top, "lat", -1)
     wide = shape(2 * HALO * PLANES + 40, CELLS)
     square = scratch(CELLS, CELLS)
@@ -625,18 +657,35 @@
     west, east = ring(to_east, "lon", 1), ring(to_west, "lon", -1)
 
     def numbers(block):
-        return block[:, 0].astype(jnp.int32)
+        return block[:, 0].astype(jnp.int32) - 1
 
     on_edge = jnp.stack([lat == 0, lat == n_lat - 1, lon == 0, lon == n_lon - 1]).astype(jnp.int32)
-    own = numbers(places)
+    own, before, after = numbers(places), numbers(west[-8:]), numbers(east[-8:])
+    above, below = numbers(north[16]), numbers(south[16])
 
     def side(block, base, last):
         return jnp.where(last, block[base + 2 : base + 4], block[base : base + 2])
 
-    pick = [side(x, 0, lat > 0) for x in (own, numbers(west[-8:]), numbers(east[-8:]))]
-    pick += [side(x, 4, lon > 0) for x in (own, numbers(north[16]), numbers(south[16]))]
+    pick = [side(x, 0, lat > 0) for x in (own, before, after)]
+    pick += [side(x, 4, lon > 0) for x in (own, above, below)]
+    pick = jnp.concatenate(pick)
+
+    def slot_of(chosen, listed, most):
+        same = (listed >= 0)[None] & (listed[None] // n_lon == chosen[:, None] // n_lon)
+        earlier = same & (listed[None] < chosen[:, None])
+        return jnp.minimum(jnp.sum(earlier.astype(jnp.int32), axis=1), most)
+
+    slot = slot_of(pick, jnp.concatenate([own, before, after, above, below]), SLOTS - 1)
+    from_lat = jnp.maximum(pick, 0) // n_lon
+    mine = jnp.concatenate([pick[0:2], pick[6:8]])
+    mine_from = jnp.concatenate([from_lat[0:2], from_lat[6:8]])
+    warm_at = [mine_from * (SLOTS + 1) + SLOTS, slot_of(mine, own, 3)]
     bases = jnp.stack([jnp.where(lat > 0, 2, 0), jnp.where(lon > 0, 6, 4)]).astype(jnp.int32)
-    ints = jnp.concatenate([own_row, on_edge] + pick + [bases])
+
+    def integers(slots):
+        return jnp.concatenate([own_row, on_edge, bases, chunk, from_lat * slots + slot, *warm_at])
+
+    ints_first, ints = integers(SLOTS + 1), integers(SLOTS)
 
     state = shape(8, 2, ROWS, CELLS)
     state_s = scratch(8, 2, ROWS, CELLS)
@@ -661,31 +710,30 @@
         out_specs=[HBM] * 3 + [VMEM] * 4,
         name="build",
     )
-    relayed = numbers(to_relay(places))
     ghost = shape(8, LANES)
     ghost_s = scratch(8, LANES)
-    first_arrived = arrived
     for sweep in range(SWEEPS - 1):
-        lat_ghost, lon_ghost, row = call(
+        lat_ghost, lon_ghost, chunks = call(
             blend_kernel,
-            [ghost, ghost, shape(8, CELLS)],
-            (ints, strip, factors, arrived, high, low),
+            [ghost, ghost, shape(2 * n_lon, 8, CELLS)],
+            (ints_first if sweep == 0 else ints, strip, factors, arrived, high, low),
             [],
             name="blend",
             limit=4,
             keep=(1, 2, 3, 4, 5),
         )
-        (buffer,) = call(
-            refill_kernel,
-            [shape(devices, 8, CELLS)],
-            (chunks, swap(row), buffer),
-            [],
-            aliases={2: 0},
-            name="refill",
-            limit=4,
-            keep=(2,),
-        )
-        arrived = deliver(buffer)
+        if sweep == 0:
+            (warm,) = call(
+                heat_kernel,
+                [shape(2, 2, ROWS, CELLS)],
+                (ints, warm, arrived, weights),
+                [scratch(4, CELLS, CELLS), scratch(16, CELLS), ghost_s, ghost_s, square, square, square]
+                + [semaphores(3)],
+                specs=[SMEM, HBM, VMEM, HBM],
+                name="heat",
+                limit=4,
+            )
+        arrived = along(table[: n_lat * SLOTS], across(chunks), SLOTS)
         fields, strip = call(
             sweep_kernel,
             [state, strips],
@@ -695,26 +743,6 @@
             out_specs=[HBM, VMEM],
             name="sweep",
         )
-        if sweep == 0:
-            (blocks,) = call(
-                relay_kernel,
-                [shape(16, CELLS)],
-                (relayed, first_arrived),
-                [],
-                name="relay",
-                limit=4,
-            )
-            blocks = to_relay(blocks).reshape(8, 2, CELLS)
-            blocks = jnp.pad(blocks, ((0, 0), (0, 14), (0, 0)))
-            (warm,) = call(
-                heat_kernel,
-                [shape(2, 2, ROWS, CELLS)],
-                (ints, warm, blocks, weights),
-                [scratch(4, CELLS, CELLS), ghost_s, ghost_s, square, square, square, semaphores(3)],
-                specs=[SMEM, HBM, VMEM, HBM],
-                name="heat",
-                limit=4,
-            )
     ready, beside, above = call(
         ahead_kernel,
         [shape(8, CELLS, CELLS), shape(3, 2, CELLS, CELLS), shape(2, 3, 2, 8, CELLS)],

time: 152 us -> 153 us (level)
  blocking collectives: 0 us -> 38.6 us
  starting transfers between devices: 59.4 us -> 37.1 us
  waiting for transfers between devices: 49.7 us -> 31.6 us
  other arithmetic: 0.91 us -> 3.68 us
    all_to_all x0 -> x3, blocking collectives: none -> 38.6 us  [across(): return lax.all_to_all(chunks, ('patch', 'lon'), 0, 0, tiled=True)]
    all_to_all x4 -> x5, starting transfers between devices: 42.3 us -> 26.2 us  [the longest x4 18.6 us: along(): lax.all_to_all(packed, 'lat', 0, 0, tiled=True)]
    all_to_all x4 -> x5, waiting for transfers between devices: 35.8 us -> 24.1 us  [the longest x4 24.1 us: along(): lax.all_to_all(packed, 'lat', 0, 0, tiled=True)]
    ppermute x7 -> x0, waiting for transfers between devices: 9.73 us -> none  [the longest x2 6.27 us: to_relay(): return lax.ppermute(x, 'lon', [(i, i ^ 2) for i in range(n_lon)])]
    ppermute x7 -> x0, starting transfers between devices: 6.19 us -> none  [the longest x2 4.3 us: to_relay(): return lax.ppermute(x, 'lon', [(i, i ^ 2) for i in range(n_lon)])]
    ppermute x4, waiting for transfers between devices: 4.15 us -> 7.54 us  [ring(): return lax.ppermute(x, axis, pairs)]
    pallas_call x17 -> x16, Pallas kernels: 37.6 us -> 36.5 us  [call(): pl.pallas_call(kernel, out_shape=outs, in_specs=specs, out_specs=out_spec...]
  transfers between devices with their start and end apart: 15 -> 9, of which waited for: 10 -> 7; matrix products, arithmetic and copies ran while one was open for 1% -> 1% of each run, Pallas kernels for 18% -> 16%
where the time goes in v5:
time: 153 us; the launch traced here: 150 us
  blocking collectives  38.6 us (25%)
  starting transfers between devices  37.1 us (24%)
  Pallas kernels  36.5 us (24%)
  waiting for transfers between devices  31.6 us (21%)
  other arithmetic  3.68 us (2%)
  between operations  2.2 us (1%)
    all_to_all x3, blocking collectives, across(): return lax.all_to_all(chunks, ('patch', 'lon'), 0, 0, tiled=True)  38.6 us
    pallas_call x16, Pallas kernels, call(): pl.pallas_call(kernel, out_shape=outs, in_specs=specs, out_specs=out_spec...  36.5 us
    all_to_all x4, waiting for transfers between devices, along(): lax.all_to_all(packed, 'lat', 0, 0, tiled=True)  24.1 us
    all_to_all x4, starting transfers between devices, along(): lax.all_to_all(packed, 'lat', 0, 0, tiled=True)  18.6 us
    ppermute x4, starting transfers between devices, ring(): return lax.ppermute(x, axis, pairs)  11 us
    all_to_all x1, starting transfers between devices, across(): return lax.all_to_all(chunks, ('patch', 'lon'), 0, 0, tiled=True)  7.63 us
    ppermute x4, waiting for transfers between devices, ring(): return lax.ppermute(x, axis, pairs)  7.54 us
  transfers between devices with their start and end apart: 9, of which 7 were waited for; matrix products, arithmetic and copies ran while one was open for 1% of the time, Pallas kernels for 16%

profile of v5, /device:TPU:2, one launch (start us, length us, event | category | flops | bytes accessed | tf_op | source)
XLA Modules:
  0.0 150.4 jit_solution(10015067078418681484)
XLA Ops:
  1.9 0.7 clamp_add_fusion
  2.6 0.1 pad_add_fusion.at
  2.7 2.3 %start.1 = (f32[32,16,128]{2,1,0:T(8,128)}, f32[17,8,128]{2,1,0:T(8,128)S(1)}, f32[17,8,128]{2,1,0:T(8,128)S(1)}, f32[8,128]{1,0:T(8,128)S(1)}) custom-call(s32[5]{0:T(128)S(1)} %pad_add_fusion.at, s32[1,128]{1,0:T(1,128)} %bitcast.54, f32[6,128,128]{2,1,0:T(8,128)} %bitcast.42, f32[2,128,128]{2,1,0:T(8,128)} %bitcast.45, f32[2,128,128]{2,1,0:T(8,128)} %bitcast.48, ...), custom_call_target="tpu_custom_call" | custom-call | tf_op jit(solution)/shard_map/start/pallas_call | solution.py:552
  4.9 7.6 %all-to-all-start = ((f32[32,16,128]{2,1,0:T(8,128)}), f32[32,16,128]{2,1,0:T(8,128)S(1)}, u32[]{:S(2)}, u32[]{:S(2)}) async-start(f32[32,16,128]{2,1,0:T(8,128)} %get-tuple-element.41), calls=%async_computation | async-start | bytes 524288 | tf_op jit(solution)/shard_map/all_to_all | solution.py:610
  12.6 3.8 %collective-permute-start = (f32[17,8,128]{2,1,0:T(8,128)S(1)}, f32[17,8,128]{2,1,0:T(8,128)S(1)}, u32[]{:S(2)}, u32[]{:S(2)}) collective-permute-start(f32[17,8,128]{2,1,0:T(8,128)S(1)} %get-tuple-element.37), channel_id=1, source_target_pairs={{0,16},{16,32},{32,48},{48,64},{64,80},{80,96},{96,112},{1,17},{17... | collective-permute-start | bytes 208904 | tf_op jit(solution)/shard_map/ppermute | solution.py:591
  16.4 1.3 collective-permute-start.1
  17.8 0.1 convert_add_fusion.2
  17.9 0.1 select_reduce_fusion.4
  18.1 0.1 and_select_fusion.2
  18.1 0.2 convert_reduce_fusion.3
  18.3 0.1 add_convert_fusion
  18.4 0.1 convert_add_fusion.1
  18.5 4.1 %collective-permute-done.1.south = f32[17,8,128]{2,1,0:T(8,128)S(1)} collective-permute-done((f32[17,8,128]{2,1,0:T(8,128)S(1)}, f32[17,8,128]{2,1,0:T(8,128)S(1)}, u32[]{:S(2)}, u32[]{:S(2)}) %collective-permute-start.1) | collective-permute-done | bytes 69664 | tf_op jit(solution)/shard_map/ppermute | solution.py:591
  22.6 0.1 convert_add_fusion
  22.7 1.6 %columns.1 = (f32[136,128]{1,0:T(8,128)S(1)}, f32[136,128]{1,0:T(8,128)S(1)}) custom-call(f32[6,128,128]{2,1,0:T(8,128)} %bitcast.43, f32[2,128,128]{2,1,0:T(8,128)} %bitcast.46, f32[2,128,128]{2,1,0:T(8,128)} %bitcast.49, f32[2,128,128]{2,1,0:T(8,128)} %bitcast.52, f32[8,128,128]{2,1,0:T(8,128)} %bitcast.39, f32[17,8,128]{2,1,0:T(8,128)S(1)} %collective-permute-done.north, ...), custom_call_target="tpu_custom_call" | custom-call | tf_op jit(solution)/shard_map/columns/pallas_call | solution.py:552
  24.3 3.4 %collective-permute-start.2 = (f32[136,128]{1,0:T(8,128)S(1)}, f32[136,128]{1,0:T(8,128)S(1)}, u32[]{:S(2)}, u32[]{:S(2)}) collective-permute-start(f32[136,128]{1,0:T(8,128)S(1)} %get-tuple-element.39), channel_id=1, source_target_pairs={{0,1},{1,2},{2,3},{3,4},{4,5},{5,6},{6,7},{7,8},{8,9},{9,10},{10,1... | collective-permute-start | bytes 208904 | tf_op jit(solution)/shard_map/ppermute | solution.py:591
  27.7 2.5 %collective-permute-start.3 = (f32[136,128]{1,0:T(8,128)S(1)}, f32[136,128]{1,0:T(8,128)S(1)}, u32[]{:S(2)}, u32[]{:S(2)}) collective-permute-start(f32[136,128]{1,0:T(8,128)S(1)} %get-tuple-element.40), channel_id=1, source_target_pairs={{1,0},{2,1},{3,2},{4,3},{5,4},{6,5},{7,6},{8,7},{9,8},{10,9},{11,1... | collective-permute-start | bytes 208904 | tf_op jit(solution)/shard_map/ppermute | solution.py:591
  30.2 0.1 select_reduce_fusion.2
  30.4 0.2 collective-permute-done.2.west
  30.6 0.1 fusion.3
  30.7 3.3 %collective-permute-done.3.east = f32[136,128]{1,0:T(8,128)S(1)} collective-permute-done((f32[136,128]{1,0:T(8,128)S(1)}, f32[136,128]{1,0:T(8,128)S(1)}, u32[]{:S(2)}, u32[]{:S(2)}) %collective-permute-start.3) | collective-permute-done | bytes 69664 | tf_op jit(solution)/shard_map/ppermute | solution.py:591
  33.9 0.1 fusion.2
  34.0 0.1 concatenate.71
  34.1 0.1 select_reduce_fusion.5
  34.3 0.1 concatenate.70
  34.4 0.2 convert_reduce_fusion.2
  34.6 0.0 all-to-all-done.arrived
  34.6 0.4 add_reduce_fusion
  35.0 0.3 convert_reduce_fusion
  35.4 0.1 select_reduce_fusion.1
  35.6 0.1 copy.14
  35.6 0.1 add.169
  35.7 0.2 select_reduce_fusion
  36.0 0.1 add.165.table
  36.0 0.1 pad_add_fusion.2.table
  36.1 1.3 pack.4
  37.4 8.3 %all-to-all-start.1 = ((f32[8,9,8,128]{3,2,1,0:T(8,128)}), f32[8,9,8,128]{3,2,1,0:T(8,128)S(1)}, u32[]{:S(2)}, u32[]{:S(2)}) async-start(f32[8,9,8,128]{3,2,1,0:T(8,128)} %pack.4), calls=%async_computation.1 | async-start | bytes 589824 | tf_op jit(solution)/shard_map/all_to_all | solution.py:622
  45.8 0.1 fusion.16
  45.8 0.1 fusion.10
  45.9 0.1 concatenate.74.ints
  46.0 0.1 concatenate.75.ints
  46.1 4.2 %build.1 = (f32[8,2,144,128]{3,2,1,0:T(8,128)}, f32[8,2,2,144,128]{4,3,2,1,0:T(8,128)}, f32[2,2,144,128]{3,2,1,0:T(8,128)}, f32[4,8,128]{2,1,0:T(8,128)S(1)}, f3...) custom-call(s32[30]{0:T(128)S(1)} %concatenate.74.ints, ...), custom_call_target="tpu_custom_call" | custom-call | tf_op jit(solution)/shard_map/build/pallas_call | solution.py:552
  50.3 6.3 %all-to-all-done.1 = f32[8,9,8,128]{3,2,1,0:T(8,128)S(1)} async-done(((f32[8,9,8,128]{3,2,1,0:T(8,128)}), f32[8,9,8,128]{3,2,1,0:T(8,128)S(1)}, u32[]{:S(2)}, u32[]{:S(2)}) %all-to-all-start.1) | async-done | bytes 294944 | tf_op jit(solution)/shard_map/all_to_all | solution.py:622
  56.6 0.8 blend.3
  57.4 15.3 %all_to_all.40.arrived = f32[32,8,128]{2,1,0:T(8,128)S(1)} all-to-all(f32[32,8,128]{2,1,0:T(8,128)S(1)} %get-tuple-element.52), channel_id=1, replica_groups=mesh['patch'=2,'lat'=8,'lon'=16] {'patch','lon'}, dimensions={0} | all-to-all | bytes 262144 | tf_op jit(solution)/shard_map/all_to_all | solution.py:610
  72.8 1.3 pack.5
  74.1 3.4 %all-to-all-start.3 = ((f32[8,8,8,128]{3,2,1,0:T(8,128)}), f32[8,8,8,128]{3,2,1,0:T(8,128)S(1)}, u32[]{:S(2)}, u32[]{:S(2)}) async-start(f32[8,8,8,128]{3,2,1,0:T(8,128)} %pack.5), calls=%async_computation.3 | async-start | bytes 524288 | tf_op jit(solution)/shard_map/all_to_all | solution.py:622
  77.5 4.3 %sweep.3 = (f32[8,2,144,128]{3,2,1,0:T(8,128)}, f32[4,8,128]{2,1,0:T(8,128)S(1)}) custom-call(s32[30]{0:T(128)S(1)} %concatenate.74.ints, f32[8,2,144,128]{3,2,1,0:T(8,128)} %get-tuple-element.42.fields, f32[8,2,2,144,128]{4,3,2,1,0:T(8,128)} %get-tuple-element.43.coef, f32[8,256]{1,0:T(8,128)S(1)} %get-tuple-element.48.lat_ghost, ...), custom_call_target="tpu_custom_call" | custom-call | tf_op jit(solution)/shard_map/sweep/pallas_call | solution.py:552
  81.8 7.9 %all-to-all-done.3 = f32[8,8,8,128]{3,2,1,0:T(8,128)S(1)} async-done(((f32[8,8,8,128]{3,2,1,0:T(8,128)}), f32[8,8,8,128]{3,2,1,0:T(8,128)S(1)}, u32[]{:S(2)}, u32[]{:S(2)}) %all-to-all-start.3) | async-done | bytes 262176 | tf_op jit(solution)/shard_map/all_to_all | solution.py:622
  89.7 0.8 blend.4
  90.5 11.6 %all_to_all.41.arrived = f32[32,8,128]{2,1,0:T(8,128)S(1)} all-to-all(f32[32,8,128]{2,1,0:T(8,128)S(1)} %get-tuple-element.56), channel_id=1, replica_groups=mesh['patch'=2,'lat'=8,'lon'=16] {'patch','lon'}, dimensions={0} | all-to-all | bytes 262144 | tf_op jit(solution)/shard_map/all_to_all | solution.py:610
  102.2 1.3 pack.6
  103.5 3.4 %all-to-all-start.5 = ((f32[8,8,8,128]{3,2,1,0:T(8,128)}), f32[8,8,8,128]{3,2,1,0:T(8,128)S(1)}, u32[]{:S(2)}, u32[]{:S(2)}) async-start(f32[8,8,8,128]{3,2,1,0:T(8,128)} %pack.6), calls=%async_computation.5 | async-start | bytes 524288 | tf_op jit(solution)/shard_map/all_to_all | solution.py:622
  106.9 4.3 %sweep.4 = (f32[8,2,144,128]{3,2,1,0:T(8,128)}, f32[4,8,128]{2,1,0:T(8,128)S(1)}) custom-call(s32[30]{0:T(128)S(1)} %concatenate.74.ints, f32[8,2,144,128]{3,2,1,0:T(8,128)} %get-tuple-element.50.fields, f32[8,2,2,144,128]{4,3,2,1,0:T(8,128)} %get-tuple-element.43.coef, f32[8,256]{1,0:T(8,128)S(1)} %get-tuple-element.53.lat_ghost, ...), custom_call_target="tpu_custom_call" | custom-call | tf_op jit(solution)/shard_map/sweep/pallas_call | solution.py:552
  111.2 7.9 %all-to-all-done.5 = f32[8,8,8,128]{3,2,1,0:T(8,128)S(1)} async-done(((f32[8,8,8,128]{3,2,1,0:T(8,128)}), f32[8,8,8,128]{3,2,1,0:T(8,128)S(1)}, u32[]{:S(2)}, u32[]{:S(2)}) %all-to-all-start.5) | async-done | bytes 262176 | tf_op jit(solution)/shard_map/all_to_all | solution.py:622
  119.0 0.8 blend.5
  119.9 11.6 %all_to_all.42.arrived = f32[32,8,128]{2,1,0:T(8,128)S(1)} all-to-all(f32[32,8,128]{2,1,0:T(8,128)S(1)} %get-tuple-element.57), channel_id=1, replica_groups=mesh['patch'=2,'lat'=8,'lon'=16] {'patch','lon'}, dimensions={0} | all-to-all | bytes 262144 | tf_op jit(solution)/shard_map/all_to_all | solution.py:610
  131.5 1.3 pack.7
  132.8 3.4 %all-to-all-start.7 = ((f32[8,8,8,128]{3,2,1,0:T(8,128)}), f32[8,8,8,128]{3,2,1,0:T(8,128)S(1)}, u32[]{:S(2)}, u32[]{:S(2)}) async-start(f32[8,8,8,128]{3,2,1,0:T(8,128)} %pack.7), calls=%async_computation.7 | async-start | bytes 524288 | tf_op jit(solution)/shard_map/all_to_all | solution.py:622
  136.2 2.0 %heat.1.warm = f32[2,2,144,128]{3,2,1,0:T(8,128)S(1)} custom-call(s32[30]{0:T(128)S(1)} %concatenate.74.ints, f32[2,2,144,128]{3,2,1,0:T(8,128)} %get-tuple-element.65.warm, f32[72,8,128]{2,1,0:T(8,128)S(1)} %bitcast.34, f32[8,128,128]{2,1,0:T(8,128)} %bitcast.41), custom_call_target="tpu_custom_call" | custom-call | tf_op jit(solution)/shard_map/heat/pallas_call | solution.py:552
  138.3 4.9 %sweep.5 = (f32[8,2,144,128]{3,2,1,0:T(8,128)}, f32[4,8,128]{2,1,0:T(8,128)}) custom-call(s32[30]{0:T(128)S(1)} %concatenate.74.ints, f32[8,2,144,128]{3,2,1,0:T(8,128)} %get-tuple-element.58.fields, f32[8,2,2,144,128]{4,3,2,1,0:T(8,128)} %get-tuple-element.43.coef, f32[8,256]{1,0:T(8,128)S(1)} %get-tuple-element.59.lat_ghost, ...), custom_call_target="tpu_custom_call" | custom-call | tf_op jit(solution)/shard_map/sweep/pallas_call | solution.py:552
  143.2 3.2 %ahead.1 = (f32[8,128,128]{2,1,0:T(8,128)S(1)}, f32[3,2,128,128]{3,2,1,0:T(8,128)S(1)}, f32[2,3,2,8,128]{4,3,2,1,0:T(8,128)S(1)}) custom-call(s32[30]{0:T(128)S(1)} %concatenate.74.ints, f32[8,2,144,128]{3,2,1,0:T(8,128)} %get-tuple-element.61.fields, f32[8,2,2,144,128]{4,3,2,1,0:T(8,128)} %get-tuple-element.43.coef), custom_call_target="tpu_custom_call" | custom-call | tf_op jit(solution)/shard_map/ahead/pallas_call | solution.py:552
  146.4 2.0 %all-to-all-done.7 = f32[8,8,8,128]{3,2,1,0:T(8,128)S(1)} async-done(((f32[8,8,8,128]{3,2,1,0:T(8,128)}), f32[8,8,8,128]{3,2,1,0:T(8,128)S(1)}, u32[]{:S(2)}, u32[]{:S(2)}) %all-to-all-start.7) | async-done | bytes 262176 | tf_op jit(solution)/shard_map/all_to_all | solution.py:622
  148.4 1.9 %final.1 = (f32[6,128,128]{2,1,0:T(8,128)}, f32[2,128,128]{2,1,0:T(8,128)}, f32[2,128,128]{2,1,0:T(8,128)}) custom-call(s32[30]{0:T(128)S(1)} %concatenate.74.ints, f32[64,8,128]{2,1,0:T(8,128)S(1)} %bitcast.35, bf16[2,256,256]{2,1,0:T(8,128)(2,1)S(1)} %get-tuple-element.46.high, bf16[2,256,256]{2,1,0:T(8,128)(2,1)S(1)} %get-tuple-element.47.low, ...), custom_call_target="tpu_custom_call" | custom-call | tf_op jit(solution)/shard_map/final/pallas_call | solution.py:552
  (17 shorter events, 0.1 us)
Async XLA Ops:
  4.9 29.7 %all-to-all-start = ((f32[32,16,128]{2,1,0:T(8,128)}), f32[32,16,128]{2,1,0:T(8,128)S(1)}, u32[]{:S(2)}, u32[]{:S(2)}) async-start(f32[32,16,128]{2,1,0:T(8,128)} %get-tuple-element.41), calls=%async_computation | async-start | bytes 524288 | tf_op jit(solution)/shard_map/all_to_all | solution.py:610
  12.6 5.8 %collective-permute-start = (f32[17,8,128]{2,1,0:T(8,128)S(1)}, f32[17,8,128]{2,1,0:T(8,128)S(1)}, u32[]{:S(2)}, u32[]{:S(2)}) collective-permute-start(f32[17,8,128]{2,1,0:T(8,128)S(1)} %get-tuple-element.37), channel_id=1, source_target_pairs={{0,16},{16,32},{32,48},{48,64},{64,80},{80,96},{96,112},{1,17},{17... | collective-permute-start | bytes 208904 | tf_op jit(solution)/shard_map/ppermute | solution.py:591
  16.4 6.2 %collective-permute-start.1 = (f32[17,8,128]{2,1,0:T(8,128)S(1)}, f32[17,8,128]{2,1,0:T(8,128)S(1)}, u32[]{:S(2)}, u32[]{:S(2)}) collective-permute-start(f32[17,8,128]{2,1,0:T(8,128)S(1)} %get-tuple-element.38), channel_id=1, source_target_pairs={{16,0},{32,16},{48,32},{64,48},{80,64},{96,80},{112,96},{17,1},{33... | collective-permute-start | bytes 208904 | tf_op jit(solution)/shard_map/ppermute | solution.py:591
  24.3 6.2 %collective-permute-start.2 = (f32[136,128]{1,0:T(8,128)S(1)}, f32[136,128]{1,0:T(8,128)S(1)}, u32[]{:S(2)}, u32[]{:S(2)}) collective-permute-start(f32[136,128]{1,0:T(8,128)S(1)} %get-tuple-element.39), channel_id=1, source_target_pairs={{0,1},{1,2},{2,3},{3,4},{4,5},{5,6},{6,7},{7,8},{8,9},{9,10},{10,1... | collective-permute-start | bytes 208904 | tf_op jit(solution)/shard_map/ppermute | solution.py:591
  27.7 6.2 %collective-permute-start.3 = (f32[136,128]{1,0:T(8,128)S(1)}, f32[136,128]{1,0:T(8,128)S(1)}, u32[]{:S(2)}, u32[]{:S(2)}) collective-permute-start(f32[136,128]{1,0:T(8,128)S(1)} %get-tuple-element.40), channel_id=1, source_target_pairs={{1,0},{2,1},{3,2},{4,3},{5,4},{6,5},{7,6},{8,7},{9,8},{10,9},{11,1... | collective-permute-start | bytes 208904 | tf_op jit(solution)/shard_map/ppermute | solution.py:591
  37.4 19.2 %all-to-all-start.1 = ((f32[8,9,8,128]{3,2,1,0:T(8,128)}), f32[8,9,8,128]{3,2,1,0:T(8,128)S(1)}, u32[]{:S(2)}, u32[]{:S(2)}) async-start(f32[8,9,8,128]{3,2,1,0:T(8,128)} %pack.4), calls=%async_computation.1 | async-start | bytes 589824 | tf_op jit(solution)/shard_map/all_to_all | solution.py:622
  74.1 15.6 %all-to-all-start.3 = ((f32[8,8,8,128]{3,2,1,0:T(8,128)}), f32[8,8,8,128]{3,2,1,0:T(8,128)S(1)}, u32[]{:S(2)}, u32[]{:S(2)}) async-start(f32[8,8,8,128]{3,2,1,0:T(8,128)} %pack.5), calls=%async_computation.3 | async-start | bytes 524288 | tf_op jit(solution)/shard_map/all_to_all | solution.py:622
  103.5 15.6 %all-to-all-start.5 = ((f32[8,8,8,128]{3,2,1,0:T(8,128)}), f32[8,8,8,128]{3,2,1,0:T(8,128)S(1)}, u32[]{:S(2)}, u32[]{:S(2)}) async-start(f32[8,8,8,128]{3,2,1,0:T(8,128)} %pack.6), calls=%async_computation.5 | async-start | bytes 524288 | tf_op jit(solution)/shard_map/all_to_all | solution.py:622
  132.8 15.6 %all-to-all-start.7 = ((f32[8,8,8,128]{3,2,1,0:T(8,128)}), f32[8,8,8,128]{3,2,1,0:T(8,128)S(1)}, u32[]{:S(2)}, u32[]{:S(2)}) async-start(f32[8,8,8,128]{3,2,1,0:T(8,128)} %pack.7), calls=%async_computation.7 | async-start | bytes 524288 | tf_op jit(solution)/shard_map/all_to_all | solution.py:622

commit v6 on v1

v6 whole, which is shorter than its diff:
```python
import jax
import jax.numpy as jnp
from jax import lax
from jax.experimental import pallas as pl
from jax.experimental.pallas import tpu as pltpu
from jax.sharding import PartitionSpec as P

SWEEPS = 4
CELLS = 128
TILES = 16
PLANES = 12
SLOTS = 4
F32 = jnp.float32
VMEM = pl.BlockSpec(memory_space=pltpu.VMEM)
SMEM = pl.BlockSpec(memory_space=pltpu.SMEM)
HBM = pl.BlockSpec(memory_space=pltpu.HBM)
ROW, NORTH, SOUTH, WEST, EAST, LAT_BASE, LON_BASE = range(7)
CHUNK, TO_WEST, TO_EAST = 7, 8, 9
FROM_NORTH, FROM_SOUTH = 10, 11
BLOCKS, RANKS = 12, 16


def lanes():
    return lax.broadcasted_iota(jnp.int32, (8, CELLS), 1)


def sublanes():
    return lax.broadcasted_iota(jnp.int32, (8, CELLS), 0)


def turn(x, shift):
    shift = shift % CELLS
    return x if shift == 0 else pltpu.roll(x, shift, 1)


def tile(b):
    return pl.ds(8 * b, 8)


class Copies:
    def __init__(self, sems):
        self.sems, self.going = sems, []

    def start(self, source, target):
        copy = pltpu.make_async_copy(source, target, self.sems.at[len(self.going)])
        copy.start()
        self.going.append(copy)

    def wait(self, first=0, last=None):
        for copy in self.going[first:last]:
            copy.wait()


def own_lanes(f):
    return 2 * f, (2 * f - 1) % CELLS


def gather_edge(block, f, gathered):
    west, east = own_lanes(f)
    lane = lanes()
    return jnp.where((lane == west) | (lane == east), turn(block, 2 * f), gathered)


def ghost_columns(west, east, rows_s, cols_s):
    rows_s[...] = jnp.zeros((CELLS, CELLS), F32)
    for f, (w, e) in enumerate(zip(west, east)):
        to_w, to_e = own_lanes(f)
        rows_s[to_w : to_w + 1, :] = w
        rows_s[to_e : to_e + 1, :] = e
    cols_s[...] = rows_s[...].T


def around(ref, b, north, south, column, f):
    here = ref[tile(b), :]
    sub, lane = sublanes(), lanes()
    if b == 0:
        up = jnp.where(sub == 0, north, pltpu.roll(here, 1, 0))
    else:
        up = ref[8 * b - 1 : 8 * b + 7, :]
    if b == TILES - 1:
        down = jnp.where(sub == 7, south, pltpu.roll(here, 7, 0))
    else:
        down = ref[8 * b + 1 : 8 * b + 9, :]
    turned = turn(column, -2 * f)
    left = jnp.where(lane == 0, turned, pltpu.roll(here, 1, 1))
    right = jnp.where(lane == CELLS - 1, turned, pltpu.roll(here, CELLS - 1, 1))
    return here, up, down, left, right


def start_kernel(
    ints, slots, flow, pressure, heat, friction,
    chunks, north, south, places, own, named, row, cols_s, rows_s, sems,
):
    copies = Copies(sems)
    copies.start(slots, named)
    copies.start(flow, own.at[0:6])
    copies.start(pressure, own.at[6:8])
    copies.start(heat, own.at[8:10])
    copies.start(friction, own.at[10:12])
    row[8:16, :] = jnp.broadcast_to((ints[4] + 1).astype(F32), (8, CELLS))
    chunks[...] = jnp.zeros(chunks.shape, F32)
    north[...] = jnp.zeros(north.shape, F32)
    south[...] = jnp.zeros(south.shape, F32)
    copies.wait()
    mine = jnp.broadcast_to(named[...], (8, CELLS)) == sublanes()
    place = jnp.sum(jnp.where(mine, lanes() + 1, 0).astype(F32), axis=1, keepdims=True)
    places[...] = jnp.broadcast_to(place, (8, CELLS))
    for f in range(10):
        to = f if f < 8 else f + 1
        row[to : to + 1, :] = own[f, pl.ds(ints[0], 1), :]
    for b in range(TILES):
        gathered = jnp.zeros((8, CELLS), F32)
        for f in range(PLANES):
            gathered = gather_edge(own[f, tile(b), :], f, gathered)
        cols_s[tile(b), :] = gathered
    rows_s[...] = cols_s[...].T
    chunks[ints[1]] = row[...]
    for f in range(PLANES):
        west, east = own_lanes(f)
        chunks[ints[2], f : f + 1, :] = rows_s[west : west + 1, :]
        chunks[ints[3], f : f + 1, :] = rows_s[east : east + 1, :]
        n, at = divmod(f, 8)
        north[n, at : at + 1, :] = own[f, 0:1, :]
        south[n, at : at + 1, :] = own[f, CELLS - 1 : CELLS, :]


def pack_kernel(table, arrived, north, south, out):
    lats, count = out.shape[0], out.shape[1]
    halos = north.shape[0]
    for lat in range(lats):
        for n in range(SLOTS):
            block = table[2 + SLOTS * lat + n]
            out[lat, n] = arrived[block, 0:8, :]
            if count > SLOTS + 1:
                out[lat, count - 1, 2 * n : 2 * n + 2, :] = arrived[block, 9:11, :]
        for n in range(halos):
            out[lat, SLOTS + n] = jnp.zeros((8, CELLS), F32)
    for n in range(halos):
        out[table[0], SLOTS + n] = north[n]
        out[table[1], SLOTS + n] = south[n]


def split(x):
    high = x.astype(jnp.bfloat16)
    return high, (x - high.astype(F32)).astype(jnp.bfloat16)


def times(left, right):
    return lax.dot_general(left, right, (((1,), (1,)), ((), ())), preferred_element_type=F32)


def weights_kernel(ints, weights, high, low, chosen, sems):
    copies = Copies(sems)
    copies.start(weights.at[pl.ds(ints[LAT_BASE], 2)], chosen.at[0:2])
    copies.start(weights.at[pl.ds(ints[LON_BASE], 2)], chosen.at[2:4])
    copies.wait()
    for side in range(2):
        for term in range(2):
            cut = slice(term * CELLS, (term + 1) * CELLS)
            high[side, :, cut], low[side, :, cut] = split(chosen[2 * side + term])


def blend(ints, blocks_of, high, low, ghosts):
    for n, (first, last) in enumerate(((NORTH, SOUTH), (WEST, EAST))):
        ghosts[n] = jnp.zeros((8, CELLS), F32)

        @pl.when(ints[first] + ints[last] > 0)
        def _():
            block = jnp.concatenate([blocks_of(2 * n + t) for t in range(2)], axis=1)
            b_high, b_low = split(block)
            both = times(jnp.concatenate([b_high, b_low], axis=0), high[n])
            ghosts[n] = both[0:8] + both[8:16] + times(b_high, low[n])


def row_block(ints, arrived, slots):
    return lambda n: arrived[ints[BLOCKS + n], ints[RANKS + n]]


def edge_ghosts(ints, arrived, chunks, ghosts, slot, rows):
    halos = (
        arrived[ints[FROM_NORTH], slot],
        arrived[ints[FROM_SOUTH], slot],
        chunks[ints[TO_WEST], rows, :],
        chunks[ints[TO_EAST], rows, :],
    )
    flags = (ints[NORTH], ints[SOUTH], ints[WEST], ints[EAST])
    return [
        jnp.where(flag > 0, ghosts[n // 2], halo) for n, (flag, halo) in enumerate(zip(flags, halos))
    ]


def coefficient_kernel(ints, friction, heat, arrived, chunks, out, halos, cols_s, rows_s):
    slot = SLOTS + 1
    halos[0] = arrived[ints[FROM_NORTH], slot]
    halos[1] = arrived[ints[FROM_SOUTH], slot]
    lane, sub = lanes(), sublanes()
    west = [chunks[ints[TO_WEST], 10 + k : 11 + k, :] for k in range(2)]
    east = [chunks[ints[TO_EAST], 10 + k : 11 + k, :] for k in range(2)]
    ghost_columns(west, east, rows_s, cols_s)
    at_north, at_south = ints[NORTH] > 0, ints[SOUTH] > 0
    at_west, at_east = ints[WEST] > 0, ints[EAST] > 0
    for b in range(TILES):
        centre = [friction[k, tile(b), :] for k in range(2)]
        for k in range(2):
            north, south = halos[0, 2 + k : 3 + k, :], halos[1, 2 + k : 3 + k, :]
            here, up, down, left, right = around(
                friction.at[k], b, north, south, cols_s[tile(b), :], k
            )
            if b == 0:
                up = jnp.where((sub == 0) & at_north, here, up)
            if b == TILES - 1:
                down = jnp.where((sub == 7) & at_south, here, down)
            left = jnp.where((lane == 0) & at_west, here, left)
            right = jnp.where((lane == CELLS - 1) & at_east, here, right)
            faces = [0.5 * (here + other) for other in (up, down, left, right)]
            between = 0.5 * (centre[0] + centre[1])
            diagonal = (faces[0] + faces[1]) + (faces[2] + faces[3]) + (between + here)
            inverse = 0.8 / diagonal
            for n, face in enumerate(faces):
                out[n, k, tile(b), :] = inverse * face
            out[4, k, tile(b), :] = inverse * between
            out[5, k, tile(b), :] = 0.5 * inverse
            out[6, k, tile(b), :] = inverse * heat[k, tile(b), :]
            out[7, k, tile(b), :] = 0.125 * here


def relaxed(planes, coef, ghosts, column, b):
    at = [
        around(planes(f), b, ghosts[0, f : f + 1, :], ghosts[1, f : f + 1, :], column, f)
        for f in range(8)
    ]

    def factor(n, k):
        return coef[n, k, tile(b), :]

    new = []
    for component in range(3):
        for k in range(2):
            here, up, down, left, right = at[2 * component + k]
            value = 0.2 * here + factor(0, k) * up + factor(1, k) * down
            value = value + factor(2, k) * left + factor(3, k) * right
            value = value + factor(4, k) * at[2 * component + 1 - k][0]
            if component == 0:
                value = value + factor(6, k)
                slope = at[7][0] if k == 0 else -at[6][0]
            elif component == 1:
                slope = at[6 + k][2] - at[6 + k][1]
            else:
                slope = at[6 + k][4] - at[6 + k][3]
            new.append(value - factor(5, k) * slope)
    for k in range(2):
        divergence = (at[2 + k][2] - at[2 + k][1]) + (at[4 + k][4] - at[4 + k][3])
        divergence = divergence + at[1][0] if k == 0 else divergence - at[0][0]
        new.append(at[6 + k][0] - factor(7, k) * divergence)
    return new


def fill_ghosts(ints, arrived, chunks, high, low, sides, ghosts, cols_s, rows_s):
    blend(ints, row_block(ints, arrived, SLOTS), high, low, sides)
    found = edge_ghosts(ints, arrived, chunks, sides, SLOTS, slice(0, 8))
    for n in range(4):
        ghosts[n] = found[n]
    west = [ghosts[2, f : f + 1, :] for f in range(8)]
    east = [ghosts[3, f : f + 1, :] for f in range(8)]
    ghost_columns(west, east, rows_s, cols_s)


def sweep_kernel(
    ints, flow, pressure, coef, arrived, chunks_in, high, low,
    flow_out, pressure_out, chunks, north, south, sides, ghosts, cols_s, rows_s, edge_s,
):
    def planes(f):
        return flow.at[f] if f < 6 else pressure.at[f - 6]

    def planes_out(f):
        return flow_out.at[f] if f < 6 else pressure_out.at[f - 6]

    fill_ghosts(ints, arrived, chunks_in, high, low, sides, ghosts, cols_s, rows_s)
    chunks[...] = jnp.zeros(chunks.shape, F32)
    for b in range(TILES):
        new = relaxed(planes, coef, ghosts, cols_s[tile(b), :], b)
        gathered = jnp.zeros((8, CELLS), F32)
        for f in range(8):
            planes_out(f)[tile(b), :] = new[f]
            gathered = gather_edge(new[f], f, gathered)
            if b == 0:
                north[0, f : f + 1, :] = new[f][0:1, :]
            if b == TILES - 1:
                south[0, f : f + 1, :] = new[f][7:8, :]
        edge_s[tile(b), :] = gathered
    rows_s[...] = edge_s[...].T
    for f in range(8):
        west, east = own_lanes(f)
        chunks[ints[TO_WEST], f : f + 1, :] = rows_s[west : west + 1, :]
        chunks[ints[TO_EAST], f : f + 1, :] = rows_s[east : east + 1, :]
    for f in range(8):
        chunks[ints[CHUNK], f : f + 1, :] = planes_out(f)[pl.ds(ints[ROW], 1), :]


def heat_kernel(ints, heat, arrived, chunks, high, low, out, ghosts_out, block, sides):
    out[...] = heat[...]
    block[...] = jnp.zeros((4, 8, CELLS), F32)
    last = SLOTS + 2
    for n in range(4):
        for k in range(2):
            line = arrived[ints[BLOCKS + n], last, pl.ds(2 * ints[RANKS + n] + k, 1), :]
            block[n, k : k + 1, :] = line
    blend(ints, lambda n: block[n], high, low, sides)
    found = edge_ghosts(ints, arrived, chunks, sides, SLOTS + 1, slice(8, 16))
    for n in range(4):
        ghosts_out[n] = found[n]


def final_kernel(
    ints, flow, pressure, coef, arrived, chunks_in, high, low, heat, heat_ghosts,
    flow_out, pressure_out, heat_out, sides, ghosts, cols_s, rows_s, heat_cols_s,
):
    def planes(f):
        return flow.at[f] if f < 6 else pressure.at[f - 6]

    west = [heat_ghosts[2, k : k + 1, :] for k in range(2)]
    east = [heat_ghosts[3, k : k + 1, :] for k in range(2)]
    ghost_columns(west, east, rows_s, heat_cols_s)
    fill_ghosts(ints, arrived, chunks_in, high, low, sides, ghosts, cols_s, rows_s)
    for b in range(TILES):
        new = relaxed(planes, coef, ghosts, cols_s[tile(b), :], b)
        for f in range(6):
            flow_out[f, tile(b), :] = new[f]
        for k in range(2):
            pressure_out[k, tile(b), :] = new[6 + k]
        layers = [
            around(
                heat.at[k],
                b,
                heat_ghosts[0, k : k + 1, :],
                heat_ghosts[1, k : k + 1, :],
                heat_cols_s[tile(b), :],
                k,
            )
            for k in range(2)
        ]
        for k in range(2):
            here, up, down, left, right = layers[k]
            under = jnp.ones((8, CELLS), F32) if k == 0 else layers[0][0]
            over = layers[1][0] if k == 0 else jnp.zeros((8, CELLS), F32)
            advect = jnp.zeros((8, CELLS), F32)
            for component, minus, plus in ((0, under, over), (1, up, down), (2, left, right)):
                speed = new[2 * component + k]
                advect = advect + jnp.maximum(speed, 0.0) * (here - minus)
                advect = advect + jnp.minimum(speed, 0.0) * (plus - here)
            spread = (up + down) + (left + right) + (under + over) - 6.0 * here
            heat_out[k, tile(b), :] = here + 0.1 * (spread - advect)


def shape(*dims):
    return jax.ShapeDtypeStruct(dims, F32)


def scratch(*dims):
    return pltpu.VMEM(dims, F32)


def semaphores(count):
    return pltpu.SemaphoreType.DMA((count,))


def call(kernel, outs, ins, scratches, name, specs=None, limit=4, keep=()):
    specs = specs or [SMEM] + [VMEM] * (len(ins) - 1)
    placed = []
    for n, (x, spec) in enumerate(zip(ins, specs)):
        if spec is HBM or n in keep:
            x = pltpu.with_memory_space_constraint(x, spec.memory_space)
        placed.append(x)
    return pl.pallas_call(
        kernel,
        out_shape=outs,
        in_specs=specs,
        out_specs=[VMEM] * len(outs),
        scratch_shapes=scratches,
        compiler_params=pltpu.CompilerParams(vmem_limit_bytes=limit * 1024 * 1024),
        name=name,
    )(*placed)


def shards(
    flow_vector,
    normal_stress,
    thermal_field,
    shear_resistance,
    departing_bands,
    receiving_processor,
    shift_filled_by_lane,
    blending_factors,
):
    flow = flow_vector.reshape(6, CELLS, CELLS)
    pressure = normal_stress[0]
    heat = thermal_field[0]
    friction = shear_resistance[0]
    weights = blending_factors.reshape(8, CELLS, CELLS)
    lat, lon = lax.axis_index("lat"), lax.axis_index("lon")
    n_lat, n_lon = lax.axis_size("lat"), lax.axis_size("lon")
    patch = lax.axis_index("patch")
    own_row = departing_bands.reshape(1)
    receiver = receiving_processor.reshape(1)
    other = (1 - patch) * n_lon

    chunk = other + jnp.maximum(receiver, 0) % n_lon
    beside = patch * n_lon + jnp.clip(lon + jnp.array([-1, 1], jnp.int32), 0, n_lon - 1)
    beyond = jnp.clip(lat + jnp.array([-1, 1], jnp.int32), 0, n_lat - 1)
    first = jnp.concatenate([own_row, chunk, beside, receiver])

    square = scratch(CELLS, CELLS)
    tiles = 2 * n_lon
    chunks, north, south, places = call(
        start_kernel,
        [shape(tiles, 16, CELLS), shape(2, 8, CELLS), shape(2, 8, CELLS), shape(8, CELLS)],
        (first, shift_filled_by_lane.reshape(1, CELLS), flow, pressure, heat, friction),
        [scratch(PLANES, CELLS, CELLS), pltpu.VMEM((1, CELLS), jnp.int32), scratch(16, CELLS)]
        + [square, square, semaphores(5)],
        "start",
        specs=[SMEM] + [HBM] * 5,
    )

    def across(chunks):
        return lax.all_to_all(chunks, ("patch", "lon"), 0, 0, tiled=True)

    def along(table, blocks, north, south, count):
        (packed,) = call(
            pack_kernel,
            [shape(n_lat, count, 8, CELLS)],
            (table, blocks, north, south),
            [],
            "pack",
            keep=(1,),
        )
        return lax.all_to_all(packed, "lat", 0, 0, tiled=True)

    came = across(chunks)
    sent_to = lax.dynamic_slice(came, (other, 8, 0), (n_lon, 1, 1)).reshape(n_lon)
    sent_to = sent_to.astype(jnp.int32) - 1
    every_lat = jnp.arange(n_lat, dtype=jnp.int32)[:, None]
    wanted = sent_to[None] == every_lat * n_lon + lon
    order = jnp.arange(n_lon, dtype=jnp.int32)
    earlier = wanted[:, None, :] & (order[None, None, :] < order[None, :, None])
    rank = jnp.sum(earlier.astype(jnp.int32), axis=2)
    mine = wanted[:, None, :] & (rank[:, None, :] == jnp.arange(SLOTS)[None, :, None])
    found = jnp.sum(jnp.where(mine, order[None, None, :], 0), axis=2).reshape(-1)
    table = jnp.concatenate([beyond, other + found]).astype(jnp.int32)
    arrived = along(table, came, north, south, SLOTS + 3)

    on_edge = jnp.stack([lat == 0, lat == n_lat - 1, lon == 0, lon == n_lon - 1]).astype(jnp.int32)
    own = places[:, 0].astype(jnp.int32) - 1
    pick = jnp.concatenate(
        [jnp.where(lat > 0, own[2:4], own[0:2]), jnp.where(lon > 0, own[6:8], own[4:6])]
    )
    same = (own >= 0)[None] & (own[None] // n_lon == pick[:, None] // n_lon)
    slot = jnp.sum((same & (own[None] < pick[:, None])).astype(jnp.int32), axis=1)
    bases = jnp.stack([jnp.where(lat > 0, 2, 0), jnp.where(lon > 0, 6, 4)]).astype(jnp.int32)
    ints = [own_row, on_edge, bases, chunk, beside, beyond]
    ints += [jnp.maximum(pick, 0) // n_lon, jnp.minimum(slot, SLOTS - 1)]
    ints = jnp.concatenate(ints).astype(jnp.int32)

    joined = jax.ShapeDtypeStruct((2, CELLS, 2 * CELLS), jnp.bfloat16)
    high, low = call(
        weights_kernel,
        [joined, joined],
        (ints, weights),
        [scratch(4, CELLS, CELLS), semaphores(2)],
        "weights",
        specs=[SMEM, HBM],
    )
    (coef,) = call(
        coefficient_kernel,
        [shape(8, 2, CELLS, CELLS)],
        (ints, friction, heat, arrived, came),
        [scratch(2, 8, CELLS), square, square],
        "coefficients",
        keep=(3, 4),
    )
    sides, ghosts = scratch(2, 8, CELLS), scratch(4, 8, CELLS)
    state = [shape(6, CELLS, CELLS), shape(2, CELLS, CELLS)]
    for sweep in range(SWEEPS - 1):
        if sweep == 0:
            warm, warm_ghosts = call(
                heat_kernel,
                [shape(2, CELLS, CELLS), shape(4, 8, CELLS)],
                (ints, heat, arrived, came, high, low),
                [scratch(4, 8, CELLS), sides],
                "heat",
                keep=(2, 3, 4, 5),
            )
        flow, pressure, chunks, north, south = call(
            sweep_kernel,
            state + [shape(tiles, 8, CELLS), shape(1, 8, CELLS), shape(1, 8, CELLS)],
            (ints, flow, pressure, coef, arrived, came, high, low),
            [sides, ghosts, square, square, square],
            "sweep",
            limit=8,
            keep=(3, 4, 5, 6, 7),
        )
        came = across(chunks)
        arrived = along(table, came, north, south, SLOTS + 1)
    flow, pressure, heat = call(
        final_kernel,
        state + [shape(2, CELLS, CELLS)],
        (ints, flow, pressure, coef, arrived, came, high, low, warm, warm_ghosts),
        [sides, ghosts, square, square, square],
        "final",
        limit=8,
        keep=(1, 2, 3, 4, 5, 6, 7, 8, 9),
    )
    return flow.reshape(3, 1, 2, CELLS, CELLS), pressure[None], heat[None]


def solution(mesh):
    placed = (
        P(None, "patch", None, "lat", "lon"),
        P("patch", None, "lat", "lon"),
        P("patch", None, "lat", "lon"),
        P("patch", None, "lat", "lon"),
        P("patch", "lat", "lon", None),
        P("patch", "lat", "lon", None),
        P("patch", "lat", "lon", None),
        P("patch", "lat", "lon", None, None, None),
    )
    return jax.shard_map(
        shards,
        mesh=mesh,
        in_specs=placed,
        out_specs=(
            P(None, "patch", None, "lat", "lon"),
            P("patch", None, "lat", "lon"),
            P("patch", None, "lat", "lon"),
        ),
        check_vma=False,
    )
```

time: 166 us -> 129 us (0.78)
  starting transfers between devices: 87.3 us -> 19.5 us
  blocking collectives: 0 us -> 60.3 us
  waiting for transfers between devices: 52.1 us -> 25.5 us
  local copies, waits for them, and re-layouts: 8.78 us -> 0.91 us
  Pallas kernels: 9.82 us -> 17.6 us
  other arithmetic: 5.07 us -> 1.64 us
    all_to_all x0 -> x5, blocking collectives: none -> 60.3 us  [the longest x3 35.2 us: across(): return lax.all_to_all(chunks, ('patch', 'lon'), 0, 0, tiled=True)]
    ppermute x21 -> x0, starting transfers between devices: 43.8 us -> none  [the longest x4 13.6 us: exchange(): lax.ppermute(south, 'lat', down)]
    ppermute x21 -> x0, waiting for transfers between devices: 25.1 us -> none  [the longest x4 10.3 us: exchange(): lax.ppermute(north, 'lat', up)]
    all_to_all x4 -> x3, starting transfers between devices: 43.5 us -> 19.5 us  [the longest x2 11.8 us: along(): return lax.all_to_all(packed, 'lat', 0, 0, tiled=True)]
    unnamed x48 -> x10, local copies, waits for them, and re-layouts: 8.78 us -> 0.67 us
    pallas_call x6 -> x12, Pallas kernels: 9.82 us -> 17.6 us  [call(): pl.pallas_call(kernel, out_shape=outs, in_specs=specs, out_specs=[VMEM] *...]
    select_n x4, other arithmetic: 4.2 us -> 0.25 us  [the longest x1 0.15 us: shards(): jnp.where(lat > 0, own[2:4], own[0:2])]
    all_to_all x4 -> x3, waiting for transfers between devices: 27 us -> 25.5 us  [the longest x2 18 us: along(): return lax.all_to_all(packed, 'lat', 0, 0, tiled=True)]
  transfers between devices with their start and end apart: 25 -> 3, of which waited for: 16 -> 3; matrix products, arithmetic and copies ran while one was open for 1% -> 1% of each run, Pallas kernels for 1% -> 2%
where the time goes in v6:
time: 129 us; the launch traced here: 128 us
  blocking collectives  60.3 us (47%)
  waiting for transfers between devices  25.5 us (20%)
  starting transfers between devices  19.5 us (15%)
  Pallas kernels  17.6 us (14%)
  between operations  2.16 us (2%)
  other arithmetic  1.64 us (1%)
    all_to_all x3, blocking collectives, across(): return lax.all_to_all(chunks, ('patch', 'lon'), 0, 0, tiled=True)  35.2 us
    all_to_all x2, blocking collectives, along(): return lax.all_to_all(packed, 'lat', 0, 0, tiled=True)  25.1 us
    all_to_all x2, waiting for transfers between devices, along(): return lax.all_to_all(packed, 'lat', 0, 0, tiled=True)  18 us
    pallas_call x12, Pallas kernels, call(): pl.pallas_call(kernel, out_shape=outs, in_specs=specs, out_specs=[VMEM] *...  17.6 us
    all_to_all x2, starting transfers between devices, along(): return lax.all_to_all(packed, 'lat', 0, 0, tiled=True)  11.8 us
    all_to_all x1, starting transfers between devices, across(): return lax.all_to_all(chunks, ('patch', 'lon'), 0, 0, tiled=True)  7.63 us
    all_to_all x1, waiting for transfers between devices, across(): return lax.all_to_all(chunks, ('patch', 'lon'), 0, 0, tiled=True)  7.44 us
  transfers between devices with their start and end apart: 3, of which 3 were waited for; matrix products, arithmetic and copies ran while one was open for 1% of the time, Pallas kernels for 2%

profile of v6, /device:TPU:2, one launch (start us, length us, event | category | flops | bytes accessed | tf_op | source)
XLA Modules:
  0.0 127.6 jit_solution(8442090251136325182)
XLA Ops:
  1.9 0.0 copy-start.4
  1.9 0.6 copy-done.4
  2.6 0.1 pad_add_fusion.ints
  2.7 2.8 %start.1 = (f32[32,16,128]{2,1,0:T(8,128)}, f32[2,8,128]{2,1,0:T(8,128)S(1)}, f32[2,8,128]{2,1,0:T(8,128)S(1)}, f32[8,128]{1,0:T(8,128)S(1)}) custom-call(s32[5]{0:T(128)S(1)} %pad_add_fusion.ints, s32[1,128]{1,0:T(1,128)} %bitcast.34, f32[6,128,128]{2,1,0:T(8,128)} %bitcast.24, f32[2,128,128]{2,1,0:T(8,128)} %bitcast.29, f32[2,128,128]{2,1,0:T(8,128)} %bitcast.26, ...), custom_call_target="tpu_custom_call" | custom-call | tf_op jit(solution)/shard_map/start/pallas_call | solution.py:374
  5.5 7.6 %all-to-all-start = ((f32[32,16,128]{2,1,0:T(8,128)}), f32[32,16,128]{2,1,0:T(8,128)S(1)}, u32[]{:S(2)}, u32[]{:S(2)}) async-start(f32[32,16,128]{2,1,0:T(8,128)} %get-tuple-element.30), calls=%async_computation | async-start | bytes 524288 | tf_op jit(solution)/shard_map/all_to_all | solution.py:425
  13.1 0.1 fusion.1
  13.3 0.1 select_reduce_fusion.2
  13.4 0.1 and_select_fusion
  13.5 7.4 %all-to-all-done.arrived.chunks.chunks_in = f32[32,16,128]{2,1,0:T(8,128)S(1)} async-done(((f32[32,16,128]{2,1,0:T(8,128)}), f32[32,16,128]{2,1,0:T(8,128)S(1)}, u32[]{:S(2)}, u32[]{:S(2)}) %all-to-all-start) | async-done | bytes 262176 | tf_op jit(solution)/shard_map/all_to_all | solution.py:425
  21.0 0.4 add_reduce_fusion
  21.4 0.1 broadcast_compare_fusion
  21.4 0.2 convert_reduce_fusion
  21.7 0.1 select_reduce_fusion
  21.8 0.1 copy.15
  21.9 0.1 add.98
  22.0 0.1 pad_add_fusion.2.table
  22.1 1.3 pack.4
  23.3 8.5 %all-to-all-start.1 = ((f32[8,7,8,128]{3,2,1,0:T(8,128)}), f32[8,7,8,128]{3,2,1,0:T(8,128)S(1)}, u32[]{:S(2)}, u32[]{:S(2)}) async-start(f32[8,7,8,128]{3,2,1,0:T(8,128)} %pack.4), calls=%async_computation.1 | async-start | bytes 458752 | tf_op jit(solution)/shard_map/all_to_all | solution.py:436
  31.8 0.1 add_convert_fusion
  31.9 0.2 convert_reduce_fusion.1
  32.1 0.1 concatenate.27.ints
  32.2 0.0 copy-start.1
  32.2 0.0 copy-start.3
  32.2 1.6 %weights.1 = (bf16[2,128,256]{2,1,0:T(8,128)(2,1)S(1)}, bf16[2,128,256]{2,1,0:T(8,128)(2,1)S(1)}) custom-call(s32[20]{0:T(128)S(1)} %concatenate.27.ints, f32[8,128,128]{2,1,0:T(8,128)} %bitcast.33), custom_call_target="tpu_custom_call" | custom-call | tf_op jit(solution)/shard_map/weights/pallas_call | solution.py:374
  33.8 0.0 copy-start
  33.8 0.0 copy-start.2
  33.8 8.7 %all-to-all-done.1.arrived = f32[8,7,8,128]{3,2,1,0:T(8,128)S(1)} async-done(((f32[8,7,8,128]{3,2,1,0:T(8,128)}), f32[8,7,8,128]{3,2,1,0:T(8,128)S(1)}, u32[]{:S(2)}, u32[]{:S(2)}) %all-to-all-start.1) | async-done | bytes 229408 | tf_op jit(solution)/shard_map/all_to_all | solution.py:436
  42.5 0.0 copy-done.1
  42.5 0.0 copy-done.3
  42.5 0.8 coefficients.1.coef
  43.3 0.0 copy-done
  43.3 0.0 copy-done.2
  43.3 2.0 %sweep.3 = (f32[6,128,128]{2,1,0:T(8,128)S(1)}, f32[2,128,128]{2,1,0:T(8,128)S(1)}, f32[32,8,128]{2,1,0:T(8,128)S(1)}, f32[1,8,128]{2,1,0:T(8,128)S(1)}, f32[1,8,128]{2,1,0:T(8,128)S(1)}) custom-call(s32[20]{0:T(128)S(1)} %concatenate.27.ints, f32[6,128,128]{2,1,0:T(8,128)S(1)} %bitcast.25, f32[2,128,128]{2,1,0:T(8,128)S(1)} %bitcast.30, ...), custom_call_target="tpu_custom_call" | custom-call | tf_op jit(solution)/shard_map/sweep/pallas_call | solution.py:374
  45.3 12.1 %all_to_all.40.arrived.chunks_in = f32[32,8,128]{2,1,0:T(8,128)S(1)} all-to-all(f32[32,8,128]{2,1,0:T(8,128)S(1)} %get-tuple-element.37), channel_id=1, replica_groups=mesh['patch'=2,'lat'=8,'lon'=16] {'patch','lon'}, dimensions={0} | all-to-all | bytes 262144 | tf_op jit(solution)/shard_map/all_to_all | solution.py:425
  57.5 0.6 pack.5
  58.0 12.5 %all_to_all.41.arrived = f32[8,5,8,128]{3,2,1,0:T(8,128)S(1)} all-to-all(f32[8,5,8,128]{3,2,1,0:T(8,128)S(1)} %pack.5), channel_id=1, replica_groups=mesh['patch'=2,'lat'=8,'lon'=16] {'lat'}, dimensions={0} | all-to-all | bytes 327680 | tf_op jit(solution)/shard_map/all_to_all | solution.py:436
  70.6 2.0 %sweep.4 = (f32[6,128,128]{2,1,0:T(8,128)S(1)}, f32[2,128,128]{2,1,0:T(8,128)S(1)}, f32[32,8,128]{2,1,0:T(8,128)S(1)}, f32[1,8,128]{2,1,0:T(8,128)S(1)}, f32[1,8,128]{2,1,0:T(8,128)S(1)}) custom-call(s32[20]{0:T(128)S(1)} %concatenate.27.ints, f32[6,128,128]{2,1,0:T(8,128)S(1)} %get-tuple-element.35.flow, f32[2,128,128]{2,1,0:T(8,128)S(1)} %get-tuple-element.36.pressure, ...), custom_call_target="tpu_custom_call" | custom-call | tf_op jit(solution)/shard_map/sweep/pallas_call | solution.py:374
  72.6 11.6 %all_to_all.42.arrived.chunks_in = f32[32,8,128]{2,1,0:T(8,128)S(1)} all-to-all(f32[32,8,128]{2,1,0:T(8,128)S(1)} %get-tuple-element.42), channel_id=1, replica_groups=mesh['patch'=2,'lat'=8,'lon'=16] {'patch','lon'}, dimensions={0} | all-to-all | bytes 262144 | tf_op jit(solution)/shard_map/all_to_all | solution.py:425
  84.1 0.6 pack.6
  84.7 12.5 %all_to_all.43.arrived = f32[8,5,8,128]{3,2,1,0:T(8,128)S(1)} all-to-all(f32[8,5,8,128]{3,2,1,0:T(8,128)S(1)} %pack.6), channel_id=1, replica_groups=mesh['patch'=2,'lat'=8,'lon'=16] {'lat'}, dimensions={0} | all-to-all | bytes 327680 | tf_op jit(solution)/shard_map/all_to_all | solution.py:436
  97.3 2.0 %sweep.5 = (f32[6,128,128]{2,1,0:T(8,128)S(1)}, f32[2,128,128]{2,1,0:T(8,128)S(1)}, f32[32,8,128]{2,1,0:T(8,128)S(1)}, f32[1,8,128]{2,1,0:T(8,128)S(1)}, f32[1,8,128]{2,1,0:T(8,128)S(1)}) custom-call(s32[20]{0:T(128)S(1)} %concatenate.27.ints, f32[6,128,128]{2,1,0:T(8,128)S(1)} %get-tuple-element.40.flow, f32[2,128,128]{2,1,0:T(8,128)S(1)} %get-tuple-element.41.pressure, ...), custom_call_target="tpu_custom_call" | custom-call | tf_op jit(solution)/shard_map/sweep/pallas_call | solution.py:374
  99.3 11.5 %all_to_all.44.arrived.chunks_in = f32[32,8,128]{2,1,0:T(8,128)S(1)} all-to-all(f32[32,8,128]{2,1,0:T(8,128)S(1)} %get-tuple-element.47), channel_id=1, replica_groups=mesh['patch'=2,'lat'=8,'lon'=16] {'patch','lon'}, dimensions={0} | all-to-all | bytes 262144 | tf_op jit(solution)/shard_map/all_to_all | solution.py:425
  110.8 1.2 pack.7
  112.1 3.4 %all-to-all-start.7 = ((f32[8,5,8,128]{3,2,1,0:T(8,128)}), f32[8,5,8,128]{3,2,1,0:T(8,128)S(1)}, u32[]{:S(2)}, u32[]{:S(2)}) async-start(f32[8,5,8,128]{3,2,1,0:T(8,128)} %pack.7), calls=%async_computation.7 | async-start | bytes 327680 | tf_op jit(solution)/shard_map/all_to_all | solution.py:436
  115.5 0.7 heat.1
  116.2 9.3 %all-to-all-done.7.arrived = f32[8,5,8,128]{3,2,1,0:T(8,128)S(1)} async-done(((f32[8,5,8,128]{3,2,1,0:T(8,128)}), f32[8,5,8,128]{3,2,1,0:T(8,128)S(1)}, u32[]{:S(2)}, u32[]{:S(2)}) %all-to-all-start.7) | async-done | bytes 163872 | tf_op jit(solution)/shard_map/all_to_all | solution.py:436
  125.5 2.1 %final.1 = (f32[6,128,128]{2,1,0:T(8,128)}, f32[2,128,128]{2,1,0:T(8,128)}, f32[2,128,128]{2,1,0:T(8,128)}) custom-call(s32[20]{0:T(128)S(1)} %concatenate.27.ints, f32[6,128,128]{2,1,0:T(8,128)S(1)} %get-tuple-element.45.flow, f32[2,128,128]{2,1,0:T(8,128)S(1)} %get-tuple-element.46.pressure, f32[8,2,128,128]{3,2,1,0:T(8,128)S(1)} %coefficients.1.coef, ...), custom_call_target="tpu_custom_call" | custom-call | tf_op jit(solution)/shard_map/final/pallas_call | solution.py:374
  (7 shorter events, 0.1 us)
Async XLA Ops:
  1.9 0.7 copy-start.4
  5.5 15.5 %all-to-all-start = ((f32[32,16,128]{2,1,0:T(8,128)}), f32[32,16,128]{2,1,0:T(8,128)S(1)}, u32[]{:S(2)}, u32[]{:S(2)}) async-start(f32[32,16,128]{2,1,0:T(8,128)} %get-tuple-element.30), calls=%async_computation | async-start | bytes 524288 | tf_op jit(solution)/shard_map/all_to_all | solution.py:425
  23.3 19.1 %all-to-all-start.1 = ((f32[8,7,8,128]{3,2,1,0:T(8,128)}), f32[8,7,8,128]{3,2,1,0:T(8,128)S(1)}, u32[]{:S(2)}, u32[]{:S(2)}) async-start(f32[8,7,8,128]{3,2,1,0:T(8,128)} %pack.4), calls=%async_computation.1 | async-start | bytes 458752 | tf_op jit(solution)/shard_map/all_to_all | solution.py:436
  32.2 10.3 %copy-start.1 = (f32[1,2,128,128]{3,2,1,0:T(8,128)S(1)}, f32[1,2,128,128]{3,2,1,0:T(8,128)}, u32[]{:S(2)}) copy-start(f32[1,2,128,128]{3,2,1,0:T(8,128)} %param.12) | copy-start | bytes 393220
  32.2 10.3 %copy-start.3 = (f32[1,2,128,128]{3,2,1,0:T(8,128)S(1)}, f32[1,2,128,128]{3,2,1,0:T(8,128)}, u32[]{:S(2)}) copy-start(f32[1,2,128,128]{3,2,1,0:T(8,128)} %param.13) | copy-start | bytes 393220
  33.8 9.5 %copy-start = (f32[3,1,2,128,128]{4,3,2,1,0:T(8,128)S(1)}, f32[3,1,2,128,128]{4,3,2,1,0:T(8,128)}, u32[]{:S(2)}) copy-start(f32[3,1,2,128,128]{4,3,2,1,0:T(8,128)} %param.10) | copy-start | bytes 1179652
  33.8 9.5 %copy-start.2 = (f32[1,2,128,128]{3,2,1,0:T(8,128)S(1)}, f32[1,2,128,128]{3,2,1,0:T(8,128)}, u32[]{:S(2)}) copy-start(f32[1,2,128,128]{3,2,1,0:T(8,128)} %param.11) | copy-start | bytes 393220
  112.1 13.4 %all-to-all-start.7 = ((f32[8,5,8,128]{3,2,1,0:T(8,128)}), f32[8,5,8,128]{3,2,1,0:T(8,128)S(1)}, u32[]{:S(2)}, u32[]{:S(2)}) async-start(f32[8,5,8,128]{3,2,1,0:T(8,128)} %pack.7), calls=%async_computation.7 | async-start | bytes 327680 | tf_op jit(solution)/shard_map/all_to_all | solution.py:436

commit v7 on v6

--- a/solution.py
+++ b/solution.py
@@ -162,21 +162,18 @@
 
 def blend(ints, blocks_of, high, low, ghosts):
     for n, (first, last) in enumerate(((NORTH, SOUTH), (WEST, EAST))):
-        ghosts[n] = jnp.zeros((8, CELLS), F32)
+        count = ghosts.shape[1]
+        ghosts[n] = jnp.zeros((count, CELLS), F32)
 
         @pl.when(ints[first] + ints[last] > 0)
         def _():
             block = jnp.concatenate([blocks_of(2 * n + t) for t in range(2)], axis=1)
             b_high, b_low = split(block)
             both = times(jnp.concatenate([b_high, b_low], axis=0), high[n])
-            ghosts[n] = both[0:8] + both[8:16] + times(b_high, low[n])
-
-
-def row_block(ints, arrived, slots):
-    return lambda n: arrived[ints[BLOCKS + n], ints[RANKS + n]]
-
-
-def edge_ghosts(ints, arrived, chunks, ghosts, slot, rows):
+            ghosts[n] = both[0:count] + both[count:] + times(b_high, low[n])
+
+
+def edge_ghosts(ints, arrived, chunks, ghosts, slot, rows, of):
     halos = (
         arrived[ints[FROM_NORTH], slot],
         arrived[ints[FROM_SOUTH], slot],
@@ -185,52 +182,61 @@
     )
     flags = (ints[NORTH], ints[SOUTH], ints[WEST], ints[EAST])
     return [
-        jnp.where(flag > 0, ghosts[n // 2], halo) for n, (flag, halo) in enumerate(zip(flags, halos))
+        jnp.where(flag > 0, ghosts[n // 2, of, :], halo)
+        for n, (flag, halo) in enumerate(zip(flags, halos))
     ]
 
 
-def coefficient_kernel(ints, friction, heat, arrived, chunks, out, halos, cols_s, rows_s):
-    slot = SLOTS + 1
-    halos[0] = arrived[ints[FROM_NORTH], slot]
-    halos[1] = arrived[ints[FROM_SOUTH], slot]
+def coefficients(ints, friction, heat, north, south, column, f, b, put):
     lane, sub = lanes(), sublanes()
+    centre = [friction[k, tile(b), :] for k in range(2)]
+    for k in range(2):
+        here, up, down, left, right = around(
+            friction.at[k], b, north[k], south[k], column, f + k
+        )
+        if b == 0:
+            up = jnp.where((sub == 0) & (ints[NORTH] > 0), here, up)
+        if b == TILES - 1:
+            down = jnp.where((sub == 7) & (ints[SOUTH] > 0), here, down)
+        left = jnp.where((lane == 0) & (ints[WEST] > 0), here, left)
+        right = jnp.where((lane == CELLS - 1) & (ints[EAST] > 0), here, right)
+        faces = [0.5 * (here + other) for other in (up, down, left, right)]
+        between = 0.5 * (centre[0] + centre[1])
+        diagonal = (faces[0] + faces[1]) + (faces[2] + faces[3]) + (between + here)
+        inverse = 0.8 / diagonal
+        for n, face in enumerate(faces):
+            put(n, k, inverse * face)
+        put(4, k, inverse * between)
+        put(5, k, 0.5 * inverse)
+        put(6, k, inverse * heat[k, tile(b), :])
+        put(7, k, 0.125 * here)
+
+
+def coefficient_kernel(ints, friction, heat, chunks, out, cols_s, rows_s):
     west = [chunks[ints[TO_WEST], 10 + k : 11 + k, :] for k in range(2)]
     east = [chunks[ints[TO_EAST], 10 + k : 11 + k, :] for k in range(2)]
     ghost_columns(west, east, rows_s, cols_s)
-    at_north, at_south = ints[NORTH] > 0, ints[SOUTH] > 0
-    at_west, at_east = ints[WEST] > 0, ints[EAST] > 0
-    for b in range(TILES):
-        centre = [friction[k, tile(b), :] for k in range(2)]
-        for k in range(2):
-            north, south = halos[0, 2 + k : 3 + k, :], halos[1, 2 + k : 3 + k, :]
-            here, up, down, left, right = around(
-                friction.at[k], b, north, south, cols_s[tile(b), :], k
-            )
-            if b == 0:
-                up = jnp.where((sub == 0) & at_north, here, up)
-            if b == TILES - 1:
-                down = jnp.where((sub == 7) & at_south, here, down)
-            left = jnp.where((lane == 0) & at_west, here, left)
-            right = jnp.where((lane == CELLS - 1) & at_east, here, right)
-            faces = [0.5 * (here + other) for other in (up, down, left, right)]
-            between = 0.5 * (centre[0] + centre[1])
-            diagonal = (faces[0] + faces[1]) + (faces[2] + faces[3]) + (between + here)
-            inverse = 0.8 / diagonal
-            for n, face in enumerate(faces):
-                out[n, k, tile(b), :] = inverse * face
-            out[4, k, tile(b), :] = inverse * between
-            out[5, k, tile(b), :] = 0.5 * inverse
-            out[6, k, tile(b), :] = inverse * heat[k, tile(b), :]
-            out[7, k, tile(b), :] = 0.125 * here
-
-
-def relaxed(planes, coef, ghosts, column, b):
+    for b in range(1, TILES - 1):
+
+        def put(n, k, value):
+            out[n, k, tile(b), :] = value
+
+        coefficients(ints, friction, heat, (None, None), (None, None), cols_s[tile(b), :], 0, b, put)
+    for b in (0, TILES - 1):
+        for n in range(8):
+            for k in range(2):
+                out[n, k, tile(b), :] = jnp.zeros((8, CELLS), F32)
+
+
+def relaxed(planes, coef, ends, ghosts, column, b):
     at = [
         around(planes(f), b, ghosts[0, f : f + 1, :], ghosts[1, f : f + 1, :], column, f)
         for f in range(8)
     ]
 
     def factor(n, k):
+        if b == 0 or b == TILES - 1:
+            return ends[n, k, tile(0 if b == 0 else 1), :]
         return coef[n, k, tile(b), :]
 
     new = []
@@ -255,19 +261,69 @@
     return new
 
 
-def fill_ghosts(ints, arrived, chunks, high, low, sides, ghosts, cols_s, rows_s):
-    blend(ints, row_block(ints, arrived, SLOTS), high, low, sides)
-    found = edge_ghosts(ints, arrived, chunks, sides, SLOTS, slice(0, 8))
+def fill_ghosts(ints, arrived, chunks, high, low, sides, ghosts, cols_s, rows_s, others=()):
+    count = sides.shape[1]
+
+    def block(n):
+        rows = arrived[ints[BLOCKS + n], ints[RANKS + n]]
+        if count == 8:
+            return rows
+        warm = [
+            arrived[ints[BLOCKS + n], SLOTS + 2, pl.ds(2 * ints[RANKS + n] + k, 1), :]
+            for k in range(2)
+        ]
+        return jnp.concatenate([rows, *warm, jnp.zeros((6, CELLS), F32)], axis=0)
+
+    blend(ints, block, high, low, sides)
+    found = edge_ghosts(ints, arrived, chunks, sides, SLOTS, slice(0, 8), slice(0, 8))
     for n in range(4):
         ghosts[n] = found[n]
     west = [ghosts[2, f : f + 1, :] for f in range(8)]
     east = [ghosts[3, f : f + 1, :] for f in range(8)]
-    ghost_columns(west, east, rows_s, cols_s)
+    ghost_columns(west + [w for w, _ in others], east + [e for _, e in others], rows_s, cols_s)
+
+
+def first_kernel(
+    ints, flow, pressure, coef, friction, heat, arrived, chunks_in, high, low,
+    flow_out, pressure_out, chunks, north, south, ends, heat_ghosts,
+    sides, ghosts, cols_s, rows_s, edge_s, halos,
+):
+    others = [
+        [chunks_in[ints[at], 10 + k : 11 + k, :] for at in (TO_WEST, TO_EAST)] for k in range(2)
+    ]
+    fill_ghosts(ints, arrived, chunks_in, high, low, sides, ghosts, cols_s, rows_s, others)
+    found = edge_ghosts(ints, arrived, chunks_in, sides, SLOTS + 1, slice(8, 16), slice(8, 16))
+    for n in range(4):
+        heat_ghosts[n] = found[n]
+    halos[0] = arrived[ints[FROM_NORTH], SLOTS + 1]
+    halos[1] = arrived[ints[FROM_SOUTH], SLOTS + 1]
+    for end, b in enumerate((0, TILES - 1)):
+
+        def put(n, k, value):
+            ends[n, k, tile(end), :] = value
+
+        lines = [[halos[side, 2 + k : 3 + k, :] for k in range(2)] for side in range(2)]
+        coefficients(ints, friction, heat, *lines, cols_s[tile(b), :], 8, b, put)
+    sweep(
+        ints, flow, pressure, coef, ends, ghosts, cols_s, rows_s, edge_s,
+        flow_out, pressure_out, chunks, north, south,
+    )
 
 
 def sweep_kernel(
-    ints, flow, pressure, coef, arrived, chunks_in, high, low,
+    ints, flow, pressure, coef, ends, arrived, chunks_in, high, low,
     flow_out, pressure_out, chunks, north, south, sides, ghosts, cols_s, rows_s, edge_s,
+):
+    fill_ghosts(ints, arrived, chunks_in, high, low, sides, ghosts, cols_s, rows_s)
+    sweep(
+        ints, flow, pressure, coef, ends, ghosts, cols_s, rows_s, edge_s,
+        flow_out, pressure_out, chunks, north, south,
+    )
+
+
+def sweep(
+    ints, flow, pressure, coef, ends, ghosts, cols_s, rows_s, edge_s,
+    flow_out, pressure_out, chunks, north, south,
 ):
     def planes(f):
         return flow.at[f] if f < 6 else pressure.at[f - 6]
@@ -275,10 +331,9 @@
     def planes_out(f):
         return flow_out.at[f] if f < 6 else pressure_out.at[f - 6]
 
-    fill_ghosts(ints, arrived, chunks_in, high, low, sides, ghosts, cols_s, rows_s)
     chunks[...] = jnp.zeros(chunks.shape, F32)
     for b in range(TILES):
-        new = relaxed(planes, coef, ghosts, cols_s[tile(b), :], b)
+        new = relaxed(planes, coef, ends, ghosts, cols_s[tile(b), :], b)
         gathered = jnp.zeros((8, CELLS), F32)
         for f in range(8):
             planes_out(f)[tile(b), :] = new[f]
@@ -297,22 +352,8 @@
         chunks[ints[CHUNK], f : f + 1, :] = planes_out(f)[pl.ds(ints[ROW], 1), :]
 
 
-def heat_kernel(ints, heat, arrived, chunks, high, low, out, ghosts_out, block, sides):
-    out[...] = heat[...]
-    block[...] = jnp.zeros((4, 8, CELLS), F32)
-    last = SLOTS + 2
-    for n in range(4):
-        for k in range(2):
-            line = arrived[ints[BLOCKS + n], last, pl.ds(2 * ints[RANKS + n] + k, 1), :]
-            block[n, k : k + 1, :] = line
-    blend(ints, lambda n: block[n], high, low, sides)
-    found = edge_ghosts(ints, arrived, chunks, sides, SLOTS + 1, slice(8, 16))
-    for n in range(4):
-        ghosts_out[n] = found[n]
-
-
 def final_kernel(
-    ints, flow, pressure, coef, arrived, chunks_in, high, low, heat, heat_ghosts,
+    ints, flow, pressure, coef, ends, arrived, chunks_in, high, low, heat, heat_ghosts,
     flow_out, pressure_out, heat_out, sides, ghosts, cols_s, rows_s, heat_cols_s,
 ):
     def planes(f):
@@ -323,7 +364,7 @@
     ghost_columns(west, east, rows_s, heat_cols_s)
     fill_ghosts(ints, arrived, chunks_in, high, low, sides, ghosts, cols_s, rows_s)
     for b in range(TILES):
-        new = relaxed(planes, coef, ghosts, cols_s[tile(b), :], b)
+        new = relaxed(planes, coef, ends, ghosts, cols_s[tile(b), :], b)
         for f in range(6):
             flow_out[f, tile(b), :] = new[f]
         for k in range(2):
@@ -364,13 +405,14 @@
     return pltpu.SemaphoreType.DMA((count,))
 
 
-def call(kernel, outs, ins, scratches, name, specs=None, limit=4, keep=()):
+def call(kernel, outs, ins, scratches, name, specs=None, limit=4, keep=(), pin=()):
     specs = specs or [SMEM] + [VMEM] * (len(ins) - 1)
     placed = []
     for n, (x, spec) in enumerate(zip(ins, specs)):
         if spec is HBM or n in keep:
             x = pltpu.with_memory_space_constraint(x, spec.memory_space)
         placed.append(x)
+    outs = [pltpu.VMEM(x.shape, x.dtype) if n in pin else x for n, x in enumerate(outs)]
     return pl.pallas_call(
         kernel,
         out_shape=outs,
@@ -405,8 +447,10 @@
     other = (1 - patch) * n_lon
 
     chunk = other + jnp.maximum(receiver, 0) % n_lon
-    beside = patch * n_lon + jnp.clip(lon + jnp.array([-1, 1], jnp.int32), 0, n_lon - 1)
-    beyond = jnp.clip(lat + jnp.array([-1, 1], jnp.int32), 0, n_lat - 1)
+    beside = jnp.stack([jnp.maximum(lon - 1, 0), jnp.minimum(lon + 1, n_lon - 1)])
+    beside = (beside + patch * n_lon).astype(jnp.int32)
+    beyond = jnp.stack([jnp.maximum(lat - 1, 0), jnp.minimum(lat + 1, n_lat - 1)])
+    beyond = beyond.astype(jnp.int32)
     first = jnp.concatenate([own_row, chunk, beside, receiver])
 
     square = scratch(CELLS, CELLS)
@@ -419,6 +463,7 @@
         + [square, square, semaphores(5)],
         "start",
         specs=[SMEM] + [HBM] * 5,
+        pin=(0,),
     )
 
     def across(chunks):
@@ -432,6 +477,7 @@
             [],
             "pack",
             keep=(1,),
+            pin=(0,),
         )
         return lax.all_to_all(packed, "lat", 0, 0, tiled=True)
 
@@ -472,42 +518,47 @@
     (coef,) = call(
         coefficient_kernel,
         [shape(8, 2, CELLS, CELLS)],
-        (ints, friction, heat, arrived, came),
-        [scratch(2, 8, CELLS), square, square],
+        (ints, friction, heat, came),
+        [square, square],
         "coefficients",
-        keep=(3, 4),
+        keep=(3,),
     )
     sides, ghosts = scratch(2, 8, CELLS), scratch(4, 8, CELLS)
     state = [shape(6, CELLS, CELLS), shape(2, CELLS, CELLS)]
     for sweep in range(SWEEPS - 1):
+        outs = state + [shape(tiles, 8, CELLS), shape(1, 8, CELLS), shape(1, 8, CELLS)]
         if sweep == 0:
-            warm, warm_ghosts = call(
-                heat_kernel,
-                [shape(2, CELLS, CELLS), shape(4, 8, CELLS)],
-                (ints, heat, arrived, came, high, low),
-                [scratch(4, 8, CELLS), sides],
-                "heat",
-                keep=(2, 3, 4, 5),
+            flow, pressure, chunks, north, south, ends, heat_ghosts = call(
+                first_kernel,
+                outs + [shape(8, 2, 16, CELLS), shape(4, 8, CELLS)],
+                (ints, flow, pressure, coef, friction, heat, arrived, came, high, low),
+                [scratch(2, 16, CELLS), ghosts, square, square, square, scratch(2, 8, CELLS)],
+                "first_sweep",
+                limit=8,
+                keep=(3, 6, 7, 8, 9),
+                pin=(2,),
             )
-        flow, pressure, chunks, north, south = call(
-            sweep_kernel,
-            state + [shape(tiles, 8, CELLS), shape(1, 8, CELLS), shape(1, 8, CELLS)],
-            (ints, flow, pressure, coef, arrived, came, high, low),
-            [sides, ghosts, square, square, square],
-            "sweep",
-            limit=8,
-            keep=(3, 4, 5, 6, 7),
-        )
+        else:
+            flow, pressure, chunks, north, south = call(
+                sweep_kernel,
+                outs,
+                (ints, flow, pressure, coef, ends, arrived, came, high, low),
+                [sides, ghosts, square, square, square],
+                "sweep",
+                limit=8,
+                keep=(3, 4, 5, 6, 7, 8),
+                pin=(2,),
+            )
         came = across(chunks)
         arrived = along(table, came, north, south, SLOTS + 1)
     flow, pressure, heat = call(
         final_kernel,
         state + [shape(2, CELLS, CELLS)],
-        (ints, flow, pressure, coef, arrived, came, high, low, warm, warm_ghosts),
+        (ints, flow, pressure, coef, ends, arrived, came, high, low, heat, heat_ghosts),
         [sides, ghosts, square, square, square],
         "final",
         limit=8,
-        keep=(1, 2, 3, 4, 5, 6, 7, 8, 9),
+        keep=(1, 2, 3, 4, 5, 6, 7, 8),
     )
     return flow.reshape(3, 1, 2, CELLS, CELLS), pressure[None], heat[None]
 

time: 129 us -> 126 us (0.977)
  blocking collectives: 60.3 us -> 72.8 us
  waiting for transfers between devices: 25.5 us -> 15.3 us
  starting transfers between devices: 19.5 us -> 16.1 us
  Pallas kernels: 17.6 us -> 16.3 us
    all_to_all x2 -> x3, blocking collectives: 25.1 us -> 37.6 us  [along(): return lax.all_to_all(packed, 'lat', 0, 0, tiled=True)]
    all_to_all x2 -> x1, waiting for transfers between devices: 18 us -> 7.86 us  [along(): return lax.all_to_all(packed, 'lat', 0, 0, tiled=True)]
    all_to_all x2 -> x1, starting transfers between devices: 11.8 us -> 8.47 us  [along(): return lax.all_to_all(packed, 'lat', 0, 0, tiled=True)]
    pallas_call x12 -> x11, Pallas kernels: 17.6 us -> 16.3 us  [call(): pl.pallas_call(kernel, out_shape=outs, in_specs=specs, out_specs=[VMEM] *...]
  transfers between devices with their start and end apart: 3 -> 2, of which waited for: 3 -> 2; matrix products, arithmetic and copies ran while one was open for 1% -> 1% of each run, Pallas kernels for 2% -> 2%
where the time goes in v7:
time: 126 us; the launch traced here: 125 us
  blocking collectives  72.8 us (58%)
  Pallas kernels  16.3 us (13%)
  starting transfers between devices  16.1 us (13%)
  waiting for transfers between devices  15.3 us (12%)
  between operations  2.15 us (2%)
  other arithmetic  1.72 us (1%)
    all_to_all x3, blocking collectives, along(): return lax.all_to_all(packed, 'lat', 0, 0, tiled=True)  37.6 us
    all_to_all x3, blocking collectives, across(): return lax.all_to_all(chunks, ('patch', 'lon'), 0, 0, tiled=True)  35.2 us
    pallas_call x11, Pallas kernels, call(): pl.pallas_call(kernel, out_shape=outs, in_specs=specs, out_specs=[VMEM] *...  16.3 us
    all_to_all x1, starting transfers between devices, along(): return lax.all_to_all(packed, 'lat', 0, 0, tiled=True)  8.47 us
    all_to_all x1, waiting for transfers between devices, along(): return lax.all_to_all(packed, 'lat', 0, 0, tiled=True)  7.86 us
    all_to_all x1, starting transfers between devices, across(): return lax.all_to_all(chunks, ('patch', 'lon'), 0, 0, tiled=True)  7.63 us
    all_to_all x1, waiting for transfers between devices, across(): return lax.all_to_all(chunks, ('patch', 'lon'), 0, 0, tiled=True)  7.43 us
  transfers between devices with their start and end apart: 2, of which 2 were waited for; matrix products, arithmetic and copies ran while one was open for 1% of the time, Pallas kernels for 2%

profile of v7, /device:TPU:2, one launch (start us, length us, event | category | flops | bytes accessed | tf_op | source)
XLA Modules:
  0.0 124.7 jit_solution(2086285539144543266)
XLA Ops:
  1.9 0.1 add_add_fusion
  2.0 0.1 pad_add_fusion.ints
  2.1 2.8 %start.1 = (f32[32,16,128]{2,1,0:T(8,128)}, f32[2,8,128]{2,1,0:T(8,128)S(1)}, f32[2,8,128]{2,1,0:T(8,128)S(1)}, f32[8,128]{1,0:T(8,128)S(1)}) custom-call(s32[5]{0:T(128)S(1)} %pad_add_fusion.ints, s32[1,128]{1,0:T(1,128)} %bitcast.40, f32[6,128,128]{2,1,0:T(8,128)} %bitcast.32, f32[2,128,128]{2,1,0:T(8,128)} %bitcast.37, f32[2,128,128]{2,1,0:T(8,128)} %bitcast.28, ...), custom_call_target="tpu_custom_call" | custom-call | tf_op jit(solution)/shard_map/start/pallas_call | solution.py:416
  4.9 7.6 %all-to-all-start = ((f32[32,16,128]{2,1,0:T(8,128)}), f32[32,16,128]{2,1,0:T(8,128)S(1)}, u32[]{:S(2)}, u32[]{:S(2)}) async-start(f32[32,16,128]{2,1,0:T(8,128)} %get-tuple-element.30), calls=%async_computation | async-start | bytes 524288 | tf_op jit(solution)/shard_map/all_to_all | solution.py:470
  12.6 0.1 fusion.1
  12.7 0.1 select_reduce_fusion.2
  12.8 0.1 and_select_fusion
  13.0 7.4 %all-to-all-done.chunks.arrived.chunks_in = f32[32,16,128]{2,1,0:T(8,128)S(1)} async-done(((f32[32,16,128]{2,1,0:T(8,128)}), f32[32,16,128]{2,1,0:T(8,128)S(1)}, u32[]{:S(2)}, u32[]{:S(2)}) %all-to-all-start) | async-done | bytes 262176 | tf_op jit(solution)/shard_map/all_to_all | solution.py:470
  20.4 0.4 add_reduce_fusion
  20.8 0.1 broadcast_compare_fusion
  20.9 0.2 convert_reduce_fusion
  21.1 0.1 select_reduce_fusion
  21.2 0.1 copy.13
  21.3 0.1 add.92
  21.4 0.1 pad_add_fusion.2.table
  21.5 1.3 %pack.4 = f32[8,7,8,128]{3,2,1,0:T(8,128)} custom-call(s32[34]{0:T(128)S(1)} %pad_add_fusion.2.table, f32[32,16,128]{2,1,0:T(8,128)S(1)} %all-to-all-done.chunks.arrived.chunks_in, f32[2,8,128]{2,1,0:T(8,128)S(1)} %get-tuple-element.31.north, f32[2,8,128]{2,1,0:T(8,128)S(1)} %get-tuple-element.32.south), custom_call_target="tpu_custom_call" | custom-call | tf_op jit(solution)/shard_map/pack/pallas_call | solution.py:416
  22.8 8.5 %all-to-all-start.1 = ((f32[8,7,8,128]{3,2,1,0:T(8,128)}), f32[8,7,8,128]{3,2,1,0:T(8,128)S(1)}, u32[]{:S(2)}, u32[]{:S(2)}) async-start(f32[8,7,8,128]{3,2,1,0:T(8,128)} %pack.4), calls=%async_computation.1 | async-start | bytes 458752 | tf_op jit(solution)/shard_map/all_to_all | solution.py:482
  31.2 0.1 add_convert_fusion
  31.3 0.2 convert_reduce_fusion.1
  31.5 0.1 concatenate.29.ints
  31.6 0.0 copy-start
  31.6 0.0 copy-start.2
  31.6 1.6 %weights.1 = (bf16[2,128,256]{2,1,0:T(8,128)(2,1)S(1)}, bf16[2,128,256]{2,1,0:T(8,128)(2,1)S(1)}) custom-call(s32[20]{0:T(128)S(1)} %concatenate.29.ints, f32[8,128,128]{2,1,0:T(8,128)} %bitcast.39), custom_call_target="tpu_custom_call" | custom-call | tf_op jit(solution)/shard_map/weights/pallas_call | solution.py:416
  33.2 0.0 copy-done
  33.2 0.0 copy-done.2
  33.2 0.0 copy-start.1
  33.2 0.0 copy-start.3
  33.2 0.8 coefficients.1.coef
  34.0 7.9 %all-to-all-done.1.arrived = f32[8,7,8,128]{3,2,1,0:T(8,128)S(1)} async-done(((f32[8,7,8,128]{3,2,1,0:T(8,128)}), f32[8,7,8,128]{3,2,1,0:T(8,128)S(1)}, u32[]{:S(2)}, u32[]{:S(2)}) %all-to-all-start.1) | async-done | bytes 229408 | tf_op jit(solution)/shard_map/all_to_all | solution.py:482
  41.9 0.0 copy-done.1
  41.9 0.0 copy-done.3
  41.9 2.0 %first_sweep.1 = (f32[6,128,128]{2,1,0:T(8,128)S(1)}, f32[2,128,128]{2,1,0:T(8,128)S(1)}, f32[32,8,128]{2,1,0:T(8,128)S(1)}, f32[1,8,128]{2,1,0:T(8,128)S(1)}, f...) custom-call(s32[20]{0:T(128)S(1)} %concatenate.29.ints, ...), custom_call_target="tpu_custom_call" | custom-call | tf_op jit(solution)/shard_map/first_sweep/pallas_call | solution.py:416
  44.0 12.1 %all_to_all.40.arrived.chunks_in = f32[32,8,128]{2,1,0:T(8,128)S(1)} all-to-all(f32[32,8,128]{2,1,0:T(8,128)S(1)} %get-tuple-element.38), channel_id=1, replica_groups=mesh['patch'=2,'lat'=8,'lon'=16] {'patch','lon'}, dimensions={0} | all-to-all | bytes 262144 | tf_op jit(solution)/shard_map/all_to_all | solution.py:470
  56.1 0.6 pack.5
  56.7 12.5 %all_to_all.41.arrived = f32[8,5,8,128]{3,2,1,0:T(8,128)S(1)} all-to-all(f32[8,5,8,128]{3,2,1,0:T(8,128)S(1)} %pack.5), channel_id=1, replica_groups=mesh['patch'=2,'lat'=8,'lon'=16] {'lat'}, dimensions={0} | all-to-all | bytes 327680 | tf_op jit(solution)/shard_map/all_to_all | solution.py:482
  69.2 2.0 %sweep.2 = (f32[6,128,128]{2,1,0:T(8,128)S(1)}, f32[2,128,128]{2,1,0:T(8,128)S(1)}, f32[32,8,128]{2,1,0:T(8,128)S(1)}, f32[1,8,128]{2,1,0:T(8,128)S(1)}, f32[1,8,128]{2,1,0:T(8,128)S(1)}) custom-call(s32[20]{0:T(128)S(1)} %concatenate.29.ints, f32[6,128,128]{2,1,0:T(8,128)S(1)} %get-tuple-element.35.flow, f32[2,128,128]{2,1,0:T(8,128)S(1)} %get-tuple-element.36.pressure, ...), custom_call_target="tpu_custom_call" | custom-call | tf_op jit(solution)/shard_map/sweep/pallas_call | solution.py:416
  71.2 11.6 %all_to_all.42.arrived.chunks_in = f32[32,8,128]{2,1,0:T(8,128)S(1)} all-to-all(f32[32,8,128]{2,1,0:T(8,128)S(1)} %get-tuple-element.43), channel_id=1, replica_groups=mesh['patch'=2,'lat'=8,'lon'=16] {'patch','lon'}, dimensions={0} | all-to-all | bytes 262144 | tf_op jit(solution)/shard_map/all_to_all | solution.py:470
  82.8 0.6 pack.6
  83.4 12.5 %all_to_all.43.arrived = f32[8,5,8,128]{3,2,1,0:T(8,128)S(1)} all-to-all(f32[8,5,8,128]{3,2,1,0:T(8,128)S(1)} %pack.6), channel_id=1, replica_groups=mesh['patch'=2,'lat'=8,'lon'=16] {'lat'}, dimensions={0} | all-to-all | bytes 327680 | tf_op jit(solution)/shard_map/all_to_all | solution.py:482
  95.9 2.0 %sweep.3 = (f32[6,128,128]{2,1,0:T(8,128)S(1)}, f32[2,128,128]{2,1,0:T(8,128)S(1)}, f32[32,8,128]{2,1,0:T(8,128)S(1)}, f32[1,8,128]{2,1,0:T(8,128)S(1)}, f32[1,8,128]{2,1,0:T(8,128)S(1)}) custom-call(s32[20]{0:T(128)S(1)} %concatenate.29.ints, f32[6,128,128]{2,1,0:T(8,128)S(1)} %get-tuple-element.41.flow, f32[2,128,128]{2,1,0:T(8,128)S(1)} %get-tuple-element.42.pressure, ...), custom_call_target="tpu_custom_call" | custom-call | tf_op jit(solution)/shard_map/sweep/pallas_call | solution.py:416
  97.9 11.6 %all_to_all.44.arrived.chunks_in = f32[32,8,128]{2,1,0:T(8,128)S(1)} all-to-all(f32[32,8,128]{2,1,0:T(8,128)S(1)} %get-tuple-element.48), channel_id=1, replica_groups=mesh['patch'=2,'lat'=8,'lon'=16] {'patch','lon'}, dimensions={0} | all-to-all | bytes 262144 | tf_op jit(solution)/shard_map/all_to_all | solution.py:470
  109.5 0.6 pack.7
  110.1 12.5 %all_to_all.45.arrived = f32[8,5,8,128]{3,2,1,0:T(8,128)S(1)} all-to-all(f32[8,5,8,128]{3,2,1,0:T(8,128)S(1)} %pack.7), channel_id=1, replica_groups=mesh['patch'=2,'lat'=8,'lon'=16] {'lat'}, dimensions={0} | all-to-all | bytes 327680 | tf_op jit(solution)/shard_map/all_to_all | solution.py:482
  122.6 2.1 %final.1 = (f32[6,128,128]{2,1,0:T(8,128)}, f32[2,128,128]{2,1,0:T(8,128)}, f32[2,128,128]{2,1,0:T(8,128)}) custom-call(s32[20]{0:T(128)S(1)} %concatenate.29.ints, f32[6,128,128]{2,1,0:T(8,128)S(1)} %get-tuple-element.46.flow, f32[2,128,128]{2,1,0:T(8,128)S(1)} %get-tuple-element.47.pressure, f32[8,2,128,128]{3,2,1,0:T(8,128)S(1)} %coefficients.1.coef, ...), custom_call_target="tpu_custom_call" | custom-call | tf_op jit(solution)/shard_map/final/pallas_call | solution.py:416
  (6 shorter events, 0.0 us)
Async XLA Ops:
  4.9 15.5 %all-to-all-start = ((f32[32,16,128]{2,1,0:T(8,128)}), f32[32,16,128]{2,1,0:T(8,128)S(1)}, u32[]{:S(2)}, u32[]{:S(2)}) async-start(f32[32,16,128]{2,1,0:T(8,128)} %get-tuple-element.30), calls=%async_computation | async-start | bytes 524288 | tf_op jit(solution)/shard_map/all_to_all | solution.py:470
  22.8 19.1 %all-to-all-start.1 = ((f32[8,7,8,128]{3,2,1,0:T(8,128)}), f32[8,7,8,128]{3,2,1,0:T(8,128)S(1)}, u32[]{:S(2)}, u32[]{:S(2)}) async-start(f32[8,7,8,128]{3,2,1,0:T(8,128)} %pack.4), calls=%async_computation.1 | async-start | bytes 458752 | tf_op jit(solution)/shard_map/all_to_all | solution.py:482
  31.6 1.6 %copy-start = (f32[1,2,128,128]{3,2,1,0:T(8,128)S(1)}, f32[1,2,128,128]{3,2,1,0:T(8,128)}, u32[]{:S(2)}) copy-start(f32[1,2,128,128]{3,2,1,0:T(8,128)} %param.10) | copy-start | bytes 393220
  31.6 1.6 %copy-start.2 = (f32[1,2,128,128]{3,2,1,0:T(8,128)S(1)}, f32[1,2,128,128]{3,2,1,0:T(8,128)}, u32[]{:S(2)}) copy-start(f32[1,2,128,128]{3,2,1,0:T(8,128)} %param.11) | copy-start | bytes 393220
  33.2 8.7 %copy-start.1 = (f32[3,1,2,128,128]{4,3,2,1,0:T(8,128)S(1)}, f32[3,1,2,128,128]{4,3,2,1,0:T(8,128)}, u32[]{:S(2)}) copy-start(f32[3,1,2,128,128]{4,3,2,1,0:T(8,128)} %param.8) | copy-start | bytes 1179652
  33.2 8.7 %copy-start.3 = (f32[1,2,128,128]{3,2,1,0:T(8,128)S(1)}, f32[1,2,128,128]{3,2,1,0:T(8,128)}, u32[]{:S(2)}) copy-start(f32[1,2,128,128]{3,2,1,0:T(8,128)} %param.9) | copy-start | bytes 393220

commit v8 on v7

--- a/solution.py
+++ b/solution.py
@@ -17,7 +17,8 @@
 ROW, NORTH, SOUTH, WEST, EAST, LAT_BASE, LON_BASE = range(7)
 CHUNK, TO_WEST, TO_EAST = 7, 8, 9
 FROM_NORTH, FROM_SOUTH = 10, 11
-BLOCKS, RANKS = 12, 16
+OTHER, LON = 12, 13
+BLOCKS, RANKS = 14, 18
 
 
 def lanes():
@@ -51,22 +52,18 @@
             copy.wait()
 
 
-def own_lanes(f):
-    return 2 * f, (2 * f - 1) % CELLS
-
-
 def gather_edge(block, f, gathered):
-    west, east = own_lanes(f)
     lane = lanes()
-    return jnp.where((lane == west) | (lane == east), turn(block, 2 * f), gathered)
-
-
-def ghost_columns(west, east, rows_s, cols_s):
-    rows_s[...] = jnp.zeros((CELLS, CELLS), F32)
-    for f, (w, e) in enumerate(zip(west, east)):
-        to_w, to_e = own_lanes(f)
-        rows_s[to_w : to_w + 1, :] = w
-        rows_s[to_e : to_e + 1, :] = e
+    return jnp.where(lane // 2 == f, turn(block, 2 * f + 1), gathered)
+
+
+def every_second(first, count=8):
+    return pl.ds(first, count, stride=2)
+
+
+def ghost_columns(west, east, rows_s, cols_s, first=0):
+    rows_s[every_second(2 * first + 1), :] = west
+    rows_s[every_second(2 * first), :] = east
     cols_s[...] = rows_s[...].T
 
 
@@ -81,7 +78,7 @@
         down = jnp.where(sub == 7, south, pltpu.roll(here, 7, 0))
     else:
         down = ref[8 * b + 1 : 8 * b + 9, :]
-    turned = turn(column, -2 * f)
+    turned = turn(column, -2 * f - 1)
     left = jnp.where(lane == 0, turned, pltpu.roll(here, 1, 1))
     right = jnp.where(lane == CELLS - 1, turned, pltpu.roll(here, CELLS - 1, 1))
     return here, up, down, left, right
@@ -115,29 +112,39 @@
         cols_s[tile(b), :] = gathered
     rows_s[...] = cols_s[...].T
     chunks[ints[1]] = row[...]
+    chunks[ints[2]] = rows_s[every_second(1, 16), :]
+    chunks[ints[3]] = rows_s[every_second(0, 16), :]
     for f in range(PLANES):
-        west, east = own_lanes(f)
-        chunks[ints[2], f : f + 1, :] = rows_s[west : west + 1, :]
-        chunks[ints[3], f : f + 1, :] = rows_s[east : east + 1, :]
         n, at = divmod(f, 8)
         north[n, at : at + 1, :] = own[f, 0:1, :]
         south[n, at : at + 1, :] = own[f, CELLS - 1 : CELLS, :]
 
 
-def pack_kernel(table, arrived, north, south, out):
+def pack_kernel(ints, sent_to, arrived, north, south, out, filled):
     lats, count = out.shape[0], out.shape[1]
+    sources = sent_to.shape[0]
     halos = north.shape[0]
+    out[...] = jnp.zeros(out.shape, F32)
     for lat in range(lats):
-        for n in range(SLOTS):
-            block = table[2 + SLOTS * lat + n]
-            out[lat, n] = arrived[block, 0:8, :]
+        filled[lat] = 0
+    for n in range(sources):
+        number = sent_to[n]
+        lat = jnp.maximum(number, 0) // sources
+
+        @pl.when((number >= 0) & (number == lat * sources + ints[LON]))
+        def _():
+            slot = filled[lat]
+            filled[lat] = slot + 1
+            block = ints[OTHER] + n
+            out[lat, slot] = arrived[block, 0:8, :]
             if count > SLOTS + 1:
-                out[lat, count - 1, 2 * n : 2 * n + 2, :] = arrived[block, 9:11, :]
-        for n in range(halos):
-            out[lat, SLOTS + n] = jnp.zeros((8, CELLS), F32)
+                for k in range(2):
+                    to = pl.ds(2 * slot + k, 1)
+                    out[lat, count - 1, to, :] = arrived[block, 9 + k : 10 + k, :]
+
     for n in range(halos):
-        out[table[0], SLOTS + n] = north[n]
-        out[table[1], SLOTS + n] = south[n]
+        out[ints[FROM_NORTH], SLOTS + n] = north[n]
+        out[ints[FROM_SOUTH], SLOTS + n] = south[n]
 
 
 def split(x):
@@ -213,15 +220,14 @@
 
 
 def coefficient_kernel(ints, friction, heat, chunks, out, cols_s, rows_s):
-    west = [chunks[ints[TO_WEST], 10 + k : 11 + k, :] for k in range(2)]
-    east = [chunks[ints[TO_EAST], 10 + k : 11 + k, :] for k in range(2)]
+    west, east = chunks[ints[TO_WEST], 8:16, :], chunks[ints[TO_EAST], 8:16, :]
     ghost_columns(west, east, rows_s, cols_s)
     for b in range(1, TILES - 1):
 
         def put(n, k, value):
             out[n, k, tile(b), :] = value
 
-        coefficients(ints, friction, heat, (None, None), (None, None), cols_s[tile(b), :], 0, b, put)
+        coefficients(ints, friction, heat, (None, None), (None, None), cols_s[tile(b), :], 2, b, put)
     for b in (0, TILES - 1):
         for n in range(8):
             for k in range(2):
@@ -261,7 +267,7 @@
     return new
 
 
-def fill_ghosts(ints, arrived, chunks, high, low, sides, ghosts, cols_s, rows_s, others=()):
+def fill_ghosts(ints, arrived, chunks, high, low, sides, ghosts, cols_s, rows_s):
     count = sides.shape[1]
 
     def block(n):
@@ -278,9 +284,7 @@
     found = edge_ghosts(ints, arrived, chunks, sides, SLOTS, slice(0, 8), slice(0, 8))
     for n in range(4):
         ghosts[n] = found[n]
-    west = [ghosts[2, f : f + 1, :] for f in range(8)]
-    east = [ghosts[3, f : f + 1, :] for f in range(8)]
-    ghost_columns(west + [w for w, _ in others], east + [e for _, e in others], rows_s, cols_s)
+    ghost_columns(found[2], found[3], rows_s, cols_s)
 
 
 def first_kernel(
@@ -288,10 +292,9 @@
     flow_out, pressure_out, chunks, north, south, ends, heat_ghosts,
     sides, ghosts, cols_s, rows_s, edge_s, halos,
 ):
-    others = [
-        [chunks_in[ints[at], 10 + k : 11 + k, :] for at in (TO_WEST, TO_EAST)] for k in range(2)
-    ]
-    fill_ghosts(ints, arrived, chunks_in, high, low, sides, ghosts, cols_s, rows_s, others)
+    rows_s[every_second(17), :] = chunks_in[ints[TO_WEST], 8:16, :]
+    rows_s[every_second(16), :] = chunks_in[ints[TO_EAST], 8:16, :]
+    fill_ghosts(ints, arrived, chunks_in, high, low, sides, ghosts, cols_s, rows_s)
     found = edge_ghosts(ints, arrived, chunks_in, sides, SLOTS + 1, slice(8, 16), slice(8, 16))
     for n in range(4):
         heat_ghosts[n] = found[n]
@@ -303,7 +306,7 @@
             ends[n, k, tile(end), :] = value
 
         lines = [[halos[side, 2 + k : 3 + k, :] for k in range(2)] for side in range(2)]
-        coefficients(ints, friction, heat, *lines, cols_s[tile(b), :], 8, b, put)
+        coefficients(ints, friction, heat, *lines, cols_s[tile(b), :], 10, b, put)
     sweep(
         ints, flow, pressure, coef, ends, ghosts, cols_s, rows_s, edge_s,
         flow_out, pressure_out, chunks, north, south,
@@ -344,12 +347,11 @@
                 south[0, f : f + 1, :] = new[f][7:8, :]
         edge_s[tile(b), :] = gathered
     rows_s[...] = edge_s[...].T
+    chunks[ints[TO_WEST]] = rows_s[every_second(1), :]
+    chunks[ints[TO_EAST]] = rows_s[every_second(0), :]
     for f in range(8):
-        west, east = own_lanes(f)
-        chunks[ints[TO_WEST], f : f + 1, :] = rows_s[west : west + 1, :]
-        chunks[ints[TO_EAST], f : f + 1, :] = rows_s[east : east + 1, :]
-    for f in range(8):
-        chunks[ints[CHUNK], f : f + 1, :] = planes_out(f)[pl.ds(ints[ROW], 1), :]
+        edge_s[f : f + 1, :] = planes_out(f)[pl.ds(ints[ROW], 1), :]
+    chunks[ints[CHUNK]] = edge_s[0:8, :]
 
 
 def final_kernel(
@@ -359,9 +361,7 @@
     def planes(f):
         return flow.at[f] if f < 6 else pressure.at[f - 6]
 
-    west = [heat_ghosts[2, k : k + 1, :] for k in range(2)]
-    east = [heat_ghosts[3, k : k + 1, :] for k in range(2)]
-    ghost_columns(west, east, rows_s, heat_cols_s)
+    ghost_columns(heat_ghosts[2], heat_ghosts[3], rows_s, heat_cols_s)
     fill_ghosts(ints, arrived, chunks_in, high, low, sides, ghosts, cols_s, rows_s)
     for b in range(TILES):
         new = relaxed(planes, coef, ends, ghosts, cols_s[tile(b), :], b)
@@ -452,6 +452,10 @@
     beyond = jnp.stack([jnp.maximum(lat - 1, 0), jnp.minimum(lat + 1, n_lat - 1)])
     beyond = beyond.astype(jnp.int32)
     first = jnp.concatenate([own_row, chunk, beside, receiver])
+    on_edge = jnp.stack([lat == 0, lat == n_lat - 1, lon == 0, lon == n_lon - 1]).astype(jnp.int32)
+    bases = jnp.stack([jnp.where(lat > 0, 2, 0), jnp.where(lon > 0, 6, 4)]).astype(jnp.int32)
+    here = jnp.stack([other, lon]).astype(jnp.int32)
+    places_of = jnp.concatenate([own_row, on_edge, bases, chunk, beside, beyond, here])
 
     square = scratch(CELLS, CELLS)
     tiles = 2 * n_lon
@@ -469,41 +473,31 @@
     def across(chunks):
         return lax.all_to_all(chunks, ("patch", "lon"), 0, 0, tiled=True)
 
-    def along(table, blocks, north, south, count):
+    def along(blocks, north, south, count):
         (packed,) = call(
             pack_kernel,
             [shape(n_lat, count, 8, CELLS)],
-            (table, blocks, north, south),
-            [],
+            (places_of, sent_to, blocks, north, south),
+            [pltpu.SMEM((n_lat,), jnp.int32)],
             "pack",
-            keep=(1,),
+            specs=[SMEM, SMEM, VMEM, VMEM, VMEM],
+            keep=(2,),
             pin=(0,),
         )
         return lax.all_to_all(packed, "lat", 0, 0, tiled=True)
 
-    came = across(chunks)
+    came, places = lax.optimization_barrier((across(chunks), places))
     sent_to = lax.dynamic_slice(came, (other, 8, 0), (n_lon, 1, 1)).reshape(n_lon)
     sent_to = sent_to.astype(jnp.int32) - 1
-    every_lat = jnp.arange(n_lat, dtype=jnp.int32)[:, None]
-    wanted = sent_to[None] == every_lat * n_lon + lon
-    order = jnp.arange(n_lon, dtype=jnp.int32)
-    earlier = wanted[:, None, :] & (order[None, None, :] < order[None, :, None])
-    rank = jnp.sum(earlier.astype(jnp.int32), axis=2)
-    mine = wanted[:, None, :] & (rank[:, None, :] == jnp.arange(SLOTS)[None, :, None])
-    found = jnp.sum(jnp.where(mine, order[None, None, :], 0), axis=2).reshape(-1)
-    table = jnp.concatenate([beyond, other + found]).astype(jnp.int32)
-    arrived = along(table, came, north, south, SLOTS + 3)
-
-    on_edge = jnp.stack([lat == 0, lat == n_lat - 1, lon == 0, lon == n_lon - 1]).astype(jnp.int32)
+    arrived = along(came, north, south, SLOTS + 3)
+
     own = places[:, 0].astype(jnp.int32) - 1
     pick = jnp.concatenate(
         [jnp.where(lat > 0, own[2:4], own[0:2]), jnp.where(lon > 0, own[6:8], own[4:6])]
     )
     same = (own >= 0)[None] & (own[None] // n_lon == pick[:, None] // n_lon)
     slot = jnp.sum((same & (own[None] < pick[:, None])).astype(jnp.int32), axis=1)
-    bases = jnp.stack([jnp.where(lat > 0, 2, 0), jnp.where(lon > 0, 6, 4)]).astype(jnp.int32)
-    ints = [own_row, on_edge, bases, chunk, beside, beyond]
-    ints += [jnp.maximum(pick, 0) // n_lon, jnp.minimum(slot, SLOTS - 1)]
+    ints = [places_of, jnp.maximum(pick, 0) // n_lon, jnp.minimum(slot, SLOTS - 1)]
     ints = jnp.concatenate(ints).astype(jnp.int32)
 
     joined = jax.ShapeDtypeStruct((2, CELLS, 2 * CELLS), jnp.bfloat16)
@@ -550,7 +544,7 @@
                 pin=(2,),
             )
         came = across(chunks)
-        arrived = along(table, came, north, south, SLOTS + 1)
+        arrived = along(came, north, south, SLOTS + 1)
     flow, pressure, heat = call(
         final_kernel,
         state + [shape(2, CELLS, CELLS)],

time: 126 us -> 127 us (level)
  transfers between devices with their start and end apart: 2 -> 2, of which waited for: 2 -> 2; matrix products, arithmetic and copies ran while one was open for 1% -> 0% of each run, Pallas kernels for 2% -> 2%
where the time goes in v8:
time: 127 us; the launch traced here: 126 us
  blocking collectives  72.9 us (57%)
  Pallas kernels  17.5 us (14%)
  starting transfers between devices  16.2 us (13%)
  waiting for transfers between devices  15.5 us (12%)
  between operations  2.09 us (2%)
    all_to_all x3, blocking collectives, along(): return lax.all_to_all(packed, 'lat', 0, 0, tiled=True)  37.6 us
    all_to_all x3, blocking collectives, across(): return lax.all_to_all(chunks, ('patch', 'lon'), 0, 0, tiled=True)  35.2 us
    pallas_call x11, Pallas kernels, call(): pl.pallas_call(kernel, out_shape=outs, in_specs=specs, out_specs=[VMEM] *...  17.5 us
    all_to_all x1, starting transfers between devices, along(): return lax.all_to_all(packed, 'lat', 0, 0, tiled=True)  8.6 us
    all_to_all x1, waiting for transfers between devices, along(): return lax.all_to_all(packed, 'lat', 0, 0, tiled=True)  7.86 us
    all_to_all x1, waiting for transfers between devices, across(): return lax.all_to_all(chunks, ('patch', 'lon'), 0, 0, tiled=True)  7.68 us
    all_to_all x1, starting transfers between devices, across(): return lax.all_to_all(chunks, ('patch', 'lon'), 0, 0, tiled=True)  7.63 us
  transfers between devices with their start and end apart: 2, of which 2 were waited for; matrix products, arithmetic and copies ran while one was open for 0% of the time, Pallas kernels for 2%

profile of v8, /device:TPU:2, one launch (start us, length us, event | category | flops | bytes accessed | tf_op | source)
XLA Modules:
  0.0 125.6 jit_solution(16092090499296210689)
XLA Ops:
  1.9 0.1 add_add_fusion
  2.0 0.1 pad_add_fusion.ints
  2.1 2.8 %start.1 = (f32[32,16,128]{2,1,0:T(8,128)}, f32[2,8,128]{2,1,0:T(8,128)S(1)}, f32[2,8,128]{2,1,0:T(8,128)S(1)}, f32[8,128]{1,0:T(8,128)S(1)}) custom-call(s32[5]{0:T(128)S(1)} %pad_add_fusion.ints, s32[1,128]{1,0:T(1,128)} %bitcast.42, f32[6,128,128]{2,1,0:T(8,128)} %bitcast.34, f32[2,128,128]{2,1,0:T(8,128)} %bitcast.39, f32[2,128,128]{2,1,0:T(8,128)} %bitcast.30, ...), custom_call_target="tpu_custom_call" | custom-call | tf_op jit(solution)/shard_map/start/pallas_call | solution.py:416
  4.9 7.6 %all-to-all-start = ((f32[32,16,128]{2,1,0:T(8,128)}), f32[32,16,128]{2,1,0:T(8,128)S(1)}, u32[]{:S(2)}, u32[]{:S(2)}) async-start(f32[32,16,128]{2,1,0:T(8,128)} %get-tuple-element.31), calls=%async_computation | async-start | bytes 524288 | tf_op jit(solution)/shard_map/all_to_all | solution.py:474
  12.5 0.1 add_convert_fusion
  12.6 0.1 concatenate.29.ints
  12.7 7.7 %all-to-all-done.chunks.arrived.chunks_in = f32[32,16,128]{2,1,0:T(8,128)S(1)} async-done(((f32[32,16,128]{2,1,0:T(8,128)}), f32[32,16,128]{2,1,0:T(8,128)S(1)}, u32[]{:S(2)}, u32[]{:S(2)}) %all-to-all-start) | async-done | bytes 262176 | tf_op jit(solution)/shard_map/all_to_all | solution.py:474
  20.4 0.1 fusion
  20.5 0.1 select_reduce_fusion.1
  20.7 0.4 add_reduce_fusion.sent_to
  21.1 1.5 %pack.4 = f32[8,7,8,128]{3,2,1,0:T(8,128)} custom-call(s32[14]{0:T(128)S(1)} %concatenate.29.ints, s32[16]{0:T(128)S(1)} %add_reduce_fusion.sent_to, f32[32,16,128]{2,1,0:T(8,128)S(1)} %all-to-all-done.chunks.arrived.chunks_in, f32[2,8,128]{2,1,0:T(8,128)S(1)} %get-tuple-element.35.north, f32[2,8,128]{2,1,0:T(8,128)S(1)} %get-tuple-element.36.south), custom_call_target="tpu_custom_call" | custom-call | tf_op jit(solution)/shard_map/pack/pallas_call | solution.py:416
  22.5 0.0 copy-start
  22.5 0.0 copy-start.2
  22.5 8.6 %all-to-all-start.1 = ((f32[8,7,8,128]{3,2,1,0:T(8,128)}), f32[8,7,8,128]{3,2,1,0:T(8,128)S(1)}, u32[]{:S(2)}, u32[]{:S(2)}) async-start(f32[8,7,8,128]{3,2,1,0:T(8,128)} %pack.4), calls=%async_computation.1 | async-start | bytes 458752 | tf_op jit(solution)/shard_map/all_to_all | solution.py:487
  31.1 0.1 and_select_fusion
  31.2 0.2 convert_reduce_fusion
  31.4 0.1 concatenate.28.ints
  31.5 0.0 copy-done
  31.5 0.0 copy-done.2
  31.5 0.8 coefficients.1.coef
  32.3 0.0 copy-start.1
  32.4 0.0 copy-start.3
  32.4 1.6 %weights.1 = (bf16[2,128,256]{2,1,0:T(8,128)(2,1)S(1)}, bf16[2,128,256]{2,1,0:T(8,128)(2,1)S(1)}) custom-call(s32[22]{0:T(128)S(1)} %concatenate.28.ints, f32[8,128,128]{2,1,0:T(8,128)} %bitcast.41), custom_call_target="tpu_custom_call" | custom-call | tf_op jit(solution)/shard_map/weights/pallas_call | solution.py:416
  33.9 7.9 %all-to-all-done.1.arrived = f32[8,7,8,128]{3,2,1,0:T(8,128)S(1)} async-done(((f32[8,7,8,128]{3,2,1,0:T(8,128)}), f32[8,7,8,128]{3,2,1,0:T(8,128)S(1)}, u32[]{:S(2)}, u32[]{:S(2)}) %all-to-all-start.1) | async-done | bytes 229408 | tf_op jit(solution)/shard_map/all_to_all | solution.py:487
  41.8 0.0 copy-done.1
  41.8 0.0 copy-done.3
  41.8 2.2 %first_sweep.1 = (f32[6,128,128]{2,1,0:T(8,128)S(1)}, f32[2,128,128]{2,1,0:T(8,128)S(1)}, f32[32,8,128]{2,1,0:T(8,128)S(1)}, f32[1,8,128]{2,1,0:T(8,128)S(1)}, f...) custom-call(s32[22]{0:T(128)S(1)} %concatenate.28.ints, ...), custom_call_target="tpu_custom_call" | custom-call | tf_op jit(solution)/shard_map/first_sweep/pallas_call | solution.py:416
  44.0 12.1 %all_to_all.40.arrived.chunks_in = f32[32,8,128]{2,1,0:T(8,128)S(1)} all-to-all(f32[32,8,128]{2,1,0:T(8,128)S(1)} %get-tuple-element.42), channel_id=1, replica_groups=mesh['patch'=2,'lat'=8,'lon'=16] {'patch','lon'}, dimensions={0} | all-to-all | bytes 262144 | tf_op jit(solution)/shard_map/all_to_all | solution.py:474
  56.1 0.8 pack.5
  56.9 12.5 %all_to_all.41.arrived = f32[8,5,8,128]{3,2,1,0:T(8,128)S(1)} all-to-all(f32[8,5,8,128]{3,2,1,0:T(8,128)S(1)} %pack.5), channel_id=1, replica_groups=mesh['patch'=2,'lat'=8,'lon'=16] {'lat'}, dimensions={0} | all-to-all | bytes 327680 | tf_op jit(solution)/shard_map/all_to_all | solution.py:487
  69.5 2.1 %sweep.2 = (f32[6,128,128]{2,1,0:T(8,128)S(1)}, f32[2,128,128]{2,1,0:T(8,128)S(1)}, f32[32,8,128]{2,1,0:T(8,128)S(1)}, f32[1,8,128]{2,1,0:T(8,128)S(1)}, f32[1,8,128]{2,1,0:T(8,128)S(1)}) custom-call(s32[22]{0:T(128)S(1)} %concatenate.28.ints, f32[6,128,128]{2,1,0:T(8,128)S(1)} %get-tuple-element.39.flow, f32[2,128,128]{2,1,0:T(8,128)S(1)} %get-tuple-element.40.pressure, ...), custom_call_target="tpu_custom_call" | custom-call | tf_op jit(solution)/shard_map/sweep/pallas_call | solution.py:416
  71.6 11.5 %all_to_all.42.arrived.chunks_in = f32[32,8,128]{2,1,0:T(8,128)S(1)} all-to-all(f32[32,8,128]{2,1,0:T(8,128)S(1)} %get-tuple-element.47), channel_id=1, replica_groups=mesh['patch'=2,'lat'=8,'lon'=16] {'patch','lon'}, dimensions={0} | all-to-all | bytes 262144 | tf_op jit(solution)/shard_map/all_to_all | solution.py:474
  83.1 0.8 pack.6
  83.9 12.5 %all_to_all.43.arrived = f32[8,5,8,128]{3,2,1,0:T(8,128)S(1)} all-to-all(f32[8,5,8,128]{3,2,1,0:T(8,128)S(1)} %pack.6), channel_id=1, replica_groups=mesh['patch'=2,'lat'=8,'lon'=16] {'lat'}, dimensions={0} | all-to-all | bytes 327680 | tf_op jit(solution)/shard_map/all_to_all | solution.py:487
  96.4 2.1 %sweep.3 = (f32[6,128,128]{2,1,0:T(8,128)S(1)}, f32[2,128,128]{2,1,0:T(8,128)S(1)}, f32[32,8,128]{2,1,0:T(8,128)S(1)}, f32[1,8,128]{2,1,0:T(8,128)S(1)}, f32[1,8,128]{2,1,0:T(8,128)S(1)}) custom-call(s32[22]{0:T(128)S(1)} %concatenate.28.ints, f32[6,128,128]{2,1,0:T(8,128)S(1)} %get-tuple-element.45.flow, f32[2,128,128]{2,1,0:T(8,128)S(1)} %get-tuple-element.46.pressure, ...), custom_call_target="tpu_custom_call" | custom-call | tf_op jit(solution)/shard_map/sweep/pallas_call | solution.py:416
  98.5 11.5 %all_to_all.44.arrived.chunks_in = f32[32,8,128]{2,1,0:T(8,128)S(1)} all-to-all(f32[32,8,128]{2,1,0:T(8,128)S(1)} %get-tuple-element.52), channel_id=1, replica_groups=mesh['patch'=2,'lat'=8,'lon'=16] {'patch','lon'}, dimensions={0} | all-to-all | bytes 262144 | tf_op jit(solution)/shard_map/all_to_all | solution.py:474
  110.1 0.8 pack.7
  110.9 12.5 %all_to_all.45.arrived = f32[8,5,8,128]{3,2,1,0:T(8,128)S(1)} all-to-all(f32[8,5,8,128]{3,2,1,0:T(8,128)S(1)} %pack.7), channel_id=1, replica_groups=mesh['patch'=2,'lat'=8,'lon'=16] {'lat'}, dimensions={0} | all-to-all | bytes 327680 | tf_op jit(solution)/shard_map/all_to_all | solution.py:487
  123.4 2.2 %final.1 = (f32[6,128,128]{2,1,0:T(8,128)}, f32[2,128,128]{2,1,0:T(8,128)}, f32[2,128,128]{2,1,0:T(8,128)}) custom-call(s32[22]{0:T(128)S(1)} %concatenate.28.ints, f32[6,128,128]{2,1,0:T(8,128)S(1)} %get-tuple-element.50.flow, f32[2,128,128]{2,1,0:T(8,128)S(1)} %get-tuple-element.51.pressure, f32[8,2,128,128]{3,2,1,0:T(8,128)S(1)} %coefficients.1.coef, ...), custom_call_target="tpu_custom_call" | custom-call | tf_op jit(solution)/shard_map/final/pallas_call | solution.py:416
  (3 shorter events, 0.0 us)
Async XLA Ops:
  4.9 15.5 %all-to-all-start = ((f32[32,16,128]{2,1,0:T(8,128)}), f32[32,16,128]{2,1,0:T(8,128)S(1)}, u32[]{:S(2)}, u32[]{:S(2)}) async-start(f32[32,16,128]{2,1,0:T(8,128)} %get-tuple-element.31), calls=%async_computation | async-start | bytes 524288 | tf_op jit(solution)/shard_map/all_to_all | solution.py:474
  22.5 9.0 %copy-start = (f32[1,2,128,128]{3,2,1,0:T(8,128)S(1)}, f32[1,2,128,128]{3,2,1,0:T(8,128)}, u32[]{:S(2)}) copy-start(f32[1,2,128,128]{3,2,1,0:T(8,128)} %param.10) | copy-start | bytes 393220
  22.5 9.0 %copy-start.2 = (f32[1,2,128,128]{3,2,1,0:T(8,128)S(1)}, f32[1,2,128,128]{3,2,1,0:T(8,128)}, u32[]{:S(2)}) copy-start(f32[1,2,128,128]{3,2,1,0:T(8,128)} %param.11) | copy-start | bytes 393220
  22.5 19.3 %all-to-all-start.1 = ((f32[8,7,8,128]{3,2,1,0:T(8,128)}), f32[8,7,8,128]{3,2,1,0:T(8,128)S(1)}, u32[]{:S(2)}, u32[]{:S(2)}) async-start(f32[8,7,8,128]{3,2,1,0:T(8,128)} %pack.4), calls=%async_computation.1 | async-start | bytes 458752 | tf_op jit(solution)/shard_map/all_to_all | solution.py:487
  32.3 9.5 %copy-start.1 = (f32[3,1,2,128,128]{4,3,2,1,0:T(8,128)S(1)}, f32[3,1,2,128,128]{4,3,2,1,0:T(8,128)}, u32[]{:S(2)}) copy-start(f32[3,1,2,128,128]{4,3,2,1,0:T(8,128)} %param.8) | copy-start | bytes 1179652
  32.4 9.5 %copy-start.3 = (f32[1,2,128,128]{3,2,1,0:T(8,128)S(1)}, f32[1,2,128,128]{3,2,1,0:T(8,128)}, u32[]{:S(2)}) copy-start(f32[1,2,128,128]{3,2,1,0:T(8,128)} %param.9) | copy-start | bytes 393220

commit v9 on v8

--- a/solution.py
+++ b/solution.py
@@ -17,8 +17,8 @@
 ROW, NORTH, SOUTH, WEST, EAST, LAT_BASE, LON_BASE = range(7)
 CHUNK, TO_WEST, TO_EAST = 7, 8, 9
 FROM_NORTH, FROM_SOUTH = 10, 11
-OTHER, LON = 12, 13
-BLOCKS, RANKS = 14, 18
+OTHER, LON, RECEIVER = 12, 13, 14
+BLOCKS, RANKS = 15, 19
 
 
 def lanes():
@@ -94,7 +94,7 @@
     copies.start(pressure, own.at[6:8])
     copies.start(heat, own.at[8:10])
     copies.start(friction, own.at[10:12])
-    row[8:16, :] = jnp.broadcast_to((ints[4] + 1).astype(F32), (8, CELLS))
+    row[8:16, :] = jnp.broadcast_to((ints[RECEIVER] + 1).astype(F32), (8, CELLS))
     chunks[...] = jnp.zeros(chunks.shape, F32)
     north[...] = jnp.zeros(north.shape, F32)
     south[...] = jnp.zeros(south.shape, F32)
@@ -104,23 +104,32 @@
     places[...] = jnp.broadcast_to(place, (8, CELLS))
     for f in range(10):
         to = f if f < 8 else f + 1
-        row[to : to + 1, :] = own[f, pl.ds(ints[0], 1), :]
+        row[to : to + 1, :] = own[f, pl.ds(ints[ROW], 1), :]
     for b in range(TILES):
         gathered = jnp.zeros((8, CELLS), F32)
         for f in range(PLANES):
             gathered = gather_edge(own[f, tile(b), :], f, gathered)
         cols_s[tile(b), :] = gathered
     rows_s[...] = cols_s[...].T
-    chunks[ints[1]] = row[...]
-    chunks[ints[2]] = rows_s[every_second(1, 16), :]
-    chunks[ints[3]] = rows_s[every_second(0, 16), :]
+    chunks[ints[CHUNK]] = row[...]
+    chunks[ints[TO_WEST]] = rows_s[every_second(1, 16), :]
+    chunks[ints[TO_EAST]] = rows_s[every_second(0, 16), :]
     for f in range(PLANES):
         n, at = divmod(f, 8)
         north[n, at : at + 1, :] = own[f, 0:1, :]
         south[n, at : at + 1, :] = own[f, CELLS - 1 : CELLS, :]
 
 
-def pack_kernel(ints, sent_to, arrived, north, south, out, filled):
+def pack_kernel(table, arrived, north, south, out):
+    out[:, SLOTS] = jnp.zeros((out.shape[0], 8, CELLS), F32)
+    for lat in range(out.shape[0]):
+        for n in range(SLOTS):
+            out[lat, n] = arrived[table[2 + SLOTS * lat + n]]
+    out[table[0], SLOTS] = north[0]
+    out[table[1], SLOTS] = south[0]
+
+
+def sort_kernel(ints, sent_to, arrived, north, south, out, filled):
     lats, count = out.shape[0], out.shape[1]
     sources = sent_to.shape[0]
     halos = north.shape[0]
@@ -137,10 +146,9 @@
             filled[lat] = slot + 1
             block = ints[OTHER] + n
             out[lat, slot] = arrived[block, 0:8, :]
-            if count > SLOTS + 1:
-                for k in range(2):
-                    to = pl.ds(2 * slot + k, 1)
-                    out[lat, count - 1, to, :] = arrived[block, 9 + k : 10 + k, :]
+            for k in range(2):
+                to = pl.ds(2 * slot + k, 1)
+                out[lat, count - 1, to, :] = arrived[block, 9 + k : 10 + k, :]
 
     for n in range(halos):
         out[ints[FROM_NORTH], SLOTS + n] = north[n]
@@ -337,15 +345,16 @@
     chunks[...] = jnp.zeros(chunks.shape, F32)
     for b in range(TILES):
         new = relaxed(planes, coef, ends, ghosts, cols_s[tile(b), :], b)
+        for f in range(8):
+            planes_out(f)[tile(b), :] = new[f]
+    for b in range(TILES):
         gathered = jnp.zeros((8, CELLS), F32)
         for f in range(8):
-            planes_out(f)[tile(b), :] = new[f]
-            gathered = gather_edge(new[f], f, gathered)
-            if b == 0:
-                north[0, f : f + 1, :] = new[f][0:1, :]
-            if b == TILES - 1:
-                south[0, f : f + 1, :] = new[f][7:8, :]
+            gathered = gather_edge(planes_out(f)[tile(b), :], f, gathered)
         edge_s[tile(b), :] = gathered
+    for f in range(8):
+        north[0, f : f + 1, :] = planes_out(f)[0:1, :]
+        south[0, f : f + 1, :] = planes_out(f)[CELLS - 1 : CELLS, :]
     rows_s[...] = edge_s[...].T
     chunks[ints[TO_WEST]] = rows_s[every_second(1), :]
     chunks[ints[TO_EAST]] = rows_s[every_second(0), :]
@@ -356,7 +365,8 @@
 
 def final_kernel(
     ints, flow, pressure, coef, ends, arrived, chunks_in, high, low, heat, heat_ghosts,
-    flow_out, pressure_out, heat_out, sides, ghosts, cols_s, rows_s, heat_cols_s,
+    flow_out, pressure_out, heat_out,
+    sides, ghosts, cols_s, rows_s, heat_cols_s, answer, warm, sems,
 ):
     def planes(f):
         return flow.at[f] if f < 6 else pressure.at[f - 6]
@@ -365,10 +375,12 @@
     fill_ghosts(ints, arrived, chunks_in, high, low, sides, ghosts, cols_s, rows_s)
     for b in range(TILES):
         new = relaxed(planes, coef, ends, ghosts, cols_s[tile(b), :], b)
-        for f in range(6):
-            flow_out[f, tile(b), :] = new[f]
-        for k in range(2):
-            pressure_out[k, tile(b), :] = new[6 + k]
+        for f in range(8):
+            answer[f, tile(b), :] = new[f]
+    copies = Copies(sems)
+    copies.start(answer.at[0:6], flow_out)
+    copies.start(answer.at[6:8], pressure_out)
+    for b in range(TILES):
         layers = [
             around(
                 heat.at[k],
@@ -386,11 +398,13 @@
             over = layers[1][0] if k == 0 else jnp.zeros((8, CELLS), F32)
             advect = jnp.zeros((8, CELLS), F32)
             for component, minus, plus in ((0, under, over), (1, up, down), (2, left, right)):
-                speed = new[2 * component + k]
+                speed = answer[2 * component + k, tile(b), :]
                 advect = advect + jnp.maximum(speed, 0.0) * (here - minus)
                 advect = advect + jnp.minimum(speed, 0.0) * (plus - here)
             spread = (up + down) + (left + right) + (under + over) - 6.0 * here
-            heat_out[k, tile(b), :] = here + 0.1 * (spread - advect)
+            warm[k, tile(b), :] = here + 0.1 * (spread - advect)
+    copies.start(warm, heat_out)
+    copies.wait()
 
 
 def shape(*dims):
@@ -405,19 +419,29 @@
     return pltpu.SemaphoreType.DMA((count,))
 
 
-def call(kernel, outs, ins, scratches, name, specs=None, limit=4, keep=(), pin=()):
+def call(
+    kernel, outs, ins, scratches, name, specs=None, out_specs=None, limit=4, keep=(), pin=()
+):
+    out_specs = out_specs or [VMEM] * len(outs)
     specs = specs or [SMEM] + [VMEM] * (len(ins) - 1)
     placed = []
     for n, (x, spec) in enumerate(zip(ins, specs)):
         if spec is HBM or n in keep:
             x = pltpu.with_memory_space_constraint(x, spec.memory_space)
         placed.append(x)
-    outs = [pltpu.VMEM(x.shape, x.dtype) if n in pin else x for n, x in enumerate(outs)]
+    outs = [
+        pltpu.HBM(x.shape, x.dtype)
+        if spec is HBM
+        else pltpu.VMEM(x.shape, x.dtype)
+        if n in pin
+        else x
+        for n, (x, spec) in enumerate(zip(outs, out_specs))
+    ]
     return pl.pallas_call(
         kernel,
         out_shape=outs,
         in_specs=specs,
-        out_specs=[VMEM] * len(outs),
+        out_specs=out_specs,
         scratch_shapes=scratches,
         compiler_params=pltpu.CompilerParams(vmem_limit_bytes=limit * 1024 * 1024),
         name=name,
@@ -451,11 +475,10 @@
     beside = (beside + patch * n_lon).astype(jnp.int32)
     beyond = jnp.stack([jnp.maximum(lat - 1, 0), jnp.minimum(lat + 1, n_lat - 1)])
     beyond = beyond.astype(jnp.int32)
-    first = jnp.concatenate([own_row, chunk, beside, receiver])
     on_edge = jnp.stack([lat == 0, lat == n_lat - 1, lon == 0, lon == n_lon - 1]).astype(jnp.int32)
     bases = jnp.stack([jnp.where(lat > 0, 2, 0), jnp.where(lon > 0, 6, 4)]).astype(jnp.int32)
     here = jnp.stack([other, lon]).astype(jnp.int32)
-    places_of = jnp.concatenate([own_row, on_edge, bases, chunk, beside, beyond, here])
+    first = jnp.concatenate([own_row, on_edge, bases, chunk, beside, beyond, here, receiver])
 
     square = scratch(CELLS, CELLS)
     tiles = 2 * n_lon
@@ -473,23 +496,35 @@
     def across(chunks):
         return lax.all_to_all(chunks, ("patch", "lon"), 0, 0, tiled=True)
 
-    def along(blocks, north, south, count):
-        (packed,) = call(
-            pack_kernel,
-            [shape(n_lat, count, 8, CELLS)],
-            (places_of, sent_to, blocks, north, south),
-            [pltpu.SMEM((n_lat,), jnp.int32)],
-            "pack",
-            specs=[SMEM, SMEM, VMEM, VMEM, VMEM],
-            keep=(2,),
-            pin=(0,),
-        )
+    def along(packed):
         return lax.all_to_all(packed, "lat", 0, 0, tiled=True)
 
-    came, places = lax.optimization_barrier((across(chunks), places))
+    came, places, lon, lat, other = lax.optimization_barrier(
+        (across(chunks), places, lon, lat, other)
+    )
     sent_to = lax.dynamic_slice(came, (other, 8, 0), (n_lon, 1, 1)).reshape(n_lon)
     sent_to = sent_to.astype(jnp.int32) - 1
-    arrived = along(came, north, south, SLOTS + 3)
+    (packed,) = call(
+        sort_kernel,
+        [shape(n_lat, SLOTS + 3, 8, CELLS)],
+        (first, sent_to, came, north, south),
+        [pltpu.SMEM((n_lat,), jnp.int32)],
+        "sort",
+        specs=[SMEM, SMEM, VMEM, VMEM, VMEM],
+        keep=(2,),
+        pin=(0,),
+    )
+    arrived = along(packed)
+
+    packed, sent_to = lax.optimization_barrier((packed, sent_to))
+    every_lat = jnp.arange(n_lat, dtype=jnp.int32)[:, None]
+    wanted = sent_to[None] == every_lat * n_lon + lon
+    order = jnp.arange(n_lon, dtype=jnp.int32)
+    earlier = wanted[:, None, :] & (order[None, None, :] < order[None, :, None])
+    rank = jnp.sum(earlier.astype(jnp.int32), axis=2)
+    mine = wanted[:, None, :] & (rank[:, None, :] == jnp.arange(SLOTS)[None, :, None])
+    found = jnp.sum(jnp.where(mine, order[None, None, :], 0), axis=2).reshape(-1)
+    table = jnp.concatenate([beyond, other + found]).astype(jnp.int32)
 
     own = places[:, 0].astype(jnp.int32) - 1
     pick = jnp.concatenate(
@@ -497,7 +532,7 @@
     )
     same = (own >= 0)[None] & (own[None] // n_lon == pick[:, None] // n_lon)
     slot = jnp.sum((same & (own[None] < pick[:, None])).astype(jnp.int32), axis=1)
-    ints = [places_of, jnp.maximum(pick, 0) // n_lon, jnp.minimum(slot, SLOTS - 1)]
+    ints = [first, jnp.maximum(pick, 0) // n_lon, jnp.minimum(slot, SLOTS - 1)]
     ints = jnp.concatenate(ints).astype(jnp.int32)
 
     joined = jax.ShapeDtypeStruct((2, CELLS, 2 * CELLS), jnp.bfloat16)
@@ -544,13 +579,24 @@
                 pin=(2,),
             )
         came = across(chunks)
-        arrived = along(came, north, south, SLOTS + 1)
+        (packed,) = call(
+            pack_kernel,
+            [shape(n_lat, SLOTS + 1, 8, CELLS)],
+            (table, came, north, south),
+            [],
+            "pack",
+            keep=(1,),
+            pin=(0,),
+        )
+        arrived = along(packed)
     flow, pressure, heat = call(
         final_kernel,
         state + [shape(2, CELLS, CELLS)],
         (ints, flow, pressure, coef, ends, arrived, came, high, low, heat, heat_ghosts),
-        [sides, ghosts, square, square, square],
+        [sides, ghosts, square, square, square]
+        + [scratch(8, CELLS, CELLS), scratch(2, CELLS, CELLS), semaphores(3)],
         "final",
+        out_specs=[HBM] * 3,
         limit=8,
         keep=(1, 2, 3, 4, 5, 6, 7, 8),
     )

time: 127 us -> 125 us (0.984)
  blocking collectives: 72.9 us -> 60.7 us
  waiting for transfers between devices: 15.5 us -> 21.5 us
  starting transfers between devices: 16.2 us -> 22 us
  Pallas kernels: 17.5 us -> 15.5 us
    all_to_all x3 -> x2, blocking collectives: 35.2 us -> 23.1 us  [across(): return lax.all_to_all(chunks, ('patch', 'lon'), 0, 0, tiled=True)]
    all_to_all x1 -> x2, waiting for transfers between devices: 7.68 us -> 14.2 us  [across(): return lax.all_to_all(chunks, ('patch', 'lon'), 0, 0, tiled=True)]
    all_to_all x1 -> x2, starting transfers between devices: 7.63 us -> 13.4 us  [across(): return lax.all_to_all(chunks, ('patch', 'lon'), 0, 0, tiled=True)]
    pallas_call x11, Pallas kernels: 17.5 us -> 15.5 us  [call(): pl.pallas_call(kernel, out_shape=outs, in_specs=specs, out_specs=out_spec...]
  transfers between devices with their start and end apart: 2 -> 3, of which waited for: 2 -> 3; matrix products, arithmetic and copies ran while one was open for 0% -> 1% of each run, Pallas kernels for 2% -> 2%
where the time goes in v9:
time: 125 us; the launch traced here: 124 us
  blocking collectives  60.7 us (49%)
  starting transfers between devices  22 us (18%)
  waiting for transfers between devices  21.5 us (17%)
  Pallas kernels  15.5 us (12%)
  between operations  2.11 us (2%)
  other arithmetic  1.62 us (1%)
    all_to_all x3, blocking collectives, along(): return lax.all_to_all(packed, 'lat', 0, 0, tiled=True)  37.6 us
    all_to_all x2, blocking collectives, across(): return lax.all_to_all(chunks, ('patch', 'lon'), 0, 0, tiled=True)  23.1 us
    pallas_call x11, Pallas kernels, call(): pl.pallas_call(kernel, out_shape=outs, in_specs=specs, out_specs=out_spec...  15.5 us
    all_to_all x2, waiting for transfers between devices, across(): return lax.all_to_all(chunks, ('patch', 'lon'), 0, 0, tiled=True)  14.2 us
    all_to_all x2, starting transfers between devices, across(): return lax.all_to_all(chunks, ('patch', 'lon'), 0, 0, tiled=True)  13.4 us
    all_to_all x1, starting transfers between devices, along(): return lax.all_to_all(packed, 'lat', 0, 0, tiled=True)  8.6 us
    all_to_all x1, waiting for transfers between devices, along(): return lax.all_to_all(packed, 'lat', 0, 0, tiled=True)  7.25 us
  transfers between devices with their start and end apart: 3, of which 3 were waited for; matrix products, arithmetic and copies ran while one was open for 1% of the time, Pallas kernels for 2%

profile of v9, /device:TPU:2, one launch (start us, length us, event | category | flops | bytes accessed | tf_op | source)
XLA Modules:
  0.0 123.7 jit_solution(13206313376763178140)
XLA Ops:
  2.0 0.1 add_add_fusion
  2.0 0.1 add_convert_fusion
  2.1 0.1 concatenate.28.ints
  2.2 2.8 %start.1 = (f32[32,16,128]{2,1,0:T(8,128)}, f32[2,8,128]{2,1,0:T(8,128)S(1)}, f32[2,8,128]{2,1,0:T(8,128)S(1)}, f32[8,128]{1,0:T(8,128)S(1)}) custom-call(s32[15]{0:T(128)S(1)} %concatenate.28.ints, s32[1,128]{1,0:T(1,128)} %bitcast.42, f32[6,128,128]{2,1,0:T(8,128)} %bitcast.34, f32[2,128,128]{2,1,0:T(8,128)} %bitcast.39, f32[2,128,128]{2,1,0:T(8,128)} %bitcast.30, ...), custom_call_target="tpu_custom_call" | custom-call | tf_op jit(solution)/shard_map/start/pallas_call | solution.py:440
  5.0 7.6 %all-to-all-start = ((f32[32,16,128]{2,1,0:T(8,128)}), f32[32,16,128]{2,1,0:T(8,128)S(1)}, u32[]{:S(2)}, u32[]{:S(2)}) async-start(f32[32,16,128]{2,1,0:T(8,128)} %get-tuple-element.35), calls=%async_computation | async-start | bytes 524288 | tf_op jit(solution)/shard_map/all_to_all | solution.py:497
  12.6 7.9 %all-to-all-done.chunks.arrived.chunks_in = f32[32,16,128]{2,1,0:T(8,128)S(1)} async-done(((f32[32,16,128]{2,1,0:T(8,128)}), f32[32,16,128]{2,1,0:T(8,128)S(1)}, u32[]{:S(2)}, u32[]{:S(2)}) %all-to-all-start) | async-done | bytes 262176 | tf_op jit(solution)/shard_map/all_to_all | solution.py:497
  20.5 0.1 fusion.1
  20.6 0.4 add_reduce_fusion.sent_to
  21.0 1.5 %sort.1 = f32[8,7,8,128]{3,2,1,0:T(8,128)} custom-call(s32[15]{0:T(128)S(1)} %concatenate.28.ints, s32[16]{0:T(128)S(1)} %add_reduce_fusion.sent_to, f32[32,16,128]{2,1,0:T(8,128)S(1)} %all-to-all-done.chunks.arrived.chunks_in, f32[2,8,128]{2,1,0:T(8,128)S(1)} %get-tuple-element.42.north, f32[2,8,128]{2,1,0:T(8,128)S(1)} %get-tuple-element.43.south), custom_call_target="tpu_custom_call" | custom-call | tf_op jit(solution)/shard_map/sort/pallas_call | solution.py:440
  22.5 0.0 copy-start
  22.5 0.0 copy-start.2
  22.5 8.6 %all-to-all-start.1 = ((f32[8,7,8,128]{3,2,1,0:T(8,128)}), f32[8,7,8,128]{3,2,1,0:T(8,128)S(1)}, u32[]{:S(2)}, u32[]{:S(2)}) async-start(f32[8,7,8,128]{3,2,1,0:T(8,128)} %sort.1), calls=%async_computation.1 | async-start | bytes 458752 | tf_op jit(solution)/shard_map/all_to_all | solution.py:500
  31.1 0.1 select_reduce_fusion.2
  31.2 0.1 and_select_fusion
  31.3 0.2 convert_reduce_fusion.1
  31.5 0.1 concatenate.30.ints
  31.6 0.0 copy-done
  31.6 0.0 copy-done.2
  31.7 0.8 coefficients.1.coef
  32.5 0.0 copy-start.1
  32.5 0.0 copy-start.3
  32.5 1.6 %weights.1 = (bf16[2,128,256]{2,1,0:T(8,128)(2,1)S(1)}, bf16[2,128,256]{2,1,0:T(8,128)(2,1)S(1)}) custom-call(s32[23]{0:T(128)S(1)} %concatenate.30.ints, f32[8,128,128]{2,1,0:T(8,128)} %bitcast.41), custom_call_target="tpu_custom_call" | custom-call | tf_op jit(solution)/shard_map/weights/pallas_call | solution.py:440
  34.1 0.1 broadcast_compare_fusion
  34.2 0.2 convert_reduce_fusion
  34.4 0.1 select_reduce_fusion
  34.5 7.2 %all-to-all-done.1.arrived = f32[8,7,8,128]{3,2,1,0:T(8,128)S(1)} async-done(((f32[8,7,8,128]{3,2,1,0:T(8,128)}), f32[8,7,8,128]{3,2,1,0:T(8,128)S(1)}, u32[]{:S(2)}, u32[]{:S(2)}) %all-to-all-start.1) | async-done | bytes 229408 | tf_op jit(solution)/shard_map/all_to_all | solution.py:500
  41.8 0.0 copy-done.1
  41.8 0.0 copy-done.3
  41.8 2.1 %first_sweep.1 = (f32[6,128,128]{2,1,0:T(8,128)S(1)}, f32[2,128,128]{2,1,0:T(8,128)S(1)}, f32[32,8,128]{2,1,0:T(8,128)}, f32[1,8,128]{2,1,0:T(8,128)S(1)}, f32[1...) custom-call(s32[23]{0:T(128)S(1)} %concatenate.30.ints, f32[6,128,128]{2,1,0:T(8,128)S(1)} %bitcast.35, ...), custom_call_target="tpu_custom_call" | custom-call | tf_op jit(solution)/shard_map/first_sweep/pallas_call | solution.py:440
  43.9 5.7 %all-to-all-start.2 = ((f32[32,8,128]{2,1,0:T(8,128)}), f32[32,8,128]{2,1,0:T(8,128)S(1)}, u32[]{:S(2)}, u32[]{:S(2)}) async-start(f32[32,8,128]{2,1,0:T(8,128)} %get-tuple-element.50), calls=%async_computation.2 | async-start | bytes 262144 | tf_op jit(solution)/shard_map/all_to_all | solution.py:497
  49.6 0.1 copy.13
  49.7 0.1 add.88
  49.8 0.1 pad_add_fusion.1.table
  49.9 6.4 %all-to-all-done.2.arrived.chunks_in = f32[32,8,128]{2,1,0:T(8,128)S(1)} async-done(((f32[32,8,128]{2,1,0:T(8,128)}), f32[32,8,128]{2,1,0:T(8,128)S(1)}, u32[]{:S(2)}, u32[]{:S(2)}) %all-to-all-start.2) | async-done | bytes 131104 | tf_op jit(solution)/shard_map/all_to_all | solution.py:497
  56.2 0.6 pack.3
  56.8 12.5 %all_to_all.40.arrived = f32[8,5,8,128]{3,2,1,0:T(8,128)S(1)} all-to-all(f32[8,5,8,128]{3,2,1,0:T(8,128)S(1)} %pack.3), channel_id=1, replica_groups=mesh['patch'=2,'lat'=8,'lon'=16] {'lat'}, dimensions={0} | all-to-all | bytes 327680 | tf_op jit(solution)/shard_map/all_to_all | solution.py:500
  69.4 1.5 %sweep.2 = (f32[6,128,128]{2,1,0:T(8,128)S(1)}, f32[2,128,128]{2,1,0:T(8,128)S(1)}, f32[32,8,128]{2,1,0:T(8,128)S(1)}, f32[1,8,128]{2,1,0:T(8,128)S(1)}, f32[1,8,128]{2,1,0:T(8,128)S(1)}) custom-call(s32[23]{0:T(128)S(1)} %concatenate.30.ints, f32[6,128,128]{2,1,0:T(8,128)S(1)} %get-tuple-element.46.flow, f32[2,128,128]{2,1,0:T(8,128)S(1)} %get-tuple-element.47.pressure, ...), custom_call_target="tpu_custom_call" | custom-call | tf_op jit(solution)/shard_map/sweep/pallas_call | solution.py:440
  70.8 11.5 %all_to_all.41.arrived.chunks_in = f32[32,8,128]{2,1,0:T(8,128)S(1)} all-to-all(f32[32,8,128]{2,1,0:T(8,128)S(1)} %get-tuple-element.55), channel_id=1, replica_groups=mesh['patch'=2,'lat'=8,'lon'=16] {'patch','lon'}, dimensions={0} | all-to-all | bytes 262144 | tf_op jit(solution)/shard_map/all_to_all | solution.py:497
  82.4 0.6 pack.4
  82.9 12.5 %all_to_all.42.arrived = f32[8,5,8,128]{3,2,1,0:T(8,128)S(1)} all-to-all(f32[8,5,8,128]{3,2,1,0:T(8,128)S(1)} %pack.4), channel_id=1, replica_groups=mesh['patch'=2,'lat'=8,'lon'=16] {'lat'}, dimensions={0} | all-to-all | bytes 327680 | tf_op jit(solution)/shard_map/all_to_all | solution.py:500
  95.5 1.5 %sweep.3 = (f32[6,128,128]{2,1,0:T(8,128)S(1)}, f32[2,128,128]{2,1,0:T(8,128)S(1)}, f32[32,8,128]{2,1,0:T(8,128)S(1)}, f32[1,8,128]{2,1,0:T(8,128)S(1)}, f32[1,8,128]{2,1,0:T(8,128)S(1)}) custom-call(s32[23]{0:T(128)S(1)} %concatenate.30.ints, f32[6,128,128]{2,1,0:T(8,128)S(1)} %get-tuple-element.53.flow, f32[2,128,128]{2,1,0:T(8,128)S(1)} %get-tuple-element.54.pressure, ...), custom_call_target="tpu_custom_call" | custom-call | tf_op jit(solution)/shard_map/sweep/pallas_call | solution.py:440
  96.9 11.5 %all_to_all.43.arrived.chunks_in = f32[32,8,128]{2,1,0:T(8,128)S(1)} all-to-all(f32[32,8,128]{2,1,0:T(8,128)S(1)} %get-tuple-element.60), channel_id=1, replica_groups=mesh['patch'=2,'lat'=8,'lon'=16] {'patch','lon'}, dimensions={0} | all-to-all | bytes 262144 | tf_op jit(solution)/shard_map/all_to_all | solution.py:497
  108.5 0.6 pack.5
  109.1 12.5 %all_to_all.44.arrived = f32[8,5,8,128]{3,2,1,0:T(8,128)S(1)} all-to-all(f32[8,5,8,128]{3,2,1,0:T(8,128)S(1)} %pack.5), channel_id=1, replica_groups=mesh['patch'=2,'lat'=8,'lon'=16] {'lat'}, dimensions={0} | all-to-all | bytes 327680 | tf_op jit(solution)/shard_map/all_to_all | solution.py:500
  121.6 2.1 %final.1 = (f32[6,128,128]{2,1,0:T(8,128)}, f32[2,128,128]{2,1,0:T(8,128)}, f32[2,128,128]{2,1,0:T(8,128)}) custom-call(s32[23]{0:T(128)S(1)} %concatenate.30.ints, f32[6,128,128]{2,1,0:T(8,128)S(1)} %get-tuple-element.58.flow, f32[2,128,128]{2,1,0:T(8,128)S(1)} %get-tuple-element.59.pressure, f32[8,2,128,128]{3,2,1,0:T(8,128)S(1)} %coefficients.1.coef, ...), custom_call_target="tpu_custom_call" | custom-call | tf_op jit(solution)/shard_map/final/pallas_call | solution.py:440
  (6 shorter events, 0.0 us)
Async XLA Ops:
  5.0 15.5 %all-to-all-start = ((f32[32,16,128]{2,1,0:T(8,128)}), f32[32,16,128]{2,1,0:T(8,128)S(1)}, u32[]{:S(2)}, u32[]{:S(2)}) async-start(f32[32,16,128]{2,1,0:T(8,128)} %get-tuple-element.35), calls=%async_computation | async-start | bytes 524288 | tf_op jit(solution)/shard_map/all_to_all | solution.py:497
  22.5 9.1 %copy-start = (f32[1,2,128,128]{3,2,1,0:T(8,128)S(1)}, f32[1,2,128,128]{3,2,1,0:T(8,128)}, u32[]{:S(2)}) copy-start(f32[1,2,128,128]{3,2,1,0:T(8,128)} %param.10) | copy-start | bytes 393220
  22.5 9.1 %copy-start.2 = (f32[1,2,128,128]{3,2,1,0:T(8,128)S(1)}, f32[1,2,128,128]{3,2,1,0:T(8,128)}, u32[]{:S(2)}) copy-start(f32[1,2,128,128]{3,2,1,0:T(8,128)} %param.11) | copy-start | bytes 393220
  22.5 19.3 %all-to-all-start.1 = ((f32[8,7,8,128]{3,2,1,0:T(8,128)}), f32[8,7,8,128]{3,2,1,0:T(8,128)S(1)}, u32[]{:S(2)}, u32[]{:S(2)}) async-start(f32[8,7,8,128]{3,2,1,0:T(8,128)} %sort.1), calls=%async_computation.1 | async-start | bytes 458752 | tf_op jit(solution)/shard_map/all_to_all | solution.py:500
  32.5 9.3 %copy-start.1 = (f32[3,1,2,128,128]{4,3,2,1,0:T(8,128)S(1)}, f32[3,1,2,128,128]{4,3,2,1,0:T(8,128)}, u32[]{:S(2)}) copy-start(f32[3,1,2,128,128]{4,3,2,1,0:T(8,128)} %param.8) | copy-start | bytes 1179652
  32.5 9.3 %copy-start.3 = (f32[1,2,128,128]{3,2,1,0:T(8,128)S(1)}, f32[1,2,128,128]{3,2,1,0:T(8,128)}, u32[]{:S(2)}) copy-start(f32[1,2,128,128]{3,2,1,0:T(8,128)} %param.9) | copy-start | bytes 393220
  43.9 12.4 %all-to-all-start.2 = ((f32[32,8,128]{2,1,0:T(8,128)}), f32[32,8,128]{2,1,0:T(8,128)S(1)}, u32[]{:S(2)}, u32[]{:S(2)}) async-start(f32[32,8,128]{2,1,0:T(8,128)} %get-tuple-element.50), calls=%async_computation.2 | async-start | bytes 262144 | tf_op jit(solution)/shard_map/all_to_all | solution.py:497

commit v10 on v9

--- a/solution.py
+++ b/solution.py
@@ -129,11 +129,8 @@
     out[table[1], SLOTS] = south[0]
 
 
-def sort_kernel(ints, sent_to, arrived, north, south, out, filled):
-    lats, count = out.shape[0], out.shape[1]
+def for_each_block(ints, sent_to, filled, lats, act):
     sources = sent_to.shape[0]
-    halos = north.shape[0]
-    out[...] = jnp.zeros(out.shape, F32)
     for lat in range(lats):
         filled[lat] = 0
     for n in range(sources):
@@ -144,13 +141,33 @@
         def _():
             slot = filled[lat]
             filled[lat] = slot + 1
-            block = ints[OTHER] + n
-            out[lat, slot] = arrived[block, 0:8, :]
-            for k in range(2):
-                to = pl.ds(2 * slot + k, 1)
-                out[lat, count - 1, to, :] = arrived[block, 9 + k : 10 + k, :]
-
-    for n in range(halos):
+            act(lat, slot, ints[OTHER] + n)
+
+
+def table_kernel(ints, sent_to, table, filled):
+    table[0] = ints[FROM_NORTH]
+    table[1] = ints[FROM_SOUTH]
+    for n in range(2, table.shape[0]):
+        table[n] = ints[OTHER]
+
+    def act(lat, slot, block):
+        table[2 + SLOTS * lat + slot] = block
+
+    for_each_block(ints, sent_to, filled, (table.shape[0] - 2) // SLOTS, act)
+
+
+def sort_kernel(ints, sent_to, arrived, north, south, out, filled):
+    lats, count = out.shape[0], out.shape[1]
+    out[...] = jnp.zeros(out.shape, F32)
+
+    def act(lat, slot, block):
+        out[lat, slot] = arrived[block, 0:8, :]
+        for k in range(2):
+            to = pl.ds(2 * slot + k, 1)
+            out[lat, count - 1, to, :] = arrived[block, 9 + k : 10 + k, :]
+
+    for_each_block(ints, sent_to, filled, lats, act)
+    for n in range(north.shape[0]):
         out[ints[FROM_NORTH], SLOTS + n] = north[n]
         out[ints[FROM_SOUTH], SLOTS + n] = south[n]
 
@@ -516,15 +533,16 @@
     )
     arrived = along(packed)
 
-    packed, sent_to = lax.optimization_barrier((packed, sent_to))
-    every_lat = jnp.arange(n_lat, dtype=jnp.int32)[:, None]
-    wanted = sent_to[None] == every_lat * n_lon + lon
-    order = jnp.arange(n_lon, dtype=jnp.int32)
-    earlier = wanted[:, None, :] & (order[None, None, :] < order[None, :, None])
-    rank = jnp.sum(earlier.astype(jnp.int32), axis=2)
-    mine = wanted[:, None, :] & (rank[:, None, :] == jnp.arange(SLOTS)[None, :, None])
-    found = jnp.sum(jnp.where(mine, order[None, None, :], 0), axis=2).reshape(-1)
-    table = jnp.concatenate([beyond, other + found]).astype(jnp.int32)
+    (table,) = call(
+        table_kernel,
+        [jax.ShapeDtypeStruct((2 + n_lat * SLOTS,), jnp.int32)],
+        lax.optimization_barrier((first, sent_to, packed))[:2],
+        [pltpu.SMEM((n_lat,), jnp.int32)],
+        "table",
+        specs=[SMEM, SMEM],
+        out_specs=[SMEM],
+    )
+    arrived, table = lax.optimization_barrier((arrived, table))
 
     own = places[:, 0].astype(jnp.int32) - 1
     pick = jnp.concatenate(

time: 125 us -> 123 us (0.984)
  blocking collectives: 60.7 us -> 88.1 us
  waiting for transfers between devices: 21.5 us -> 6.4 us
  starting transfers between devices: 22 us -> 8.59 us
    all_to_all x2 -> x4, blocking collectives: 23.1 us -> 50.5 us  [across(): return lax.all_to_all(chunks, ('patch', 'lon'), 0, 0, tiled=True)]
    all_to_all x2 -> x0, waiting for transfers between devices: 14.2 us -> none  [across(): return lax.all_to_all(chunks, ('patch', 'lon'), 0, 0, tiled=True)]
    all_to_all x2 -> x0, starting transfers between devices: 13.4 us -> none  [across(): return lax.all_to_all(chunks, ('patch', 'lon'), 0, 0, tiled=True)]
    pallas_call x11 -> x12, Pallas kernels: 15.5 us -> 15.5 us  [call(): pl.pallas_call(kernel, out_shape=outs, in_specs=specs, out_specs=out_spec...]
  transfers between devices with their start and end apart: 3 -> 1, of which waited for: 3 -> 1; matrix products, arithmetic and copies ran while one was open for 1% -> 0% of each run, Pallas kernels for 2% -> 3%
where the time goes in v10:
time: 123 us; the launch traced here: 122 us
  blocking collectives  88.1 us (72%)
  Pallas kernels  15.5 us (13%)
  starting transfers between devices  8.59 us (7%)
  waiting for transfers between devices  6.4 us (5%)
  between operations  2.08 us (2%)
    all_to_all x4, blocking collectives, across(): return lax.all_to_all(chunks, ('patch', 'lon'), 0, 0, tiled=True)  50.5 us
    all_to_all x3, blocking collectives, along(): return lax.all_to_all(packed, 'lat', 0, 0, tiled=True)  37.6 us
    pallas_call x12, Pallas kernels, call(): pl.pallas_call(kernel, out_shape=outs, in_specs=specs, out_specs=out_spec...  15.5 us
    all_to_all x1, starting transfers between devices, along(): return lax.all_to_all(packed, 'lat', 0, 0, tiled=True)  8.59 us
    all_to_all x1, waiting for transfers between devices, along(): return lax.all_to_all(packed, 'lat', 0, 0, tiled=True)  6.4 us
  transfers between devices with their start and end apart: 1, of which 1 were waited for; matrix products, arithmetic and copies ran while one was open for 0% of the time, Pallas kernels for 3%

profile of v10, /device:TPU:2, one launch (start us, length us, event | category | flops | bytes accessed | tf_op | source)
XLA Modules:
  0.0 122.0 jit_solution(376764282938394741)
XLA Ops:
  2.0 0.1 add_add_fusion
  2.0 0.1 add_convert_fusion
  2.1 0.1 concatenate.23.ints
  2.2 2.1 %start.1 = (f32[32,16,128]{2,1,0:T(8,128)S(1)}, f32[2,8,128]{2,1,0:T(8,128)S(1)}, f32[2,8,128]{2,1,0:T(8,128)S(1)}, f32[8,128]{1,0:T(8,128)S(1)}) custom-call(s32[15]{0:T(128)S(1)} %concatenate.23.ints, s32[1,128]{1,0:T(1,128)} %bitcast.42, f32[6,128,128]{2,1,0:T(8,128)} %bitcast.34, f32[2,128,128]{2,1,0:T(8,128)} %bitcast.39, f32[2,128,128]{2,1,0:T(8,128)} %bitcast.30, ...), custom_call_target="tpu_custom_call" | custom-call | tf_op jit(solution)/shard_map/start/pallas_call | solution.py:457
  4.3 15.3 %all_to_all.40.chunks.arrived.chunks_in = f32[32,16,128]{2,1,0:T(8,128)S(1)} all-to-all(f32[32,16,128]{2,1,0:T(8,128)S(1)} %get-tuple-element.38), channel_id=1, replica_groups=mesh['patch'=2,'lat'=8,'lon'=16] {'patch','lon'}, dimensions={0} | all-to-all | bytes 524288 | tf_op jit(solution)/shard_map/all_to_all | solution.py:514
  19.6 0.1 fusion
  19.7 0.4 add_reduce_fusion.sent_to
  20.1 1.5 %sort.1 = f32[8,7,8,128]{3,2,1,0:T(8,128)} custom-call(s32[15]{0:T(128)S(1)} %concatenate.23.ints, s32[16]{0:T(128)S(1)} %add_reduce_fusion.sent_to, f32[32,16,128]{2,1,0:T(8,128)S(1)} %all_to_all.40.chunks.arrived.chunks_in, f32[2,8,128]{2,1,0:T(8,128)S(1)} %get-tuple-element.45.north, f32[2,8,128]{2,1,0:T(8,128)S(1)} %get-tuple-element.46.south), custom_call_target="tpu_custom_call" | custom-call | tf_op jit(solution)/shard_map/sort/pallas_call | solution.py:457
  21.6 0.0 copy-start
  21.6 0.0 copy-start.2
  21.6 8.6 %all-to-all-start.1 = ((f32[8,7,8,128]{3,2,1,0:T(8,128)}), f32[8,7,8,128]{3,2,1,0:T(8,128)S(1)}, u32[]{:S(2)}, u32[]{:S(2)}) async-start(f32[8,7,8,128]{3,2,1,0:T(8,128)} %sort.1), calls=%async_computation.1 | async-start | bytes 458752 | tf_op jit(solution)/shard_map/all_to_all | solution.py:517
  30.2 0.1 select_reduce_fusion.1
  30.3 0.1 and_select_fusion
  30.4 0.2 convert_reduce_fusion
  30.6 0.1 concatenate.25.ints
  30.7 0.0 copy-done
  30.7 0.0 copy-done.2
  30.7 0.8 coefficients.1.coef
  31.6 0.0 copy-start.1
  31.6 0.0 copy-start.3
  31.6 1.6 %weights.1 = (bf16[2,128,256]{2,1,0:T(8,128)(2,1)S(1)}, bf16[2,128,256]{2,1,0:T(8,128)(2,1)S(1)}) custom-call(s32[23]{0:T(128)S(1)} %concatenate.25.ints, f32[8,128,128]{2,1,0:T(8,128)} %bitcast.41), custom_call_target="tpu_custom_call" | custom-call | tf_op jit(solution)/shard_map/weights/pallas_call | solution.py:457
  33.2 1.3 %table.1 = s32[34]{0:T(128)S(1)} custom-call(s32[15]{0:T(128)S(1)} %concatenate.23.ints, s32[16]{0:T(128)S(1)} %add_reduce_fusion.sent_to), custom_call_target="tpu_custom_call" | custom-call | tf_op jit(solution)/shard_map/table/pallas_call | solution.py:457
  34.5 6.4 %all-to-all-done.1.arrived = f32[8,7,8,128]{3,2,1,0:T(8,128)S(1)} async-done(((f32[8,7,8,128]{3,2,1,0:T(8,128)}), f32[8,7,8,128]{3,2,1,0:T(8,128)S(1)}, u32[]{:S(2)}, u32[]{:S(2)}) %all-to-all-start.1) | async-done | bytes 229408 | tf_op jit(solution)/shard_map/all_to_all | solution.py:517
  40.9 0.0 copy-done.1
  40.9 0.0 copy-done.3
  40.9 1.5 %first_sweep.1 = (f32[6,128,128]{2,1,0:T(8,128)S(1)}, f32[2,128,128]{2,1,0:T(8,128)S(1)}, f32[32,8,128]{2,1,0:T(8,128)S(1)}, f32[1,8,128]{2,1,0:T(8,128)S(1)}, f...) custom-call(s32[23]{0:T(128)S(1)} %concatenate.25.ints, ...), custom_call_target="tpu_custom_call" | custom-call | tf_op jit(solution)/shard_map/first_sweep/pallas_call | solution.py:457
  42.3 12.1 %all_to_all.41.arrived.chunks_in = f32[32,8,128]{2,1,0:T(8,128)S(1)} all-to-all(f32[32,8,128]{2,1,0:T(8,128)S(1)} %get-tuple-element.56), channel_id=1, replica_groups=mesh['patch'=2,'lat'=8,'lon'=16] {'patch','lon'}, dimensions={0} | all-to-all | bytes 262144 | tf_op jit(solution)/shard_map/all_to_all | solution.py:514
  54.5 0.6 pack.3
  55.1 12.5 %all_to_all.42.arrived = f32[8,5,8,128]{3,2,1,0:T(8,128)S(1)} all-to-all(f32[8,5,8,128]{3,2,1,0:T(8,128)S(1)} %pack.3), channel_id=1, replica_groups=mesh['patch'=2,'lat'=8,'lon'=16] {'lat'}, dimensions={0} | all-to-all | bytes 327680 | tf_op jit(solution)/shard_map/all_to_all | solution.py:517
  67.6 1.5 %sweep.2 = (f32[6,128,128]{2,1,0:T(8,128)S(1)}, f32[2,128,128]{2,1,0:T(8,128)S(1)}, f32[32,8,128]{2,1,0:T(8,128)S(1)}, f32[1,8,128]{2,1,0:T(8,128)S(1)}, f32[1,8,128]{2,1,0:T(8,128)S(1)}) custom-call(s32[23]{0:T(128)S(1)} %concatenate.25.ints, f32[6,128,128]{2,1,0:T(8,128)S(1)} %get-tuple-element.52.flow, f32[2,128,128]{2,1,0:T(8,128)S(1)} %get-tuple-element.53.pressure, ...), custom_call_target="tpu_custom_call" | custom-call | tf_op jit(solution)/shard_map/sweep/pallas_call | solution.py:457
  69.1 11.5 %all_to_all.43.arrived.chunks_in = f32[32,8,128]{2,1,0:T(8,128)S(1)} all-to-all(f32[32,8,128]{2,1,0:T(8,128)S(1)} %get-tuple-element.61), channel_id=1, replica_groups=mesh['patch'=2,'lat'=8,'lon'=16] {'patch','lon'}, dimensions={0} | all-to-all | bytes 262144 | tf_op jit(solution)/shard_map/all_to_all | solution.py:514
  80.6 0.6 pack.4
  81.2 12.5 %all_to_all.44.arrived = f32[8,5,8,128]{3,2,1,0:T(8,128)S(1)} all-to-all(f32[8,5,8,128]{3,2,1,0:T(8,128)S(1)} %pack.4), channel_id=1, replica_groups=mesh['patch'=2,'lat'=8,'lon'=16] {'lat'}, dimensions={0} | all-to-all | bytes 327680 | tf_op jit(solution)/shard_map/all_to_all | solution.py:517
  93.7 1.5 %sweep.3 = (f32[6,128,128]{2,1,0:T(8,128)S(1)}, f32[2,128,128]{2,1,0:T(8,128)S(1)}, f32[32,8,128]{2,1,0:T(8,128)S(1)}, f32[1,8,128]{2,1,0:T(8,128)S(1)}, f32[1,8,128]{2,1,0:T(8,128)S(1)}) custom-call(s32[23]{0:T(128)S(1)} %concatenate.25.ints, f32[6,128,128]{2,1,0:T(8,128)S(1)} %get-tuple-element.59.flow, f32[2,128,128]{2,1,0:T(8,128)S(1)} %get-tuple-element.60.pressure, ...), custom_call_target="tpu_custom_call" | custom-call | tf_op jit(solution)/shard_map/sweep/pallas_call | solution.py:457
  95.2 11.5 %all_to_all.45.arrived.chunks_in = f32[32,8,128]{2,1,0:T(8,128)S(1)} all-to-all(f32[32,8,128]{2,1,0:T(8,128)S(1)} %get-tuple-element.66), channel_id=1, replica_groups=mesh['patch'=2,'lat'=8,'lon'=16] {'patch','lon'}, dimensions={0} | all-to-all | bytes 262144 | tf_op jit(solution)/shard_map/all_to_all | solution.py:514
  106.8 0.6 pack.5
  107.3 12.5 %all_to_all.46.arrived = f32[8,5,8,128]{3,2,1,0:T(8,128)S(1)} all-to-all(f32[8,5,8,128]{3,2,1,0:T(8,128)S(1)} %pack.5), channel_id=1, replica_groups=mesh['patch'=2,'lat'=8,'lon'=16] {'lat'}, dimensions={0} | all-to-all | bytes 327680 | tf_op jit(solution)/shard_map/all_to_all | solution.py:517
  119.9 2.1 %final.1 = (f32[6,128,128]{2,1,0:T(8,128)}, f32[2,128,128]{2,1,0:T(8,128)}, f32[2,128,128]{2,1,0:T(8,128)}) custom-call(s32[23]{0:T(128)S(1)} %concatenate.25.ints, f32[6,128,128]{2,1,0:T(8,128)S(1)} %get-tuple-element.64.flow, f32[2,128,128]{2,1,0:T(8,128)S(1)} %get-tuple-element.65.pressure, f32[8,2,128,128]{3,2,1,0:T(8,128)S(1)} %coefficients.1.coef, ...), custom_call_target="tpu_custom_call" | custom-call | tf_op jit(solution)/shard_map/final/pallas_call | solution.py:457
  (3 shorter events, 0.0 us)
Async XLA Ops:
  21.6 9.1 %copy-start = (f32[1,2,128,128]{3,2,1,0:T(8,128)S(1)}, f32[1,2,128,128]{3,2,1,0:T(8,128)}, u32[]{:S(2)}) copy-start(f32[1,2,128,128]{3,2,1,0:T(8,128)} %param.10) | copy-start | bytes 393220
  21.6 9.1 %copy-start.2 = (f32[1,2,128,128]{3,2,1,0:T(8,128)S(1)}, f32[1,2,128,128]{3,2,1,0:T(8,128)}, u32[]{:S(2)}) copy-start(f32[1,2,128,128]{3,2,1,0:T(8,128)} %param.11) | copy-start | bytes 393220
  21.6 19.3 %all-to-all-start.1 = ((f32[8,7,8,128]{3,2,1,0:T(8,128)}), f32[8,7,8,128]{3,2,1,0:T(8,128)S(1)}, u32[]{:S(2)}, u32[]{:S(2)}) async-start(f32[8,7,8,128]{3,2,1,0:T(8,128)} %sort.1), calls=%async_computation.1 | async-start | bytes 458752 | tf_op jit(solution)/shard_map/all_to_all | solution.py:517
  31.6 9.3 %copy-start.1 = (f32[3,1,2,128,128]{4,3,2,1,0:T(8,128)S(1)}, f32[3,1,2,128,128]{4,3,2,1,0:T(8,128)}, u32[]{:S(2)}) copy-start(f32[3,1,2,128,128]{4,3,2,1,0:T(8,128)} %param.8) | copy-start | bytes 1179652
  31.6 9.3 %copy-start.3 = (f32[1,2,128,128]{3,2,1,0:T(8,128)S(1)}, f32[1,2,128,128]{3,2,1,0:T(8,128)}, u32[]{:S(2)}) copy-start(f32[1,2,128,128]{3,2,1,0:T(8,128)} %param.9) | copy-start | bytes 393220

commit v11 on v10

--- a/solution.py
+++ b/solution.py
@@ -90,34 +90,41 @@
 ):
     copies = Copies(sems)
     copies.start(slots, named)
+    copies.start(friction, own.at[10:12])
+    copies.start(heat, own.at[8:10])
+    copies.start(pressure, own.at[6:8])
     copies.start(flow, own.at[0:6])
-    copies.start(pressure, own.at[6:8])
-    copies.start(heat, own.at[8:10])
-    copies.start(friction, own.at[10:12])
     row[8:16, :] = jnp.broadcast_to((ints[RECEIVER] + 1).astype(F32), (8, CELLS))
     chunks[...] = jnp.zeros(chunks.shape, F32)
     north[...] = jnp.zeros(north.shape, F32)
     south[...] = jnp.zeros(south.shape, F32)
-    copies.wait()
+    copies.wait(0, 1)
     mine = jnp.broadcast_to(named[...], (8, CELLS)) == sublanes()
     place = jnp.sum(jnp.where(mine, lanes() + 1, 0).astype(F32), axis=1, keepdims=True)
     places[...] = jnp.broadcast_to(place, (8, CELLS))
-    for f in range(10):
-        to = f if f < 8 else f + 1
-        row[to : to + 1, :] = own[f, pl.ds(ints[ROW], 1), :]
-    for b in range(TILES):
-        gathered = jnp.zeros((8, CELLS), F32)
-        for f in range(PLANES):
-            gathered = gather_edge(own[f, tile(b), :], f, gathered)
-        cols_s[tile(b), :] = gathered
+
+    def collect(first, last):
+        for b in range(TILES):
+            gathered = jnp.zeros((8, CELLS), F32) if last == PLANES else cols_s[tile(b), :]
+            for f in range(first, last):
+                gathered = gather_edge(own[f, tile(b), :], f, gathered)
+            cols_s[tile(b), :] = gathered
+        for f in range(first, last):
+            if f < 10:
+                to = f if f < 8 else f + 1
+                row[to : to + 1, :] = own[f, pl.ds(ints[ROW], 1), :]
+            n, at = divmod(f, 8)
+            north[n, at : at + 1, :] = own[f, 0:1, :]
+            south[n, at : at + 1, :] = own[f, CELLS - 1 : CELLS, :]
+
+    copies.wait(1, 4)
+    collect(6, PLANES)
+    copies.wait(4)
+    collect(0, 6)
     rows_s[...] = cols_s[...].T
     chunks[ints[CHUNK]] = row[...]
     chunks[ints[TO_WEST]] = rows_s[every_second(1, 16), :]
     chunks[ints[TO_EAST]] = rows_s[every_second(0, 16), :]
-    for f in range(PLANES):
-        n, at = divmod(f, 8)
-        north[n, at : at + 1, :] = own[f, 0:1, :]
-        south[n, at : at + 1, :] = own[f, CELLS - 1 : CELLS, :]
 
 
 def pack_kernel(table, arrived, north, south, out):
@@ -192,17 +199,13 @@
             high[side, :, cut], low[side, :, cut] = split(chosen[2 * side + term])
 
 
-def blend(ints, blocks_of, high, low, ghosts):
-    for n, (first, last) in enumerate(((NORTH, SOUTH), (WEST, EAST))):
-        count = ghosts.shape[1]
-        ghosts[n] = jnp.zeros((count, CELLS), F32)
-
-        @pl.when(ints[first] + ints[last] > 0)
-        def _():
-            block = jnp.concatenate([blocks_of(2 * n + t) for t in range(2)], axis=1)
-            b_high, b_low = split(block)
-            both = times(jnp.concatenate([b_high, b_low], axis=0), high[n])
-            ghosts[n] = both[0:count] + both[count:] + times(b_high, low[n])
+def blend(blocks_of, high, low, ghosts):
+    count = ghosts.shape[1]
+    for n in range(2):
+        block = jnp.concatenate([blocks_of(2 * n + t) for t in range(2)], axis=1)
+        b_high, b_low = split(block)
+        both = times(jnp.concatenate([b_high, b_low], axis=0), high[n])
+        ghosts[n] = both[0:count] + both[count:] + times(b_high, low[n])
 
 
 def edge_ghosts(ints, arrived, chunks, ghosts, slot, rows, of):
@@ -305,7 +308,7 @@
         ]
         return jnp.concatenate([rows, *warm, jnp.zeros((6, CELLS), F32)], axis=0)
 
-    blend(ints, block, high, low, sides)
+    blend(block, high, low, sides)
     found = edge_ghosts(ints, arrived, chunks, sides, SLOTS, slice(0, 8), slice(0, 8))
     for n in range(4):
         ghosts[n] = found[n]
@@ -531,6 +534,7 @@
         keep=(2,),
         pin=(0,),
     )
+    packed, places = lax.optimization_barrier((packed, places))
     arrived = along(packed)
 
     (table,) = call(

time: 123 us -> 122 us (level)
  no operation moved by 1% of the time
where the time goes in v11:
time: 122 us; the launch traced here: 121 us
  blocking collectives  87.7 us (72%)
  Pallas kernels  15.2 us (12%)
  starting transfers between devices  8.61 us (7%)
  waiting for transfers between devices  6.4 us (5%)
  between operations  2.09 us (2%)
    all_to_all x4, blocking collectives, across(): return lax.all_to_all(chunks, ('patch', 'lon'), 0, 0, tiled=True)  50.1 us
    all_to_all x3, blocking collectives, along(): return lax.all_to_all(packed, 'lat', 0, 0, tiled=True)  37.6 us
    pallas_call x12, Pallas kernels, call(): pl.pallas_call(kernel, out_shape=outs, in_specs=specs, out_specs=out_spec...  15.2 us
    all_to_all x1, starting transfers between devices, along(): return lax.all_to_all(packed, 'lat', 0, 0, tiled=True)  8.61 us
    all_to_all x1, waiting for transfers between devices, along(): return lax.all_to_all(packed, 'lat', 0, 0, tiled=True)  6.4 us
  transfers between devices with their start and end apart: 1, of which 1 were waited for; matrix products, arithmetic and copies ran while one was open for 0% of the time, Pallas kernels for 3%

profile of v11, /device:TPU:2, one launch (start us, length us, event | category | flops | bytes accessed | tf_op | source)
XLA Modules:
  0.0 121.3 jit_solution(6296757658139275156)
XLA Ops:
  2.0 0.1 add_add_fusion
  2.0 0.1 add_convert_fusion
  2.1 0.1 concatenate.23.ints
  2.2 2.1 %start.1 = (f32[32,16,128]{2,1,0:T(8,128)S(1)}, f32[2,8,128]{2,1,0:T(8,128)S(1)}, f32[2,8,128]{2,1,0:T(8,128)S(1)}, f32[8,128]{1,0:T(8,128)S(1)}) custom-call(s32[15]{0:T(128)S(1)} %concatenate.23.ints, s32[1,128]{1,0:T(1,128)} %bitcast.42, f32[6,128,128]{2,1,0:T(8,128)} %bitcast.34, f32[2,128,128]{2,1,0:T(8,128)} %bitcast.39, f32[2,128,128]{2,1,0:T(8,128)} %bitcast.30, ...), custom_call_target="tpu_custom_call" | custom-call | tf_op jit(solution)/shard_map/start/pallas_call | solution.py:460
  4.3 15.3 %all_to_all.40.arrived.chunks.chunks_in = f32[32,16,128]{2,1,0:T(8,128)S(1)} all-to-all(f32[32,16,128]{2,1,0:T(8,128)S(1)} %get-tuple-element.40), channel_id=1, replica_groups=mesh['patch'=2,'lat'=8,'lon'=16] {'patch','lon'}, dimensions={0} | all-to-all | bytes 524288 | tf_op jit(solution)/shard_map/all_to_all | solution.py:517
  19.6 0.4 add_reduce_fusion.sent_to
  19.9 1.5 %sort.1 = f32[8,7,8,128]{3,2,1,0:T(8,128)} custom-call(s32[15]{0:T(128)S(1)} %concatenate.23.ints, s32[16]{0:T(128)S(1)} %add_reduce_fusion.sent_to, f32[32,16,128]{2,1,0:T(8,128)S(1)} %all_to_all.40.arrived.chunks.chunks_in, f32[2,8,128]{2,1,0:T(8,128)S(1)} %get-tuple-element.45.north, f32[2,8,128]{2,1,0:T(8,128)S(1)} %get-tuple-element.46.south), custom_call_target="tpu_custom_call" | custom-call | tf_op jit(solution)/shard_map/sort/pallas_call | solution.py:460
  21.4 0.1 fusion
  21.6 0.0 copy-start
  21.6 0.0 copy-start.2
  21.6 8.6 %all-to-all-start.1 = ((f32[8,7,8,128]{3,2,1,0:T(8,128)}), f32[8,7,8,128]{3,2,1,0:T(8,128)S(1)}, u32[]{:S(2)}, u32[]{:S(2)}) async-start(f32[8,7,8,128]{3,2,1,0:T(8,128)} %sort.1), calls=%async_computation.1 | async-start | bytes 458752 | tf_op jit(solution)/shard_map/all_to_all | solution.py:520
  30.2 0.1 select_reduce_fusion.1
  30.3 0.1 and_select_fusion
  30.4 0.2 convert_reduce_fusion
  30.6 0.1 concatenate.25.ints
  30.7 0.0 copy-done
  30.7 0.0 copy-done.2
  30.7 0.8 coefficients.1.coef
  31.6 0.0 copy-start.1
  31.6 0.0 copy-start.3
  31.6 1.6 %weights.1 = (bf16[2,128,256]{2,1,0:T(8,128)(2,1)S(1)}, bf16[2,128,256]{2,1,0:T(8,128)(2,1)S(1)}) custom-call(s32[23]{0:T(128)S(1)} %concatenate.25.ints, f32[8,128,128]{2,1,0:T(8,128)} %bitcast.41), custom_call_target="tpu_custom_call" | custom-call | tf_op jit(solution)/shard_map/weights/pallas_call | solution.py:460
  33.2 1.3 %table.1 = s32[34]{0:T(128)S(1)} custom-call(s32[15]{0:T(128)S(1)} %concatenate.23.ints, s32[16]{0:T(128)S(1)} %add_reduce_fusion.sent_to), custom_call_target="tpu_custom_call" | custom-call | tf_op jit(solution)/shard_map/table/pallas_call | solution.py:460
  34.5 6.4 %all-to-all-done.1.arrived = f32[8,7,8,128]{3,2,1,0:T(8,128)S(1)} async-done(((f32[8,7,8,128]{3,2,1,0:T(8,128)}), f32[8,7,8,128]{3,2,1,0:T(8,128)S(1)}, u32[]{:S(2)}, u32[]{:S(2)}) %all-to-all-start.1) | async-done | bytes 229408 | tf_op jit(solution)/shard_map/all_to_all | solution.py:520
  40.9 0.0 copy-done.1
  40.9 0.0 copy-done.3
  40.9 1.4 %first_sweep.1 = (f32[6,128,128]{2,1,0:T(8,128)S(1)}, f32[2,128,128]{2,1,0:T(8,128)S(1)}, f32[32,8,128]{2,1,0:T(8,128)S(1)}, f32[1,8,128]{2,1,0:T(8,128)S(1)}, f...) custom-call(s32[23]{0:T(128)S(1)} %concatenate.25.ints, ...), custom_call_target="tpu_custom_call" | custom-call | tf_op jit(solution)/shard_map/first_sweep/pallas_call | solution.py:460
  42.3 12.0 %all_to_all.41.arrived.chunks_in = f32[32,8,128]{2,1,0:T(8,128)S(1)} all-to-all(f32[32,8,128]{2,1,0:T(8,128)S(1)} %get-tuple-element.60), channel_id=1, replica_groups=mesh['patch'=2,'lat'=8,'lon'=16] {'patch','lon'}, dimensions={0} | all-to-all | bytes 262144 | tf_op jit(solution)/shard_map/all_to_all | solution.py:517
  54.3 0.6 pack.3
  54.8 12.5 %all_to_all.42.arrived = f32[8,5,8,128]{3,2,1,0:T(8,128)S(1)} all-to-all(f32[8,5,8,128]{3,2,1,0:T(8,128)S(1)} %pack.3), channel_id=1, replica_groups=mesh['patch'=2,'lat'=8,'lon'=16] {'lat'}, dimensions={0} | all-to-all | bytes 327680 | tf_op jit(solution)/shard_map/all_to_all | solution.py:520
  67.4 1.4 %sweep.2 = (f32[6,128,128]{2,1,0:T(8,128)S(1)}, f32[2,128,128]{2,1,0:T(8,128)S(1)}, f32[32,8,128]{2,1,0:T(8,128)S(1)}, f32[1,8,128]{2,1,0:T(8,128)S(1)}, f32[1,8,128]{2,1,0:T(8,128)S(1)}) custom-call(s32[23]{0:T(128)S(1)} %concatenate.25.ints, f32[6,128,128]{2,1,0:T(8,128)S(1)} %get-tuple-element.56.flow, f32[2,128,128]{2,1,0:T(8,128)S(1)} %get-tuple-element.57.pressure, ...), custom_call_target="tpu_custom_call" | custom-call | tf_op jit(solution)/shard_map/sweep/pallas_call | solution.py:460
  68.8 11.4 %all_to_all.43.arrived.chunks_in = f32[32,8,128]{2,1,0:T(8,128)S(1)} all-to-all(f32[32,8,128]{2,1,0:T(8,128)S(1)} %get-tuple-element.65), channel_id=1, replica_groups=mesh['patch'=2,'lat'=8,'lon'=16] {'patch','lon'}, dimensions={0} | all-to-all | bytes 262144 | tf_op jit(solution)/shard_map/all_to_all | solution.py:517
  80.2 0.6 pack.4
  80.8 12.5 %all_to_all.44.arrived = f32[8,5,8,128]{3,2,1,0:T(8,128)S(1)} all-to-all(f32[8,5,8,128]{3,2,1,0:T(8,128)S(1)} %pack.4), channel_id=1, replica_groups=mesh['patch'=2,'lat'=8,'lon'=16] {'lat'}, dimensions={0} | all-to-all | bytes 327680 | tf_op jit(solution)/shard_map/all_to_all | solution.py:520
  93.3 1.4 %sweep.3 = (f32[6,128,128]{2,1,0:T(8,128)S(1)}, f32[2,128,128]{2,1,0:T(8,128)S(1)}, f32[32,8,128]{2,1,0:T(8,128)S(1)}, f32[1,8,128]{2,1,0:T(8,128)S(1)}, f32[1,8,128]{2,1,0:T(8,128)S(1)}) custom-call(s32[23]{0:T(128)S(1)} %concatenate.25.ints, f32[6,128,128]{2,1,0:T(8,128)S(1)} %get-tuple-element.63.flow, f32[2,128,128]{2,1,0:T(8,128)S(1)} %get-tuple-element.64.pressure, ...), custom_call_target="tpu_custom_call" | custom-call | tf_op jit(solution)/shard_map/sweep/pallas_call | solution.py:460
  94.7 11.4 %all_to_all.45.arrived.chunks_in = f32[32,8,128]{2,1,0:T(8,128)S(1)} all-to-all(f32[32,8,128]{2,1,0:T(8,128)S(1)} %get-tuple-element.70), channel_id=1, replica_groups=mesh['patch'=2,'lat'=8,'lon'=16] {'patch','lon'}, dimensions={0} | all-to-all | bytes 262144 | tf_op jit(solution)/shard_map/all_to_all | solution.py:517
  106.1 0.6 pack.5
  106.7 12.5 %all_to_all.46.arrived = f32[8,5,8,128]{3,2,1,0:T(8,128)S(1)} all-to-all(f32[8,5,8,128]{3,2,1,0:T(8,128)S(1)} %pack.5), channel_id=1, replica_groups=mesh['patch'=2,'lat'=8,'lon'=16] {'lat'}, dimensions={0} | all-to-all | bytes 327680 | tf_op jit(solution)/shard_map/all_to_all | solution.py:520
  119.2 2.1 %final.1 = (f32[6,128,128]{2,1,0:T(8,128)}, f32[2,128,128]{2,1,0:T(8,128)}, f32[2,128,128]{2,1,0:T(8,128)}) custom-call(s32[23]{0:T(128)S(1)} %concatenate.25.ints, f32[6,128,128]{2,1,0:T(8,128)S(1)} %get-tuple-element.68.flow, f32[2,128,128]{2,1,0:T(8,128)S(1)} %get-tuple-element.69.pressure, f32[8,2,128,128]{3,2,1,0:T(8,128)S(1)} %coefficients.1.coef, ...), custom_call_target="tpu_custom_call" | custom-call | tf_op jit(solution)/shard_map/final/pallas_call | solution.py:460
  (3 shorter events, 0.0 us)
Async XLA Ops:
  21.6 9.2 %copy-start = (f32[1,2,128,128]{3,2,1,0:T(8,128)S(1)}, f32[1,2,128,128]{3,2,1,0:T(8,128)}, u32[]{:S(2)}) copy-start(f32[1,2,128,128]{3,2,1,0:T(8,128)} %param.10) | copy-start | bytes 393220
  21.6 9.2 %copy-start.2 = (f32[1,2,128,128]{3,2,1,0:T(8,128)S(1)}, f32[1,2,128,128]{3,2,1,0:T(8,128)}, u32[]{:S(2)}) copy-start(f32[1,2,128,128]{3,2,1,0:T(8,128)} %param.11) | copy-start | bytes 393220
  21.6 19.3 %all-to-all-start.1 = ((f32[8,7,8,128]{3,2,1,0:T(8,128)}), f32[8,7,8,128]{3,2,1,0:T(8,128)S(1)}, u32[]{:S(2)}, u32[]{:S(2)}) async-start(f32[8,7,8,128]{3,2,1,0:T(8,128)} %sort.1), calls=%async_computation.1 | async-start | bytes 458752 | tf_op jit(solution)/shard_map/all_to_all | solution.py:520
  31.6 9.3 %copy-start.1 = (f32[3,1,2,128,128]{4,3,2,1,0:T(8,128)S(1)}, f32[3,1,2,128,128]{4,3,2,1,0:T(8,128)}, u32[]{:S(2)}) copy-start(f32[3,1,2,128,128]{4,3,2,1,0:T(8,128)} %param.8) | copy-start | bytes 1179652
  31.6 9.3 %copy-start.3 = (f32[1,2,128,128]{3,2,1,0:T(8,128)S(1)}, f32[1,2,128,128]{3,2,1,0:T(8,128)}, u32[]{:S(2)}) copy-start(f32[1,2,128,128]{3,2,1,0:T(8,128)} %param.9) | copy-start | bytes 393220

commit v12 on v11

--- a/solution.py
+++ b/solution.py
@@ -90,10 +90,11 @@
 ):
     copies = Copies(sems)
     copies.start(slots, named)
-    copies.start(friction, own.at[10:12])
-    copies.start(heat, own.at[8:10])
-    copies.start(pressure, own.at[6:8])
-    copies.start(flow, own.at[0:6])
+    for n, source in ((10, friction), (8, heat), (6, pressure)):
+        for k in range(2):
+            copies.start(source.at[k], own.at[n + k])
+    for n in range(6):
+        copies.start(flow.at[n], own.at[n])
     row[8:16, :] = jnp.broadcast_to((ints[RECEIVER] + 1).astype(F32), (8, CELLS))
     chunks[...] = jnp.zeros(chunks.shape, F32)
     north[...] = jnp.zeros(north.shape, F32)
@@ -117,9 +118,9 @@
             north[n, at : at + 1, :] = own[f, 0:1, :]
             south[n, at : at + 1, :] = own[f, CELLS - 1 : CELLS, :]
 
-    copies.wait(1, 4)
+    copies.wait(1, 7)
     collect(6, PLANES)
-    copies.wait(4)
+    copies.wait(7)
     collect(0, 6)
     rows_s[...] = cols_s[...].T
     chunks[ints[CHUNK]] = row[...]
@@ -393,13 +394,15 @@
 
     ghost_columns(heat_ghosts[2], heat_ghosts[3], rows_s, heat_cols_s)
     fill_ghosts(ints, arrived, chunks_in, high, low, sides, ghosts, cols_s, rows_s)
+    copies = Copies(sems)
     for b in range(TILES):
         new = relaxed(planes, coef, ends, ghosts, cols_s[tile(b), :], b)
         for f in range(8):
             answer[f, tile(b), :] = new[f]
-    copies = Copies(sems)
-    copies.start(answer.at[0:6], flow_out)
-    copies.start(answer.at[6:8], pressure_out)
+        if b % 4 == 3:
+            part = pl.ds(8 * (b - 3), 32)
+            copies.start(answer.at[0:6, part, :], flow_out.at[:, part, :])
+            copies.start(answer.at[6:8, part, :], pressure_out.at[:, part, :])
     for b in range(TILES):
         layers = [
             around(
@@ -423,7 +426,9 @@
                 advect = advect + jnp.minimum(speed, 0.0) * (plus - here)
             spread = (up + down) + (left + right) + (under + over) - 6.0 * here
             warm[k, tile(b), :] = here + 0.1 * (spread - advect)
-    copies.start(warm, heat_out)
+        if b % 8 == 7:
+            part = pl.ds(8 * (b - 7), 64)
+            copies.start(warm.at[:, part, :], heat_out.at[:, part, :])
     copies.wait()
 
 
@@ -507,7 +512,7 @@
         [shape(tiles, 16, CELLS), shape(2, 8, CELLS), shape(2, 8, CELLS), shape(8, CELLS)],
         (first, shift_filled_by_lane.reshape(1, CELLS), flow, pressure, heat, friction),
         [scratch(PLANES, CELLS, CELLS), pltpu.VMEM((1, CELLS), jnp.int32), scratch(16, CELLS)]
-        + [square, square, semaphores(5)],
+        + [square, square, semaphores(13)],
         "start",
         specs=[SMEM] + [HBM] * 5,
         pin=(0,),
@@ -534,7 +539,6 @@
         keep=(2,),
         pin=(0,),
     )
-    packed, places = lax.optimization_barrier((packed, places))
     arrived = along(packed)
 
     (table,) = call(
@@ -546,8 +550,7 @@
         specs=[SMEM, SMEM],
         out_specs=[SMEM],
     )
-    arrived, table = lax.optimization_barrier((arrived, table))
-
+    table, places = lax.optimization_barrier((table, places))
     own = places[:, 0].astype(jnp.int32) - 1
     pick = jnp.concatenate(
         [jnp.where(lat > 0, own[2:4], own[0:2]), jnp.where(lon > 0, own[6:8], own[4:6])]
@@ -556,6 +559,7 @@
     slot = jnp.sum((same & (own[None] < pick[:, None])).astype(jnp.int32), axis=1)
     ints = [first, jnp.maximum(pick, 0) // n_lon, jnp.minimum(slot, SLOTS - 1)]
     ints = jnp.concatenate(ints).astype(jnp.int32)
+    arrived, table, ints = lax.optimization_barrier((arrived, table, ints))
 
     joined = jax.ShapeDtypeStruct((2, CELLS, 2 * CELLS), jnp.bfloat16)
     high, low = call(
@@ -616,7 +620,7 @@
         state + [shape(2, CELLS, CELLS)],
         (ints, flow, pressure, coef, ends, arrived, came, high, low, heat, heat_ghosts),
         [sides, ghosts, square, square, square]
-        + [scratch(8, CELLS, CELLS), scratch(2, CELLS, CELLS), semaphores(3)],
+        + [scratch(8, CELLS, CELLS), scratch(2, CELLS, CELLS), semaphores(10)],
         "final",
         out_specs=[HBM] * 3,
         limit=8,

time: 122 us -> 126 us (1.033)
  waiting for transfers between devices: 6.4 us -> 10.1 us
    all_to_all x1, waiting for transfers between devices: 6.4 us -> 10.1 us  [along(): return lax.all_to_all(packed, 'lat', 0, 0, tiled=True)]
  transfers between devices with their start and end apart: 1 -> 1, of which waited for: 1 -> 1; matrix products, arithmetic and copies ran while one was open for 0% -> 0% of each run, Pallas kernels for 3% -> 0%
where the time goes in v12:
time: 126 us; the launch traced here: 125 us
  blocking collectives  87.7 us (70%)
  Pallas kernels  15.4 us (12%)
  waiting for transfers between devices  10.1 us (8%)
  starting transfers between devices  8.61 us (7%)
  between operations  2.1 us (2%)
    all_to_all x4, blocking collectives, across(): return lax.all_to_all(chunks, ('patch', 'lon'), 0, 0, tiled=True)  50.1 us
    all_to_all x3, blocking collectives, along(): return lax.all_to_all(packed, 'lat', 0, 0, tiled=True)  37.6 us
    pallas_call x12, Pallas kernels, call(): pl.pallas_call(kernel, out_shape=outs, in_specs=specs, out_specs=out_spec...  15.4 us
    all_to_all x1, waiting for transfers between devices, along(): return lax.all_to_all(packed, 'lat', 0, 0, tiled=True)  10.1 us
    all_to_all x1, starting transfers between devices, along(): return lax.all_to_all(packed, 'lat', 0, 0, tiled=True)  8.61 us
  transfers between devices with their start and end apart: 1, of which 1 were waited for; matrix products, arithmetic and copies ran while one was open for 0% of the time, Pallas kernels for 0%

profile of v12, /device:TPU:2, one launch (start us, length us, event | category | flops | bytes accessed | tf_op | source)
XLA Modules:
  0.0 125.2 jit_solution(8177274618746293880)
XLA Ops:
  2.0 0.1 add_add_fusion
  2.0 0.1 add_convert_fusion
  2.1 0.1 concatenate.23.ints
  2.2 2.1 %start.1 = (f32[32,16,128]{2,1,0:T(8,128)S(1)}, f32[2,8,128]{2,1,0:T(8,128)S(1)}, f32[2,8,128]{2,1,0:T(8,128)S(1)}, f32[8,128]{1,0:T(8,128)S(1)}) custom-call(s32[15]{0:T(128)S(1)} %concatenate.23.ints, s32[1,128]{1,0:T(1,128)} %bitcast.42, f32[6,128,128]{2,1,0:T(8,128)} %bitcast.34, f32[2,128,128]{2,1,0:T(8,128)} %bitcast.39, f32[2,128,128]{2,1,0:T(8,128)} %bitcast.30, ...), custom_call_target="tpu_custom_call" | custom-call | tf_op jit(solution)/shard_map/start/pallas_call | solution.py:465
  4.3 15.3 %all_to_all.40.arrived.chunks.chunks_in = f32[32,16,128]{2,1,0:T(8,128)S(1)} all-to-all(f32[32,16,128]{2,1,0:T(8,128)S(1)} %get-tuple-element.41), channel_id=1, replica_groups=mesh['patch'=2,'lat'=8,'lon'=16] {'patch','lon'}, dimensions={0} | all-to-all | bytes 524288 | tf_op jit(solution)/shard_map/all_to_all | solution.py:522
  19.6 0.4 add_reduce_fusion.sent_to
  20.0 1.5 %sort.1 = f32[8,7,8,128]{3,2,1,0:T(8,128)} custom-call(s32[15]{0:T(128)S(1)} %concatenate.23.ints, s32[16]{0:T(128)S(1)} %add_reduce_fusion.sent_to, f32[32,16,128]{2,1,0:T(8,128)S(1)} %all_to_all.40.arrived.chunks.chunks_in, f32[2,8,128]{2,1,0:T(8,128)S(1)} %get-tuple-element.45.north, f32[2,8,128]{2,1,0:T(8,128)S(1)} %get-tuple-element.46.south), custom_call_target="tpu_custom_call" | custom-call | tf_op jit(solution)/shard_map/sort/pallas_call | solution.py:465
  21.5 1.3 %table.1 = s32[34]{0:T(128)S(1)} custom-call(s32[15]{0:T(128)S(1)} %concatenate.23.ints, s32[16]{0:T(128)S(1)} %add_reduce_fusion.sent_to), custom_call_target="tpu_custom_call" | custom-call | tf_op jit(solution)/shard_map/table/pallas_call | solution.py:465
  22.8 0.1 fusion
  22.9 0.0 copy-start
  22.9 0.0 copy-start.2
  22.9 8.6 %all-to-all-start.1 = ((f32[8,7,8,128]{3,2,1,0:T(8,128)}), f32[8,7,8,128]{3,2,1,0:T(8,128)S(1)}, u32[]{:S(2)}, u32[]{:S(2)}) async-start(f32[8,7,8,128]{3,2,1,0:T(8,128)} %sort.1), calls=%async_computation.1 | async-start | bytes 458752 | tf_op jit(solution)/shard_map/all_to_all | solution.py:525
  31.5 0.1 select_reduce_fusion.1
  31.7 0.1 and_select_fusion
  31.8 0.2 convert_reduce_fusion
  32.0 0.1 concatenate.25.ints
  32.1 10.1 %all-to-all-done.1.arrived = f32[8,7,8,128]{3,2,1,0:T(8,128)S(1)} async-done(((f32[8,7,8,128]{3,2,1,0:T(8,128)}), f32[8,7,8,128]{3,2,1,0:T(8,128)S(1)}, u32[]{:S(2)}, u32[]{:S(2)}) %all-to-all-start.1) | async-done | bytes 229408 | tf_op jit(solution)/shard_map/all_to_all | solution.py:525
  42.2 0.0 copy-done
  42.2 0.0 copy-done.2
  42.2 0.8 coefficients.1.coef
  43.0 0.0 copy-start.1
  43.0 0.0 copy-start.3
  43.0 1.6 %weights.1 = (bf16[2,128,256]{2,1,0:T(8,128)(2,1)S(1)}, bf16[2,128,256]{2,1,0:T(8,128)(2,1)S(1)}) custom-call(s32[23]{0:T(128)S(1)} %concatenate.25.ints, f32[8,128,128]{2,1,0:T(8,128)} %bitcast.41), custom_call_target="tpu_custom_call" | custom-call | tf_op jit(solution)/shard_map/weights/pallas_call | solution.py:465
  44.6 0.0 copy-done.1
  44.6 0.0 copy-done.3
  44.6 1.5 %first_sweep.1 = (f32[6,128,128]{2,1,0:T(8,128)S(1)}, f32[2,128,128]{2,1,0:T(8,128)S(1)}, f32[32,8,128]{2,1,0:T(8,128)S(1)}, f32[1,8,128]{2,1,0:T(8,128)S(1)}, f...) custom-call(s32[23]{0:T(128)S(1)} %concatenate.25.ints, ...), custom_call_target="tpu_custom_call" | custom-call | tf_op jit(solution)/shard_map/first_sweep/pallas_call | solution.py:465
  46.1 12.0 %all_to_all.41.arrived.chunks_in = f32[32,8,128]{2,1,0:T(8,128)S(1)} all-to-all(f32[32,8,128]{2,1,0:T(8,128)S(1)} %get-tuple-element.62), channel_id=1, replica_groups=mesh['patch'=2,'lat'=8,'lon'=16] {'patch','lon'}, dimensions={0} | all-to-all | bytes 262144 | tf_op jit(solution)/shard_map/all_to_all | solution.py:522
  58.1 0.6 pack.3
  58.7 12.5 %all_to_all.42.arrived = f32[8,5,8,128]{3,2,1,0:T(8,128)S(1)} all-to-all(f32[8,5,8,128]{3,2,1,0:T(8,128)S(1)} %pack.3), channel_id=1, replica_groups=mesh['patch'=2,'lat'=8,'lon'=16] {'lat'}, dimensions={0} | all-to-all | bytes 327680 | tf_op jit(solution)/shard_map/all_to_all | solution.py:525
  71.2 1.4 %sweep.2 = (f32[6,128,128]{2,1,0:T(8,128)S(1)}, f32[2,128,128]{2,1,0:T(8,128)S(1)}, f32[32,8,128]{2,1,0:T(8,128)S(1)}, f32[1,8,128]{2,1,0:T(8,128)S(1)}, f32[1,8,128]{2,1,0:T(8,128)S(1)}) custom-call(s32[23]{0:T(128)S(1)} %concatenate.25.ints, f32[6,128,128]{2,1,0:T(8,128)S(1)} %get-tuple-element.58.flow, f32[2,128,128]{2,1,0:T(8,128)S(1)} %get-tuple-element.59.pressure, ...), custom_call_target="tpu_custom_call" | custom-call | tf_op jit(solution)/shard_map/sweep/pallas_call | solution.py:465
  72.7 11.4 %all_to_all.43.arrived.chunks_in = f32[32,8,128]{2,1,0:T(8,128)S(1)} all-to-all(f32[32,8,128]{2,1,0:T(8,128)S(1)} %get-tuple-element.67), channel_id=1, replica_groups=mesh['patch'=2,'lat'=8,'lon'=16] {'patch','lon'}, dimensions={0} | all-to-all | bytes 262144 | tf_op jit(solution)/shard_map/all_to_all | solution.py:522
  84.1 0.6 pack.4
  84.6 12.5 %all_to_all.44.arrived = f32[8,5,8,128]{3,2,1,0:T(8,128)S(1)} all-to-all(f32[8,5,8,128]{3,2,1,0:T(8,128)S(1)} %pack.4), channel_id=1, replica_groups=mesh['patch'=2,'lat'=8,'lon'=16] {'lat'}, dimensions={0} | all-to-all | bytes 327680 | tf_op jit(solution)/shard_map/all_to_all | solution.py:525
  97.2 1.4 %sweep.3 = (f32[6,128,128]{2,1,0:T(8,128)S(1)}, f32[2,128,128]{2,1,0:T(8,128)S(1)}, f32[32,8,128]{2,1,0:T(8,128)S(1)}, f32[1,8,128]{2,1,0:T(8,128)S(1)}, f32[1,8,128]{2,1,0:T(8,128)S(1)}) custom-call(s32[23]{0:T(128)S(1)} %concatenate.25.ints, f32[6,128,128]{2,1,0:T(8,128)S(1)} %get-tuple-element.65.flow, f32[2,128,128]{2,1,0:T(8,128)S(1)} %get-tuple-element.66.pressure, ...), custom_call_target="tpu_custom_call" | custom-call | tf_op jit(solution)/shard_map/sweep/pallas_call | solution.py:465
  98.6 11.4 %all_to_all.45.arrived.chunks_in = f32[32,8,128]{2,1,0:T(8,128)S(1)} all-to-all(f32[32,8,128]{2,1,0:T(8,128)S(1)} %get-tuple-element.72), channel_id=1, replica_groups=mesh['patch'=2,'lat'=8,'lon'=16] {'patch','lon'}, dimensions={0} | all-to-all | bytes 262144 | tf_op jit(solution)/shard_map/all_to_all | solution.py:522
  110.0 0.6 pack.5
  110.6 12.5 %all_to_all.46.arrived = f32[8,5,8,128]{3,2,1,0:T(8,128)S(1)} all-to-all(f32[8,5,8,128]{3,2,1,0:T(8,128)S(1)} %pack.5), channel_id=1, replica_groups=mesh['patch'=2,'lat'=8,'lon'=16] {'lat'}, dimensions={0} | all-to-all | bytes 327680 | tf_op jit(solution)/shard_map/all_to_all | solution.py:525
  123.1 2.1 %final.1 = (f32[6,128,128]{2,1,0:T(8,128)}, f32[2,128,128]{2,1,0:T(8,128)}, f32[2,128,128]{2,1,0:T(8,128)}) custom-call(s32[23]{0:T(128)S(1)} %concatenate.25.ints, f32[6,128,128]{2,1,0:T(8,128)S(1)} %get-tuple-element.70.flow, f32[2,128,128]{2,1,0:T(8,128)S(1)} %get-tuple-element.71.pressure, f32[8,2,128,128]{3,2,1,0:T(8,128)S(1)} %coefficients.1.coef, ...), custom_call_target="tpu_custom_call" | custom-call | tf_op jit(solution)/shard_map/final/pallas_call | solution.py:465
  (3 shorter events, 0.0 us)
Async XLA Ops:
  22.9 19.3 %copy-start = (f32[1,2,128,128]{3,2,1,0:T(8,128)S(1)}, f32[1,2,128,128]{3,2,1,0:T(8,128)}, u32[]{:S(2)}) copy-start(f32[1,2,128,128]{3,2,1,0:T(8,128)} %param.10) | copy-start | bytes 393220
  22.9 19.3 %copy-start.2 = (f32[1,2,128,128]{3,2,1,0:T(8,128)S(1)}, f32[1,2,128,128]{3,2,1,0:T(8,128)}, u32[]{:S(2)}) copy-start(f32[1,2,128,128]{3,2,1,0:T(8,128)} %param.11) | copy-start | bytes 393220
  22.9 19.3 %all-to-all-start.1 = ((f32[8,7,8,128]{3,2,1,0:T(8,128)}), f32[8,7,8,128]{3,2,1,0:T(8,128)S(1)}, u32[]{:S(2)}, u32[]{:S(2)}) async-start(f32[8,7,8,128]{3,2,1,0:T(8,128)} %sort.1), calls=%async_computation.1 | async-start | bytes 458752 | tf_op jit(solution)/shard_map/all_to_all | solution.py:525
  43.0 1.6 %copy-start.1 = (f32[3,1,2,128,128]{4,3,2,1,0:T(8,128)S(1)}, f32[3,1,2,128,128]{4,3,2,1,0:T(8,128)}, u32[]{:S(2)}) copy-start(f32[3,1,2,128,128]{4,3,2,1,0:T(8,128)} %param.8) | copy-start | bytes 1179652
  43.0 1.6 %copy-start.3 = (f32[1,2,128,128]{3,2,1,0:T(8,128)S(1)}, f32[1,2,128,128]{3,2,1,0:T(8,128)}, u32[]{:S(2)}) copy-start(f32[1,2,128,128]{3,2,1,0:T(8,128)} %param.9) | copy-start | bytes 393220

commit v13 on v11

--- a/solution.py
+++ b/solution.py
@@ -263,35 +263,35 @@
 
 
 def relaxed(planes, coef, ends, ghosts, column, b):
-    at = [
-        around(planes(f), b, ghosts[0, f : f + 1, :], ghosts[1, f : f + 1, :], column, f)
-        for f in range(8)
-    ]
+    def at(f):
+        return around(planes(f), b, ghosts[0, f : f + 1, :], ghosts[1, f : f + 1, :], column, f)
 
     def factor(n, k):
         if b == 0 or b == TILES - 1:
             return ends[n, k, tile(0 if b == 0 else 1), :]
         return coef[n, k, tile(b), :]
 
+    stress = [at(6 + k) for k in range(2)]
+    centre = [stress[k][0] for k in range(2)]
+    slopes = [[centre[1], -centre[0]]]
+    slopes += [[stress[k][n + 1] - stress[k][n] for k in range(2)] for n in (1, 3)]
     new = []
+    divergence = []
     for component in range(3):
+        cells = [at(2 * component + k) for k in range(2)]
         for k in range(2):
-            here, up, down, left, right = at[2 * component + k]
+            here, up, down, left, right = cells[k]
             value = 0.2 * here + factor(0, k) * up + factor(1, k) * down
             value = value + factor(2, k) * left + factor(3, k) * right
-            value = value + factor(4, k) * at[2 * component + 1 - k][0]
+            value = value + factor(4, k) * cells[1 - k][0]
             if component == 0:
                 value = value + factor(6, k)
-                slope = at[7][0] if k == 0 else -at[6][0]
-            elif component == 1:
-                slope = at[6 + k][2] - at[6 + k][1]
+                divergence.append(cells[1][0] if k == 0 else -cells[0][0])
             else:
-                slope = at[6 + k][4] - at[6 + k][3]
-            new.append(value - factor(5, k) * slope)
+                divergence[k] = divergence[k] + (down - up if component == 1 else right - left)
+            new.append(value - factor(5, k) * slopes[component][k])
     for k in range(2):
-        divergence = (at[2 + k][2] - at[2 + k][1]) + (at[4 + k][4] - at[4 + k][3])
-        divergence = divergence + at[1][0] if k == 0 else divergence - at[0][0]
-        new.append(at[6 + k][0] - factor(7, k) * divergence)
+        new.append(centre[k] - factor(7, k) * divergence[k])
     return new
 
 

time: 122 us -> 122 us (level)
  no operation moved by 1% of the time
where the time goes in v13:
time: 122 us; the launch traced here: 121 us
  blocking collectives  87.7 us (72%)
  Pallas kernels  15.2 us (12%)
  starting transfers between devices  8.61 us (7%)
  waiting for transfers between devices  6.4 us (5%)
  between operations  2.1 us (2%)
    all_to_all x4, blocking collectives, across(): return lax.all_to_all(chunks, ('patch', 'lon'), 0, 0, tiled=True)  50.1 us
    all_to_all x3, blocking collectives, along(): return lax.all_to_all(packed, 'lat', 0, 0, tiled=True)  37.6 us
    pallas_call x12, Pallas kernels, call(): pl.pallas_call(kernel, out_shape=outs, in_specs=specs, out_specs=out_spec...  15.2 us
    all_to_all x1, starting transfers between devices, along(): return lax.all_to_all(packed, 'lat', 0, 0, tiled=True)  8.61 us
    all_to_all x1, waiting for transfers between devices, along(): return lax.all_to_all(packed, 'lat', 0, 0, tiled=True)  6.4 us
  transfers between devices with their start and end apart: 1, of which 1 were waited for; matrix products, arithmetic and copies ran while one was open for 0% of the time, Pallas kernels for 3%

profile of v13, /device:TPU:2, one launch (start us, length us, event | category | flops | bytes accessed | tf_op | source)
XLA Modules:
  0.0 121.3 jit_solution(10115991548181145781)
XLA Ops:
  2.0 0.1 add_add_fusion
  2.0 0.1 add_convert_fusion
  2.1 0.1 concatenate.23.ints
  2.2 2.1 %start.1 = (f32[32,16,128]{2,1,0:T(8,128)S(1)}, f32[2,8,128]{2,1,0:T(8,128)S(1)}, f32[2,8,128]{2,1,0:T(8,128)S(1)}, f32[8,128]{1,0:T(8,128)S(1)}) custom-call(s32[15]{0:T(128)S(1)} %concatenate.23.ints, s32[1,128]{1,0:T(1,128)} %bitcast.42, f32[6,128,128]{2,1,0:T(8,128)} %bitcast.34, f32[2,128,128]{2,1,0:T(8,128)} %bitcast.39, f32[2,128,128]{2,1,0:T(8,128)} %bitcast.30, ...), custom_call_target="tpu_custom_call" | custom-call | tf_op jit(solution)/shard_map/start/pallas_call | solution.py:460
  4.3 15.3 %all_to_all.40.arrived.chunks.chunks_in = f32[32,16,128]{2,1,0:T(8,128)S(1)} all-to-all(f32[32,16,128]{2,1,0:T(8,128)S(1)} %get-tuple-element.40), channel_id=1, replica_groups=mesh['patch'=2,'lat'=8,'lon'=16] {'patch','lon'}, dimensions={0} | all-to-all | bytes 524288 | tf_op jit(solution)/shard_map/all_to_all | solution.py:517
  19.6 0.4 add_reduce_fusion.sent_to
  19.9 1.5 %sort.1 = f32[8,7,8,128]{3,2,1,0:T(8,128)} custom-call(s32[15]{0:T(128)S(1)} %concatenate.23.ints, s32[16]{0:T(128)S(1)} %add_reduce_fusion.sent_to, f32[32,16,128]{2,1,0:T(8,128)S(1)} %all_to_all.40.arrived.chunks.chunks_in, f32[2,8,128]{2,1,0:T(8,128)S(1)} %get-tuple-element.45.north, f32[2,8,128]{2,1,0:T(8,128)S(1)} %get-tuple-element.46.south), custom_call_target="tpu_custom_call" | custom-call | tf_op jit(solution)/shard_map/sort/pallas_call | solution.py:460
  21.4 0.1 fusion
  21.6 0.0 copy-start
  21.6 0.0 copy-start.2
  21.6 8.6 %all-to-all-start.1 = ((f32[8,7,8,128]{3,2,1,0:T(8,128)}), f32[8,7,8,128]{3,2,1,0:T(8,128)S(1)}, u32[]{:S(2)}, u32[]{:S(2)}) async-start(f32[8,7,8,128]{3,2,1,0:T(8,128)} %sort.1), calls=%async_computation.1 | async-start | bytes 458752 | tf_op jit(solution)/shard_map/all_to_all | solution.py:520
  30.2 0.1 select_reduce_fusion.1
  30.3 0.1 and_select_fusion
  30.4 0.2 convert_reduce_fusion
  30.6 0.1 concatenate.25.ints
  30.7 0.0 copy-done
  30.7 0.0 copy-done.2
  30.7 0.8 coefficients.1.coef
  31.6 0.0 copy-start.1
  31.6 0.0 copy-start.3
  31.6 1.6 %weights.1 = (bf16[2,128,256]{2,1,0:T(8,128)(2,1)S(1)}, bf16[2,128,256]{2,1,0:T(8,128)(2,1)S(1)}) custom-call(s32[23]{0:T(128)S(1)} %concatenate.25.ints, f32[8,128,128]{2,1,0:T(8,128)} %bitcast.41), custom_call_target="tpu_custom_call" | custom-call | tf_op jit(solution)/shard_map/weights/pallas_call | solution.py:460
  33.2 1.3 %table.1 = s32[34]{0:T(128)S(1)} custom-call(s32[15]{0:T(128)S(1)} %concatenate.23.ints, s32[16]{0:T(128)S(1)} %add_reduce_fusion.sent_to), custom_call_target="tpu_custom_call" | custom-call | tf_op jit(solution)/shard_map/table/pallas_call | solution.py:460
  34.5 6.4 %all-to-all-done.1.arrived = f32[8,7,8,128]{3,2,1,0:T(8,128)S(1)} async-done(((f32[8,7,8,128]{3,2,1,0:T(8,128)}), f32[8,7,8,128]{3,2,1,0:T(8,128)S(1)}, u32[]{:S(2)}, u32[]{:S(2)}) %all-to-all-start.1) | async-done | bytes 229408 | tf_op jit(solution)/shard_map/all_to_all | solution.py:520
  40.9 0.0 copy-done.1
  40.9 0.0 copy-done.3
  40.9 1.4 %first_sweep.1 = (f32[6,128,128]{2,1,0:T(8,128)S(1)}, f32[2,128,128]{2,1,0:T(8,128)S(1)}, f32[32,8,128]{2,1,0:T(8,128)S(1)}, f32[1,8,128]{2,1,0:T(8,128)S(1)}, f...) custom-call(s32[23]{0:T(128)S(1)} %concatenate.25.ints, ...), custom_call_target="tpu_custom_call" | custom-call | tf_op jit(solution)/shard_map/first_sweep/pallas_call | solution.py:460
  42.3 12.0 %all_to_all.41.arrived.chunks_in = f32[32,8,128]{2,1,0:T(8,128)S(1)} all-to-all(f32[32,8,128]{2,1,0:T(8,128)S(1)} %get-tuple-element.60), channel_id=1, replica_groups=mesh['patch'=2,'lat'=8,'lon'=16] {'patch','lon'}, dimensions={0} | all-to-all | bytes 262144 | tf_op jit(solution)/shard_map/all_to_all | solution.py:517
  54.2 0.6 pack.3
  54.8 12.5 %all_to_all.42.arrived = f32[8,5,8,128]{3,2,1,0:T(8,128)S(1)} all-to-all(f32[8,5,8,128]{3,2,1,0:T(8,128)S(1)} %pack.3), channel_id=1, replica_groups=mesh['patch'=2,'lat'=8,'lon'=16] {'lat'}, dimensions={0} | all-to-all | bytes 327680 | tf_op jit(solution)/shard_map/all_to_all | solution.py:520
  67.4 1.4 %sweep.2 = (f32[6,128,128]{2,1,0:T(8,128)S(1)}, f32[2,128,128]{2,1,0:T(8,128)S(1)}, f32[32,8,128]{2,1,0:T(8,128)S(1)}, f32[1,8,128]{2,1,0:T(8,128)S(1)}, f32[1,8,128]{2,1,0:T(8,128)S(1)}) custom-call(s32[23]{0:T(128)S(1)} %concatenate.25.ints, f32[6,128,128]{2,1,0:T(8,128)S(1)} %get-tuple-element.56.flow, f32[2,128,128]{2,1,0:T(8,128)S(1)} %get-tuple-element.57.pressure, ...), custom_call_target="tpu_custom_call" | custom-call | tf_op jit(solution)/shard_map/sweep/pallas_call | solution.py:460
  68.8 11.4 %all_to_all.43.arrived.chunks_in = f32[32,8,128]{2,1,0:T(8,128)S(1)} all-to-all(f32[32,8,128]{2,1,0:T(8,128)S(1)} %get-tuple-element.65), channel_id=1, replica_groups=mesh['patch'=2,'lat'=8,'lon'=16] {'patch','lon'}, dimensions={0} | all-to-all | bytes 262144 | tf_op jit(solution)/shard_map/all_to_all | solution.py:517
  80.2 0.6 pack.4
  80.8 12.5 %all_to_all.44.arrived = f32[8,5,8,128]{3,2,1,0:T(8,128)S(1)} all-to-all(f32[8,5,8,128]{3,2,1,0:T(8,128)S(1)} %pack.4), channel_id=1, replica_groups=mesh['patch'=2,'lat'=8,'lon'=16] {'lat'}, dimensions={0} | all-to-all | bytes 327680 | tf_op jit(solution)/shard_map/all_to_all | solution.py:520
  93.3 1.4 %sweep.3 = (f32[6,128,128]{2,1,0:T(8,128)S(1)}, f32[2,128,128]{2,1,0:T(8,128)S(1)}, f32[32,8,128]{2,1,0:T(8,128)S(1)}, f32[1,8,128]{2,1,0:T(8,128)S(1)}, f32[1,8,128]{2,1,0:T(8,128)S(1)}) custom-call(s32[23]{0:T(128)S(1)} %concatenate.25.ints, f32[6,128,128]{2,1,0:T(8,128)S(1)} %get-tuple-element.63.flow, f32[2,128,128]{2,1,0:T(8,128)S(1)} %get-tuple-element.64.pressure, ...), custom_call_target="tpu_custom_call" | custom-call | tf_op jit(solution)/shard_map/sweep/pallas_call | solution.py:460
  94.7 11.4 %all_to_all.45.arrived.chunks_in = f32[32,8,128]{2,1,0:T(8,128)S(1)} all-to-all(f32[32,8,128]{2,1,0:T(8,128)S(1)} %get-tuple-element.70), channel_id=1, replica_groups=mesh['patch'=2,'lat'=8,'lon'=16] {'patch','lon'}, dimensions={0} | all-to-all | bytes 262144 | tf_op jit(solution)/shard_map/all_to_all | solution.py:517
  106.1 0.6 pack.5
  106.7 12.5 %all_to_all.46.arrived = f32[8,5,8,128]{3,2,1,0:T(8,128)S(1)} all-to-all(f32[8,5,8,128]{3,2,1,0:T(8,128)S(1)} %pack.5), channel_id=1, replica_groups=mesh['patch'=2,'lat'=8,'lon'=16] {'lat'}, dimensions={0} | all-to-all | bytes 327680 | tf_op jit(solution)/shard_map/all_to_all | solution.py:520
  119.2 2.1 %final.1 = (f32[6,128,128]{2,1,0:T(8,128)}, f32[2,128,128]{2,1,0:T(8,128)}, f32[2,128,128]{2,1,0:T(8,128)}) custom-call(s32[23]{0:T(128)S(1)} %concatenate.25.ints, f32[6,128,128]{2,1,0:T(8,128)S(1)} %get-tuple-element.68.flow, f32[2,128,128]{2,1,0:T(8,128)S(1)} %get-tuple-element.69.pressure, f32[8,2,128,128]{3,2,1,0:T(8,128)S(1)} %coefficients.1.coef, ...), custom_call_target="tpu_custom_call" | custom-call | tf_op jit(solution)/shard_map/final/pallas_call | solution.py:460
  (3 shorter events, 0.0 us)
Async XLA Ops:
  21.6 9.2 %copy-start = (f32[1,2,128,128]{3,2,1,0:T(8,128)S(1)}, f32[1,2,128,128]{3,2,1,0:T(8,128)}, u32[]{:S(2)}) copy-start(f32[1,2,128,128]{3,2,1,0:T(8,128)} %param.10) | copy-start | bytes 393220
  21.6 9.2 %copy-start.2 = (f32[1,2,128,128]{3,2,1,0:T(8,128)S(1)}, f32[1,2,128,128]{3,2,1,0:T(8,128)}, u32[]{:S(2)}) copy-start(f32[1,2,128,128]{3,2,1,0:T(8,128)} %param.11) | copy-start | bytes 393220
  21.6 19.3 %all-to-all-start.1 = ((f32[8,7,8,128]{3,2,1,0:T(8,128)}), f32[8,7,8,128]{3,2,1,0:T(8,128)S(1)}, u32[]{:S(2)}, u32[]{:S(2)}) async-start(f32[8,7,8,128]{3,2,1,0:T(8,128)} %sort.1), calls=%async_computation.1 | async-start | bytes 458752 | tf_op jit(solution)/shard_map/all_to_all | solution.py:520
  31.6 9.3 %copy-start.1 = (f32[3,1,2,128,128]{4,3,2,1,0:T(8,128)S(1)}, f32[3,1,2,128,128]{4,3,2,1,0:T(8,128)}, u32[]{:S(2)}) copy-start(f32[3,1,2,128,128]{4,3,2,1,0:T(8,128)} %param.8) | copy-start | bytes 1179652
  31.6 9.3 %copy-start.3 = (f32[1,2,128,128]{3,2,1,0:T(8,128)S(1)}, f32[1,2,128,128]{3,2,1,0:T(8,128)}, u32[]{:S(2)}) copy-start(f32[1,2,128,128]{3,2,1,0:T(8,128)} %param.9) | copy-start | bytes 393220

commit v14 on v11

--- a/solution.py
+++ b/solution.py
@@ -85,8 +85,8 @@
 
 
 def start_kernel(
-    ints, slots, flow, pressure, heat, friction,
-    chunks, north, south, places, own, named, row, cols_s, rows_s, sems,
+    ints, slots, flow, pressure, heat, friction, weights,
+    chunks, north, south, places, high, low, own, named, row, chosen, cols_s, rows_s, sems,
 ):
     copies = Copies(sems)
     copies.start(slots, named)
@@ -94,6 +94,8 @@
     copies.start(heat, own.at[8:10])
     copies.start(pressure, own.at[6:8])
     copies.start(flow, own.at[0:6])
+    copies.start(weights.at[pl.ds(ints[LAT_BASE], 2)], chosen.at[0:2])
+    copies.start(weights.at[pl.ds(ints[LON_BASE], 2)], chosen.at[2:4])
     row[8:16, :] = jnp.broadcast_to((ints[RECEIVER] + 1).astype(F32), (8, CELLS))
     chunks[...] = jnp.zeros(chunks.shape, F32)
     north[...] = jnp.zeros(north.shape, F32)
@@ -119,12 +121,17 @@
 
     copies.wait(1, 4)
     collect(6, PLANES)
-    copies.wait(4)
+    copies.wait(4, 5)
     collect(0, 6)
     rows_s[...] = cols_s[...].T
     chunks[ints[CHUNK]] = row[...]
     chunks[ints[TO_WEST]] = rows_s[every_second(1, 16), :]
     chunks[ints[TO_EAST]] = rows_s[every_second(0, 16), :]
+    copies.wait(5)
+    for side in range(2):
+        for term in range(2):
+            cut = slice(term * CELLS, (term + 1) * CELLS)
+            high[side, :, cut], low[side, :, cut] = split(chosen[2 * side + term])
 
 
 def pack_kernel(table, arrived, north, south, out):
@@ -151,7 +158,9 @@
             act(lat, slot, ints[OTHER] + n)
 
 
-def table_kernel(ints, sent_to, table, filled):
+def sort_kernel(ints, sent_to, arrived, north, south, out, table, filled):
+    lats, count = out.shape[0], out.shape[1]
+    out[...] = jnp.zeros(out.shape, F32)
     table[0] = ints[FROM_NORTH]
     table[1] = ints[FROM_SOUTH]
     for n in range(2, table.shape[0]):
@@ -159,15 +168,6 @@
 
     def act(lat, slot, block):
         table[2 + SLOTS * lat + slot] = block
-
-    for_each_block(ints, sent_to, filled, (table.shape[0] - 2) // SLOTS, act)
-
-
-def sort_kernel(ints, sent_to, arrived, north, south, out, filled):
-    lats, count = out.shape[0], out.shape[1]
-    out[...] = jnp.zeros(out.shape, F32)
-
-    def act(lat, slot, block):
         out[lat, slot] = arrived[block, 0:8, :]
         for k in range(2):
             to = pl.ds(2 * slot + k, 1)
@@ -186,17 +186,6 @@
 
 def times(left, right):
     return lax.dot_general(left, right, (((1,), (1,)), ((), ())), preferred_element_type=F32)
-
-
-def weights_kernel(ints, weights, high, low, chosen, sems):
-    copies = Copies(sems)
-    copies.start(weights.at[pl.ds(ints[LAT_BASE], 2)], chosen.at[0:2])
-    copies.start(weights.at[pl.ds(ints[LON_BASE], 2)], chosen.at[2:4])
-    copies.wait()
-    for side in range(2):
-        for term in range(2):
-            cut = slice(term * CELLS, (term + 1) * CELLS)
-            high[side, :, cut], low[side, :, cut] = split(chosen[2 * side + term])
 
 
 def blend(blocks_of, high, low, ghosts):
@@ -247,30 +236,13 @@
         put(7, k, 0.125 * here)
 
 
-def coefficient_kernel(ints, friction, heat, chunks, out, cols_s, rows_s):
-    west, east = chunks[ints[TO_WEST], 8:16, :], chunks[ints[TO_EAST], 8:16, :]
-    ghost_columns(west, east, rows_s, cols_s)
-    for b in range(1, TILES - 1):
-
-        def put(n, k, value):
-            out[n, k, tile(b), :] = value
-
-        coefficients(ints, friction, heat, (None, None), (None, None), cols_s[tile(b), :], 2, b, put)
-    for b in (0, TILES - 1):
-        for n in range(8):
-            for k in range(2):
-                out[n, k, tile(b), :] = jnp.zeros((8, CELLS), F32)
-
-
-def relaxed(planes, coef, ends, ghosts, column, b):
+def relaxed(planes, coef, ghosts, column, b):
     at = [
         around(planes(f), b, ghosts[0, f : f + 1, :], ghosts[1, f : f + 1, :], column, f)
         for f in range(8)
     ]
 
     def factor(n, k):
-        if b == 0 or b == TILES - 1:
-            return ends[n, k, tile(0 if b == 0 else 1), :]
         return coef[n, k, tile(b), :]
 
     new = []
@@ -316,8 +288,8 @@
 
 
 def first_kernel(
-    ints, flow, pressure, coef, friction, heat, arrived, chunks_in, high, low,
-    flow_out, pressure_out, chunks, north, south, ends, heat_ghosts,
+    ints, flow, pressure, friction, heat, arrived, chunks_in, high, low,
+    flow_out, pressure_out, chunks, north, south, coef, heat_ghosts,
     sides, ghosts, cols_s, rows_s, edge_s, halos,
 ):
     rows_s[every_second(17), :] = chunks_in[ints[TO_WEST], 8:16, :]
@@ -328,32 +300,32 @@
         heat_ghosts[n] = found[n]
     halos[0] = arrived[ints[FROM_NORTH], SLOTS + 1]
     halos[1] = arrived[ints[FROM_SOUTH], SLOTS + 1]
-    for end, b in enumerate((0, TILES - 1)):
+    lines = [[halos[side, 2 + k : 3 + k, :] for k in range(2)] for side in range(2)]
+    for b in range(TILES):
 
         def put(n, k, value):
-            ends[n, k, tile(end), :] = value
-
-        lines = [[halos[side, 2 + k : 3 + k, :] for k in range(2)] for side in range(2)]
+            coef[n, k, tile(b), :] = value
+
         coefficients(ints, friction, heat, *lines, cols_s[tile(b), :], 10, b, put)
     sweep(
-        ints, flow, pressure, coef, ends, ghosts, cols_s, rows_s, edge_s,
+        ints, flow, pressure, coef, ghosts, cols_s, rows_s, edge_s,
         flow_out, pressure_out, chunks, north, south,
     )
 
 
 def sweep_kernel(
-    ints, flow, pressure, coef, ends, arrived, chunks_in, high, low,
+    ints, flow, pressure, coef, arrived, chunks_in, high, low,
     flow_out, pressure_out, chunks, north, south, sides, ghosts, cols_s, rows_s, edge_s,
 ):
     fill_ghosts(ints, arrived, chunks_in, high, low, sides, ghosts, cols_s, rows_s)
     sweep(
-        ints, flow, pressure, coef, ends, ghosts, cols_s, rows_s, edge_s,
+        ints, flow, pressure, coef, ghosts, cols_s, rows_s, edge_s,
         flow_out, pressure_out, chunks, north, south,
     )
 
 
 def sweep(
-    ints, flow, pressure, coef, ends, ghosts, cols_s, rows_s, edge_s,
+    ints, flow, pressure, coef, ghosts, cols_s, rows_s, edge_s,
     flow_out, pressure_out, chunks, north, south,
 ):
     def planes(f):
@@ -364,7 +336,7 @@
 
     chunks[...] = jnp.zeros(chunks.shape, F32)
     for b in range(TILES):
-        new = relaxed(planes, coef, ends, ghosts, cols_s[tile(b), :], b)
+        new = relaxed(planes, coef, ghosts, cols_s[tile(b), :], b)
         for f in range(8):
             planes_out(f)[tile(b), :] = new[f]
     for b in range(TILES):
@@ -384,7 +356,7 @@
 
 
 def final_kernel(
-    ints, flow, pressure, coef, ends, arrived, chunks_in, high, low, heat, heat_ghosts,
+    ints, flow, pressure, coef, arrived, chunks_in, high, low, heat, heat_ghosts,
     flow_out, pressure_out, heat_out,
     sides, ghosts, cols_s, rows_s, heat_cols_s, answer, warm, sems,
 ):
@@ -394,7 +366,7 @@
     ghost_columns(heat_ghosts[2], heat_ghosts[3], rows_s, heat_cols_s)
     fill_ghosts(ints, arrived, chunks_in, high, low, sides, ghosts, cols_s, rows_s)
     for b in range(TILES):
-        new = relaxed(planes, coef, ends, ghosts, cols_s[tile(b), :], b)
+        new = relaxed(planes, coef, ghosts, cols_s[tile(b), :], b)
         for f in range(8):
             answer[f, tile(b), :] = new[f]
     copies = Copies(sems)
@@ -502,14 +474,16 @@
 
     square = scratch(CELLS, CELLS)
     tiles = 2 * n_lon
-    chunks, north, south, places = call(
+    joined = jax.ShapeDtypeStruct((2, CELLS, 2 * CELLS), jnp.bfloat16)
+    chunks, north, south, places, high, low = call(
         start_kernel,
-        [shape(tiles, 16, CELLS), shape(2, 8, CELLS), shape(2, 8, CELLS), shape(8, CELLS)],
-        (first, shift_filled_by_lane.reshape(1, CELLS), flow, pressure, heat, friction),
+        [shape(tiles, 16, CELLS), shape(2, 8, CELLS), shape(2, 8, CELLS), shape(8, CELLS)]
+        + [joined, joined],
+        (first, shift_filled_by_lane.reshape(1, CELLS), flow, pressure, heat, friction, weights),
         [scratch(PLANES, CELLS, CELLS), pltpu.VMEM((1, CELLS), jnp.int32), scratch(16, CELLS)]
-        + [square, square, semaphores(5)],
+        + [scratch(4, CELLS, CELLS), square, square, semaphores(7)],
         "start",
-        specs=[SMEM] + [HBM] * 5,
+        specs=[SMEM] + [HBM] * 6,
         pin=(0,),
     )
 
@@ -524,30 +498,6 @@
     )
     sent_to = lax.dynamic_slice(came, (other, 8, 0), (n_lon, 1, 1)).reshape(n_lon)
     sent_to = sent_to.astype(jnp.int32) - 1
-    (packed,) = call(
-        sort_kernel,
-        [shape(n_lat, SLOTS + 3, 8, CELLS)],
-        (first, sent_to, came, north, south),
-        [pltpu.SMEM((n_lat,), jnp.int32)],
-        "sort",
-        specs=[SMEM, SMEM, VMEM, VMEM, VMEM],
-        keep=(2,),
-        pin=(0,),
-    )
-    packed, places = lax.optimization_barrier((packed, places))
-    arrived = along(packed)
-
-    (table,) = call(
-        table_kernel,
-        [jax.ShapeDtypeStruct((2 + n_lat * SLOTS,), jnp.int32)],
-        lax.optimization_barrier((first, sent_to, packed))[:2],
-        [pltpu.SMEM((n_lat,), jnp.int32)],
-        "table",
-        specs=[SMEM, SMEM],
-        out_specs=[SMEM],
-    )
-    arrived, table = lax.optimization_barrier((arrived, table))
-
     own = places[:, 0].astype(jnp.int32) - 1
     pick = jnp.concatenate(
         [jnp.where(lat > 0, own[2:4], own[0:2]), jnp.where(lon > 0, own[6:8], own[4:6])]
@@ -557,47 +507,46 @@
     ints = [first, jnp.maximum(pick, 0) // n_lon, jnp.minimum(slot, SLOTS - 1)]
     ints = jnp.concatenate(ints).astype(jnp.int32)
 
-    joined = jax.ShapeDtypeStruct((2, CELLS, 2 * CELLS), jnp.bfloat16)
-    high, low = call(
-        weights_kernel,
-        [joined, joined],
-        (ints, weights),
-        [scratch(4, CELLS, CELLS), semaphores(2)],
-        "weights",
-        specs=[SMEM, HBM],
-    )
-    (coef,) = call(
-        coefficient_kernel,
-        [shape(8, 2, CELLS, CELLS)],
-        (ints, friction, heat, came),
-        [square, square],
-        "coefficients",
-        keep=(3,),
-    )
+    packed, table = call(
+        sort_kernel,
+        [
+            shape(n_lat, SLOTS + 3, 8, CELLS),
+            jax.ShapeDtypeStruct((2 + n_lat * SLOTS,), jnp.int32),
+        ],
+        (ints, sent_to, came, north, south),
+        [pltpu.SMEM((n_lat,), jnp.int32)],
+        "sort",
+        specs=[SMEM, SMEM, VMEM, VMEM, VMEM],
+        out_specs=[VMEM, SMEM],
+        keep=(2,),
+        pin=(0,),
+    )
+    arrived = along(packed)
+
     sides, ghosts = scratch(2, 8, CELLS), scratch(4, 8, CELLS)
     state = [shape(6, CELLS, CELLS), shape(2, CELLS, CELLS)]
     for sweep in range(SWEEPS - 1):
         outs = state + [shape(tiles, 8, CELLS), shape(1, 8, CELLS), shape(1, 8, CELLS)]
         if sweep == 0:
-            flow, pressure, chunks, north, south, ends, heat_ghosts = call(
+            flow, pressure, chunks, north, south, coef, heat_ghosts = call(
                 first_kernel,
-                outs + [shape(8, 2, 16, CELLS), shape(4, 8, CELLS)],
-                (ints, flow, pressure, coef, friction, heat, arrived, came, high, low),
+                outs + [shape(8, 2, CELLS, CELLS), shape(4, 8, CELLS)],
+                (ints, flow, pressure, friction, heat, arrived, came, high, low),
                 [scratch(2, 16, CELLS), ghosts, square, square, square, scratch(2, 8, CELLS)],
                 "first_sweep",
                 limit=8,
-                keep=(3, 6, 7, 8, 9),
+                keep=(5, 6, 7, 8),
                 pin=(2,),
             )
         else:
             flow, pressure, chunks, north, south = call(
                 sweep_kernel,
                 outs,
-                (ints, flow, pressure, coef, ends, arrived, came, high, low),
+                (ints, flow, pressure, coef, arrived, came, high, low),
                 [sides, ghosts, square, square, square],
                 "sweep",
                 limit=8,
-                keep=(3, 4, 5, 6, 7, 8),
+                keep=(3, 4, 5, 6, 7),
                 pin=(2,),
             )
         came = across(chunks)
@@ -614,13 +563,13 @@
     flow, pressure, heat = call(
         final_kernel,
         state + [shape(2, CELLS, CELLS)],
-        (ints, flow, pressure, coef, ends, arrived, came, high, low, heat, heat_ghosts),
+        (ints, flow, pressure, coef, arrived, came, high, low, heat, heat_ghosts),
         [sides, ghosts, square, square, square]
         + [scratch(8, CELLS, CELLS), scratch(2, CELLS, CELLS), semaphores(3)],
         "final",
         out_specs=[HBM] * 3,
         limit=8,
-        keep=(1, 2, 3, 4, 5, 6, 7, 8),
+        keep=(1, 2, 3, 4, 5, 6, 7),
     )
     return flow.reshape(3, 1, 2, CELLS, CELLS), pressure[None], heat[None]
 

time: 122 us -> 123 us (level)
  blocking collectives: 87.7 us -> 107 us
  starting transfers between devices: 8.61 us -> 0 us
  waiting for transfers between devices: 6.4 us -> 0 us
  Pallas kernels: 15.2 us -> 11.8 us
    all_to_all x3 -> x4, blocking collectives: 37.6 us -> 56.7 us  [along(): return lax.all_to_all(packed, 'lat', 0, 0, tiled=True)]
    all_to_all x1 -> x0, starting transfers between devices: 8.61 us -> none  [along(): return lax.all_to_all(packed, 'lat', 0, 0, tiled=True)]
    all_to_all x1 -> x0, waiting for transfers between devices: 6.4 us -> none  [along(): return lax.all_to_all(packed, 'lat', 0, 0, tiled=True)]
    pallas_call x12 -> x9, Pallas kernels: 15.2 us -> 11.8 us  [call(): pl.pallas_call(kernel, out_shape=outs, in_specs=specs, out_specs=out_spec...]
  transfers between devices with their start and end apart: 1 -> 0, of which waited for: 1 -> 0; matrix products, arithmetic and copies ran while one was open for 0% -> 0% of each run, Pallas kernels for 3% -> 0%
where the time goes in v14:
time: 123 us; the launch traced here: 122 us
  blocking collectives  107 us (87%)
  Pallas kernels  11.8 us (10%)
  between operations  2.08 us (2%)
    all_to_all x4, blocking collectives, along(): return lax.all_to_all(packed, 'lat', 0, 0, tiled=True)  56.7 us
    all_to_all x4, blocking collectives, across(): return lax.all_to_all(chunks, ('patch', 'lon'), 0, 0, tiled=True)  50.1 us
    pallas_call x9, Pallas kernels, call(): pl.pallas_call(kernel, out_shape=outs, in_specs=specs, out_specs=out_spec...  11.8 us

profile of v14, /device:TPU:2, one launch (start us, length us, event | category | flops | bytes accessed | tf_op | source)
XLA Modules:
  0.0 121.9 jit_solution(16841381095802259907)
XLA Ops:
  2.0 0.1 add_add_fusion
  2.0 0.1 add_convert_fusion
  2.1 0.1 concatenate.23.ints
  2.2 2.1 %start.1 = (f32[32,16,128]{2,1,0:T(8,128)S(1)}, f32[2,8,128]{2,1,0:T(8,128)S(1)}, f32[2,8,128]{2,1,0:T(8,128)S(1)}, f32[8,128]{1,0:T(8,128)S(1)}, bf16[2,128,256...) custom-call(s32[15]{0:T(128)S(1)} %concatenate.23.ints, s32[1,128]{1,0:T(1,128)} %bitcast.40, ...), custom_call_target="tpu_custom_call" | custom-call | tf_op jit(solution)/shard_map/start/pallas_call | solution.py:432
  4.3 15.3 %all_to_all.40.arrived.chunks_in = f32[32,16,128]{2,1,0:T(8,128)S(1)} all-to-all(f32[32,16,128]{2,1,0:T(8,128)S(1)} %get-tuple-element.36), channel_id=1, replica_groups=mesh['patch'=2,'lat'=8,'lon'=16] {'patch','lon'}, dimensions={0} | all-to-all | bytes 524288 | tf_op jit(solution)/shard_map/all_to_all | solution.py:491
  19.6 0.1 fusion
  19.8 0.1 select_reduce_fusion.1
  19.9 0.0 copy-start
  19.9 0.1 and_select_fusion
  20.0 0.2 convert_reduce_fusion
  20.2 0.4 add_reduce_fusion.sent_to
  20.6 0.1 concatenate.25.ints
  20.7 1.4 %sort.1 = (f32[8,7,8,128]{3,2,1,0:T(8,128)S(1)}, s32[34]{0:T(128)S(1)}) custom-call(s32[23]{0:T(128)S(1)} %concatenate.25.ints, s32[16]{0:T(128)S(1)} %add_reduce_fusion.sent_to, f32[32,16,128]{2,1,0:T(8,128)S(1)} %all_to_all.40.arrived.chunks_in, f32[2,8,128]{2,1,0:T(8,128)S(1)} %get-tuple-element.43.north, f32[2,8,128]{2,1,0:T(8,128)S(1)} %get-tuple-element.44.south), custom_call_target="tpu_custom_call" | custom-call | tf_op jit(solution)/shard_map/sort/pallas_call | solution.py:432
  22.1 0.0 copy-start.1
  22.1 0.0 copy-start.2
  22.1 0.0 copy-start.3
  22.1 19.1 %all_to_all.41.arrived = f32[8,7,8,128]{3,2,1,0:T(8,128)S(1)} all-to-all(f32[8,7,8,128]{3,2,1,0:T(8,128)S(1)} %get-tuple-element.45), channel_id=1, replica_groups=mesh['patch'=2,'lat'=8,'lon'=16] {'lat'}, dimensions={0} | all-to-all | bytes 458752 | tf_op jit(solution)/shard_map/all_to_all | solution.py:494
  41.2 0.0 copy-done
  41.2 0.0 copy-done.1
  41.2 0.0 copy-done.2
  41.2 0.0 copy-done.3
  41.2 1.6 %first_sweep.1 = (f32[6,128,128]{2,1,0:T(8,128)S(1)}, f32[2,128,128]{2,1,0:T(8,128)S(1)}, f32[32,8,128]{2,1,0:T(8,128)S(1)}, f32[1,8,128]{2,1,0:T(8,128)S(1)}, f...) custom-call(s32[23]{0:T(128)S(1)} %concatenate.25.ints, ...), custom_call_target="tpu_custom_call" | custom-call | tf_op jit(solution)/shard_map/first_sweep/pallas_call | solution.py:432
  42.8 12.0 %all_to_all.42.arrived.chunks_in = f32[32,8,128]{2,1,0:T(8,128)S(1)} all-to-all(f32[32,8,128]{2,1,0:T(8,128)S(1)} %get-tuple-element.52), channel_id=1, replica_groups=mesh['patch'=2,'lat'=8,'lon'=16] {'patch','lon'}, dimensions={0} | all-to-all | bytes 262144 | tf_op jit(solution)/shard_map/all_to_all | solution.py:491
  54.8 0.6 pack.3
  55.4 12.5 %all_to_all.43.arrived = f32[8,5,8,128]{3,2,1,0:T(8,128)S(1)} all-to-all(f32[8,5,8,128]{3,2,1,0:T(8,128)S(1)} %pack.3), channel_id=1, replica_groups=mesh['patch'=2,'lat'=8,'lon'=16] {'lat'}, dimensions={0} | all-to-all | bytes 327680 | tf_op jit(solution)/shard_map/all_to_all | solution.py:494
  67.9 1.4 %sweep.2 = (f32[6,128,128]{2,1,0:T(8,128)S(1)}, f32[2,128,128]{2,1,0:T(8,128)S(1)}, f32[32,8,128]{2,1,0:T(8,128)S(1)}, f32[1,8,128]{2,1,0:T(8,128)S(1)}, f32[1,8,128]{2,1,0:T(8,128)S(1)}) custom-call(s32[23]{0:T(128)S(1)} %concatenate.25.ints, f32[6,128,128]{2,1,0:T(8,128)S(1)} %get-tuple-element.48.flow, f32[2,128,128]{2,1,0:T(8,128)S(1)} %get-tuple-element.49.pressure, ...), custom_call_target="tpu_custom_call" | custom-call | tf_op jit(solution)/shard_map/sweep/pallas_call | solution.py:432
  69.3 11.4 %all_to_all.44.arrived.chunks_in = f32[32,8,128]{2,1,0:T(8,128)S(1)} all-to-all(f32[32,8,128]{2,1,0:T(8,128)S(1)} %get-tuple-element.57), channel_id=1, replica_groups=mesh['patch'=2,'lat'=8,'lon'=16] {'patch','lon'}, dimensions={0} | all-to-all | bytes 262144 | tf_op jit(solution)/shard_map/all_to_all | solution.py:491
  80.7 0.6 pack.4
  81.3 12.5 %all_to_all.45.arrived = f32[8,5,8,128]{3,2,1,0:T(8,128)S(1)} all-to-all(f32[8,5,8,128]{3,2,1,0:T(8,128)S(1)} %pack.4), channel_id=1, replica_groups=mesh['patch'=2,'lat'=8,'lon'=16] {'lat'}, dimensions={0} | all-to-all | bytes 327680 | tf_op jit(solution)/shard_map/all_to_all | solution.py:494
  93.9 1.4 %sweep.3 = (f32[6,128,128]{2,1,0:T(8,128)S(1)}, f32[2,128,128]{2,1,0:T(8,128)S(1)}, f32[32,8,128]{2,1,0:T(8,128)S(1)}, f32[1,8,128]{2,1,0:T(8,128)S(1)}, f32[1,8,128]{2,1,0:T(8,128)S(1)}) custom-call(s32[23]{0:T(128)S(1)} %concatenate.25.ints, f32[6,128,128]{2,1,0:T(8,128)S(1)} %get-tuple-element.55.flow, f32[2,128,128]{2,1,0:T(8,128)S(1)} %get-tuple-element.56.pressure, ...), custom_call_target="tpu_custom_call" | custom-call | tf_op jit(solution)/shard_map/sweep/pallas_call | solution.py:432
  95.3 11.4 %all_to_all.46.arrived.chunks_in = f32[32,8,128]{2,1,0:T(8,128)S(1)} all-to-all(f32[32,8,128]{2,1,0:T(8,128)S(1)} %get-tuple-element.62), channel_id=1, replica_groups=mesh['patch'=2,'lat'=8,'lon'=16] {'patch','lon'}, dimensions={0} | all-to-all | bytes 262144 | tf_op jit(solution)/shard_map/all_to_all | solution.py:491
  106.7 0.6 pack.5
  107.3 12.5 %all_to_all.47.arrived = f32[8,5,8,128]{3,2,1,0:T(8,128)S(1)} all-to-all(f32[8,5,8,128]{3,2,1,0:T(8,128)S(1)} %pack.5), channel_id=1, replica_groups=mesh['patch'=2,'lat'=8,'lon'=16] {'lat'}, dimensions={0} | all-to-all | bytes 327680 | tf_op jit(solution)/shard_map/all_to_all | solution.py:494
  119.8 2.1 %final.1 = (f32[6,128,128]{2,1,0:T(8,128)}, f32[2,128,128]{2,1,0:T(8,128)}, f32[2,128,128]{2,1,0:T(8,128)}) custom-call(s32[23]{0:T(128)S(1)} %concatenate.25.ints, f32[6,128,128]{2,1,0:T(8,128)S(1)} %get-tuple-element.60.flow, f32[2,128,128]{2,1,0:T(8,128)S(1)} %get-tuple-element.61.pressure, f32[8,2,128,128]{3,2,1,0:T(8,128)S(1)} %get-tuple-element.50.coef, ...), custom_call_target="tpu_custom_call" | custom-call | tf_op jit(solution)/shard_map/final/pallas_call | solution.py:432
  (3 shorter events, 0.0 us)
Async XLA Ops:
  19.9 21.3 %copy-start = (f32[3,1,2,128,128]{4,3,2,1,0:T(8,128)S(1)}, f32[3,1,2,128,128]{4,3,2,1,0:T(8,128)}, u32[]{:S(2)}) copy-start(f32[3,1,2,128,128]{4,3,2,1,0:T(8,128)} %param.8) | copy-start | bytes 1179652
  22.1 19.1 %copy-start.1 = (f32[1,2,128,128]{3,2,1,0:T(8,128)S(1)}, f32[1,2,128,128]{3,2,1,0:T(8,128)}, u32[]{:S(2)}) copy-start(f32[1,2,128,128]{3,2,1,0:T(8,128)} %param.10) | copy-start | bytes 393220
  22.1 19.1 %copy-start.2 = (f32[1,2,128,128]{3,2,1,0:T(8,128)S(1)}, f32[1,2,128,128]{3,2,1,0:T(8,128)}, u32[]{:S(2)}) copy-start(f32[1,2,128,128]{3,2,1,0:T(8,128)} %param.9) | copy-start | bytes 393220
  22.1 19.1 %copy-start.3 = (f32[1,2,128,128]{3,2,1,0:T(8,128)S(1)}, f32[1,2,128,128]{3,2,1,0:T(8,128)}, u32[]{:S(2)}) copy-start(f32[1,2,128,128]{3,2,1,0:T(8,128)} %param.11) | copy-start | bytes 393220

commit v15 on v11

--- a/solution.py
+++ b/solution.py
@@ -167,13 +167,22 @@
     lats, count = out.shape[0], out.shape[1]
     out[...] = jnp.zeros(out.shape, F32)
 
-    def act(lat, slot, block):
-        out[lat, slot] = arrived[block, 0:8, :]
+    sources = sent_to.shape[0]
+    for lat in range(lats):
+        filled[lat] = 0
+    for n in range(sources):
+        number = sent_to[n]
+        lat = jnp.maximum(number, 0) // sources
+        here = (number >= 0) & (number == lat * sources + ints[LON])
+        slot = filled[lat]
+        filled[lat] = slot + here.astype(jnp.int32)
+        block = ints[OTHER] + n
+        out[lat, jnp.where(here, slot, SLOTS)] = arrived[block, 0:8, :]
+        warm = jnp.where(here, count - 1, SLOTS + 1)
+        row = jnp.where(here, 2 * slot, 0)
         for k in range(2):
-            to = pl.ds(2 * slot + k, 1)
-            out[lat, count - 1, to, :] = arrived[block, 9 + k : 10 + k, :]
-
-    for_each_block(ints, sent_to, filled, lats, act)
+            out[lat, warm, pl.ds(row + k, 1), :] = arrived[block, 9 + k : 10 + k, :]
+
     for n in range(north.shape[0]):
         out[ints[FROM_NORTH], SLOTS + n] = north[n]
         out[ints[FROM_SOUTH], SLOTS + n] = south[n]

time: 122 us -> 122 us (level)
  no operation moved by 1% of the time
where the time goes in v15:
time: 122 us; the launch traced here: 121 us
  blocking collectives  87.7 us (72%)
  Pallas kernels  15.2 us (12%)
  starting transfers between devices  8.61 us (7%)
  waiting for transfers between devices  6.4 us (5%)
  between operations  2.09 us (2%)
    all_to_all x4, blocking collectives, across(): return lax.all_to_all(chunks, ('patch', 'lon'), 0, 0, tiled=True)  50.1 us
    all_to_all x3, blocking collectives, along(): return lax.all_to_all(packed, 'lat', 0, 0, tiled=True)  37.6 us
    pallas_call x12, Pallas kernels, call(): pl.pallas_call(kernel, out_shape=outs, in_specs=specs, out_specs=out_spec...  15.2 us
    all_to_all x1, starting transfers between devices, along(): return lax.all_to_all(packed, 'lat', 0, 0, tiled=True)  8.61 us
    all_to_all x1, waiting for transfers between devices, along(): return lax.all_to_all(packed, 'lat', 0, 0, tiled=True)  6.4 us
  transfers between devices with their start and end apart: 1, of which 1 were waited for; matrix products, arithmetic and copies ran while one was open for 0% of the time, Pallas kernels for 3%

profile of v15, /device:TPU:2, one launch (start us, length us, event | category | flops | bytes accessed | tf_op | source)
XLA Modules:
  0.0 121.2 jit_solution(8051487287957276073)
XLA Ops:
  2.0 0.1 add_add_fusion
  2.0 0.1 add_convert_fusion
  2.1 0.1 concatenate.23.ints
  2.2 2.1 %start.1 = (f32[32,16,128]{2,1,0:T(8,128)S(1)}, f32[2,8,128]{2,1,0:T(8,128)S(1)}, f32[2,8,128]{2,1,0:T(8,128)S(1)}, f32[8,128]{1,0:T(8,128)S(1)}) custom-call(s32[15]{0:T(128)S(1)} %concatenate.23.ints, s32[1,128]{1,0:T(1,128)} %bitcast.42, f32[6,128,128]{2,1,0:T(8,128)} %bitcast.34, f32[2,128,128]{2,1,0:T(8,128)} %bitcast.39, f32[2,128,128]{2,1,0:T(8,128)} %bitcast.30, ...), custom_call_target="tpu_custom_call" | custom-call | tf_op jit(solution)/shard_map/start/pallas_call | solution.py:469
  4.3 15.3 %all_to_all.40.arrived.chunks.chunks_in = f32[32,16,128]{2,1,0:T(8,128)S(1)} all-to-all(f32[32,16,128]{2,1,0:T(8,128)S(1)} %get-tuple-element.40), channel_id=1, replica_groups=mesh['patch'=2,'lat'=8,'lon'=16] {'patch','lon'}, dimensions={0} | all-to-all | bytes 524288 | tf_op jit(solution)/shard_map/all_to_all | solution.py:526
  19.6 0.4 add_reduce_fusion.sent_to
  19.9 1.4 %sort.1 = f32[8,7,8,128]{3,2,1,0:T(8,128)} custom-call(s32[15]{0:T(128)S(1)} %concatenate.23.ints, s32[16]{0:T(128)S(1)} %add_reduce_fusion.sent_to, f32[32,16,128]{2,1,0:T(8,128)S(1)} %all_to_all.40.arrived.chunks.chunks_in, f32[2,8,128]{2,1,0:T(8,128)S(1)} %get-tuple-element.45.north, f32[2,8,128]{2,1,0:T(8,128)S(1)} %get-tuple-element.46.south), custom_call_target="tpu_custom_call" | custom-call | tf_op jit(solution)/shard_map/sort/pallas_call | solution.py:469
  21.4 0.1 fusion
  21.5 0.0 copy-start
  21.5 0.0 copy-start.2
  21.5 8.6 %all-to-all-start.1 = ((f32[8,7,8,128]{3,2,1,0:T(8,128)}), f32[8,7,8,128]{3,2,1,0:T(8,128)S(1)}, u32[]{:S(2)}, u32[]{:S(2)}) async-start(f32[8,7,8,128]{3,2,1,0:T(8,128)} %sort.1), calls=%async_computation.1 | async-start | bytes 458752 | tf_op jit(solution)/shard_map/all_to_all | solution.py:529
  30.1 0.1 select_reduce_fusion.1
  30.3 0.1 and_select_fusion
  30.4 0.2 convert_reduce_fusion
  30.6 0.1 concatenate.25.ints
  30.7 0.0 copy-done
  30.7 0.0 copy-done.2
  30.7 0.8 coefficients.1.coef
  31.5 0.0 copy-start.1
  31.5 0.0 copy-start.3
  31.5 1.6 %weights.1 = (bf16[2,128,256]{2,1,0:T(8,128)(2,1)S(1)}, bf16[2,128,256]{2,1,0:T(8,128)(2,1)S(1)}) custom-call(s32[23]{0:T(128)S(1)} %concatenate.25.ints, f32[8,128,128]{2,1,0:T(8,128)} %bitcast.41), custom_call_target="tpu_custom_call" | custom-call | tf_op jit(solution)/shard_map/weights/pallas_call | solution.py:469
  33.1 1.3 %table.1 = s32[34]{0:T(128)S(1)} custom-call(s32[15]{0:T(128)S(1)} %concatenate.23.ints, s32[16]{0:T(128)S(1)} %add_reduce_fusion.sent_to), custom_call_target="tpu_custom_call" | custom-call | tf_op jit(solution)/shard_map/table/pallas_call | solution.py:469
  34.4 6.4 %all-to-all-done.1.arrived = f32[8,7,8,128]{3,2,1,0:T(8,128)S(1)} async-done(((f32[8,7,8,128]{3,2,1,0:T(8,128)}), f32[8,7,8,128]{3,2,1,0:T(8,128)S(1)}, u32[]{:S(2)}, u32[]{:S(2)}) %all-to-all-start.1) | async-done | bytes 229408 | tf_op jit(solution)/shard_map/all_to_all | solution.py:529
  40.8 0.0 copy-done.1
  40.8 0.0 copy-done.3
  40.8 1.4 %first_sweep.1 = (f32[6,128,128]{2,1,0:T(8,128)S(1)}, f32[2,128,128]{2,1,0:T(8,128)S(1)}, f32[32,8,128]{2,1,0:T(8,128)S(1)}, f32[1,8,128]{2,1,0:T(8,128)S(1)}, f...) custom-call(s32[23]{0:T(128)S(1)} %concatenate.25.ints, ...), custom_call_target="tpu_custom_call" | custom-call | tf_op jit(solution)/shard_map/first_sweep/pallas_call | solution.py:469
  42.2 12.0 %all_to_all.41.arrived.chunks_in = f32[32,8,128]{2,1,0:T(8,128)S(1)} all-to-all(f32[32,8,128]{2,1,0:T(8,128)S(1)} %get-tuple-element.60), channel_id=1, replica_groups=mesh['patch'=2,'lat'=8,'lon'=16] {'patch','lon'}, dimensions={0} | all-to-all | bytes 262144 | tf_op jit(solution)/shard_map/all_to_all | solution.py:526
  54.2 0.6 pack.3
  54.8 12.5 %all_to_all.42.arrived = f32[8,5,8,128]{3,2,1,0:T(8,128)S(1)} all-to-all(f32[8,5,8,128]{3,2,1,0:T(8,128)S(1)} %pack.3), channel_id=1, replica_groups=mesh['patch'=2,'lat'=8,'lon'=16] {'lat'}, dimensions={0} | all-to-all | bytes 327680 | tf_op jit(solution)/shard_map/all_to_all | solution.py:529
  67.3 1.4 %sweep.2 = (f32[6,128,128]{2,1,0:T(8,128)S(1)}, f32[2,128,128]{2,1,0:T(8,128)S(1)}, f32[32,8,128]{2,1,0:T(8,128)S(1)}, f32[1,8,128]{2,1,0:T(8,128)S(1)}, f32[1,8,128]{2,1,0:T(8,128)S(1)}) custom-call(s32[23]{0:T(128)S(1)} %concatenate.25.ints, f32[6,128,128]{2,1,0:T(8,128)S(1)} %get-tuple-element.56.flow, f32[2,128,128]{2,1,0:T(8,128)S(1)} %get-tuple-element.57.pressure, ...), custom_call_target="tpu_custom_call" | custom-call | tf_op jit(solution)/shard_map/sweep/pallas_call | solution.py:469
  68.7 11.4 %all_to_all.43.arrived.chunks_in = f32[32,8,128]{2,1,0:T(8,128)S(1)} all-to-all(f32[32,8,128]{2,1,0:T(8,128)S(1)} %get-tuple-element.65), channel_id=1, replica_groups=mesh['patch'=2,'lat'=8,'lon'=16] {'patch','lon'}, dimensions={0} | all-to-all | bytes 262144 | tf_op jit(solution)/shard_map/all_to_all | solution.py:526
  80.1 0.6 pack.4
  80.7 12.5 %all_to_all.44.arrived = f32[8,5,8,128]{3,2,1,0:T(8,128)S(1)} all-to-all(f32[8,5,8,128]{3,2,1,0:T(8,128)S(1)} %pack.4), channel_id=1, replica_groups=mesh['patch'=2,'lat'=8,'lon'=16] {'lat'}, dimensions={0} | all-to-all | bytes 327680 | tf_op jit(solution)/shard_map/all_to_all | solution.py:529
  93.2 1.4 %sweep.3 = (f32[6,128,128]{2,1,0:T(8,128)S(1)}, f32[2,128,128]{2,1,0:T(8,128)S(1)}, f32[32,8,128]{2,1,0:T(8,128)S(1)}, f32[1,8,128]{2,1,0:T(8,128)S(1)}, f32[1,8,128]{2,1,0:T(8,128)S(1)}) custom-call(s32[23]{0:T(128)S(1)} %concatenate.25.ints, f32[6,128,128]{2,1,0:T(8,128)S(1)} %get-tuple-element.63.flow, f32[2,128,128]{2,1,0:T(8,128)S(1)} %get-tuple-element.64.pressure, ...), custom_call_target="tpu_custom_call" | custom-call | tf_op jit(solution)/shard_map/sweep/pallas_call | solution.py:469
  94.6 11.4 %all_to_all.45.arrived.chunks_in = f32[32,8,128]{2,1,0:T(8,128)S(1)} all-to-all(f32[32,8,128]{2,1,0:T(8,128)S(1)} %get-tuple-element.70), channel_id=1, replica_groups=mesh['patch'=2,'lat'=8,'lon'=16] {'patch','lon'}, dimensions={0} | all-to-all | bytes 262144 | tf_op jit(solution)/shard_map/all_to_all | solution.py:526
  106.0 0.6 pack.5
  106.6 12.5 %all_to_all.46.arrived = f32[8,5,8,128]{3,2,1,0:T(8,128)S(1)} all-to-all(f32[8,5,8,128]{3,2,1,0:T(8,128)S(1)} %pack.5), channel_id=1, replica_groups=mesh['patch'=2,'lat'=8,'lon'=16] {'lat'}, dimensions={0} | all-to-all | bytes 327680 | tf_op jit(solution)/shard_map/all_to_all | solution.py:529
  119.2 2.1 %final.1 = (f32[6,128,128]{2,1,0:T(8,128)}, f32[2,128,128]{2,1,0:T(8,128)}, f32[2,128,128]{2,1,0:T(8,128)}) custom-call(s32[23]{0:T(128)S(1)} %concatenate.25.ints, f32[6,128,128]{2,1,0:T(8,128)S(1)} %get-tuple-element.68.flow, f32[2,128,128]{2,1,0:T(8,128)S(1)} %get-tuple-element.69.pressure, f32[8,2,128,128]{3,2,1,0:T(8,128)S(1)} %coefficients.1.coef, ...), custom_call_target="tpu_custom_call" | custom-call | tf_op jit(solution)/shard_map/final/pallas_call | solution.py:469
  (3 shorter events, 0.0 us)
Async XLA Ops:
  21.5 9.2 %copy-start = (f32[1,2,128,128]{3,2,1,0:T(8,128)S(1)}, f32[1,2,128,128]{3,2,1,0:T(8,128)}, u32[]{:S(2)}) copy-start(f32[1,2,128,128]{3,2,1,0:T(8,128)} %param.10) | copy-start | bytes 393220
  21.5 9.2 %copy-start.2 = (f32[1,2,128,128]{3,2,1,0:T(8,128)S(1)}, f32[1,2,128,128]{3,2,1,0:T(8,128)}, u32[]{:S(2)}) copy-start(f32[1,2,128,128]{3,2,1,0:T(8,128)} %param.11) | copy-start | bytes 393220
  21.5 19.3 %all-to-all-start.1 = ((f32[8,7,8,128]{3,2,1,0:T(8,128)}), f32[8,7,8,128]{3,2,1,0:T(8,128)S(1)}, u32[]{:S(2)}, u32[]{:S(2)}) async-start(f32[8,7,8,128]{3,2,1,0:T(8,128)} %sort.1), calls=%async_computation.1 | async-start | bytes 458752 | tf_op jit(solution)/shard_map/all_to_all | solution.py:529
  31.5 9.3 %copy-start.1 = (f32[3,1,2,128,128]{4,3,2,1,0:T(8,128)S(1)}, f32[3,1,2,128,128]{4,3,2,1,0:T(8,128)}, u32[]{:S(2)}) copy-start(f32[3,1,2,128,128]{4,3,2,1,0:T(8,128)} %param.8) | copy-start | bytes 1179652
  31.5 9.3 %copy-start.3 = (f32[1,2,128,128]{3,2,1,0:T(8,128)S(1)}, f32[1,2,128,128]{3,2,1,0:T(8,128)}, u32[]{:S(2)}) copy-start(f32[1,2,128,128]{3,2,1,0:T(8,128)} %param.9) | copy-start | bytes 393220
